TPU v7x, 32 devices: a whole 2x2x4 slice. The times are simulated.
32 devices in a mesh: expert: 8 (over z, y), dp: 4 (over x, core).
Axes of the slice: x: 2, y: 2, z: 4, core: 2. Of those that a mesh axis runs over, the one named last changes fastest.
Arguments:
- prenorm_input: bfloat16 [4096, 1280], P(('expert', 'dp')), may hold values from -6 to 6
- gain: float32 [1280], replicated, may hold values from 0.25 to 1.75
- router: bfloat16 [1280, 4], replicated, may hold values from -0.15625 to 0.15625
- routes: int32 [4096, 2], P(('expert', 'dp')), may hold values from 0 to 3, all different within a row; in each aligned block of 128 rows (0 to 127, 128 to 255, ...) at most 80 rows name the same one
- w_in: bfloat16 [8, 1280, 1280], P('expert', None, 'dp'), may hold values from -0.15625 to 0.15625
- w_out: bfloat16 [8, 1280, 1280], P('expert', 'dp'), may hold values from -0.125 to 0.125
- cotangent: bfloat16 [4096, 1280], P(('expert', 'dp')), may hold values from -18 to 18
Outputs:
- input_grad: bfloat16 [4096, 1280], P(('expert', 'dp'))
- grad_in: bfloat16 [8, 1280, 1280], P('expert', None, 'dp')
- grad_out: bfloat16 [8, 1280, 1280], P('expert', 'dp')
- grad_router: float32 [1280, 4], replicated
- grad_gain: float32 [1280], replicated
Inputs may be any that keep to these rules, and one draw needn't show every extreme that they name: `routes`: each row names 2 different experts; among the rows of one device no expert is named more than 80 times.
All inputs are finite; a program needn't handle non-finite values.
Results may differ from a plain program's by a relative error of at most 0.015.
Values may be sent and summed in bfloat16 or wider, within the bound.
No kernel may reach another device: no remote copies, remote signals or barrier semaphores. Data moves between devices by JAX's collectives and lax.ppermute only.
A program may use at most 128 MiB of HBM per device.

v0:
```python
import math

import jax
import jax.numpy as jnp
from jax import lax
from jax.sharding import PartitionSpec as P


def gelu_parts(pre):
    coeff = math.sqrt(2.0 / math.pi)
    inner = coeff * (pre + 0.044715 * pre * pre * pre)
    tanh_val = jnp.tanh(inner)
    value = 0.5 * pre * (1.0 + tanh_val)
    slope = 0.5 * (1.0 + tanh_val) + 0.5 * pre * (1.0 - tanh_val * tanh_val) * coeff * (
        1.0 + 3.0 * 0.044715 * pre * pre
    )
    return (value, slope)


def norm_pieces(block, gain):
    values = block.astype(jnp.float32)
    centred_rows = values - jnp.mean(values, axis=1, keepdims=True)
    inverse_deviation = lax.rsqrt(
        jnp.mean(centred_rows * centred_rows, axis=1, keepdims=True) + 1e-06
    )
    normalized_rows = centred_rows * inverse_deviation
    return (
        normalized_rows,
        inverse_deviation,
        (normalized_rows * gain[None, :]).astype(jnp.bfloat16),
    )


def slot_index(routing_rows, expert_list, expert_capacity):
    flat = routing_rows.reshape(-1)
    onehot = (flat[:, None] == jnp.arange(expert_list, dtype=jnp.int32)[None, :]).astype(jnp.int32)
    before = jnp.cumsum(onehot, axis=0) - onehot
    slot = jnp.sum(before * onehot, axis=1)
    return flat * expert_capacity + slot


def expert_pass(rows_m, rows_d, column, w_first, w_second):
    gate = jax.nn.sigmoid(jnp.dot(rows_m, column, preferred_element_type=jnp.float32)[:, 0])
    pre = jnp.dot(rows_m, w_first, preferred_element_type=jnp.float32)
    value, slope = gelu_parts(pre)
    hidden = value.astype(jnp.bfloat16)
    back = jnp.dot(rows_d, w_second.T, preferred_element_type=jnp.float32)
    gate_gradient = jnp.sum(hidden.astype(jnp.float32) * back, axis=1)
    grad_pre = (gate[:, None] * back * slope).astype(jnp.bfloat16)
    grad_y = (gate[:, None] * rows_d.astype(jnp.float32)).astype(jnp.bfloat16)
    grad_second = jnp.dot(hidden.T, grad_y, preferred_element_type=jnp.float32)
    grad_first = jnp.dot(rows_m.T, grad_pre, preferred_element_type=jnp.float32)
    row_gradient = jnp.dot(grad_pre, w_first.T, preferred_element_type=jnp.float32)
    return (row_gradient, gate_gradient, grad_first, grad_second)


def body(prenorm_input, gain, router, routes, w_in, w_out, cotangent):
    halves = lax.axis_size("expert")
    expert_list = halves // 2
    groups = lax.axis_size("dp")
    tok_rows = prenorm_input.shape[0]
    top = routes.shape[1]
    width = prenorm_input.shape[1]
    expert_capacity = max(2, 5 * tok_rows * top // (4 * expert_list))
    slots = expert_list * expert_capacity
    hi = lax.Precision.HIGHEST
    normalized_rows, inverse_deviation, mixed_rows = norm_pieces(prenorm_input, gain)
    where = slot_index(routes, expert_list, expert_capacity)
    places = (where[None, :] == jnp.arange(slots, dtype=jnp.int32)[:, None]).astype(jnp.bfloat16)
    send_m = jnp.dot(
        places, jnp.repeat(mixed_rows, top, axis=0), preferred_element_type=jnp.float32
    ).astype(jnp.bfloat16)
    send_d = jnp.dot(
        places, jnp.repeat(cotangent, top, axis=0), preferred_element_type=jnp.float32
    ).astype(jnp.bfloat16)
    send_m = jnp.repeat(send_m.reshape(expert_list, expert_capacity, width), 2, axis=0)
    send_d = jnp.repeat(send_d.reshape(expert_list, expert_capacity, width), 2, axis=0)
    recv_m, recv_d = (
        lax.all_to_all(send_m, "expert", split_axis=0, concat_axis=0, tiled=True),
        lax.all_to_all(send_d, "expert", split_axis=0, concat_axis=0, tiled=True),
    )
    own = lax.axis_index("expert") // 2
    column = lax.dynamic_slice_in_dim(router, own, 1, 1)
    all_m, all_d = (
        lax.all_gather(recv_m[None], "dp", axis=0, tiled=True),
        lax.all_gather(recv_d[None], "dp", axis=0, tiled=True),
    )
    row_gradient, gate_gradient, grad_first, grad_second = expert_pass(
        all_m.reshape(-1, width), all_d.reshape(-1, width), column, w_in[0], w_out[0]
    )
    summed_rows, summed_gate = (
        lax.psum_scatter(
            row_gradient.reshape(groups, halves * expert_capacity, width).astype(jnp.bfloat16),
            "dp",
            scatter_dimension=0,
            tiled=True,
        ).astype(jnp.float32),
        lax.psum_scatter(
            gate_gradient.reshape(groups, halves * expert_capacity).astype(jnp.bfloat16),
            "dp",
            scatter_dimension=0,
            tiled=True,
        ).astype(jnp.float32),
    )
    back_rows = summed_rows[0].reshape(halves, expert_capacity, width)
    back_gate = summed_gate[0].reshape(halves, expert_capacity)
    grad_in = grad_first[None].astype(jnp.bfloat16)
    grad_out = grad_second[None].astype(jnp.bfloat16)
    ret_rows, ret_gate = (
        lax.all_to_all(
            back_rows.astype(jnp.bfloat16), "expert", split_axis=0, concat_axis=0, tiled=True
        ).astype(back_rows.dtype),
        lax.all_to_all(
            back_gate.astype(jnp.bfloat16), "expert", split_axis=0, concat_axis=0, tiled=True
        ).astype(back_gate.dtype),
    )
    pair_rows = jnp.sum(ret_rows.reshape(expert_list, 2, expert_capacity, width), axis=1).reshape(
        slots, width
    )
    pair_gate = jnp.sum(ret_gate.reshape(expert_list, 2, expert_capacity), axis=1).reshape(slots)
    grad_expert = jnp.sum(jnp.take(pair_rows, where, axis=0).reshape(tok_rows, top, width), axis=1)
    dgate_tok = jnp.take(pair_gate, where, axis=0).reshape(tok_rows, top)
    logits = jnp.dot(mixed_rows, router, preferred_element_type=jnp.float32)
    choose = (routes[:, :, None] == jnp.arange(expert_list, dtype=jnp.int32)[None, None, :]).astype(
        jnp.float32
    )
    gates = jax.nn.sigmoid(jnp.sum(choose * logits[:, None, :], axis=2))
    dlogit = jnp.sum(choose * (dgate_tok * gates * (1.0 - gates))[:, :, None], axis=1)
    mixed_gradient = grad_expert + jnp.dot(dlogit, router.astype(jnp.float32).T, precision=hi)
    router_term = jnp.dot(mixed_rows.astype(jnp.float32).T, dlogit, precision=hi)
    gain_product = jnp.sum(mixed_gradient * normalized_rows, axis=0)
    grad_router, grad_gain = lax.psum((router_term, gain_product), ("expert", "dp"))
    scaled_rows = mixed_gradient * gain[None, :]
    mean_first_term = jnp.mean(scaled_rows, axis=1, keepdims=True)
    mean_second_term = jnp.mean(scaled_rows * normalized_rows, axis=1, keepdims=True)
    norm_backward = inverse_deviation * (
        scaled_rows - mean_first_term - normalized_rows * mean_second_term
    )
    input_grad = (cotangent.astype(jnp.float32) + norm_backward).astype(jnp.bfloat16)
    return (input_grad, grad_in, grad_out, grad_router, grad_gain)


def solution(mesh):
    in_specs = (
        P(("expert", "dp"), None),
        P(),
        P(),
        P(("expert", "dp"), None),
        P("expert", None, "dp"),
        P("expert", "dp", None),
        P(("expert", "dp"), None),
    )
    out_specs = (
        P(("expert", "dp"), None),
        P("expert", None, "dp"),
        P("expert", "dp", None),
        P(),
        P(),
    )
    return jax.shard_map(body, mesh=mesh, in_specs=in_specs, out_specs=out_specs, check_vma=False)
```

profile of v0, /device:TPU:0, one launch (start us, length us, event | category | flops | bytes accessed | tf_op | source)
XLA Modules:
  0.0 331.4 jit_solution(14376887324306900459)
XLA Ops:
  9.5 1.2 fusion.32
  10.7 1.2 reduce-window.6
  14.7 46.2 %all_to_all.21 = bf16[8,80,1280]{2,1,0:T(8,128)(2,1)} all-to-all(bf16[8,80,1280]{2,1,0:T(8,128)(2,1)S(1)} %bitcast.70), channel_id=1, replica_groups=mesh['expert'=8,'dp'=4] {'expert'}, dimensions={0} | all-to-all | bytes 3276800 | tf_op jit(solution)/shard_map/all_to_all | solution.py:79
  62.1 41.7 %all_to_all.22 = bf16[8,80,1280]{2,1,0:T(8,128)(2,1)} all-to-all(bf16[8,80,1280]{2,1,0:T(8,128)(2,1)S(1)} %bitcast.71), channel_id=1, replica_groups=mesh['expert'=8,'dp'=4] {'expert'}, dimensions={0} | all-to-all | bytes 3276800 | tf_op jit(solution)/shard_map/all_to_all | solution.py:80
  103.9 3.4 %all-gather.5.cloned.1.call-done = bf16[32,80,1280]{2,1,0:T(8,128)(2,1)} async-done(((bf16[8,80,1280]{2,1,0:T(8,128)(2,1)}), bf16[32,80,1280]{2,1,0:T(8,128)(2,1)}) %all-gather.5.cloned.1.call-update) | async-done | bytes 6553616 | tf_op jit(solution)/shard_map/all_gather | solution.py:85
  107.3 4.8 %convolution_reduce_fusion = f32[2560]{0:T(1024)S(1)} fusion(bf16[2560,1280]{1,0:T(8,128)(2,1)} %bitcast.67, bf16[1280,4]{0,1:T(4,128)(2,1)S(1)} %copy-done.5, s32[]{:T(128)S(6)} %select_n.40), kind=kOutput, calls=%fused_computation.28 | convolution fusion | flops 6553600 | bytes 6568964 | tf_op jit(solution)/shard_map/dot_general | solution.py:43
  112.2 4.1 %fusion.15 = f32[2560,320]{0,1:T(8,128)} fusion(bf16[2560,1280]{1,0:T(8,128)(2,1)S(1)} %bitcast.69, bf16[1,1280,320]{1,2,0:T(8,128)(2,1)S(1)} %copy-done), kind=kOutput, calls=%fused_computation.30 | convolution fusion | flops 2097152000 | bytes 10649600 | tf_op jit(solution)/shard_map/dot_general | solution.py:44
  116.3 40.5 %all-gather.7.cloned.1.call-done = bf16[32,80,1280]{2,1,0:T(8,128)(2,1)} async-done(((bf16[8,80,1280]{2,1,0:T(8,128)(2,1)}), bf16[32,80,1280]{2,1,0:T(8,128)(2,1)}) %all-gather.7.cloned.1.call-update) | async-done | bytes 6553616 | tf_op jit(solution)/shard_map/all_gather | solution.py:86
  156.8 8.9 %multiply_reduce_fusion = (bf16[2560]{0:T(1024)(128)(2,1)S(1)}, bf16[2560,320]{0,1:T(8,128)(2,1)S(1)}) fusion(f32[2560,320]{0,1:T(8,128)} %fusion.15, f32[2560]{0:T(1024)S(1)} %add_divide_fusion, bf16[2560,1280]{1,0:T(8,128)(2,1)} %bitcast.79, bf16[1,320,1280]{2,1,0:T(8,128)(2,1)S(1)} %copy-done.7), kind=kOutput, calls=%fused_computation.16 | convolution fusion | flops 2117629440 | bytes 12303360 | tf_op jit(solution)/shard_map/dot_general | solution.py:47
  165.7 1.2 copy-done.8
  167.0 5.5 %convolution_convert_fusion = bf16[4,640,1280]{2,1,0:T(8,128)(2,1)} fusion(bf16[40,4,8,640]{3,2,1,0:T(8,128)(2,1)S(1)} %bitcast.81, bf16[1,1280,320]{1,2,0:T(8,128)(2,1)S(1)} %copy-done), kind=kOutput, calls=%fused_computation.5 | convolution fusion | flops 2100428800 | bytes 9011200 | tf_op jit(solution)/shard_map/dot_general | solution.py:53
  173.7 6.0 %all-reduce = bf16[4,640]{1,0:T(4,128)(2,1)S(1)} all-reduce(bf16[4,640]{1,0:T(4,128)(2,1)S(1)} %convert_element_type.107), channel_id=5, replica_groups=mesh['expert'=8,'dp'=4] {'dp'}, use_global_device_ids=true, to_apply=%region_9.10.clone | all-reduce | flops 2560 | bytes 10240
  180.5 11.9 %all_to_all.23 = bf16[8,1,80]{2,1,0:T(2,128)(2,1)S(1)} all-to-all(bf16[8,1,80]{2,1,0:T(2,128)(2,1)S(1)} %convert_element_type.119), channel_id=1, replica_groups=mesh['expert'=8,'dp'=4] {'expert'}, dimensions={0} | all-to-all | bytes 2560 | tf_op jit(solution)/shard_map/all_to_all | solution.py:113
  192.5 40.4 %reduce-scatter.2.cloned.1.call-done = bf16[1,640,1280]{2,1,0:T(8,128)(2,1)} async-done(((bf16[4,640,1280]{2,1,0:T(8,128)(2,1)}), bf16[1,640,1280]{2,1,0:T(8,128)(2,1)}) %reduce-scatter.2.cloned.1.call-update) | async-done | bytes 1638416 | tf_op jit(solution)/shard_map/reduce_scatter | solution.py:92
  232.8 5.5 %all-to-all-start.2 = ((bf16[8,80,1280]{2,1,0:T(8,128)(2,1)}), bf16[8,80,1280]{2,1,0:T(8,128)(2,1)}, u32[]{:S(2)}, u32[]{:S(2)}) async-start(bf16[8,80,1280]{2,1,0:T(8,128)(2,1)} %bitcast.74), calls=%async_computation.3 | async-start | bytes 3276800 | tf_op jit(solution)/shard_map/all_to_all | solution.py:110
  239.1 6.7 %fusion.10 = bf16[1,1280,320]{1,2,0:T(8,128)(2,1)} fusion(bf16[2560,320]{0,1:T(8,128)(2,1)} %copy-done.8, bf16[2560,1280]{1,0:T(8,128)(2,1)} %bitcast.68), kind=kOutput, calls=%fused_computation.22 | convolution fusion | flops 2097561600 | bytes 9011200 | tf_op jit(solution)/shard_map/dot_general | solution.py:52
  245.8 6.9 %fusion.11 = bf16[1,320,1280]{2,1,0:T(8,128)(2,1)} fusion(bf16[2560,1280]{1,0:T(8,128)(2,1)} %bitcast.80, f32[2560]{0:T(1024)S(1)} %add_divide_fusion, f32[2560,320]{0,1:T(8,128)S(1)} %copy-done.10), kind=kOutput, calls=%fused_computation.23 | convolution fusion | flops 2114764800 | bytes 10659840 | tf_op jit(solution)/shard_map/dot_general | solution.py:51
  252.8 1.9 gather_fusion.1
  255.4 21.5 %all-to-all-done.2 = bf16[8,80,1280]{2,1,0:T(8,128)(2,1)} async-done(((bf16[8,80,1280]{2,1,0:T(8,128)(2,1)}), bf16[8,80,1280]{2,1,0:T(8,128)(2,1)}, u32[]{:S(2)}, u32[]{:S(2)}) %all-to-all-start.2) | async-done | bytes 1638432 | tf_op jit(solution)/shard_map/all_to_all | solution.py:110
  276.9 1.9 convert_reduce_fusion
  278.7 2.2 gather_fusion
  281.0 2.1 gather.13
  283.1 1.7 select_reduce_fusion
  285.6 38.2 %all-reduce.1 = (f32[1280,4]{0,1:T(4,128)}, f32[1280]{0:T(1024)}) all-reduce(f32[1280,4]{0,1:T(4,128)S(1)} %fusion.41, f32[1280]{0:T(1024)S(1)} %get-tuple-element.5), channel_id=1, replica_groups=mesh['expert'=8,'dp'=4] {'expert','dp'}, use_global_device_ids=true, to_apply=%region_15.16 | all-reduce | flops 6400 | bytes 51200 | tf_op jit(solution)/shard_map/psum | solution.py:132
  (77 shorter events, 11.4 us)
Async XLA Ops:
  7.2 105.0 %copy-start = (bf16[1,1280,320]{1,2,0:T(8,128)(2,1)S(1)}, bf16[1,1280,320]{1,2,0:T(8,128)(2,1)}, u32[]{:S(2)}) copy-start(bf16[1,1280,320]{1,2,0:T(8,128)(2,1)} %param.11) | copy-start | bytes 2457604
  7.2 100.1 %all-gather.5.cloned.1.call-start = ((), (), s32[]{:S(2)}) async-start(), calls=%async_computation.6 | async-start | bytes 8192000 | tf_op jit(solution)/shard_map/all_gather | solution.py:85
  14.6 46.4 %copy-start.3 = (bf16[128,1280]{1,0:T(8,128)(2,1)S(1)}, bf16[128,1280]{1,0:T(8,128)(2,1)}, u32[]{:S(2)}) copy-start(bf16[128,1280]{1,0:T(8,128)(2,1)} %param.13) | copy-start | bytes 983044
  60.9 95.9 %all-gather.7.cloned.1.call-start = ((), (), s32[]{:S(2)}) async-start(), calls=%async_computation.7 | async-start | bytes 8192000 | tf_op jit(solution)/shard_map/all_gather | solution.py:86
  62.0 45.3 %copy-start.5 = (bf16[1280,4]{0,1:T(4,128)(2,1)S(1)}, bf16[1280,4]{0,1:T(4,128)(2,1)}, u32[]{:S(2)}) copy-start(bf16[1280,4]{0,1:T(4,128)(2,1)} %param.9) | copy-start | bytes 30724
  103.9 129.0 %reduce-scatter.2.cloned.1.call-start = ((), (), s32[]{:S(2)}) async-start(), calls=%async_computation.5 | async-start | bytes 8192000 | tf_op jit(solution)/shard_map/reduce_scatter | solution.py:92
  107.3 4.9 %copy-start.2 = (bf16[32,80,1280]{2,1,0:T(8,128)(2,1)S(1)}, bf16[32,80,1280]{2,1,0:T(8,128)(2,1)}, u32[]{:S(2)}) copy-start(bf16[32,80,1280]{2,1,0:T(8,128)(2,1)} %all-gather.5.cloned.1.call-done) | copy-start | bytes 19660804
  112.2 44.6 %copy-start.7 = (bf16[1,320,1280]{2,1,0:T(8,128)(2,1)S(1)}, bf16[1,320,1280]{2,1,0:T(8,128)(2,1)}, u32[]{:S(2)}) copy-start(bf16[1,320,1280]{2,1,0:T(8,128)(2,1)} %param.12) | copy-start | bytes 2457604
  165.7 1.2 copy-start.8
  172.5 0.7 copy-start.9
  172.5 65.8 %copy-start.6 = (s32[128,2]{0,1:T(2,128)S(1)}, s32[128,2]{0,1:T(2,128)}, u32[]{:S(2)}) copy-start(s32[128,2]{0,1:T(2,128)} %param.10) | copy-start | bytes 3076
  232.8 44.0 %all-to-all-start.2 = ((bf16[8,80,1280]{2,1,0:T(8,128)(2,1)}), bf16[8,80,1280]{2,1,0:T(8,128)(2,1)}, u32[]{:S(2)}, u32[]{:S(2)}) async-start(bf16[8,80,1280]{2,1,0:T(8,128)(2,1)} %bitcast.74), calls=%async_computation.3 | async-start | bytes 3276800 | tf_op jit(solution)/shard_map/all_to_all | solution.py:110
  239.1 6.7 %copy-start.10 = (f32[2560,320]{0,1:T(8,128)S(1)}, f32[2560,320]{0,1:T(8,128)}, u32[]{:S(2)}) copy-start(f32[2560,320]{0,1:T(8,128)} %fusion.15) | copy-start | bytes 9830404
  281.0 3.8 %copy-start.1 = (bf16[128,1280]{1,0:T(8,128)(2,1)S(1)}, bf16[128,1280]{1,0:T(8,128)(2,1)}, u32[]{:S(2)}) copy-start(bf16[128,1280]{1,0:T(8,128)(2,1)} %param.7) | copy-start | bytes 983044
  281.0 3.8 %copy-start.4 = (f32[1280]{0:T(1024)S(1)}, f32[1280]{0:T(1024)}, u32[]{:S(2)}) copy-start(f32[1280]{0:T(1024)} %param.8) | copy-start | bytes 15364
Sparse Core Ops, SparseCore 0:
  61.0 46.2 all-gather.4
  108.9 47.8 all-gather.6
  172.6 60.1 reduce-scatter.1
where the time goes:
time: 332 us; the launch traced here: 331 us
  blocking collectives  144 us (43%)
  waiting for transfers between devices  106 us (32%)
  matrix products  38.8 us (12%)
  between operations  14.1 us (4%)
  local copies, waits for them, and re-layouts  13.2 us (4%)
  other arithmetic  9.71 us (3%)
  starting transfers between devices  5.64 us (2%)
    all_to_all x1, blocking collectives, body(): lax.all_to_all(send_m, 'expert', split_axis=0, concat_axis=0, tiled=True)  46.2 us
    all_to_all x1, blocking collectives, body(): lax.all_to_all(send_d, 'expert', split_axis=0, concat_axis=0, tiled=True)  41.7 us
    all_gather x1, waiting for transfers between devices, body(): lax.all_gather(recv_d[None], 'dp', axis=0, tiled=True)  40.5 us
    reduce_scatter x1, waiting for transfers between devices, body(): lax.psum_scatter(row_gradient.reshape(groups, halves * expert_capacity, w...  40.4 us
    psum x1, blocking collectives, body(): lax.psum((router_term, gain_product), ('expert', 'dp'))  38.2 us
    all_to_all x1, waiting for transfers between devices, body(): lax.all_to_all(back_rows.astype(jnp.bfloat16), 'expert', split_axis=0, co...  21.5 us
    all_to_all x1, blocking collectives, body(): lax.all_to_all(back_gate.astype(jnp.bfloat16), 'expert', split_axis=0, co...  11.9 us
    dot_general x1, matrix products, expert_pass(): back = jnp.dot(rows_d, w_second.T, preferred_element_type=jnp.float32)  8.92 us
  transfers between devices with their start and end apart: 4, of which 4 were waited for; matrix products, arithmetic and copies ran while one was open for 9% of the time, Pallas kernels for 0%

commit v1 on v0

v1 whole, which is shorter than its diff:
```python
import math

import jax
import jax.numpy as jnp
from jax import lax
from jax.sharding import PartitionSpec as P

F32 = jnp.float32
BF16 = jnp.bfloat16


def gelu_parts(pre):
    coeff = math.sqrt(2.0 / math.pi)
    inner = coeff * (pre + 0.044715 * pre * pre * pre)
    tanh_val = jnp.tanh(inner)
    value = 0.5 * pre * (1.0 + tanh_val)
    slope = 0.5 * (1.0 + tanh_val) + 0.5 * pre * (1.0 - tanh_val * tanh_val) * coeff * (
        1.0 + 3.0 * 0.044715 * pre * pre
    )
    return (value, slope)


def norm_pieces(block, gain):
    values = block.astype(F32)
    centred_rows = values - jnp.mean(values, axis=1, keepdims=True)
    inverse_deviation = lax.rsqrt(
        jnp.mean(centred_rows * centred_rows, axis=1, keepdims=True) + 1e-06
    )
    normalized_rows = centred_rows * inverse_deviation
    return (
        normalized_rows,
        inverse_deviation,
        (normalized_rows * gain[None, :]).astype(BF16),
    )


def dot(a, b, a_dim, b_dim):
    return lax.dot_general(a, b, (((a_dim,), (b_dim,)), ((), ())), preferred_element_type=F32)


def body(prenorm_input, gain, router, routes, w_in, w_out, cotangent):
    halves = lax.axis_size("expert")
    experts = halves // 2
    groups = lax.axis_size("dp")
    columns = groups // 2
    tokens, width = prenorm_input.shape
    top = routes.shape[1]
    capacity = max(2, 5 * tokens * top // (4 * experts))
    slots = experts * capacity
    own = lax.axis_index("expert") // 2

    swap_half = [(i, i ^ 1) for i in range(halves)]
    swap_pair = [(i, i ^ 1) for i in range(groups)]

    def turn_columns(step):
        return [(i, (i + 2 * step) % groups) for i in range(groups)]

    def turn_experts(step):
        return [(i, (i + 2 * step) % halves) for i in range(halves)]

    first = w_in[0].T
    second = w_out[0]
    first_y = lax.ppermute(first, "expert", swap_half)
    second_y = lax.ppermute(second, "expert", swap_half)
    first_c = lax.ppermute(first, "dp", swap_pair)
    second_c = lax.ppermute(second, "dp", swap_pair)
    first_yc = lax.ppermute(first_y, "dp", swap_pair)
    second_yc = lax.ppermute(second_y, "dp", swap_pair)

    normalized_rows, inverse_deviation, mixed_rows = norm_pieces(prenorm_input, gain)
    relative = (own + jnp.arange(experts, dtype=jnp.int32)) % experts
    chosen = jnp.any(routes[None, :, :] == relative[:, None, None], axis=2)
    order = jnp.arange(tokens, dtype=jnp.int32)
    earlier = (order[:, None] < order[None, :]).astype(BF16)
    before = dot(chosen.astype(BF16), earlier, 1, 0).astype(jnp.int32)
    places = (
        chosen[:, None, :]
        & (before[:, None, :] == jnp.arange(capacity, dtype=jnp.int32)[None, :, None])
    ).astype(BF16).reshape(slots, tokens)
    send_m = dot(places, mixed_rows, 1, 0).astype(BF16).reshape(experts, 1, capacity, width)
    send_d = dot(places, cotangent, 1, 0).astype(BF16).reshape(experts, 1, capacity, width)
    send = jnp.concatenate([send_m, send_d], axis=1)

    near = [send[0]]
    for step in range(1, experts):
        near.append(lax.ppermute(send[step], "expert", turn_experts(step)))
    parts = [near]
    for step in range(1, columns):
        parts.append([lax.ppermute(piece, "dp", turn_columns(step)) for piece in near])
    pieces = [piece for part in parts for piece in part]
    rows_m = jnp.concatenate([piece[0] for piece in pieces], axis=0)
    rows_d = jnp.concatenate([piece[1] for piece in pieces], axis=0)

    column = lax.dynamic_slice_in_dim(router, own, 1, 1)
    all_first = jnp.concatenate([first, first_c, first_y, first_yc], axis=0)
    all_second = jnp.concatenate([second, second_c, second_y, second_yc], axis=0)
    gate = jax.nn.sigmoid(jnp.dot(rows_m, column, preferred_element_type=F32))
    value, slope = gelu_parts(dot(rows_m, all_first, 1, 1))
    hidden = value.astype(BF16)
    back = dot(rows_d, all_second, 1, 1)
    gate_gradient = jnp.sum(hidden.astype(F32) * back, axis=1, keepdims=True)
    logit_gradient = gate_gradient * gate * (1.0 - gate)
    grad_pre = (gate * back * slope).astype(BF16)
    grad_y = (gate * rows_d.astype(F32)).astype(BF16)
    router_row = column[:, 0].astype(F32)[None, :]

    def row_gradient(at, kind):
        part = slice(at * slots, (at + 1) * slots)
        return (
            dot(grad_pre[part], all_first, 1, 0) + logit_gradient[part] * router_row
        ).astype(kind)

    back_rows = [
        lax.ppermute(row_gradient(step, BF16), "dp", turn_columns(columns - step))
        for step in range(1, columns)
    ]
    grad_second = dot(hidden, grad_y, 0, 0)
    grad_first = dot(grad_pre, rows_m, 0, 0)
    own_rows = row_gradient(0, F32)
    for piece in back_rows:
        own_rows = own_rows + piece.astype(F32)
    own_rows = own_rows.astype(BF16).reshape(experts, capacity, width)
    returned = [own_rows[0]]
    for step in range(1, experts):
        returned.append(lax.ppermute(own_rows[step], "expert", turn_experts(experts - step)))

    units = first.shape[0]

    def weight_gradient(whole):
        blocks = whole.reshape(4, units, width)
        mine, pair, half, both = blocks[0], blocks[1], blocks[2], blocks[3]
        half = half + lax.ppermute(both.astype(BF16), "dp", swap_pair).astype(F32)
        mine = mine + lax.ppermute(pair.astype(BF16), "dp", swap_pair).astype(F32)
        return (mine + lax.ppermute(half.astype(BF16), "expert", swap_half).astype(F32)).astype(BF16)

    grad_out = weight_gradient(grad_second)[None]
    grad_in = weight_gradient(grad_first).T[None]

    partial = jnp.stack(
        [
            jnp.sum(rows_m.astype(F32) * logit_gradient, axis=0),
            jnp.sum(all_first.astype(F32) * grad_first, axis=0),
        ]
    )
    gathered = lax.all_gather(partial, ("expert", "dp"), axis=0)
    gathered = jnp.sum(gathered.reshape(experts, 2 * groups, 2, width), axis=1)
    router_t = gathered[:, 0]
    grad_router = router_t.T
    grad_gain = (
        jnp.sum(gathered[:, 1], axis=0) + jnp.sum(router_t * router.astype(F32).T, axis=0)
    ) / gain

    mixed_gradient = dot(places, jnp.concatenate(returned, axis=0), 0, 0)
    scaled_rows = mixed_gradient * gain[None, :]
    mean_first_term = jnp.mean(scaled_rows, axis=1, keepdims=True)
    mean_second_term = jnp.mean(scaled_rows * normalized_rows, axis=1, keepdims=True)
    norm_backward = inverse_deviation * (
        scaled_rows - mean_first_term - normalized_rows * mean_second_term
    )
    input_grad = (cotangent.astype(F32) + norm_backward).astype(BF16)
    return (input_grad, grad_in, grad_out, grad_router, grad_gain)


def solution(mesh):
    in_specs = (
        P(("expert", "dp"), None),
        P(),
        P(),
        P(("expert", "dp"), None),
        P("expert", None, "dp"),
        P("expert", "dp", None),
        P(("expert", "dp"), None),
    )
    out_specs = (
        P(("expert", "dp"), None),
        P("expert", None, "dp"),
        P("expert", "dp", None),
        P(),
        P(),
    )
    return jax.shard_map(body, mesh=mesh, in_specs=in_specs, out_specs=out_specs, check_vma=False)
```

time: 332 us -> 215 us (0.65)
  blocking collectives: 144 us -> 43.8 us
  starting transfers between devices: 5.64 us -> 21.7 us
  between operations: 14.1 us -> 0.99 us
  local copies, waits for them, and re-layouts: 13.2 us -> 2.36 us
  matrix products: 38.8 us -> 28.1 us
    ppermute x0 -> x23, waiting for transfers between devices: none -> 109 us  [the longest x3 38.7 us: body(): near.append(lax.ppermute(send[step], 'expert', turn_experts(step)))]
    all_to_all x3 -> x0, blocking collectives: 99.9 us -> none  [the longest x1 46.2 us: body(): lax.all_to_all(send_m, 'expert', split_axis=0, concat_axis=0, tiled=True)]
    all_gather x2 -> x0, waiting for transfers between devices: 43.9 us -> none  [the longest x1 40.5 us: body(): lax.all_gather(recv_d[None], 'dp', axis=0, tiled=True)]
    all_gather x0 -> x1, blocking collectives: none -> 43.8 us  [body(): gathered = lax.all_gather(partial, ('expert', 'dp'), axis=0)]
    reduce_scatter x1 -> x0, waiting for transfers between devices: 40.4 us -> none  [body(): lax.psum_scatter(row_gradient.reshape(groups, halves * expert_capacity, w...]
    psum x1 -> x0, blocking collectives: 38.2 us -> none  [body(): lax.psum((router_term, gain_product), ('expert', 'dp'))]
    ppermute x0 -> x23, starting transfers between devices: none -> 21.7 us  [the longest x4 5.97 us: body(): lax.ppermute(piece, 'dp', turn_columns(step))]
    all_to_all x1 -> x0, waiting for transfers between devices: 21.5 us -> none  [body(): lax.all_to_all(back_rows.astype(jnp.bfloat16), 'expert', split_axis=0, co...]
  transfers between devices with their start and end apart: 4 -> 23, of which waited for: 4 -> 11; matrix products, arithmetic and copies ran while one was open for 9% -> 13% of each run, Pallas kernels for 0% -> 0%
where the time goes in v1:
time: 215 us
  waiting for transfers between devices  109 us (51%)
  blocking collectives  43.8 us (20%)
  matrix products  28.1 us (13%)
  starting transfers between devices  21.7 us (10%)
  other arithmetic  8.51 us (4%)
  local copies, waits for them, and re-layouts  2.36 us (1%)
    all_gather x1, blocking collectives, body(): gathered = lax.all_gather(partial, ('expert', 'dp'), axis=0)  43.8 us
    ppermute x3, waiting for transfers between devices, body(): near.append(lax.ppermute(send[step], 'expert', turn_experts(step)))  38.7 us
    ppermute x4, waiting for transfers between devices, body(): lax.ppermute(piece, 'dp', turn_columns(step))  31.4 us
    dot_general x10, matrix products, dot(): lax.dot_general(a, b, (((a_dim,), (b_dim,)), ((), ())), preferred_element...  27.5 us
    ppermute x2, waiting for transfers between devices, weight_gradient(): lax.ppermute(half.astype(BF16), 'expert', swap_half).astype(F32)  25.9 us
    ppermute x3, waiting for transfers between devices, body(): lax.ppermute(own_rows[step], 'expert', turn_experts(experts - step))  13.4 us
    ppermute x4, starting transfers between devices, body(): lax.ppermute(piece, 'dp', turn_columns(step))  5.97 us
    ppermute x3, starting transfers between devices, body(): near.append(lax.ppermute(send[step], 'expert', turn_experts(step)))  5.05 us
  transfers between devices with their start and end apart: 23, of which 11 were waited for; matrix products, arithmetic and copies ran while one was open for 13% of the time, Pallas kernels for 0%

profile of v1, /device:TPU:0, one launch (start us, length us, event | category | flops | bytes accessed | tf_op | source)
XLA Modules:
  0.0 214.8 jit_solution(14523703736948877018)
XLA Ops:
  0.6 3.0 %collective-permute-start.11 = (bf16[320,1280]{1,0:T(8,128)(2,1)}, bf16[320,1280]{1,0:T(8,128)(2,1)}, u32[]{:S(2)}, u32[]{:S(2)}) collective-permute-start(bf16[320,1280]{1,0:T(8,128)(2,1)} %bitcast.114), channel_id=1, source_target_pairs={{0,4},{4,0},{8,12},{12,8},{16,20},{20,16},{24,28},{28,24},{1,5},{5... | collective-permute-start | bytes 2457608 | tf_op jit(solution)/shard_map/ppermute | solution.py:63
  10.6 1.9 collective-permute-start
  12.5 12.0 %collective-permute-done = bf16[2,80,1280]{2,1,0:T(8,128)(2,1)} collective-permute-done((bf16[2,80,1280]{2,1,0:T(8,128)(2,1)S(1)}, bf16[2,80,1280]{2,1,0:T(8,128)(2,1)}, u32[]{:S(2)}, u32[]{:S(2)}) %collective-permute-start) | collective-permute-done | bytes 409632 | tf_op jit(solution)/shard_map/ppermute | solution.py:86
  26.2 17.9 %collective-permute-done.1 = bf16[2,80,1280]{2,1,0:T(8,128)(2,1)S(1)} collective-permute-done((bf16[2,80,1280]{2,1,0:T(8,128)(2,1)S(1)}, bf16[2,80,1280]{2,1,0:T(8,128)(2,1)S(1)}, u32[]{:S(2)}, u32[]{:S(2)}) %collective-permute-start.1) | collective-permute-done | bytes 409632 | tf_op jit(solution)/shard_map/ppermute | solution.py:86
  44.1 2.5 %collective-permute-start.2 = (bf16[2,80,1280]{2,1,0:T(8,128)(2,1)S(1)}, bf16[2,80,1280]{2,1,0:T(8,128)(2,1)S(1)}, u32[]{:S(2)}, u32[]{:S(2)}) collective-permute-start(bf16[2,80,1280]{2,1,0:T(8,128)(2,1)S(1)} %get-tuple-element.18), channel_id=1, source_target_pairs={{0,24},{4,28},{8,0},{12,4},{16,8},{20,12},{24,16},{28,20},{1,25},{... | collective-permute-start | bytes 1228808 | tf_op jit(solution)/shard_map/ppermute | solution.py:86
  46.6 8.9 %collective-permute-done.2 = bf16[2,80,1280]{2,1,0:T(8,128)(2,1)S(1)} collective-permute-done((bf16[2,80,1280]{2,1,0:T(8,128)(2,1)S(1)}, bf16[2,80,1280]{2,1,0:T(8,128)(2,1)S(1)}, u32[]{:S(2)}, u32[]{:S(2)}) %collective-permute-start.2) | collective-permute-done | bytes 409632 | tf_op jit(solution)/shard_map/ppermute | solution.py:86
  55.5 1.5 collective-permute-start.3
  57.0 9.0 %collective-permute-done.3 = bf16[2,80,1280]{2,1,0:T(8,128)(2,1)S(1)} collective-permute-done((bf16[2,80,1280]{2,1,0:T(8,128)(2,1)S(1)}, bf16[2,80,1280]{2,1,0:T(8,128)(2,1)S(1)}, u32[]{:S(2)}, u32[]{:S(2)}) %collective-permute-start.3) | collective-permute-done | bytes 409632 | tf_op jit(solution)/shard_map/ppermute | solution.py:89
  67.6 8.3 %collective-permute-done.4 = bf16[2,80,1280]{2,1,0:T(8,128)(2,1)S(1)} collective-permute-done((bf16[2,80,1280]{2,1,0:T(8,128)(2,1)}, bf16[2,80,1280]{2,1,0:T(8,128)(2,1)S(1)}, u32[]{:S(2)}, u32[]{:S(2)}) %collective-permute-start.4) | collective-permute-done | bytes 409632 | tf_op jit(solution)/shard_map/ppermute | solution.py:89
  77.4 8.1 %collective-permute-done.5 = bf16[2,80,1280]{2,1,0:T(8,128)(2,1)S(1)} collective-permute-done((bf16[2,80,1280]{2,1,0:T(8,128)(2,1)S(1)}, bf16[2,80,1280]{2,1,0:T(8,128)(2,1)S(1)}, u32[]{:S(2)}, u32[]{:S(2)}) %collective-permute-start.5) | collective-permute-done | bytes 409632 | tf_op jit(solution)/shard_map/ppermute | solution.py:89
  87.6 5.9 %collective-permute-done.6 = bf16[2,80,1280]{2,1,0:T(8,128)(2,1)S(1)} collective-permute-done((bf16[2,80,1280]{2,1,0:T(8,128)(2,1)S(1)}, bf16[2,80,1280]{2,1,0:T(8,128)(2,1)S(1)}, u32[]{:S(2)}, u32[]{:S(2)}) %collective-permute-start.6) | collective-permute-done | bytes 409632 | tf_op jit(solution)/shard_map/ppermute | solution.py:89
  94.1 3.7 %fusion.81 = f32[640,1280]{1,0:T(8,128)S(1)} fusion(bf16[640,1280]{1,0:T(8,128)(2,1)S(1)} %get-tuple-element.24, bf16[320,1280]{1,0:T(8,128)(2,1)S(1)} %collective-permute-done.12, bf16[320,1280]{1,0:T(8,128)(2,1)} %collective-permute-done.11, bf16[320,1280]{1,0:T(8,128)(2,1)} %collective-permute-done.10, bf16[320,1280]{1,0:T(8,128)(2,1)S(1)} %bitcast.116), kind=kOutput, calls=%fused_computation.143 | convolution fusion | flops 2110259200 | bytes 8192000 | tf_op jit(solution)/shard_map/dot_general | solution.py:38
  97.9 3.2 %fusion.87 = (bf16[1280,1280]{1,0:T(8,128)(2,1)S(1)}, f32[1280,1280]{1,0:T(8,128)S(1)}) fusion(bf16[640,1280]{1,0:T(8,128)(2,1)S(1)} %get-tuple-element.23, f32[640]{0:T(1024)S(1)} %add_divide_fusion.1, f32[640,1280]{1,0:T(8,128)S(1)} %fusion.81), kind=kOutput, calls=%fused_computation.149 | convolution fusion | flops 2108620800 | bytes 14748160 | tf_op jit(solution)/shard_map/dot_general | solution.py:38
  101.0 7.2 %multiply_reduce_fusion.2 = (f32[640]{0:T(1024)S(1)}, bf16[640,1280]{1,0:T(8,128)(2,1)S(1)}) fusion(f32[640,1280]{1,0:T(8,128)S(1)} %fusion.81, f32[640]{0:T(1024)S(1)} %add_divide_fusion.1, bf16[640,1280]{1,0:T(8,128)(2,1)S(1)} %get-tuple-element.23, bf16[320,1280]{1,0:T(8,128)(2,1)S(1)} %collective-permute-done.9, ...), kind=kOutput, calls=%fused_computation.21 | convolution fusion | flops 2130738560 | bytes 9835520 | tf_op jit(solution)/shard_map/dot_general | solution.py:38
  108.8 2.6 %fusion.17 = bf16[320,1280]{1,0:T(8,128)(2,1)S(1)} fusion(bf16[640,1280]{1,0:T(8,128)(2,1)S(1)} %get-tuple-element.10, f32[320]{0:T(512)S(1)} %get-tuple-element.40, f32[1280]{0:T(1024)S(1)} %convert_element_type.105, bf16[320,1280]{1,0:T(8,128)(2,1)S(1)} %collective-permute-done.12, bf16[320,1280]{1,0:T(8,128)(2,1)} %collective-permute-done.11, ...), kind=kOutput, calls=%fused_computation.27 | convolution fusion | flops 1062912000 | bytes 4925440 | tf_op jit(solution)/shard_map/dot_general | solution.py:38
  111.4 1.6 collective-permute-start.13
  113.0 4.8 %multiply_reduce_fusion = (f32[1280]{0:T(1024)S(1)}, bf16[1280,1280]{1,0:T(8,128)(2,1)S(1)}, f32[1280,1280]{1,0:T(8,128)S(1)}) fusion(bf16[320,1280]{1,0:T(8,128)(2,1)S(1)} %collective-permute-done.12, bf16[320,1280]{1,0:T(8,128)(2,1)} %collective-permute-done.11, bf16[320,1280]{1,0:T(8,128)(2,1)} %collective-permute-done.10, ...), kind=kOutput, calls=%fused_computation | convolution fusion | flops 2115173120 | bytes 16389120 | tf_op jit(solution)/shard_map/dot_general | solution.py:38
  119.2 43.8 %all-gather.1 = f32[32,2,1280]{2,1,0:T(2,128)S(1)} all-gather(f32[1,2,1280]{2,1,0:T(2,128)S(1)} %maximum_bitcast_fusion), channel_id=2, replica_groups=mesh['expert'=8,'dp'=4] {'expert','dp'}, dimensions={0}, use_global_device_ids=true | all-gather | bytes 337920 | tf_op jit(solution)/shard_map/all_gather | solution.py:145
  164.4 2.7 %fusion.16 = bf16[320,1280]{1,0:T(8,128)(2,1)S(1)} fusion(bf16[320,1280]{1,0:T(8,128)(2,1)S(1)} %collective-permute-done.13, bf16[640,1280]{1,0:T(8,128)(2,1)S(1)} %get-tuple-element.10, f32[1280]{0:T(1024)S(1)} %convert_element_type.105, f32[320]{0:T(512)S(1)} %get-tuple-element.39, bf16[320,1280]{1,0:T(8,128)(2,1)S(1)} %collective-permute-done.12, ...), kind=kOutput, calls=%fused_computation.26 | convolution fusion | flops 1063731200 | bytes 5744640 | tf_op jit(solution)/shard_map/dot_general | solution.py:38
  167.5 3.8 %collective-permute-start.14 = (bf16[80,1280]{1,0:T(8,128)(2,1)S(1)}, bf16[80,1280]{1,0:T(8,128)(2,1)S(1)}, u32[]{:S(2)}, u32[]{:S(2)}) collective-permute-start(bf16[80,1280]{1,0:T(8,128)(2,1)S(1)} %get-tuple-element.22), channel_id=1, source_target_pairs={{0,24},{4,28},{8,0},{12,4},{16,8},{20,12},{24,16},{28,20},{1,25},{... | collective-permute-start | bytes 614408 | tf_op jit(solution)/shard_map/ppermute | solution.py:125
  171.5 5.5 %collective-permute-done.16 = bf16[80,1280]{1,0:T(8,128)(2,1)S(1)} collective-permute-done((bf16[80,1280]{1,0:T(8,128)(2,1)S(1)}, bf16[80,1280]{1,0:T(8,128)(2,1)S(1)}, u32[]{:S(2)}, u32[]{:S(2)}) %collective-permute-start.16) | collective-permute-done | bytes 204832 | tf_op jit(solution)/shard_map/ppermute | solution.py:125
  177.0 7.9 %collective-permute-done.15 = bf16[80,1280]{1,0:T(8,128)(2,1)S(1)} collective-permute-done((bf16[80,1280]{1,0:T(8,128)(2,1)S(1)}, bf16[80,1280]{1,0:T(8,128)(2,1)S(1)}, u32[]{:S(2)}, u32[]{:S(2)}) %collective-permute-start.15) | collective-permute-done | bytes 204832 | tf_op jit(solution)/shard_map/ppermute | solution.py:125
  186.4 11.7 %collective-permute-done.19 = bf16[320,1280]{1,0:T(8,128)(2,1)S(1)} collective-permute-done((bf16[320,1280]{1,0:T(8,128)(2,1)S(1)}, bf16[320,1280]{1,0:T(8,128)(2,1)S(1)}, u32[]{:S(2)}, u32[]{:S(2)}) %collective-permute-start.19) | collective-permute-done | bytes 819232 | tf_op jit(solution)/shard_map/ppermute | solution.py:134
  199.4 14.2 %collective-permute-done.22 = bf16[320,1280]{1,0:T(8,128)(2,1)S(1)} collective-permute-done((bf16[320,1280]{1,0:T(8,128)(2,1)S(1)}, bf16[320,1280]{1,0:T(8,128)(2,1)S(1)}, u32[]{:S(2)}, u32[]{:S(2)}) %collective-permute-start.22) | collective-permute-done | bytes 819232 | tf_op jit(solution)/shard_map/ppermute | solution.py:134
  (88 shorter events, 22.3 us)
Async XLA Ops:
  0.6 86.4 %collective-permute-start.11 = (bf16[320,1280]{1,0:T(8,128)(2,1)}, bf16[320,1280]{1,0:T(8,128)(2,1)}, u32[]{:S(2)}, u32[]{:S(2)}) collective-permute-start(bf16[320,1280]{1,0:T(8,128)(2,1)} %bitcast.114), channel_id=1, source_target_pairs={{0,4},{4,0},{8,12},{12,8},{16,20},{20,16},{24,28},{28,24},{1,5},{5... | collective-permute-start | bytes 2457608 | tf_op jit(solution)/shard_map/ppermute | solution.py:63
  3.7 90.4 %collective-permute-start.10 = (bf16[320,1280]{1,0:T(8,128)(2,1)}, bf16[320,1280]{1,0:T(8,128)(2,1)}, u32[]{:S(2)}, u32[]{:S(2)}) collective-permute-start(bf16[320,1280]{1,0:T(8,128)(2,1)} %bitcast.115), channel_id=1, source_target_pairs={{0,1},{1,0},{2,3},{3,2},{4,5},{5,4},{6,7},{7,6},{8,9},{9,8},{10,11... | collective-permute-start | bytes 2457608 | tf_op jit(solution)/shard_map/ppermute | solution.py:65
  3.7 83.4 %collective-permute-start.8 = (bf16[320,1280]{1,0:T(8,128)(2,1)}, bf16[320,1280]{1,0:T(8,128)(2,1)}, u32[]{:S(2)}, u32[]{:S(2)}) collective-permute-start(bf16[320,1280]{1,0:T(8,128)(2,1)} %bitcast.111), channel_id=1, source_target_pairs={{0,4},{4,0},{8,12},{12,8},{16,20},{20,16},{24,28},{28,24},{1,5},{5... | collective-permute-start | bytes 2457608 | tf_op jit(solution)/shard_map/ppermute | solution.py:64
  3.8 97.2 %collective-permute-start.7 = (bf16[320,1280]{1,0:T(8,128)(2,1)}, bf16[320,1280]{1,0:T(8,128)(2,1)}, u32[]{:S(2)}, u32[]{:S(2)}) collective-permute-start(bf16[320,1280]{1,0:T(8,128)(2,1)} %bitcast.112), channel_id=1, source_target_pairs={{0,1},{1,0},{2,3},{3,2},{4,5},{5,4},{6,7},{7,6},{8,9},{9,8},{10,11... | collective-permute-start | bytes 2457608 | tf_op jit(solution)/shard_map/ppermute | solution.py:66
  10.6 13.9 %collective-permute-start = (bf16[2,80,1280]{2,1,0:T(8,128)(2,1)S(1)}, bf16[2,80,1280]{2,1,0:T(8,128)(2,1)}, u32[]{:S(2)}, u32[]{:S(2)}) collective-permute-start(bf16[2,80,1280]{2,1,0:T(8,128)(2,1)S(1)} %get-tuple-element.16), channel_id=1, source_target_pairs={{0,8},{4,12},{8,16},{12,20},{16,24},{20,28},{24,0},{28,4},{1,9},{5... | collective-permute-start | bytes 1228808 | tf_op jit(solution)/shard_map/ppermute | solution.py:86
  24.5 19.7 %collective-permute-start.1 = (bf16[2,80,1280]{2,1,0:T(8,128)(2,1)S(1)}, bf16[2,80,1280]{2,1,0:T(8,128)(2,1)S(1)}, u32[]{:S(2)}, u32[]{:S(2)}) collective-permute-start(bf16[2,80,1280]{2,1,0:T(8,128)(2,1)S(1)} %get-tuple-element.17), channel_id=1, source_target_pairs={{0,16},{4,20},{8,24},{12,28},{16,0},{20,4},{24,8},{28,12},{1,17},{... | collective-permute-start | bytes 1228808 | tf_op jit(solution)/shard_map/ppermute | solution.py:86
  44.1 11.4 %collective-permute-start.2 = (bf16[2,80,1280]{2,1,0:T(8,128)(2,1)S(1)}, bf16[2,80,1280]{2,1,0:T(8,128)(2,1)S(1)}, u32[]{:S(2)}, u32[]{:S(2)}) collective-permute-start(bf16[2,80,1280]{2,1,0:T(8,128)(2,1)S(1)} %get-tuple-element.18), channel_id=1, source_target_pairs={{0,24},{4,28},{8,0},{12,4},{16,8},{20,12},{24,16},{28,20},{1,25},{... | collective-permute-start | bytes 1228808 | tf_op jit(solution)/shard_map/ppermute | solution.py:86
  46.6 47.5 %copy-start.5 = (bf16[1,1280,320]{1,2,0:T(8,128)(2,1)S(1)}, bf16[1,1280,320]{1,2,0:T(8,128)(2,1)}, u32[]{:S(2)}) copy-start(bf16[1,1280,320]{1,2,0:T(8,128)(2,1)} %param.11) | copy-start | bytes 2457604
  55.5 10.5 %collective-permute-start.3 = (bf16[2,80,1280]{2,1,0:T(8,128)(2,1)S(1)}, bf16[2,80,1280]{2,1,0:T(8,128)(2,1)S(1)}, u32[]{:S(2)}, u32[]{:S(2)}) collective-permute-start(bf16[2,80,1280]{2,1,0:T(8,128)(2,1)S(1)} %get-tuple-element.15), channel_id=1, source_target_pairs={{0,2},{1,3},{2,0},{3,1},{4,6},{5,7},{6,4},{7,5},{8,10},{9,11},{10,... | collective-permute-start | bytes 1228808 | tf_op jit(solution)/shard_map/ppermute | solution.py:89
  66.1 9.8 %collective-permute-start.4 = (bf16[2,80,1280]{2,1,0:T(8,128)(2,1)}, bf16[2,80,1280]{2,1,0:T(8,128)(2,1)S(1)}, u32[]{:S(2)}, u32[]{:S(2)}) collective-permute-start(bf16[2,80,1280]{2,1,0:T(8,128)(2,1)} %collective-permute-done), channel_id=1, source_target_pairs={{0,2},{1,3},{2,0},{3,1},{4,6},{5,7},{6,4},{7,5},{8,10},{9,11},{10,... | collective-permute-start | bytes 1228808 | tf_op jit(solution)/shard_map/ppermute | solution.py:89
  75.9 9.6 %collective-permute-start.5 = (bf16[2,80,1280]{2,1,0:T(8,128)(2,1)S(1)}, bf16[2,80,1280]{2,1,0:T(8,128)(2,1)S(1)}, u32[]{:S(2)}, u32[]{:S(2)}) collective-permute-start(bf16[2,80,1280]{2,1,0:T(8,128)(2,1)S(1)} %collective-permute-done.1), channel_id=1, source_target_pairs={{0,2},{1,3},{2,0},{3,1},{4,6},{5,7},{6,4},{7,5},{8,10},{9,11},{10,... | collective-permute-start | bytes 1228808 | tf_op jit(solution)/shard_map/ppermute | solution.py:89
  85.5 8.0 %collective-permute-start.6 = (bf16[2,80,1280]{2,1,0:T(8,128)(2,1)S(1)}, bf16[2,80,1280]{2,1,0:T(8,128)(2,1)S(1)}, u32[]{:S(2)}, u32[]{:S(2)}) collective-permute-start(bf16[2,80,1280]{2,1,0:T(8,128)(2,1)S(1)} %collective-permute-done.2), channel_id=1, source_target_pairs={{0,2},{1,3},{2,0},{3,1},{4,6},{5,7},{6,4},{7,5},{8,10},{9,11},{10,... | collective-permute-start | bytes 1228808 | tf_op jit(solution)/shard_map/ppermute | solution.py:89
  87.0 7.1 %collective-permute-start.12 = (bf16[320,1280]{1,0:T(8,128)(2,1)}, bf16[320,1280]{1,0:T(8,128)(2,1)S(1)}, u32[]{:S(2)}, u32[]{:S(2)}) collective-permute-start(bf16[320,1280]{1,0:T(8,128)(2,1)} %collective-permute-done.11), channel_id=1, source_target_pairs={{0,1},{1,0},{2,3},{3,2},{4,5},{5,4},{6,7},{7,6},{8,9},{9,8},{10,11... | collective-permute-start | bytes 2457608 | tf_op jit(solution)/shard_map/ppermute | solution.py:67
  87.0 14.0 %collective-permute-start.9 = (bf16[320,1280]{1,0:T(8,128)(2,1)}, bf16[320,1280]{1,0:T(8,128)(2,1)S(1)}, u32[]{:S(2)}, u32[]{:S(2)}) collective-permute-start(bf16[320,1280]{1,0:T(8,128)(2,1)} %collective-permute-done.8), channel_id=1, source_target_pairs={{0,1},{1,0},{2,3},{3,2},{4,5},{5,4},{6,7},{7,6},{8,9},{9,8},{10,11... | collective-permute-start | bytes 2457608 | tf_op jit(solution)/shard_map/ppermute | solution.py:68
  111.4 53.0 %collective-permute-start.13 = (bf16[320,1280]{1,0:T(8,128)(2,1)S(1)}, bf16[320,1280]{1,0:T(8,128)(2,1)S(1)}, u32[]{:S(2)}, u32[]{:S(2)}) collective-permute-start(bf16[320,1280]{1,0:T(8,128)(2,1)S(1)} %fusion.17), channel_id=1, source_target_pairs={{0,2},{1,3},{2,0},{3,1},{4,6},{5,7},{6,4},{7,5},{8,10},{9,11},{10,... | collective-permute-start | bytes 2457608 | tf_op jit(solution)/shard_map/ppermute | solution.py:114
  117.9 49.3 %collective-permute-start.18 = (bf16[320,1280]{1,0:T(8,128)(2,1)S(1)}, bf16[320,1280]{1,0:T(8,128)(2,1)S(1)}, u32[]{:S(2)}, u32[]{:S(2)}) collective-permute-start(bf16[320,1280]{1,0:T(8,128)(2,1)S(1)} %get-tuple-element.14), channel_id=1, source_target_pairs={{0,1},{1,0},{2,3},{3,2},{4,5},{5,4},{6,7},{7,6},{8,9},{9,8},{10,11... | collective-permute-start | bytes 2457608 | tf_op jit(solution)/shard_map/ppermute | solution.py:132
  118.0 68.5 %collective-permute-start.17 = (bf16[320,1280]{1,0:T(8,128)(2,1)S(1)}, bf16[320,1280]{1,0:T(8,128)(2,1)S(1)}, u32[]{:S(2)}, u32[]{:S(2)}) collective-permute-start(bf16[320,1280]{1,0:T(8,128)(2,1)S(1)} %get-tuple-element.13), channel_id=1, source_target_pairs={{0,1},{1,0},{2,3},{3,2},{4,5},{5,4},{6,7},{7,6},{8,9},{9,8},{10,11... | collective-permute-start | bytes 2457608 | tf_op jit(solution)/shard_map/ppermute | solution.py:133
  118.6 48.9 %collective-permute-start.21 = (bf16[320,1280]{1,0:T(8,128)(2,1)S(1)}, bf16[320,1280]{1,0:T(8,128)(2,1)S(1)}, u32[]{:S(2)}, u32[]{:S(2)}) collective-permute-start(bf16[320,1280]{1,0:T(8,128)(2,1)S(1)} %get-tuple-element.12), channel_id=1, source_target_pairs={{0,1},{1,0},{2,3},{3,2},{4,5},{5,4},{6,7},{7,6},{8,9},{9,8},{10,11... | collective-permute-start | bytes 2457608 | tf_op jit(solution)/shard_map/ppermute | solution.py:132
  118.7 80.7 %collective-permute-start.20 = (bf16[320,1280]{1,0:T(8,128)(2,1)S(1)}, bf16[320,1280]{1,0:T(8,128)(2,1)S(1)}, u32[]{:S(2)}, u32[]{:S(2)}) collective-permute-start(bf16[320,1280]{1,0:T(8,128)(2,1)S(1)} %get-tuple-element.11), channel_id=1, source_target_pairs={{0,1},{1,0},{2,3},{3,2},{4,5},{5,4},{6,7},{7,6},{8,9},{9,8},{10,11... | collective-permute-start | bytes 2457608 | tf_op jit(solution)/shard_map/ppermute | solution.py:133
  167.1 9.9 %collective-permute-start.16 = (bf16[80,1280]{1,0:T(8,128)(2,1)S(1)}, bf16[80,1280]{1,0:T(8,128)(2,1)S(1)}, u32[]{:S(2)}, u32[]{:S(2)}) collective-permute-start(bf16[80,1280]{1,0:T(8,128)(2,1)S(1)} %get-tuple-element.20), channel_id=1, source_target_pairs={{0,8},{4,12},{8,16},{12,20},{16,24},{20,28},{24,0},{28,4},{1,9},{5... | collective-permute-start | bytes 614408 | tf_op jit(solution)/shard_map/ppermute | solution.py:125
  167.2 17.7 %collective-permute-start.15 = (bf16[80,1280]{1,0:T(8,128)(2,1)S(1)}, bf16[80,1280]{1,0:T(8,128)(2,1)S(1)}, u32[]{:S(2)}, u32[]{:S(2)}) collective-permute-start(bf16[80,1280]{1,0:T(8,128)(2,1)S(1)} %get-tuple-element.21), channel_id=1, source_target_pairs={{0,16},{4,20},{8,24},{12,28},{16,0},{20,4},{24,8},{28,12},{1,17},{... | collective-permute-start | bytes 614408 | tf_op jit(solution)/shard_map/ppermute | solution.py:125
  167.5 17.4 %collective-permute-start.14 = (bf16[80,1280]{1,0:T(8,128)(2,1)S(1)}, bf16[80,1280]{1,0:T(8,128)(2,1)S(1)}, u32[]{:S(2)}, u32[]{:S(2)}) collective-permute-start(bf16[80,1280]{1,0:T(8,128)(2,1)S(1)} %get-tuple-element.22), channel_id=1, source_target_pairs={{0,24},{4,28},{8,0},{12,4},{16,8},{20,12},{24,16},{28,20},{1,25},{... | collective-permute-start | bytes 614408 | tf_op jit(solution)/shard_map/ppermute | solution.py:125
  177.0 21.2 %collective-permute-start.19 = (bf16[320,1280]{1,0:T(8,128)(2,1)S(1)}, bf16[320,1280]{1,0:T(8,128)(2,1)S(1)}, u32[]{:S(2)}, u32[]{:S(2)}) collective-permute-start(bf16[320,1280]{1,0:T(8,128)(2,1)S(1)} %fusion.22), channel_id=1, source_target_pairs={{0,4},{4,0},{8,12},{12,8},{16,20},{20,16},{24,28},{28,24},{1,5},{5... | collective-permute-start | bytes 2457608 | tf_op jit(solution)/shard_map/ppermute | solution.py:134
  184.8 28.8 %collective-permute-start.22 = (bf16[320,1280]{1,0:T(8,128)(2,1)S(1)}, bf16[320,1280]{1,0:T(8,128)(2,1)S(1)}, u32[]{:S(2)}, u32[]{:S(2)}) collective-permute-start(bf16[320,1280]{1,0:T(8,128)(2,1)S(1)} %fusion.19), channel_id=1, source_target_pairs={{0,4},{4,0},{8,12},{12,8},{16,20},{20,16},{24,28},{28,24},{1,5},{5... | collective-permute-start | bytes 2457608 | tf_op jit(solution)/shard_map/ppermute | solution.py:134
  (5 other events, 92.7 us)

commit v2 on v1

--- a/solution.py
+++ b/solution.py
@@ -61,9 +61,10 @@
     first = w_in[0].T
     second = w_out[0]
     first_y = lax.ppermute(first, "expert", swap_half)
-    second_y = lax.ppermute(second, "expert", swap_half)
     first_c = lax.ppermute(first, "dp", swap_pair)
     second_c = lax.ppermute(second, "dp", swap_pair)
+    second_held, first_y = lax.optimization_barrier((second, first_y))
+    second_y = lax.ppermute(second_held, "expert", swap_half)
     first_yc = lax.ppermute(first_y, "dp", swap_pair)
     second_yc = lax.ppermute(second_y, "dp", swap_pair)
 
@@ -81,9 +82,17 @@
     send_d = dot(places, cotangent, 1, 0).astype(BF16).reshape(experts, 1, capacity, width)
     send = jnp.concatenate([send_m, send_d], axis=1)
 
-    near = [send[0]]
-    for step in range(1, experts):
-        near.append(lax.ppermute(send[step], "expert", turn_experts(step)))
+    send, first_c, second_c = lax.optimization_barrier((send, first_c, second_c))
+    near = [send[0]] + [None] * (experts - 1)
+    ranks = sorted(range(1, experts), key=lambda step: min(step, experts - step))
+    waves = [[step for step in ranks if min(step, experts - step) == reach] for reach in range(1, experts)]
+    waves = [wave for wave in waves if wave]
+    held = [send[step] for step in range(experts)]
+    for number, wave in enumerate(waves):
+        for step in wave:
+            near[step] = lax.ppermute(held[step], "expert", turn_experts(step))
+        for step in waves[number + 1] if number + 1 < len(waves) else ():
+            held[step], *_ = lax.optimization_barrier((held[step], *[near[one] for one in wave]))
     parts = [near]
     for step in range(1, columns):
         parts.append([lax.ppermute(piece, "dp", turn_columns(step)) for piece in near])
@@ -97,11 +106,27 @@
     gate = jax.nn.sigmoid(jnp.dot(rows_m, column, preferred_element_type=F32))
     value, slope = gelu_parts(dot(rows_m, all_first, 1, 1))
     hidden = value.astype(BF16)
-    back = dot(rows_d, all_second, 1, 1)
+    grad_y = (gate * rows_d.astype(F32)).astype(BF16)
+    grad_second = dot(hidden, grad_y, 0, 0)
+    units = first.shape[0]
+
+    def pair_sum(whole):
+        blocks = whole.reshape(4, units, width)
+        half = blocks[2] + lax.ppermute(blocks[3].astype(BF16), "dp", swap_pair).astype(F32)
+        mine = blocks[0] + lax.ppermute(blocks[1].astype(BF16), "dp", swap_pair).astype(F32)
+        return mine, half.astype(BF16)
+
+    out_mine, out_half = pair_sum(grad_second)
+    held_d, grad_second = lax.optimization_barrier((rows_d, grad_second))
+    back = dot(held_d, all_second, 1, 1)
     gate_gradient = jnp.sum(hidden.astype(F32) * back, axis=1, keepdims=True)
     logit_gradient = gate_gradient * gate * (1.0 - gate)
     grad_pre = (gate * back * slope).astype(BF16)
-    grad_y = (gate * rows_d.astype(F32)).astype(BF16)
+    out_half, grad_pre = lax.optimization_barrier((out_half, grad_pre))
+    out_other = lax.ppermute(out_half, "expert", swap_half)
+    grad_first = dot(grad_pre, rows_m, 0, 0)
+    in_mine, in_half = pair_sum(grad_first)
+    grad_pre, grad_first = lax.optimization_barrier((grad_pre, grad_first))
     router_row = column[:, 0].astype(F32)[None, :]
 
     def row_gradient(at, kind):
@@ -114,41 +139,32 @@
         lax.ppermute(row_gradient(step, BF16), "dp", turn_columns(columns - step))
         for step in range(1, columns)
     ]
-    grad_second = dot(hidden, grad_y, 0, 0)
-    grad_first = dot(grad_pre, rows_m, 0, 0)
     own_rows = row_gradient(0, F32)
+    in_half, own_rows = lax.optimization_barrier((in_half, own_rows))
+    in_other = lax.ppermute(in_half, "expert", swap_half)
     for piece in back_rows:
         own_rows = own_rows + piece.astype(F32)
     own_rows = own_rows.astype(BF16).reshape(experts, capacity, width)
     returned = [own_rows[0]]
     for step in range(1, experts):
         returned.append(lax.ppermute(own_rows[step], "expert", turn_experts(experts - step)))
+    grad_out = (out_mine + out_other.astype(F32)).astype(BF16)[None]
+    grad_in = (in_mine + in_other.astype(F32)).astype(BF16).T[None]
 
-    units = first.shape[0]
-
-    def weight_gradient(whole):
-        blocks = whole.reshape(4, units, width)
-        mine, pair, half, both = blocks[0], blocks[1], blocks[2], blocks[3]
-        half = half + lax.ppermute(both.astype(BF16), "dp", swap_pair).astype(F32)
-        mine = mine + lax.ppermute(pair.astype(BF16), "dp", swap_pair).astype(F32)
-        return (mine + lax.ppermute(half.astype(BF16), "expert", swap_half).astype(F32)).astype(BF16)
-
-    grad_out = weight_gradient(grad_second)[None]
-    grad_in = weight_gradient(grad_first).T[None]
-
-    partial = jnp.stack(
-        [
-            jnp.sum(rows_m.astype(F32) * logit_gradient, axis=0),
-            jnp.sum(all_first.astype(F32) * grad_first, axis=0),
-        ]
-    )
-    gathered = lax.all_gather(partial, ("expert", "dp"), axis=0)
-    gathered = jnp.sum(gathered.reshape(experts, 2 * groups, 2, width), axis=1)
-    router_t = gathered[:, 0]
+    router_part = jnp.sum(rows_m.astype(F32) * logit_gradient, axis=0)
+    gain_part = jnp.sum(all_first.astype(F32) * grad_first, axis=0)
+    is_own = (jnp.arange(experts + 1, dtype=jnp.int32) == own)[:, None]
+    is_last = (jnp.arange(experts + 1, dtype=jnp.int32) == experts)[:, None]
+    router_part, gain_part, in_half = lax.optimization_barrier((router_part, gain_part, in_half))
+    total = jnp.where(is_own, router_part[None], jnp.where(is_last, gain_part[None], 0.0))
+    for name, size in (("dp", groups), ("expert", halves)):
+        bit = 1
+        while bit < size:
+            total = total + lax.ppermute(total, name, [(i, i ^ bit) for i in range(size)])
+            bit *= 2
+    router_t = total[:experts]
     grad_router = router_t.T
-    grad_gain = (
-        jnp.sum(gathered[:, 1], axis=0) + jnp.sum(router_t * router.astype(F32).T, axis=0)
-    ) / gain
+    grad_gain = (total[experts] + jnp.sum(router_t * router.astype(F32).T, axis=0)) / gain
 
     mixed_gradient = dot(places, jnp.concatenate(returned, axis=0), 0, 0)
     scaled_rows = mixed_gradient * gain[None, :]

time: 215 us -> 177 us (0.82)
  blocking collectives: 43.8 us -> 0 us
  waiting for transfers between devices: 109 us -> 122 us
  matrix products: 28.1 us -> 18.5 us
    all_gather x1 -> x0, blocking collectives: 43.8 us -> none  [body(): gathered = lax.all_gather(partial, ('expert', 'dp'), axis=0)]
    ppermute x10 -> x15, waiting for transfers between devices: 64.7 us -> 90.5 us  [the longest x5 52.5 us: body(): lax.ppermute(total, name, [(i, i ^ bit) for i in range(size)])]
    ppermute x4, waiting for transfers between devices: 31.4 us -> 16.8 us  [body(): lax.ppermute(piece, 'dp', turn_columns(step))]
    ppermute x1, waiting for transfers between devices: 0.01 us -> 10.8 us  [body(): first_y = lax.ppermute(first, 'expert', swap_half)]
    ppermute x3, waiting for transfers between devices: 13.4 us -> 3.64 us  [body(): lax.ppermute(own_rows[step], 'expert', turn_experts(experts - step))]
    dot_general x10, matrix products: 27.5 us -> 17.9 us  [dot(): lax.dot_general(a, b, (((a_dim,), (b_dim,)), ((), ())), preferred_element...]
    ppermute x10 -> x15, starting transfers between devices: 6.36 us -> 11.3 us  [the longest x3 4.34 us: body(): near[step] = lax.ppermute(held[step], 'expert', turn_experts(step))]
  transfers between devices with their start and end apart: 23 -> 28, of which waited for: 11 -> 11; matrix products, arithmetic and copies ran while one was open for 13% -> 14% of each run, Pallas kernels for 0% -> 0%
where the time goes in v2:
time: 177 us
  waiting for transfers between devices  122 us (69%)
  starting transfers between devices  23.6 us (13%)
  matrix products  18.5 us (10%)
  other arithmetic  10.2 us (6%)
    ppermute x5, waiting for transfers between devices, body(): lax.ppermute(total, name, [(i, i ^ bit) for i in range(size)])  52.5 us
    ppermute x3, waiting for transfers between devices, body(): near[step] = lax.ppermute(held[step], 'expert', turn_experts(step))  37.9 us
    dot_general x10, matrix products, dot(): lax.dot_general(a, b, (((a_dim,), (b_dim,)), ((), ())), preferred_element...  17.9 us
    ppermute x4, waiting for transfers between devices, body(): lax.ppermute(piece, 'dp', turn_columns(step))  16.8 us
    ppermute x1, waiting for transfers between devices, body(): first_y = lax.ppermute(first, 'expert', swap_half)  10.8 us
    ppermute x3, starting transfers between devices, body(): near[step] = lax.ppermute(held[step], 'expert', turn_experts(step))  4.34 us
    ppermute x4, starting transfers between devices, body(): lax.ppermute(piece, 'dp', turn_columns(step))  4.18 us
    ppermute x3, starting transfers between devices, body(): lax.ppermute(own_rows[step], 'expert', turn_experts(experts - step))  4 us
  transfers between devices with their start and end apart: 28, of which 11 were waited for; matrix products, arithmetic and copies ran while one was open for 14% of the time, Pallas kernels for 0%

profile of v2, /device:TPU:0, one launch (start us, length us, event | category | flops | bytes accessed | tf_op | source)
XLA Modules:
  0.0 176.5 jit_solution(6456518842459420044)
XLA Ops:
  0.6 3.0 %collective-permute-start.9 = (bf16[320,1280]{1,0:T(8,128)(2,1)}, bf16[320,1280]{1,0:T(8,128)(2,1)S(1)}, u32[]{:S(2)}, u32[]{:S(2)}) collective-permute-start(bf16[320,1280]{1,0:T(8,128)(2,1)} %bitcast.108), channel_id=1, source_target_pairs={{0,4},{4,0},{8,12},{12,8},{16,20},{20,16},{24,28},{28,24},{1,5},{5... | collective-permute-start | bytes 2457608 | tf_op jit(solution)/shard_map/ppermute | solution.py:63
  9.7 1.4 convolution_convert_fusion.1
  11.3 10.8 %collective-permute-done.9 = bf16[320,1280]{1,0:T(8,128)(2,1)S(1)} collective-permute-done((bf16[320,1280]{1,0:T(8,128)(2,1)}, bf16[320,1280]{1,0:T(8,128)(2,1)S(1)}, u32[]{:S(2)}, u32[]{:S(2)}) %collective-permute-start.9) | collective-permute-done | bytes 819232 | tf_op jit(solution)/shard_map/ppermute | solution.py:63
  22.1 1.7 collective-permute-start.12
  24.0 1.6 collective-permute-start.5
  25.6 3.6 %collective-permute-start.3 = (bf16[2,80,1280]{2,1,0:T(8,128)(2,1)S(1)}, bf16[2,80,1280]{2,1,0:T(8,128)(2,1)S(1)}, u32[]{:S(2)}, u32[]{:S(2)}) collective-permute-start(bf16[2,80,1280]{2,1,0:T(8,128)(2,1)S(1)} %get-tuple-element.46), channel_id=1, source_target_pairs={{0,24},{4,28},{8,0},{12,4},{16,8},{20,12},{24,16},{28,20},{1,25},{... | collective-permute-start | bytes 1228808 | tf_op jit(solution)/shard_map/ppermute | solution.py:93
  29.2 9.8 %collective-permute-done.3 = bf16[2,80,1280]{2,1,0:T(8,128)(2,1)S(1)} collective-permute-done((bf16[2,80,1280]{2,1,0:T(8,128)(2,1)S(1)}, bf16[2,80,1280]{2,1,0:T(8,128)(2,1)S(1)}, u32[]{:S(2)}, u32[]{:S(2)}) %collective-permute-start.3) | collective-permute-done | bytes 409632 | tf_op jit(solution)/shard_map/ppermute | solution.py:93
  39.0 8.9 %collective-permute-done.2 = bf16[2,80,1280]{2,1,0:T(8,128)(2,1)S(1)} collective-permute-done((bf16[2,80,1280]{2,1,0:T(8,128)(2,1)S(1)}, bf16[2,80,1280]{2,1,0:T(8,128)(2,1)S(1)}, u32[]{:S(2)}, u32[]{:S(2)}) %collective-permute-start.2) | collective-permute-done | bytes 409632 | tf_op jit(solution)/shard_map/ppermute | solution.py:93
  49.3 19.1 %collective-permute-done.4 = bf16[2,80,1280]{2,1,0:T(8,128)(2,1)S(1)} collective-permute-done((bf16[2,80,1280]{2,1,0:T(8,128)(2,1)S(1)}, bf16[2,80,1280]{2,1,0:T(8,128)(2,1)S(1)}, u32[]{:S(2)}, u32[]{:S(2)}) %collective-permute-start.4) | collective-permute-done | bytes 409632 | tf_op jit(solution)/shard_map/ppermute | solution.py:93
  69.0 1.6 collective-permute-start.7
  70.6 10.2 %collective-permute-done.6 = bf16[2,80,1280]{2,1,0:T(8,128)(2,1)S(1)} collective-permute-done((bf16[2,80,1280]{2,1,0:T(8,128)(2,1)S(1)}, bf16[2,80,1280]{2,1,0:T(8,128)(2,1)S(1)}, u32[]{:S(2)}, u32[]{:S(2)}) %collective-permute-start.6) | collective-permute-done | bytes 409632 | tf_op jit(solution)/shard_map/ppermute | solution.py:98
  80.8 6.6 %collective-permute-done.7 = bf16[2,80,1280]{2,1,0:T(8,128)(2,1)S(1)} collective-permute-done((bf16[2,80,1280]{2,1,0:T(8,128)(2,1)S(1)}, bf16[2,80,1280]{2,1,0:T(8,128)(2,1)S(1)}, u32[]{:S(2)}, u32[]{:S(2)}) %collective-permute-start.7) | collective-permute-done | bytes 409632 | tf_op jit(solution)/shard_map/ppermute | solution.py:98
  88.1 2.3 %fusion.73 = f32[640,1280]{1,0:T(8,128)S(1)} fusion(bf16[640,1280]{1,0:T(8,128)(2,1)S(1)} %get-tuple-element.53, bf16[320,1280]{1,0:T(8,128)(2,1)S(1)} %collective-permute-done.10, bf16[320,1280]{1,0:T(8,128)(2,1)S(1)} %collective-permute-done.9, bf16[320,1280]{1,0:T(8,128)(2,1)S(1)} %collective-permute-done, bf16[320,1280]{1,0:T(8,128)(2,1)S(1)} %bitcast.110), kind=kOutput, calls=%fused_computation.135 | convolution fusion | flops 2110259200 | bytes 8192000 | tf_op jit(solution)/shard_map/dot_general | solution.py:38
  90.4 3.1 %fusion.79 = (bf16[1280,1280]{1,0:T(8,128)(2,1)S(1)}, f32[1280,1280]{1,0:T(8,128)S(1)}) fusion(bf16[640,1280]{1,0:T(8,128)(2,1)S(1)} %get-tuple-element.24, f32[640]{0:T(1024)S(1)} %add_divide_fusion.1, f32[640,1280]{1,0:T(8,128)S(1)} %fusion.73), kind=kOutput, calls=%fused_computation.141 | convolution fusion | flops 2108620800 | bytes 14748160 | tf_op jit(solution)/shard_map/dot_general | solution.py:38
  93.7 3.7 %multiply_reduce_fusion.2 = (f32[640]{0:T(1024)S(1)}, bf16[640,1280]{1,0:T(8,128)(2,1)S(1)}) fusion(f32[640,1280]{1,0:T(8,128)S(1)} %fusion.73, f32[640]{0:T(1024)S(1)} %add_divide_fusion.1, bf16[640,1280]{1,0:T(8,128)(2,1)S(1)} %get-tuple-element.24, bf16[320,1280]{1,0:T(8,128)(2,1)S(1)} %collective-permute-done.13, ...), kind=kOutput, calls=%fused_computation.20 | convolution fusion | flops 2130738560 | bytes 9835520 | tf_op jit(solution)/shard_map/dot_general | solution.py:38
  98.2 3.0 %fusion.80 = (bf16[1280,1280]{1,0:T(8,128)(2,1)S(1)}, f32[1280,1280]{1,0:T(8,128)S(1)}) fusion(bf16[640,1280]{1,0:T(8,128)(2,1)S(1)} %get-tuple-element.28, bf16[640,1280]{1,0:T(8,128)(2,1)S(1)} %get-tuple-element.53), kind=kOutput, calls=%fused_computation.142 | convolution fusion | flops 2098790400 | bytes 13107200 | tf_op jit(solution)/shard_map/dot_general | solution.py:38
  106.3 1.5 collective-permute-start.24
  108.5 18.5 %collective-permute-done.24 = f32[5,1280]{1,0:T(8,128)S(1)} collective-permute-done((f32[5,1280]{1,0:T(8,128)S(1)}, f32[5,1280]{1,0:T(8,128)S(1)}, u32[]{:S(2)}, u32[]{:S(2)}) %collective-permute-start.24) | collective-permute-done | bytes 25632 | tf_op jit(solution)/shard_map/ppermute | solution.py:163
  127.6 1.6 collective-permute-start.25
  129.4 18.2 %collective-permute-done.25 = f32[5,1280]{1,0:T(8,128)S(1)} collective-permute-done((f32[5,1280]{1,0:T(8,128)S(1)}, f32[5,1280]{1,0:T(8,128)S(1)}, u32[]{:S(2)}, u32[]{:S(2)}) %collective-permute-start.25) | collective-permute-done | bytes 25632 | tf_op jit(solution)/shard_map/ppermute | solution.py:163
  147.6 3.9 %collective-permute-done.26 = f32[5,1280]{1,0:T(8,128)S(1)} collective-permute-done((f32[5,1280]{1,0:T(8,128)S(1)}, f32[5,1280]{1,0:T(8,128)S(1)}, u32[]{:S(2)}, u32[]{:S(2)}) %collective-permute-start.26) | collective-permute-done | bytes 25632 | tf_op jit(solution)/shard_map/ppermute | solution.py:163
  151.6 3.0 %collective-permute-start.17 = (bf16[80,1280]{1,0:T(8,128)(2,1)S(1)}, bf16[80,1280]{1,0:T(8,128)(2,1)S(1)}, u32[]{:S(2)}, u32[]{:S(2)}) collective-permute-start(bf16[80,1280]{1,0:T(8,128)(2,1)S(1)} %get-tuple-element.51), channel_id=1, source_target_pairs={{0,16},{4,20},{8,24},{12,28},{16,0},{20,4},{24,8},{28,12},{1,17},{... | collective-permute-start | bytes 614408 | tf_op jit(solution)/shard_map/ppermute | solution.py:150
  156.0 11.9 %collective-permute-done.27 = f32[5,1280]{1,0:T(8,128)S(1)} collective-permute-done((f32[5,1280]{1,0:T(8,128)S(1)}, f32[5,1280]{1,0:T(8,128)S(1)}, u32[]{:S(2)}, u32[]{:S(2)}) %collective-permute-start.27) | collective-permute-done | bytes 25632 | tf_op jit(solution)/shard_map/ppermute | solution.py:163
  170.1 3.6 %collective-permute-done.16 = bf16[80,1280]{1,0:T(8,128)(2,1)S(1)} collective-permute-done((bf16[80,1280]{1,0:T(8,128)(2,1)S(1)}, bf16[80,1280]{1,0:T(8,128)(2,1)S(1)}, u32[]{:S(2)}, u32[]{:S(2)}) %collective-permute-start.16) | collective-permute-done | bytes 204832 | tf_op jit(solution)/shard_map/ppermute | solution.py:150
  (101 shorter events, 22.7 us)
Async XLA Ops:
  0.6 21.5 %collective-permute-start.9 = (bf16[320,1280]{1,0:T(8,128)(2,1)}, bf16[320,1280]{1,0:T(8,128)(2,1)S(1)}, u32[]{:S(2)}, u32[]{:S(2)}) collective-permute-start(bf16[320,1280]{1,0:T(8,128)(2,1)} %bitcast.108), channel_id=1, source_target_pairs={{0,4},{4,0},{8,12},{12,8},{16,20},{20,16},{24,28},{28,24},{1,5},{5... | collective-permute-start | bytes 2457608 | tf_op jit(solution)/shard_map/ppermute | solution.py:63
  3.7 20.2 %collective-permute-start = (bf16[320,1280]{1,0:T(8,128)(2,1)}, bf16[320,1280]{1,0:T(8,128)(2,1)S(1)}, u32[]{:S(2)}, u32[]{:S(2)}) collective-permute-start(bf16[320,1280]{1,0:T(8,128)(2,1)} %bitcast.109), channel_id=1, source_target_pairs={{0,1},{1,0},{2,3},{3,2},{4,5},{5,4},{6,7},{7,6},{8,9},{9,8},{10,11... | collective-permute-start | bytes 2457608 | tf_op jit(solution)/shard_map/ppermute | solution.py:64
  3.7 20.2 %collective-permute-start.1 = (bf16[320,1280]{1,0:T(8,128)(2,1)}, bf16[320,1280]{1,0:T(8,128)(2,1)S(1)}, u32[]{:S(2)}, u32[]{:S(2)}) collective-permute-start(bf16[320,1280]{1,0:T(8,128)(2,1)} %bitcast.114), channel_id=1, source_target_pairs={{0,1},{1,0},{2,3},{3,2},{4,5},{5,4},{6,7},{7,6},{8,9},{9,8},{10,11... | collective-permute-start | bytes 2457608 | tf_op jit(solution)/shard_map/ppermute | solution.py:65
  22.1 48.4 %collective-permute-start.12 = (bf16[320,1280]{1,0:T(8,128)(2,1)S(1)}, bf16[320,1280]{1,0:T(8,128)(2,1)S(1)}, u32[]{:S(2)}, u32[]{:S(2)}) collective-permute-start(bf16[320,1280]{1,0:T(8,128)(2,1)S(1)} %bitcast.115), channel_id=1, source_target_pairs={{0,4},{4,0},{8,12},{12,8},{16,20},{20,16},{24,28},{28,24},{1,5},{5... | collective-permute-start | bytes 2457608 | tf_op jit(solution)/shard_map/ppermute | solution.py:67
  23.9 64.2 %collective-permute-start.10 = (bf16[320,1280]{1,0:T(8,128)(2,1)S(1)}, bf16[320,1280]{1,0:T(8,128)(2,1)S(1)}, u32[]{:S(2)}, u32[]{:S(2)}) collective-permute-start(bf16[320,1280]{1,0:T(8,128)(2,1)S(1)} %collective-permute-done.9), channel_id=1, source_target_pairs={{0,1},{1,0},{2,3},{3,2},{4,5},{5,4},{6,7},{7,6},{8,9},{9,8},{10,11... | collective-permute-start | bytes 2457608 | tf_op jit(solution)/shard_map/ppermute | solution.py:68
  24.0 45.0 %collective-permute-start.5 = (bf16[2,80,1280]{2,1,0:T(8,128)(2,1)S(1)}, bf16[2,80,1280]{2,1,0:T(8,128)(2,1)S(1)}, u32[]{:S(2)}, u32[]{:S(2)}) collective-permute-start(bf16[2,80,1280]{2,1,0:T(8,128)(2,1)S(1)} %get-tuple-element.45), channel_id=1, source_target_pairs={{0,2},{1,3},{2,0},{3,1},{4,6},{5,7},{6,4},{7,5},{8,10},{9,11},{10,... | collective-permute-start | bytes 1228808 | tf_op jit(solution)/shard_map/ppermute | solution.py:98
  25.6 13.5 %collective-permute-start.3 = (bf16[2,80,1280]{2,1,0:T(8,128)(2,1)S(1)}, bf16[2,80,1280]{2,1,0:T(8,128)(2,1)S(1)}, u32[]{:S(2)}, u32[]{:S(2)}) collective-permute-start(bf16[2,80,1280]{2,1,0:T(8,128)(2,1)S(1)} %get-tuple-element.46), channel_id=1, source_target_pairs={{0,24},{4,28},{8,0},{12,4},{16,8},{20,12},{24,16},{28,20},{1,25},{... | collective-permute-start | bytes 1228808 | tf_op jit(solution)/shard_map/ppermute | solution.py:93
  29.2 18.8 %collective-permute-start.2 = (bf16[2,80,1280]{2,1,0:T(8,128)(2,1)S(1)}, bf16[2,80,1280]{2,1,0:T(8,128)(2,1)S(1)}, u32[]{:S(2)}, u32[]{:S(2)}) collective-permute-start(bf16[2,80,1280]{2,1,0:T(8,128)(2,1)S(1)} %get-tuple-element.48), channel_id=1, source_target_pairs={{0,8},{4,12},{8,16},{12,20},{16,24},{20,28},{24,0},{28,4},{1,9},{5... | collective-permute-start | bytes 1228808 | tf_op jit(solution)/shard_map/ppermute | solution.py:93
  48.0 20.4 %collective-permute-start.4 = (bf16[2,80,1280]{2,1,0:T(8,128)(2,1)S(1)}, bf16[2,80,1280]{2,1,0:T(8,128)(2,1)S(1)}, u32[]{:S(2)}, u32[]{:S(2)}) collective-permute-start(bf16[2,80,1280]{2,1,0:T(8,128)(2,1)S(1)} %get-tuple-element.21), channel_id=1, source_target_pairs={{0,16},{4,20},{8,24},{12,28},{16,0},{20,4},{24,8},{28,12},{1,17},{... | collective-permute-start | bytes 1228808 | tf_op jit(solution)/shard_map/ppermute | solution.py:93
  48.7 38.8 %collective-permute-start.8 = (bf16[2,80,1280]{2,1,0:T(8,128)(2,1)S(1)}, bf16[2,80,1280]{2,1,0:T(8,128)(2,1)S(1)}, u32[]{:S(2)}, u32[]{:S(2)}) collective-permute-start(bf16[2,80,1280]{2,1,0:T(8,128)(2,1)S(1)} %collective-permute-done.3), channel_id=1, source_target_pairs={{0,2},{1,3},{2,0},{3,1},{4,6},{5,7},{6,4},{7,5},{8,10},{9,11},{10,... | collective-permute-start | bytes 1228808 | tf_op jit(solution)/shard_map/ppermute | solution.py:98
  68.4 12.4 %collective-permute-start.6 = (bf16[2,80,1280]{2,1,0:T(8,128)(2,1)S(1)}, bf16[2,80,1280]{2,1,0:T(8,128)(2,1)S(1)}, u32[]{:S(2)}, u32[]{:S(2)}) collective-permute-start(bf16[2,80,1280]{2,1,0:T(8,128)(2,1)S(1)} %collective-permute-done.2), channel_id=1, source_target_pairs={{0,2},{1,3},{2,0},{3,1},{4,6},{5,7},{6,4},{7,5},{8,10},{9,11},{10,... | collective-permute-start | bytes 1228808 | tf_op jit(solution)/shard_map/ppermute | solution.py:98
  69.0 18.4 %collective-permute-start.7 = (bf16[2,80,1280]{2,1,0:T(8,128)(2,1)S(1)}, bf16[2,80,1280]{2,1,0:T(8,128)(2,1)S(1)}, u32[]{:S(2)}, u32[]{:S(2)}) collective-permute-start(bf16[2,80,1280]{2,1,0:T(8,128)(2,1)S(1)} %collective-permute-done.4), channel_id=1, source_target_pairs={{0,2},{1,3},{2,0},{3,1},{4,6},{5,7},{6,4},{7,5},{8,10},{9,11},{10,... | collective-permute-start | bytes 1228808 | tf_op jit(solution)/shard_map/ppermute | solution.py:98
  70.6 23.2 %collective-permute-start.13 = (bf16[320,1280]{1,0:T(8,128)(2,1)S(1)}, bf16[320,1280]{1,0:T(8,128)(2,1)S(1)}, u32[]{:S(2)}, u32[]{:S(2)}) collective-permute-start(bf16[320,1280]{1,0:T(8,128)(2,1)S(1)} %collective-permute-done.12), channel_id=1, source_target_pairs={{0,1},{1,0},{2,3},{3,2},{4,5},{5,4},{6,7},{7,6},{8,9},{9,8},{10,11... | collective-permute-start | bytes 2457608 | tf_op jit(solution)/shard_map/ppermute | solution.py:69
  105.6 22.0 %collective-permute-start.15 = (bf16[320,1280]{1,0:T(8,128)(2,1)S(1)}, bf16[320,1280]{1,0:T(8,128)(2,1)S(1)}, u32[]{:S(2)}, u32[]{:S(2)}) collective-permute-start(bf16[320,1280]{1,0:T(8,128)(2,1)S(1)} %fusion.15), channel_id=1, source_target_pairs={{0,2},{1,3},{2,0},{3,1},{4,6},{5,7},{6,4},{7,5},{8,10},{9,11},{10,... | collective-permute-start | bytes 2457608 | tf_op jit(solution)/shard_map/ppermute | solution.py:139
  106.3 20.8 %collective-permute-start.24 = (f32[5,1280]{1,0:T(8,128)S(1)}, f32[5,1280]{1,0:T(8,128)S(1)}, u32[]{:S(2)}, u32[]{:S(2)}) collective-permute-start(f32[5,1280]{1,0:T(8,128)S(1)} %fusion.72), channel_id=1, source_target_pairs={{0,2},{1,3},{2,0},{3,1},{4,6},{5,7},{6,4},{7,5},{8,10},{9,11},{10,... | collective-permute-start | bytes 76808 | tf_op jit(solution)/shard_map/ppermute | solution.py:163
  107.8 43.8 %collective-permute-start.21 = (bf16[320,1280]{1,0:T(8,128)(2,1)S(1)}, bf16[320,1280]{1,0:T(8,128)(2,1)S(1)}, u32[]{:S(2)}, u32[]{:S(2)}) collective-permute-start(bf16[320,1280]{1,0:T(8,128)(2,1)S(1)} %get-tuple-element.39), channel_id=1, source_target_pairs={{0,1},{1,0},{2,3},{3,2},{4,5},{5,4},{6,7},{7,6},{8,9},{9,8},{10,11... | collective-permute-start | bytes 2457608 | tf_op jit(solution)/shard_map/ppermute | solution.py:116
  107.8 46.9 %collective-permute-start.22 = (bf16[320,1280]{1,0:T(8,128)(2,1)S(1)}, bf16[320,1280]{1,0:T(8,128)(2,1)S(1)}, u32[]{:S(2)}, u32[]{:S(2)}) collective-permute-start(bf16[320,1280]{1,0:T(8,128)(2,1)S(1)} %fusion.22), channel_id=1, source_target_pairs={{0,4},{4,0},{8,12},{12,8},{16,20},{20,16},{24,28},{28,24},{1,5},{5... | collective-permute-start | bytes 2457608 | tf_op jit(solution)/shard_map/ppermute | solution.py:126
  108.3 67.0 %collective-permute-start.19 = (bf16[320,1280]{1,0:T(8,128)(2,1)S(1)}, bf16[320,1280]{1,0:T(8,128)(2,1)S(1)}, u32[]{:S(2)}, u32[]{:S(2)}) collective-permute-start(bf16[320,1280]{1,0:T(8,128)(2,1)S(1)} %get-tuple-element.41), channel_id=1, source_target_pairs={{0,1},{1,0},{2,3},{3,2},{4,5},{5,4},{6,7},{7,6},{8,9},{9,8},{10,11... | collective-permute-start | bytes 2457608 | tf_op jit(solution)/shard_map/ppermute | solution.py:116
  127.0 48.3 %collective-permute-start.20 = (bf16[320,1280]{1,0:T(8,128)(2,1)S(1)}, bf16[320,1280]{1,0:T(8,128)(2,1)S(1)}, u32[]{:S(2)}, u32[]{:S(2)}) collective-permute-start(bf16[320,1280]{1,0:T(8,128)(2,1)S(1)} %fusion.21), channel_id=1, source_target_pairs={{0,4},{4,0},{8,12},{12,8},{16,20},{20,16},{24,28},{28,24},{1,5},{5... | collective-permute-start | bytes 2457608 | tf_op jit(solution)/shard_map/ppermute | solution.py:144
  127.6 19.9 %collective-permute-start.25 = (f32[5,1280]{1,0:T(8,128)S(1)}, f32[5,1280]{1,0:T(8,128)S(1)}, u32[]{:S(2)}, u32[]{:S(2)}) collective-permute-start(f32[5,1280]{1,0:T(8,128)S(1)} %fusion.91), channel_id=1, source_target_pairs={{0,4},{4,0},{8,12},{12,8},{16,20},{20,16},{24,28},{28,24},{1,5},{5... | collective-permute-start | bytes 76808 | tf_op jit(solution)/shard_map/ppermute | solution.py:163
  151.6 18.6 %collective-permute-start.18 = (bf16[80,1280]{1,0:T(8,128)(2,1)S(1)}, bf16[80,1280]{1,0:T(8,128)(2,1)S(1)}, u32[]{:S(2)}, u32[]{:S(2)}) collective-permute-start(bf16[80,1280]{1,0:T(8,128)(2,1)S(1)} %get-tuple-element.50), channel_id=1, source_target_pairs={{0,8},{4,12},{8,16},{12,20},{16,24},{20,28},{24,0},{28,4},{1,9},{5... | collective-permute-start | bytes 614408 | tf_op jit(solution)/shard_map/ppermute | solution.py:150
  151.6 18.5 %collective-permute-start.17 = (bf16[80,1280]{1,0:T(8,128)(2,1)S(1)}, bf16[80,1280]{1,0:T(8,128)(2,1)S(1)}, u32[]{:S(2)}, u32[]{:S(2)}) collective-permute-start(bf16[80,1280]{1,0:T(8,128)(2,1)S(1)} %get-tuple-element.51), channel_id=1, source_target_pairs={{0,16},{4,20},{8,24},{12,28},{16,0},{20,4},{24,8},{28,12},{1,17},{... | collective-permute-start | bytes 614408 | tf_op jit(solution)/shard_map/ppermute | solution.py:150
  154.6 13.3 %collective-permute-start.27 = (f32[5,1280]{1,0:T(8,128)S(1)}, f32[5,1280]{1,0:T(8,128)S(1)}, u32[]{:S(2)}, u32[]{:S(2)}) collective-permute-start(f32[5,1280]{1,0:T(8,128)S(1)} %add.124), channel_id=1, source_target_pairs={{0,16},{4,20},{8,24},{12,28},{16,0},{20,4},{24,8},{28,12},{1,17},{... | collective-permute-start | bytes 76808 | tf_op jit(solution)/shard_map/ppermute | solution.py:163
  167.9 5.9 %collective-permute-start.16 = (bf16[80,1280]{1,0:T(8,128)(2,1)S(1)}, bf16[80,1280]{1,0:T(8,128)(2,1)S(1)}, u32[]{:S(2)}, u32[]{:S(2)}) collective-permute-start(bf16[80,1280]{1,0:T(8,128)(2,1)S(1)} %get-tuple-element.52), channel_id=1, source_target_pairs={{0,24},{4,28},{8,0},{12,4},{16,8},{20,12},{24,16},{28,20},{1,25},{... | collective-permute-start | bytes 614408 | tf_op jit(solution)/shard_map/ppermute | solution.py:150
  (10 other events, 219.3 us)

commit v3 on v2

v3 whole, which is shorter than its diff:
```python
import functools
import math

import jax
import jax.numpy as jnp
from jax import lax
from jax.experimental import pallas as pl
from jax.experimental.pallas import tpu as pltpu
from jax.sharding import PartitionSpec as P

F32 = jnp.float32
BF16 = jnp.bfloat16


def gelu_parts(pre):
    coeff = math.sqrt(2.0 / math.pi)
    inner = coeff * (pre + 0.044715 * pre * pre * pre)
    tanh_val = jnp.tanh(inner)
    value = 0.5 * pre * (1.0 + tanh_val)
    slope = 0.5 * (1.0 + tanh_val) + 0.5 * pre * (1.0 - tanh_val * tanh_val) * coeff * (
        1.0 + 3.0 * 0.044715 * pre * pre
    )
    return (value, slope)


def dot(a, b, a_dim, b_dim):
    return lax.dot_general(a, b, (((a_dim,), (b_dim,)), ((), ())), preferred_element_type=F32)


def norm_pieces(block):
    values = block.astype(F32)
    centred_rows = values - jnp.mean(values, axis=1, keepdims=True)
    inverse_deviation = lax.rsqrt(
        jnp.mean(centred_rows * centred_rows, axis=1, keepdims=True) + 1e-06
    )
    return centred_rows * inverse_deviation, inverse_deviation


def slot_of(own, routes, experts, capacity):
    top, tokens = routes.shape
    relative = routes - own
    relative = jnp.where(relative < 0, relative + experts, relative)
    lanes = max(16, experts)
    expert = lax.broadcasted_iota(jnp.int32, (lanes, tokens), 0)
    picks = [expert == relative[j : j + 1, :] for j in range(top)]
    chosen = sum(jnp.where(pick, 1.0, 0.0) for pick in picks)
    earlier = lax.broadcasted_iota(jnp.int32, (tokens, tokens), 0) < lax.broadcasted_iota(
        jnp.int32, (tokens, tokens), 1
    )
    before = dot(chosen.astype(BF16), jnp.where(earlier, 1.0, 0.0).astype(BF16), 1, 0)
    return [
        relative[j : j + 1, :] * capacity
        + jnp.sum(jnp.where(pick, before, 0.0), axis=0, keepdims=True).astype(jnp.int32)
        for j, pick in enumerate(picks)
    ]


def place_matrix(slots, first, count, tokens):
    row = lax.broadcasted_iota(jnp.int32, (count, tokens), 0) + first
    hit = slots[0] == row
    for slot in slots[1:]:
        hit = hit | (slot == row)
    return jnp.where(hit, 1.0, 0.0).astype(BF16)


def dispatch_kernel(experts, capacity, own_ref, x_ref, gain_ref, routes_ref, d_ref, *send_refs):
    tokens = x_ref.shape[0]
    normalized_rows, _ = norm_pieces(x_ref[...])
    mixed_rows = (normalized_rows * gain_ref[...]).astype(BF16)
    cotangent = d_ref[...]
    slots = slot_of(own_ref[0], routes_ref[...], experts, capacity)
    for step in range(experts):
        places = place_matrix(slots, step * capacity, capacity, tokens)
        send_refs[step][0] = dot(places, mixed_rows, 1, 0).astype(BF16)
        send_refs[step][1] = dot(places, cotangent, 1, 0).astype(BF16)


def combine_kernel(experts, capacity, own_ref, x_ref, gain_ref, routes_ref, d_ref, rows_ref, out_ref):
    tokens = x_ref.shape[0]
    normalized_rows, inverse_deviation = norm_pieces(x_ref[...])
    slots = slot_of(own_ref[0], routes_ref[...], experts, capacity)
    places = place_matrix(slots, 0, experts * capacity, tokens)
    scaled_rows = dot(places, rows_ref[...], 0, 0) * gain_ref[...]
    mean_first_term = jnp.mean(scaled_rows, axis=1, keepdims=True)
    mean_second_term = jnp.mean(scaled_rows * normalized_rows, axis=1, keepdims=True)
    norm_backward = inverse_deviation * (
        scaled_rows - mean_first_term - normalized_rows * mean_second_term
    )
    out_ref[...] = (d_ref[...].astype(F32) + norm_backward).astype(BF16)


VMEM = pl.BlockSpec(memory_space=pltpu.VMEM)
SMEM = pl.BlockSpec(memory_space=pltpu.SMEM)


def tied(values, after):
    held, _ = lax.optimization_barrier((values, after))
    return held


def body(prenorm_input, gain, router, routes, w_in, w_out, cotangent):
    halves = lax.axis_size("expert")
    experts = halves // 2
    groups = lax.axis_size("dp")
    columns = groups // 2
    tokens, width = prenorm_input.shape
    top = routes.shape[1]
    capacity = max(2, 5 * tokens * top // (4 * experts))
    own = lax.axis_index("expert") // 2

    swap_half = [(i, i ^ 1) for i in range(halves)]
    swap_pair = [(i, i ^ 1) for i in range(groups)]

    def turn_columns(step):
        return [(i, (i + 2 * step) % groups) for i in range(groups)]

    def turn_experts(step):
        return [(i, (i + 2 * step) % halves) for i in range(halves)]

    own_scalar = own.astype(jnp.int32).reshape(1)
    token_args = (own_scalar, prenorm_input, gain[None, :], routes.T, cotangent)
    send = pl.pallas_call(
        functools.partial(dispatch_kernel, experts, capacity),
        out_shape=[jax.ShapeDtypeStruct((2, capacity, width), BF16)] * experts,
        in_specs=[SMEM, VMEM, VMEM, VMEM, VMEM],
        out_specs=[VMEM] * experts,
        compiler_params=pltpu.CompilerParams(vmem_limit_bytes=32 * 2**20),
        name="dispatch",
    )(*token_args)

    def over_experts(value, step):
        return lax.ppermute(value, "expert", turn_experts(step))

    def over_columns(value):
        return [lax.ppermute(value, "dp", turn_columns(step)) for step in range(1, columns)]

    def over_half(value):
        return lax.ppermute(value, "expert", swap_half)

    def over_pair(value):
        return lax.ppermute(value, "dp", swap_pair)

    first = w_in[0].T
    second = w_out[0]
    reach = [min(step, experts - step) for step in range(experts)]
    close = [step for step in range(experts) if reach[step] == 1]
    far = [step for step in range(experts) if reach[step] > 1]
    near = {0: send[0]}
    for step in close:
        near[step] = over_experts(send[step], step)
    side = {0: over_columns(send[0])}
    first_y = over_half(tied(first, send[0]))
    first_c = over_pair(tied(first, send[0]))

    stage = (first_y, first_c, side[0], [near[step] for step in close])
    second_held, far_held, close_held, first_y = tied(
        (second, [send[step] for step in far], [near[step] for step in close], first_y), stage
    )
    for step, value in zip(far, far_held):
        near[step] = over_experts(value, step)
    for step, value in zip(close, close_held):
        side[step] = over_columns(value)
    second_y = over_half(second_held)
    first_yc = over_pair(first_y)

    stage = (second_y, first_yc, [near[step] for step in far], [side[step] for step in close])
    second_held, far_held, second_y = tied(
        (second_held, [near[step] for step in far], second_y), stage
    )
    for step, value in zip(far, far_held):
        side[step] = over_columns(value)
    second_c = over_pair(second_held)
    second_yc = over_pair(second_y)

    column = lax.dynamic_slice_in_dim(router, own, 1, 1)
    all_first = jnp.concatenate([first, first_c, first_y, first_yc], axis=0)
    all_second = jnp.concatenate([second, second_c, second_y, second_yc], axis=0)

    def gather_rows(steps):
        pieces = [near[step] for step in steps]
        for turn in range(columns - 1):
            pieces = pieces + [side[step][turn] for step in steps]
        return (
            jnp.concatenate([piece[0] for piece in pieces], axis=0),
            jnp.concatenate([piece[1] for piece in pieces], axis=0),
        )

    def front(rows_m, rows_d):
        gate = jax.nn.sigmoid(jnp.dot(rows_m, column, preferred_element_type=F32))
        value, slope = gelu_parts(dot(rows_m, all_first, 1, 1))
        grad_y = (gate * rows_d.astype(F32)).astype(BF16)
        return gate, value.astype(BF16), slope, grad_y

    def middle(rows_d, gate, hidden, slope):
        back = dot(rows_d, all_second, 1, 1)
        gate_gradient = jnp.sum(hidden.astype(F32) * back, axis=1, keepdims=True)
        logit_gradient = gate_gradient * gate * (1.0 - gate)
        return logit_gradient, (gate * back * slope).astype(BF16)

    groups_of = [[0] + close] + ([far] if far else [])
    done = []
    for steps in groups_of:
        m, d = gather_rows(steps)
        gate, hidden, slope, grad_y = front(m, d)
        logit_gradient, grad_pre = middle(d, gate, hidden, slope)
        done.append((m, hidden, grad_y, logit_gradient, grad_pre))
    rows_m, hidden, grad_y, logit_gradient, grad_pre = (
        jnp.concatenate(parts, axis=0) for parts in zip(*done)
    )
    units = first.shape[0]

    def pair_sum(whole):
        blocks = whole.reshape(4, units, width)
        half = blocks[2] + over_pair(blocks[3].astype(BF16)).astype(F32)
        mine = blocks[0] + over_pair(blocks[1].astype(BF16)).astype(F32)
        return mine, half.astype(BF16)

    grad_second = dot(hidden, grad_y, 0, 0)
    out_mine, out_half = pair_sum(grad_second)
    grad_pre = tied(grad_pre, grad_second)
    router_row = column[:, 0].astype(F32)[None, :]

    def row_gradient(turn, kind):
        parts = []
        for steps, (_, _, _, logit_part, grad_part) in zip(groups_of, done):
            count = len(steps) * capacity
            part = slice(turn * count, (turn + 1) * count)
            parts.append(
                (dot(grad_part[part], all_first, 1, 0) + logit_part[part] * router_row).astype(kind)
            )
        return jnp.concatenate(parts, axis=0)

    back_rows = [
        lax.ppermute(row_gradient(turn, BF16), "dp", turn_columns(columns - turn))
        for turn in range(1, columns)
    ]
    out_half, grad_pre = lax.optimization_barrier((out_half, grad_pre))
    out_other = over_half(out_half)
    grad_first = dot(grad_pre, rows_m, 0, 0)
    in_mine, in_half = pair_sum(grad_first)
    own_rows = row_gradient(0, F32)
    in_other = over_half(in_half)
    for piece in back_rows:
        own_rows = own_rows + piece.astype(F32)
    own_rows = own_rows.astype(BF16).reshape(experts, capacity, width)
    order = [step for steps in groups_of for step in steps]
    returned = [None] * experts
    for place, step in enumerate(order):
        if step == 0:
            returned[step] = own_rows[place]
        else:
            returned[step] = over_experts(own_rows[place], experts - step)
    grad_out = (out_mine + out_other.astype(F32)).astype(BF16)[None]
    grad_in = (in_mine + in_other.astype(F32)).astype(BF16).T[None]

    router_part = jnp.sum(rows_m.astype(F32) * logit_gradient, axis=0)
    gain_part = jnp.sum(all_first.astype(F32) * grad_first, axis=0)
    is_own = (jnp.arange(experts + 1, dtype=jnp.int32) == own)[:, None]
    is_last = (jnp.arange(experts + 1, dtype=jnp.int32) == experts)[:, None]
    router_part, gain_part, in_half = lax.optimization_barrier((router_part, gain_part, in_half))
    total = jnp.where(is_own, router_part[None], jnp.where(is_last, gain_part[None], 0.0))
    for name, size in (("dp", groups), ("expert", halves)):
        bit = 1
        while bit < size:
            total = total + lax.ppermute(total, name, [(i, i ^ bit) for i in range(size)])
            bit *= 2
    router_t = total[:experts]
    grad_router = router_t.T
    grad_gain = (total[experts] + jnp.sum(router_t * router.astype(F32).T, axis=0)) / gain

    input_grad = pl.pallas_call(
        functools.partial(combine_kernel, experts, capacity),
        out_shape=jax.ShapeDtypeStruct((tokens, width), BF16),
        in_specs=[SMEM, VMEM, VMEM, VMEM, VMEM, VMEM],
        out_specs=VMEM,
        compiler_params=pltpu.CompilerParams(vmem_limit_bytes=32 * 2**20),
        name="combine",
    )(*token_args, jnp.concatenate(returned, axis=0))
    return (input_grad, grad_in, grad_out, grad_router, grad_gain)


def solution(mesh):
    in_specs = (
        P(("expert", "dp"), None),
        P(),
        P(),
        P(("expert", "dp"), None),
        P("expert", None, "dp"),
        P("expert", "dp", None),
        P(("expert", "dp"), None),
    )
    out_specs = (
        P(("expert", "dp"), None),
        P("expert", None, "dp"),
        P("expert", "dp", None),
        P(),
        P(),
    )
    return jax.shard_map(body, mesh=mesh, in_specs=in_specs, out_specs=out_specs, check_vma=False)
```

time: 177 us -> 146 us (0.82); the launches traced: 177 us -> 144 us
  waiting for transfers between devices: 122 us -> 77.5 us
  starting transfers between devices: 23.6 us -> 31.2 us
  local copies, waits for them, and re-layouts: 1.55 us -> 7.95 us
  other arithmetic: 10.2 us -> 6.14 us
  Pallas kernels: 0 us -> 2.35 us
    ppermute x5, waiting for transfers between devices: 52.5 us -> 1.11 us  [body(): lax.ppermute(total, name, [(i, i ^ bit) for i in range(size)])]
    ppermute x23, waiting for transfers between devices: 69.2 us -> 76.4 us  [the longest x6 29.2 us: over_experts(): return lax.ppermute(value, 'expert', turn_experts(step))]
    unnamed x19 -> x27, local copies, waits for them, and re-layouts: 0.22 us -> 6.01 us
    ppermute x23, starting transfers between devices: 20.3 us -> 24.5 us  [the longest x6 12.9 us: over_experts(): return lax.ppermute(value, 'expert', turn_experts(step))]
    ppermute x5, starting transfers between devices: 3.38 us -> 6.66 us  [body(): lax.ppermute(total, name, [(i, i ^ bit) for i in range(size)])]
    reduce_sum x3 -> x0, other arithmetic: 3.2 us -> none  [the longest x1 1.21 us: norm_pieces(): jnp.mean(centred_rows * centred_rows, axis=1, keepdims=True) + 1e-06]
    pallas_call x0 -> x2, Pallas kernels: none -> 2.35 us  [the longest x1 1.5 us: body(): pl.pallas_call(functools.partial(combine_kernel, experts, capacity), out_...]
  transfers between devices with their start and end apart: 28 -> 28, of which waited for: 11 -> 14; matrix products, arithmetic and copies ran while one was open for 14% -> 11% of each run, Pallas kernels for 0% -> 1%
where the time goes in v3:
time: 146 us; the launch traced here: 144 us
  waiting for transfers between devices  77.5 us (53%)
  starting transfers between devices  31.2 us (21%)
  matrix products  17.6 us (12%)
  local copies, waits for them, and re-layouts  7.95 us (5%)
  other arithmetic  6.14 us (4%)
  Pallas kernels  2.35 us (2%)
    ppermute x6, waiting for transfers between devices, over_experts(): return lax.ppermute(value, 'expert', turn_experts(step))  29.2 us
    ppermute x4, waiting for transfers between devices, over_columns(): lax.ppermute(value, 'dp', turn_columns(step))  20.5 us
    dot_general x10, matrix products, dot(): lax.dot_general(a, b, (((a_dim,), (b_dim,)), ((), ())), preferred_element...  17 us
    ppermute x1, waiting for transfers between devices, body(): lax.ppermute(row_gradient(turn, BF16), 'dp', turn_columns(columns - turn))  15.3 us
    ppermute x6, starting transfers between devices, over_experts(): return lax.ppermute(value, 'expert', turn_experts(step))  12.9 us
    ppermute x4, waiting for transfers between devices, over_half(): return lax.ppermute(value, 'expert', swap_half)  10.7 us
    ppermute x5, starting transfers between devices, body(): lax.ppermute(total, name, [(i, i ^ bit) for i in range(size)])  6.66 us
    unnamed x27, local copies, waits for them, and re-layouts  6.01 us
  transfers between devices with their start and end apart: 28, of which 14 were waited for; matrix products, arithmetic and copies ran while one was open for 11% of the time, Pallas kernels for 1%

profile of v3, /device:TPU:0, one launch (start us, length us, event | category | flops | bytes accessed | tf_op | source)
XLA Modules:
  0.0 143.7 jit_solution(5879509072757400262)
XLA Ops:
  4.8 3.0 %collective-permute-start.2 = (bf16[2,80,1280]{2,1,0:T(8,128)(2,1)S(1)}, bf16[2,80,1280]{2,1,0:T(8,128)(2,1)}, u32[]{:S(2)}, u32[]{:S(2)}) collective-permute-start(bf16[2,80,1280]{2,1,0:T(8,128)(2,1)S(1)} %get-tuple-element.23), channel_id=1, source_target_pairs={{0,2},{1,3},{2,0},{3,1},{4,6},{5,7},{6,4},{7,5},{8,10},{9,11},{10,... | collective-permute-start | bytes 1228808 | tf_op jit(solution)/shard_map/ppermute | solution.py:135
  7.8 1.5 %collective-permute-start.3 = (bf16[320,1280]{1,0:T(8,128)(2,1)}, bf16[320,1280]{1,0:T(8,128)(2,1)S(1)}, u32[]{:S(2)}, u32[]{:S(2)}) collective-permute-start(bf16[320,1280]{1,0:T(8,128)(2,1)} %bitcast.103), channel_id=1, source_target_pairs={{0,4},{4,0},{8,12},{12,8},{16,20},{20,16},{24,28},{28,24},{1,5},{5... | collective-permute-start | bytes 2457608 | tf_op jit(solution)/shard_map/ppermute | solution.py:138
  9.3 1.6 %collective-permute-start = (bf16[2,80,1280]{2,1,0:T(8,128)(2,1)S(1)}, bf16[2,80,1280]{2,1,0:T(8,128)(2,1)}, u32[]{:S(2)}, u32[]{:S(2)}) collective-permute-start(bf16[2,80,1280]{2,1,0:T(8,128)(2,1)S(1)} %get-tuple-element.24), channel_id=1, source_target_pairs={{0,8},{4,12},{8,16},{12,20},{16,24},{20,28},{24,0},{28,4},{1,9},{5... | collective-permute-start | bytes 1228808 | tf_op jit(solution)/shard_map/ppermute | solution.py:132
  10.9 2.2 %collective-permute-start.1 = (bf16[2,80,1280]{2,1,0:T(8,128)(2,1)S(1)}, bf16[2,80,1280]{2,1,0:T(8,128)(2,1)}, u32[]{:S(2)}, u32[]{:S(2)}) collective-permute-start(bf16[2,80,1280]{2,1,0:T(8,128)(2,1)S(1)} %get-tuple-element.25), channel_id=1, source_target_pairs={{0,24},{4,28},{8,0},{12,4},{16,8},{20,12},{24,16},{28,20},{1,25},{... | collective-permute-start | bytes 1228808 | tf_op jit(solution)/shard_map/ppermute | solution.py:132
  14.0 9.6 %collective-permute-done = bf16[2,80,1280]{2,1,0:T(8,128)(2,1)} collective-permute-done((bf16[2,80,1280]{2,1,0:T(8,128)(2,1)S(1)}, bf16[2,80,1280]{2,1,0:T(8,128)(2,1)}, u32[]{:S(2)}, u32[]{:S(2)}) %collective-permute-start) | collective-permute-done | bytes 409632 | tf_op jit(solution)/shard_map/ppermute | solution.py:132
  24.7 6.5 %collective-permute-done.1 = bf16[2,80,1280]{2,1,0:T(8,128)(2,1)} collective-permute-done((bf16[2,80,1280]{2,1,0:T(8,128)(2,1)S(1)}, bf16[2,80,1280]{2,1,0:T(8,128)(2,1)}, u32[]{:S(2)}, u32[]{:S(2)}) %collective-permute-start.1) | collective-permute-done | bytes 409632 | tf_op jit(solution)/shard_map/ppermute | solution.py:132
  33.9 1.6 %collective-permute-start.6 = (bf16[2,80,1280]{2,1,0:T(8,128)(2,1)}, bf16[2,80,1280]{2,1,0:T(8,128)(2,1)S(1)}, u32[]{:S(2)}, u32[]{:S(2)}) collective-permute-start(bf16[2,80,1280]{2,1,0:T(8,128)(2,1)} %collective-permute-done.1), channel_id=1, source_target_pairs={{0,2},{1,3},{2,0},{3,1},{4,6},{5,7},{6,4},{7,5},{8,10},{9,11},{10,... | collective-permute-start | bytes 1228808 | tf_op jit(solution)/shard_map/ppermute | solution.py:135
  35.5 2.4 %collective-permute-start.7 = (bf16[2,80,1280]{2,1,0:T(8,128)(2,1)S(1)}, bf16[2,80,1280]{2,1,0:T(8,128)(2,1)S(1)}, u32[]{:S(2)}, u32[]{:S(2)}) collective-permute-start(bf16[2,80,1280]{2,1,0:T(8,128)(2,1)S(1)} %get-tuple-element.31), channel_id=1, source_target_pairs={{0,16},{4,20},{8,24},{12,28},{16,0},{20,4},{24,8},{28,12},{1,17},{... | collective-permute-start | bytes 1228808 | tf_op jit(solution)/shard_map/ppermute | solution.py:132
  38.4 6.6 %collective-permute-done.5 = bf16[2,80,1280]{2,1,0:T(8,128)(2,1)S(1)} collective-permute-done((bf16[2,80,1280]{2,1,0:T(8,128)(2,1)}, bf16[2,80,1280]{2,1,0:T(8,128)(2,1)S(1)}, u32[]{:S(2)}, u32[]{:S(2)}) %collective-permute-start.5) | collective-permute-done | bytes 409632 | tf_op jit(solution)/shard_map/ppermute | solution.py:135
  45.0 7.2 %collective-permute-done.6 = bf16[2,80,1280]{2,1,0:T(8,128)(2,1)S(1)} collective-permute-done((bf16[2,80,1280]{2,1,0:T(8,128)(2,1)}, bf16[2,80,1280]{2,1,0:T(8,128)(2,1)S(1)}, u32[]{:S(2)}, u32[]{:S(2)}) %collective-permute-start.6) | collective-permute-done | bytes 409632 | tf_op jit(solution)/shard_map/ppermute | solution.py:135
  52.6 2.8 %collective-permute-done.7 = bf16[2,80,1280]{2,1,0:T(8,128)(2,1)S(1)} collective-permute-done((bf16[2,80,1280]{2,1,0:T(8,128)(2,1)S(1)}, bf16[2,80,1280]{2,1,0:T(8,128)(2,1)S(1)}, u32[]{:S(2)}, u32[]{:S(2)}) %collective-permute-start.7) | collective-permute-done | bytes 409632 | tf_op jit(solution)/shard_map/ppermute | solution.py:132
  57.1 1.8 %fusion.70 = f32[480,1280]{1,0:T(8,128)S(1)} fusion(bf16[480,1280]{1,0:T(8,128)(2,1)S(1)} %get-tuple-element.60, bf16[1280,1280]{1,0:T(8,128)(2,1)S(1)} %pad_maximum_fusion.1), kind=kOutput, calls=%fused_computation.130 | convolution fusion | flops 1572864000 | bytes 6963200 | tf_op jit(solution)/shard_map/dot_general | solution.py:27
  58.9 6.8 %collective-permute-done.12 = bf16[2,80,1280]{2,1,0:T(8,128)(2,1)S(1)} collective-permute-done((bf16[2,80,1280]{2,1,0:T(8,128)(2,1)S(1)}, bf16[2,80,1280]{2,1,0:T(8,128)(2,1)S(1)}, u32[]{:S(2)}, u32[]{:S(2)}) %collective-permute-start.12) | collective-permute-done | bytes 409632 | tf_op jit(solution)/shard_map/ppermute | solution.py:135
  67.3 3.1 %multiply_reduce_fusion.2 = (f32[480]{0:T(512)S(1)}, bf16[480,1280]{1,0:T(8,128)(2,1)S(1)}, bf16[480,1280]{1,0:T(8,128)(2,1)S(1)}, bf16[480,1280]{1,0:T(8,128)(2,1)S(1)}) fusion(f32[480,1280]{1,0:T(8,128)S(1)} %fusion.70, f32[480]{0:T(512)S(1)} %add_divide_fusion.1, bf16[480,1280]{1,0:T(8,128)(2,1)S(1)} %get-tuple-element.59, ...), kind=kOutput, calls=%fused_computation.17 | convolution fusion | flops 1603173888 | bytes 10653440 | tf_op jit(solution)/shard_map/dot_general | solution.py:27
  72.5 2.8 %fusion.69 = (bf16[1280,1280]{1,0:T(8,128)(2,1)S(1)}, f32[1280,1280]{1,0:T(8,128)S(1)}) fusion(bf16[160,1280]{1,0:T(8,128)(2,1)S(1)} %get-tuple-element.85, bf16[480,1280]{1,0:T(8,128)(2,1)S(1)} %get-tuple-element.82, bf16[160,1280]{1,0:T(8,128)(2,1)S(1)} %get-tuple-element.46, bf16[480,1280]{1,0:T(8,128)(2,1)S(1)} %get-tuple-element.42), kind=kOutput, calls=%fused_computation.129 | convolution fusion | flops 2105344000 | bytes 13107200 | tf_op jit(solution)/shard_map/dot_general | solution.py:27
  78.2 3.3 %multiply_reduce_fusion = (f32[1280]{0:T(1024)S(1)}, bf16[1280,1280]{1,0:T(8,128)(2,1)S(1)}, f32[1280,1280]{1,0:T(8,128)S(1)}) fusion(bf16[1280,1280]{1,0:T(8,128)(2,1)S(1)} %pad_maximum_fusion.1, bf16[640,1280]{1,0:T(8,128)(2,1)S(1)} %pad_maximum_fusion.2, bf16[640,1280]{1,0:T(8,128)(2,1)S(1)} %constant_dynamic-update-slice_fusion), kind=kOutput, calls=%fused_computation | convolution fusion | flops 2103704320 | bytes 16389120 | tf_op jit(solution)/shard_map/dot_general | solution.py:27
  87.5 15.3 %collective-permute-done.13 = bf16[320,1280]{1,0:T(8,128)(2,1)S(1)} collective-permute-done((bf16[320,1280]{1,0:T(8,128)(2,1)S(1)}, bf16[320,1280]{1,0:T(8,128)(2,1)S(1)}, u32[]{:S(2)}, u32[]{:S(2)}) %collective-permute-start.13) | collective-permute-done | bytes 819232 | tf_op jit(solution)/shard_map/ppermute | solution.py:234
  104.5 3.4 %collective-permute-start.15 = (bf16[80,1280]{1,0:T(8,128)(2,1)S(1)}, bf16[80,1280]{1,0:T(8,128)(2,1)S(1)}, u32[]{:S(2)}, u32[]{:S(2)}) collective-permute-start(bf16[80,1280]{1,0:T(8,128)(2,1)S(1)} %get-tuple-element.56), channel_id=1, source_target_pairs={{0,16},{4,20},{8,24},{12,28},{16,0},{20,4},{24,8},{28,12},{1,17},{... | collective-permute-start | bytes 614408 | tf_op jit(solution)/shard_map/ppermute | solution.py:132
  107.8 2.8 %collective-permute-start.14 = (bf16[80,1280]{1,0:T(8,128)(2,1)S(1)}, bf16[80,1280]{1,0:T(8,128)(2,1)S(1)}, u32[]{:S(2)}, u32[]{:S(2)}) collective-permute-start(bf16[80,1280]{1,0:T(8,128)(2,1)S(1)} %get-tuple-element.57), channel_id=1, source_target_pairs={{0,24},{4,28},{8,0},{12,4},{16,8},{20,12},{24,16},{28,20},{1,25},{... | collective-permute-start | bytes 614408 | tf_op jit(solution)/shard_map/ppermute | solution.py:132
  110.7 3.2 %collective-permute-done.16 = bf16[80,1280]{1,0:T(8,128)(2,1)S(1)} collective-permute-done((bf16[80,1280]{1,0:T(8,128)(2,1)S(1)}, bf16[80,1280]{1,0:T(8,128)(2,1)S(1)}, u32[]{:S(2)}, u32[]{:S(2)}) %collective-permute-start.16) | collective-permute-done | bytes 204832 | tf_op jit(solution)/shard_map/ppermute | solution.py:132
  113.9 7.1 %collective-permute-done.15 = bf16[80,1280]{1,0:T(8,128)(2,1)S(1)} collective-permute-done((bf16[80,1280]{1,0:T(8,128)(2,1)S(1)}, bf16[80,1280]{1,0:T(8,128)(2,1)S(1)}, u32[]{:S(2)}, u32[]{:S(2)}) %collective-permute-start.15) | collective-permute-done | bytes 204832 | tf_op jit(solution)/shard_map/ppermute | solution.py:132
  123.6 1.5 %collective-permute-start.20 = (bf16[320,1280]{1,0:T(8,128)(2,1)S(1)}, bf16[320,1280]{1,0:T(8,128)(2,1)S(1)}, u32[]{:S(2)}, u32[]{:S(2)}) collective-permute-start(bf16[320,1280]{1,0:T(8,128)(2,1)S(1)} %fusion.11), channel_id=1, source_target_pairs={{0,4},{4,0},{8,12},{12,8},{16,20},{20,16},{24,28},{28,24},{1,5},{5... | collective-permute-start | bytes 2457608 | tf_op jit(solution)/shard_map/ppermute | solution.py:138
  125.2 3.4 %collective-permute-start.27 = (f32[5,1280]{1,0:T(8,128)S(1)}, f32[5,1280]{1,0:T(8,128)S(1)}, u32[]{:S(2)}, u32[]{:S(2)}) collective-permute-start(f32[5,1280]{1,0:T(8,128)S(1)} %add.114), channel_id=1, source_target_pairs={{0,16},{4,20},{8,24},{12,28},{16,0},{20,4},{24,8},{28,12},{1,17},{... | collective-permute-start | bytes 76808 | tf_op jit(solution)/shard_map/ppermute | solution.py:265
  131.9 10.7 %collective-permute-done.20 = bf16[320,1280]{1,0:T(8,128)(2,1)S(1)} collective-permute-done((bf16[320,1280]{1,0:T(8,128)(2,1)S(1)}, bf16[320,1280]{1,0:T(8,128)(2,1)S(1)}, u32[]{:S(2)}, u32[]{:S(2)}) %collective-permute-start.20) | collective-permute-done | bytes 819232 | tf_op jit(solution)/shard_map/ppermute | solution.py:138
  (109 shorter events, 32.6 us)
Async XLA Ops:
  4.8 27.4 %collective-permute-start.2 = (bf16[2,80,1280]{2,1,0:T(8,128)(2,1)S(1)}, bf16[2,80,1280]{2,1,0:T(8,128)(2,1)}, u32[]{:S(2)}, u32[]{:S(2)}) collective-permute-start(bf16[2,80,1280]{2,1,0:T(8,128)(2,1)S(1)} %get-tuple-element.23), channel_id=1, source_target_pairs={{0,2},{1,3},{2,0},{3,1},{4,6},{5,7},{6,4},{7,5},{8,10},{9,11},{10,... | collective-permute-start | bytes 1228808 | tf_op jit(solution)/shard_map/ppermute | solution.py:135
  7.8 24.4 %collective-permute-start.4 = (bf16[320,1280]{1,0:T(8,128)(2,1)}, bf16[320,1280]{1,0:T(8,128)(2,1)S(1)}, u32[]{:S(2)}, u32[]{:S(2)}) collective-permute-start(bf16[320,1280]{1,0:T(8,128)(2,1)} %bitcast.102), channel_id=1, source_target_pairs={{0,1},{1,0},{2,3},{3,2},{4,5},{5,4},{6,7},{7,6},{8,9},{9,8},{10,11... | collective-permute-start | bytes 2457608 | tf_op jit(solution)/shard_map/ppermute | solution.py:141
  7.8 24.4 %collective-permute-start.3 = (bf16[320,1280]{1,0:T(8,128)(2,1)}, bf16[320,1280]{1,0:T(8,128)(2,1)S(1)}, u32[]{:S(2)}, u32[]{:S(2)}) collective-permute-start(bf16[320,1280]{1,0:T(8,128)(2,1)} %bitcast.103), channel_id=1, source_target_pairs={{0,4},{4,0},{8,12},{12,8},{16,20},{20,16},{24,28},{28,24},{1,5},{5... | collective-permute-start | bytes 2457608 | tf_op jit(solution)/shard_map/ppermute | solution.py:138
  9.3 14.2 %collective-permute-start = (bf16[2,80,1280]{2,1,0:T(8,128)(2,1)S(1)}, bf16[2,80,1280]{2,1,0:T(8,128)(2,1)}, u32[]{:S(2)}, u32[]{:S(2)}) collective-permute-start(bf16[2,80,1280]{2,1,0:T(8,128)(2,1)S(1)} %get-tuple-element.24), channel_id=1, source_target_pairs={{0,8},{4,12},{8,16},{12,20},{16,24},{20,28},{24,0},{28,4},{1,9},{5... | collective-permute-start | bytes 1228808 | tf_op jit(solution)/shard_map/ppermute | solution.py:132
  10.9 20.2 %collective-permute-start.1 = (bf16[2,80,1280]{2,1,0:T(8,128)(2,1)S(1)}, bf16[2,80,1280]{2,1,0:T(8,128)(2,1)}, u32[]{:S(2)}, u32[]{:S(2)}) collective-permute-start(bf16[2,80,1280]{2,1,0:T(8,128)(2,1)S(1)} %get-tuple-element.25), channel_id=1, source_target_pairs={{0,24},{4,28},{8,0},{12,4},{16,8},{20,12},{24,16},{28,20},{1,25},{... | collective-permute-start | bytes 1228808 | tf_op jit(solution)/shard_map/ppermute | solution.py:132
  32.2 12.7 %collective-permute-start.5 = (bf16[2,80,1280]{2,1,0:T(8,128)(2,1)}, bf16[2,80,1280]{2,1,0:T(8,128)(2,1)S(1)}, u32[]{:S(2)}, u32[]{:S(2)}) collective-permute-start(bf16[2,80,1280]{2,1,0:T(8,128)(2,1)} %collective-permute-done), channel_id=1, source_target_pairs={{0,2},{1,3},{2,0},{3,1},{4,6},{5,7},{6,4},{7,5},{8,10},{9,11},{10,... | collective-permute-start | bytes 1228808 | tf_op jit(solution)/shard_map/ppermute | solution.py:135
  33.9 18.2 %collective-permute-start.6 = (bf16[2,80,1280]{2,1,0:T(8,128)(2,1)}, bf16[2,80,1280]{2,1,0:T(8,128)(2,1)S(1)}, u32[]{:S(2)}, u32[]{:S(2)}) collective-permute-start(bf16[2,80,1280]{2,1,0:T(8,128)(2,1)} %collective-permute-done.1), channel_id=1, source_target_pairs={{0,2},{1,3},{2,0},{3,1},{4,6},{5,7},{6,4},{7,5},{8,10},{9,11},{10,... | collective-permute-start | bytes 1228808 | tf_op jit(solution)/shard_map/ppermute | solution.py:135
  35.5 19.9 %collective-permute-start.7 = (bf16[2,80,1280]{2,1,0:T(8,128)(2,1)S(1)}, bf16[2,80,1280]{2,1,0:T(8,128)(2,1)S(1)}, u32[]{:S(2)}, u32[]{:S(2)}) collective-permute-start(bf16[2,80,1280]{2,1,0:T(8,128)(2,1)S(1)} %get-tuple-element.31), channel_id=1, source_target_pairs={{0,16},{4,20},{8,24},{12,28},{16,0},{20,4},{24,8},{28,12},{1,17},{... | collective-permute-start | bytes 1228808 | tf_op jit(solution)/shard_map/ppermute | solution.py:132
  37.9 17.6 %collective-permute-start.8 = (bf16[320,1280]{1,0:T(8,128)(2,1)S(1)}, bf16[320,1280]{1,0:T(8,128)(2,1)S(1)}, u32[]{:S(2)}, u32[]{:S(2)}) collective-permute-start(bf16[320,1280]{1,0:T(8,128)(2,1)S(1)} %bitcast.110), channel_id=1, source_target_pairs={{0,4},{4,0},{8,12},{12,8},{16,20},{20,16},{24,28},{28,24},{1,5},{5... | collective-permute-start | bytes 2457608 | tf_op jit(solution)/shard_map/ppermute | solution.py:138
  38.4 17.1 %collective-permute-start.9 = (bf16[320,1280]{1,0:T(8,128)(2,1)S(1)}, bf16[320,1280]{1,0:T(8,128)(2,1)S(1)}, u32[]{:S(2)}, u32[]{:S(2)}) collective-permute-start(bf16[320,1280]{1,0:T(8,128)(2,1)S(1)} %collective-permute-done.3), channel_id=1, source_target_pairs={{0,1},{1,0},{2,3},{3,2},{4,5},{5,4},{6,7},{7,6},{8,9},{9,8},{10,11... | collective-permute-start | bytes 2457608 | tf_op jit(solution)/shard_map/ppermute | solution.py:141
  55.5 10.3 %collective-permute-start.12 = (bf16[2,80,1280]{2,1,0:T(8,128)(2,1)S(1)}, bf16[2,80,1280]{2,1,0:T(8,128)(2,1)S(1)}, u32[]{:S(2)}, u32[]{:S(2)}) collective-permute-start(bf16[2,80,1280]{2,1,0:T(8,128)(2,1)S(1)} %collective-permute-done.7), channel_id=1, source_target_pairs={{0,2},{1,3},{2,0},{3,1},{4,6},{5,7},{6,4},{7,5},{8,10},{9,11},{10,... | collective-permute-start | bytes 1228808 | tf_op jit(solution)/shard_map/ppermute | solution.py:135
  56.1 11.2 %collective-permute-start.10 = (bf16[320,1280]{1,0:T(8,128)(2,1)S(1)}, bf16[320,1280]{1,0:T(8,128)(2,1)S(1)}, u32[]{:S(2)}, u32[]{:S(2)}) collective-permute-start(bf16[320,1280]{1,0:T(8,128)(2,1)S(1)} %bitcast.111), channel_id=1, source_target_pairs={{0,1},{1,0},{2,3},{3,2},{4,5},{5,4},{6,7},{7,6},{8,9},{9,8},{10,11... | collective-permute-start | bytes 2457608 | tf_op jit(solution)/shard_map/ppermute | solution.py:141
  56.1 11.2 %collective-permute-start.11 = (bf16[320,1280]{1,0:T(8,128)(2,1)S(1)}, bf16[320,1280]{1,0:T(8,128)(2,1)S(1)}, u32[]{:S(2)}, u32[]{:S(2)}) collective-permute-start(bf16[320,1280]{1,0:T(8,128)(2,1)S(1)} %collective-permute-done.8), channel_id=1, source_target_pairs={{0,1},{1,0},{2,3},{3,2},{4,5},{5,4},{6,7},{7,6},{8,9},{9,8},{10,11... | collective-permute-start | bytes 2457608 | tf_op jit(solution)/shard_map/ppermute | solution.py:141
  81.8 21.0 %collective-permute-start.13 = (bf16[320,1280]{1,0:T(8,128)(2,1)S(1)}, bf16[320,1280]{1,0:T(8,128)(2,1)S(1)}, u32[]{:S(2)}, u32[]{:S(2)}) collective-permute-start(bf16[320,1280]{1,0:T(8,128)(2,1)S(1)} %pad_maximum_fusion.3), channel_id=1, source_target_pairs={{0,2},{1,3},{2,0},{3,1},{4,6},{5,7},{6,4},{7,5},{8,10},{9,11},{10,... | collective-permute-start | bytes 2457608 | tf_op jit(solution)/shard_map/ppermute | solution.py:234
  85.1 43.6 %collective-permute-start.21 = (bf16[320,1280]{1,0:T(8,128)(2,1)S(1)}, bf16[320,1280]{1,0:T(8,128)(2,1)S(1)}, u32[]{:S(2)}, u32[]{:S(2)}) collective-permute-start(bf16[320,1280]{1,0:T(8,128)(2,1)S(1)} %get-tuple-element.50), channel_id=1, source_target_pairs={{0,1},{1,0},{2,3},{3,2},{4,5},{5,4},{6,7},{7,6},{8,9},{9,8},{10,11... | collective-permute-start | bytes 2457608 | tf_op jit(solution)/shard_map/ppermute | solution.py:141
  85.5 43.1 %collective-permute-start.22 = (bf16[320,1280]{1,0:T(8,128)(2,1)S(1)}, bf16[320,1280]{1,0:T(8,128)(2,1)S(1)}, u32[]{:S(2)}, u32[]{:S(2)}) collective-permute-start(bf16[320,1280]{1,0:T(8,128)(2,1)S(1)} %fusion.14), channel_id=1, source_target_pairs={{0,4},{4,0},{8,12},{12,8},{16,20},{20,16},{24,28},{28,24},{1,5},{5... | collective-permute-start | bytes 2457608 | tf_op jit(solution)/shard_map/ppermute | solution.py:138
  86.1 17.2 %collective-permute-start.24 = (f32[5,1280]{1,0:T(8,128)S(1)}, f32[5,1280]{1,0:T(8,128)S(1)}, u32[]{:S(2)}, u32[]{:S(2)}) collective-permute-start(f32[5,1280]{1,0:T(8,128)S(1)} %fusion.63), channel_id=1, source_target_pairs={{0,2},{1,3},{2,0},{3,1},{4,6},{5,7},{6,4},{7,5},{8,10},{9,11},{10,... | collective-permute-start | bytes 76808 | tf_op jit(solution)/shard_map/ppermute | solution.py:265
  103.4 4.5 %collective-permute-start.25 = (f32[5,1280]{1,0:T(8,128)S(1)}, f32[5,1280]{1,0:T(8,128)S(1)}, u32[]{:S(2)}, u32[]{:S(2)}) collective-permute-start(f32[5,1280]{1,0:T(8,128)S(1)} %fusion.82), channel_id=1, source_target_pairs={{0,4},{4,0},{8,12},{12,8},{16,20},{20,16},{24,28},{28,24},{1,5},{5... | collective-permute-start | bytes 76808 | tf_op jit(solution)/shard_map/ppermute | solution.py:265
  104.0 9.9 %collective-permute-start.16 = (bf16[80,1280]{1,0:T(8,128)(2,1)S(1)}, bf16[80,1280]{1,0:T(8,128)(2,1)S(1)}, u32[]{:S(2)}, u32[]{:S(2)}) collective-permute-start(bf16[80,1280]{1,0:T(8,128)(2,1)S(1)} %get-tuple-element.55), channel_id=1, source_target_pairs={{0,8},{4,12},{8,16},{12,20},{16,24},{20,28},{24,0},{28,4},{1,9},{5... | collective-permute-start | bytes 614408 | tf_op jit(solution)/shard_map/ppermute | solution.py:132
  104.5 16.5 %collective-permute-start.15 = (bf16[80,1280]{1,0:T(8,128)(2,1)S(1)}, bf16[80,1280]{1,0:T(8,128)(2,1)S(1)}, u32[]{:S(2)}, u32[]{:S(2)}) collective-permute-start(bf16[80,1280]{1,0:T(8,128)(2,1)S(1)} %get-tuple-element.56), channel_id=1, source_target_pairs={{0,16},{4,20},{8,24},{12,28},{16,0},{20,4},{24,8},{28,12},{1,17},{... | collective-permute-start | bytes 614408 | tf_op jit(solution)/shard_map/ppermute | solution.py:132
  107.8 14.2 %collective-permute-start.14 = (bf16[80,1280]{1,0:T(8,128)(2,1)S(1)}, bf16[80,1280]{1,0:T(8,128)(2,1)S(1)}, u32[]{:S(2)}, u32[]{:S(2)}) collective-permute-start(bf16[80,1280]{1,0:T(8,128)(2,1)S(1)} %get-tuple-element.57), channel_id=1, source_target_pairs={{0,24},{4,28},{8,0},{12,4},{16,8},{20,12},{24,16},{28,20},{1,25},{... | collective-permute-start | bytes 614408 | tf_op jit(solution)/shard_map/ppermute | solution.py:132
  113.9 17.9 %collective-permute-start.18 = (bf16[320,1280]{1,0:T(8,128)(2,1)S(1)}, bf16[320,1280]{1,0:T(8,128)(2,1)S(1)}, u32[]{:S(2)}, u32[]{:S(2)}) collective-permute-start(bf16[320,1280]{1,0:T(8,128)(2,1)S(1)} %get-tuple-element.52), channel_id=1, source_target_pairs={{0,1},{1,0},{2,3},{3,2},{4,5},{5,4},{6,7},{7,6},{8,9},{9,8},{10,11... | collective-permute-start | bytes 2457608 | tf_op jit(solution)/shard_map/ppermute | solution.py:141
  123.6 18.9 %collective-permute-start.20 = (bf16[320,1280]{1,0:T(8,128)(2,1)S(1)}, bf16[320,1280]{1,0:T(8,128)(2,1)S(1)}, u32[]{:S(2)}, u32[]{:S(2)}) collective-permute-start(bf16[320,1280]{1,0:T(8,128)(2,1)S(1)} %fusion.11), channel_id=1, source_target_pairs={{0,4},{4,0},{8,12},{12,8},{16,20},{20,16},{24,28},{28,24},{1,5},{5... | collective-permute-start | bytes 2457608 | tf_op jit(solution)/shard_map/ppermute | solution.py:138
  125.2 5.4 %collective-permute-start.27 = (f32[5,1280]{1,0:T(8,128)S(1)}, f32[5,1280]{1,0:T(8,128)S(1)}, u32[]{:S(2)}, u32[]{:S(2)}) collective-permute-start(f32[5,1280]{1,0:T(8,128)S(1)} %add.114), channel_id=1, source_target_pairs={{0,16},{4,20},{8,24},{12,28},{16,0},{20,4},{24,8},{28,12},{1,17},{... | collective-permute-start | bytes 76808 | tf_op jit(solution)/shard_map/ppermute | solution.py:265
  (14 other events, 124.1 us)

commit v4 on v3

--- a/solution.py
+++ b/solution.py
@@ -89,8 +89,59 @@
     out_ref[...] = (d_ref[...].astype(F32) + norm_backward).astype(BF16)
 
 
+def front_kernel(tile, m_ref, d_ref, first_ref, second_ref, router_ref, hidden_ref, pre_ref, y_ref, logit_ref):
+    rows_m = m_ref[...]
+    rows_d = d_ref[...]
+    gate = jax.nn.sigmoid(jnp.sum(rows_m.astype(F32) * router_ref[...], axis=1, keepdims=True))
+    y_ref[...] = (gate * rows_d.astype(F32)).astype(BF16)
+    share = jnp.zeros_like(gate)
+    for at in range(0, first_ref.shape[0], tile):
+        units = pl.ds(at, tile)
+        value, slope = gelu_parts(dot(rows_m, first_ref[units, :], 1, 1))
+        back = dot(rows_d, second_ref[units, :], 1, 1)
+        hidden = value.astype(BF16)
+        hidden_ref[:, units] = hidden
+        pre_ref[:, units] = (gate * back * slope).astype(BF16)
+        share = share + jnp.sum(hidden.astype(F32) * back, axis=1, keepdims=True)
+    logit_ref[...] = jnp.broadcast_to(share * gate * (1.0 - gate), logit_ref.shape)
+
+
+def rows_kernel(tile, pre_ref, logit_ref, first_ref, router_ref, own_ref, side_ref):
+    count = own_ref.shape[0]
+    pre = pre_ref[...]
+    logit = logit_ref[:, :1]
+    for at in range(0, first_ref.shape[1], tile):
+        lanes = pl.ds(at, tile)
+        rows = dot(pre, first_ref[:, lanes], 1, 0) + logit * router_ref[:, lanes]
+        own_ref[:, lanes] = rows[:count]
+        side_ref[:, lanes] = rows[count:].astype(BF16)
+
+
+def weight_kernel(half, tile, left_ref, right_ref, out_ref, turned):
+    units = out_ref.shape[0]
+    turned[...] = left_ref[:, pl.ds(half * units, units)].T
+    for at in range(0, right_ref.shape[1], tile):
+        lanes = pl.ds(at, tile)
+        out_ref[:, lanes] = dot(turned[...], right_ref[:, lanes], 1, 0).astype(out_ref.dtype)
+
+
+def sums_kernel(experts, own_ref, m_ref, logit_ref, first_ref, leave_ref, stay_ref, out_ref):
+    units = stay_ref.shape[0]
+    router_part = jnp.sum(m_ref[...].astype(F32) * logit_ref[:, :1], axis=0, keepdims=True)
+    gain_part = jnp.sum(
+        first_ref[:units, :].astype(F32) * leave_ref[...].astype(F32), axis=0, keepdims=True
+    ) + jnp.sum(first_ref[units:, :].astype(F32) * stay_ref[...], axis=0, keepdims=True)
+    row = lax.broadcasted_iota(jnp.int32, out_ref.shape, 0)
+    out_ref[...] = jnp.where(
+        row == own_ref[0], router_part, jnp.where(row == experts, gain_part, 0.0)
+    )
+
+
 VMEM = pl.BlockSpec(memory_space=pltpu.VMEM)
 SMEM = pl.BlockSpec(memory_space=pltpu.SMEM)
+
+
+PARAMS = pltpu.CompilerParams(vmem_limit_bytes=40 * 2**20)
 
 
 def tied(values, after):
@@ -124,7 +175,7 @@
         out_shape=[jax.ShapeDtypeStruct((2, capacity, width), BF16)] * experts,
         in_specs=[SMEM, VMEM, VMEM, VMEM, VMEM],
         out_specs=[VMEM] * experts,
-        compiler_params=pltpu.CompilerParams(vmem_limit_bytes=32 * 2**20),
+        compiler_params=PARAMS,
         name="dispatch",
     )(*token_args)
 
@@ -142,39 +193,41 @@
 
     first = w_in[0].T
     second = w_out[0]
-    reach = [min(step, experts - step) for step in range(experts)]
-    close = [step for step in range(experts) if reach[step] == 1]
-    far = [step for step in range(experts) if reach[step] > 1]
+    units = first.shape[0]
+    steps = sorted(range(experts), key=lambda step: min(step, experts - step))
+    early, late = steps[: 3 * experts // 4], steps[3 * experts // 4 :]
     near = {0: send[0]}
-    for step in close:
+    for step in early[1:]:
         near[step] = over_experts(send[step], step)
     side = {0: over_columns(send[0])}
     first_y = over_half(tied(first, send[0]))
     first_c = over_pair(tied(first, send[0]))
 
-    stage = (first_y, first_c, side[0], [near[step] for step in close])
-    second_held, far_held, close_held, first_y = tied(
-        (second, [send[step] for step in far], [near[step] for step in close], first_y), stage
-    )
-    for step, value in zip(far, far_held):
+    stage = (first_y, first_c, side[0], [near[step] for step in early[1:]])
+    second_held, late_held, early_held, first_y = tied(
+        (second, [send[step] for step in late], [near[step] for step in early[1:]], first_y), stage
+    )
+    for step, value in zip(late, late_held):
         near[step] = over_experts(value, step)
-    for step, value in zip(close, close_held):
+    for step, value in zip(early[1:], early_held):
         side[step] = over_columns(value)
     second_y = over_half(second_held)
     first_yc = over_pair(first_y)
 
-    stage = (second_y, first_yc, [near[step] for step in far], [side[step] for step in close])
-    second_held, far_held, second_y = tied(
-        (second_held, [near[step] for step in far], second_y), stage
-    )
-    for step, value in zip(far, far_held):
+    stage = (second_y, first_yc, [near[step] for step in late], [side[step] for step in early[1:]])
+    second_held, late_held, second_y = tied(
+        (second_held, [near[step] for step in late], second_y), stage
+    )
+    for step, value in zip(late, late_held):
         side[step] = over_columns(value)
     second_c = over_pair(second_held)
     second_yc = over_pair(second_y)
 
-    column = lax.dynamic_slice_in_dim(router, own, 1, 1)
-    all_first = jnp.concatenate([first, first_c, first_y, first_yc], axis=0)
-    all_second = jnp.concatenate([second, second_c, second_y, second_yc], axis=0)
+    router_row = lax.dynamic_slice_in_dim(router, own, 1, 1).astype(F32).T
+    all_first = jnp.concatenate([first_yc, first_c, first_y, first], axis=0)
+    all_second = jnp.concatenate([second_yc, second_c, second_y, second], axis=0)
+    hidden_units = 4 * units
+    tile = 256 if hidden_units % 256 == 0 else hidden_units
 
     def gather_rows(steps):
         pieces = [near[step] for step in steps]
@@ -186,96 +239,150 @@
         )
 
     def front(rows_m, rows_d):
-        gate = jax.nn.sigmoid(jnp.dot(rows_m, column, preferred_element_type=F32))
-        value, slope = gelu_parts(dot(rows_m, all_first, 1, 1))
-        grad_y = (gate * rows_d.astype(F32)).astype(BF16)
-        return gate, value.astype(BF16), slope, grad_y
-
-    def middle(rows_d, gate, hidden, slope):
-        back = dot(rows_d, all_second, 1, 1)
-        gate_gradient = jnp.sum(hidden.astype(F32) * back, axis=1, keepdims=True)
-        logit_gradient = gate_gradient * gate * (1.0 - gate)
-        return logit_gradient, (gate * back * slope).astype(BF16)
-
-    groups_of = [[0] + close] + ([far] if far else [])
-    done = []
-    for steps in groups_of:
-        m, d = gather_rows(steps)
-        gate, hidden, slope, grad_y = front(m, d)
-        logit_gradient, grad_pre = middle(d, gate, hidden, slope)
-        done.append((m, hidden, grad_y, logit_gradient, grad_pre))
-    rows_m, hidden, grad_y, logit_gradient, grad_pre = (
-        jnp.concatenate(parts, axis=0) for parts in zip(*done)
-    )
-    units = first.shape[0]
-
-    def pair_sum(whole):
-        blocks = whole.reshape(4, units, width)
-        half = blocks[2] + over_pair(blocks[3].astype(BF16)).astype(F32)
-        mine = blocks[0] + over_pair(blocks[1].astype(BF16)).astype(F32)
-        return mine, half.astype(BF16)
-
-    grad_second = dot(hidden, grad_y, 0, 0)
-    out_mine, out_half = pair_sum(grad_second)
-    grad_pre = tied(grad_pre, grad_second)
-    router_row = column[:, 0].astype(F32)[None, :]
-
-    def row_gradient(turn, kind):
-        parts = []
-        for steps, (_, _, _, logit_part, grad_part) in zip(groups_of, done):
-            count = len(steps) * capacity
-            part = slice(turn * count, (turn + 1) * count)
-            parts.append(
-                (dot(grad_part[part], all_first, 1, 0) + logit_part[part] * router_row).astype(kind)
-            )
-        return jnp.concatenate(parts, axis=0)
-
-    back_rows = [
-        lax.ppermute(row_gradient(turn, BF16), "dp", turn_columns(columns - turn))
+        count = rows_m.shape[0]
+        return pl.pallas_call(
+            functools.partial(front_kernel, tile),
+            out_shape=[jax.ShapeDtypeStruct((count, hidden_units), BF16)] * 2
+            + [
+                jax.ShapeDtypeStruct((count, width), BF16),
+                jax.ShapeDtypeStruct((count, 128), F32),
+            ],
+            in_specs=[VMEM] * 5,
+            out_specs=[VMEM] * 4,
+            compiler_params=PARAMS,
+            cost_estimate=pl.CostEstimate(
+                flops=4 * count * width * hidden_units,
+                bytes_accessed=4 * width * hidden_units,
+                transcendentals=count * hidden_units,
+            ),
+            name="front",
+        )(rows_m, rows_d, all_first, all_second, router_row)
+
+    def row_gradients(grad_pre, logit_gradient):
+        count = grad_pre.shape[0] // columns
+        return pl.pallas_call(
+            functools.partial(rows_kernel, tile),
+            out_shape=[
+                jax.ShapeDtypeStruct((count, width), F32),
+                jax.ShapeDtypeStruct((grad_pre.shape[0] - count, width), BF16),
+            ],
+            in_specs=[VMEM] * 4,
+            out_specs=[VMEM] * 2,
+            compiler_params=PARAMS,
+            cost_estimate=pl.CostEstimate(
+                flops=2 * grad_pre.shape[0] * width * hidden_units,
+                bytes_accessed=2 * width * hidden_units,
+                transcendentals=0,
+            ),
+            name="rows",
+        )(grad_pre, logit_gradient, all_first, router_row)
+
+    def weight_half(half, left, right, kind):
+        return pl.pallas_call(
+            functools.partial(weight_kernel, half, tile),
+            out_shape=jax.ShapeDtypeStruct((2 * units, width), kind),
+            in_specs=[VMEM] * 2,
+            out_specs=VMEM,
+            scratch_shapes=[pltpu.VMEM((2 * units, left.shape[0]), BF16)],
+            compiler_params=PARAMS,
+            cost_estimate=pl.CostEstimate(
+                flops=4 * left.shape[0] * width * units,
+                bytes_accessed=8 * width * units,
+                transcendentals=0,
+            ),
+            name="weights",
+        )(left, right)
+
+    early_m, early_d = gather_rows(early)
+    early_hidden, early_pre, early_y, early_logit = front(early_m, early_d)
+    early_own, early_side = row_gradients(early_pre, early_logit)
+    for step in late:
+        near[step], side[step] = tied((near[step], side[step]), (early_own, early_side))
+    late_m, late_d = gather_rows(late)
+    late_hidden, late_pre, late_y, late_logit = front(late_m, late_d)
+    rows_m = jnp.concatenate([early_m, late_m], axis=0)
+    logit_gradient = jnp.concatenate([early_logit, late_logit], axis=0)
+    grad_pre = jnp.concatenate([early_pre, late_pre], axis=0)
+    hidden = jnp.concatenate([early_hidden, late_hidden], axis=0)
+    grad_y = jnp.concatenate([early_y, late_y], axis=0)
+
+    def pairwise(value, name, size, bit):
+        return value + lax.ppermute(value, name, [(i, i ^ bit) for i in range(size)])
+
+    in_leave = weight_half(0, grad_pre, rows_m, BF16)
+    in_pair = over_pair(in_leave)
+    in_stay = weight_half(1, tied(grad_pre, in_leave), rows_m, F32)
+    total = pl.pallas_call(
+        functools.partial(sums_kernel, experts),
+        out_shape=jax.ShapeDtypeStruct((-(-(experts + 1) // 8) * 8, width), F32),
+        in_specs=[SMEM] + [VMEM] * 5,
+        out_specs=VMEM,
+        compiler_params=PARAMS,
+        cost_estimate=pl.CostEstimate(
+            flops=6 * width * hidden_units, bytes_accessed=6 * width * hidden_units, transcendentals=0
+        ),
+        name="sums",
+    )(own_scalar, rows_m, logit_gradient, all_first, in_leave, in_stay)
+    total = pairwise(total, "expert", halves, 1)
+    late_own, late_side = row_gradients(tied(late_pre, in_stay), late_logit)
+    out_leave = weight_half(0, tied(hidden, late_own), grad_y, BF16)
+
+    stage = (in_pair, in_stay, total, late_own, late_side, out_leave)
+    in_pair, in_stay, total, late_side, early_side, out_leave, hidden = tied(
+        (in_pair, in_stay, total, late_side, early_side, out_leave, hidden), stage
+    )
+    in_sum = in_stay + in_pair.astype(F32)
+    in_half = in_sum[:units].astype(BF16)
+    in_other = over_half(in_half)
+
+    def by_turn(rows):
+        return rows.reshape(columns - 1, -1, width)
+
+    leaving = jnp.concatenate([by_turn(early_side), by_turn(late_side)], axis=1)
+    rows_back = [
+        lax.ppermute(leaving[turn - 1], "dp", turn_columns(columns - turn))
         for turn in range(1, columns)
     ]
-    out_half, grad_pre = lax.optimization_barrier((out_half, grad_pre))
-    out_other = over_half(out_half)
-    grad_first = dot(grad_pre, rows_m, 0, 0)
-    in_mine, in_half = pair_sum(grad_first)
-    own_rows = row_gradient(0, F32)
-    in_other = over_half(in_half)
-    for piece in back_rows:
+    out_pair = over_pair(out_leave)
+    out_stay = weight_half(1, tied(hidden, (in_half, leaving)), grad_y, F32)
+    total = tied(total, out_stay)
+    bit = 2
+    while bit < halves:
+        total = pairwise(total, "expert", halves, bit)
+        bit *= 2
+    total = pairwise(total, "dp", groups, 1)
+
+    stage = (in_other, rows_back, out_pair, out_stay, total)
+    in_other, rows_back, out_pair, out_stay, total = tied(stage, stage)
+    out_sum = out_stay + out_pair.astype(F32)
+    out_other = over_half(out_sum[:units].astype(BF16))
+    own_rows = jnp.concatenate([early_own, late_own], axis=0)
+    for piece in rows_back:
         own_rows = own_rows + piece.astype(F32)
     own_rows = own_rows.astype(BF16).reshape(experts, capacity, width)
-    order = [step for steps in groups_of for step in steps]
     returned = [None] * experts
-    for place, step in enumerate(order):
-        if step == 0:
-            returned[step] = own_rows[place]
-        else:
-            returned[step] = over_experts(own_rows[place], experts - step)
-    grad_out = (out_mine + out_other.astype(F32)).astype(BF16)[None]
-    grad_in = (in_mine + in_other.astype(F32)).astype(BF16).T[None]
-
-    router_part = jnp.sum(rows_m.astype(F32) * logit_gradient, axis=0)
-    gain_part = jnp.sum(all_first.astype(F32) * grad_first, axis=0)
-    is_own = (jnp.arange(experts + 1, dtype=jnp.int32) == own)[:, None]
-    is_last = (jnp.arange(experts + 1, dtype=jnp.int32) == experts)[:, None]
-    router_part, gain_part, in_half = lax.optimization_barrier((router_part, gain_part, in_half))
-    total = jnp.where(is_own, router_part[None], jnp.where(is_last, gain_part[None], 0.0))
-    for name, size in (("dp", groups), ("expert", halves)):
-        bit = 1
-        while bit < size:
-            total = total + lax.ppermute(total, name, [(i, i ^ bit) for i in range(size)])
-            bit *= 2
+    for place, step in enumerate(steps):
+        value = own_rows[place]
+        returned[step] = over_experts(value, experts - step) if step else value
+    bit = 2
+    while bit < groups:
+        total = pairwise(total, "dp", groups, bit)
+        bit *= 2
     router_t = total[:experts]
     grad_router = router_t.T
     grad_gain = (total[experts] + jnp.sum(router_t * router.astype(F32).T, axis=0)) / gain
+    grad_in = (in_sum[units:] + in_other.astype(F32)).astype(BF16).T[None]
 
     input_grad = pl.pallas_call(
         functools.partial(combine_kernel, experts, capacity),
         out_shape=jax.ShapeDtypeStruct((tokens, width), BF16),
         in_specs=[SMEM, VMEM, VMEM, VMEM, VMEM, VMEM],
         out_specs=VMEM,
-        compiler_params=pltpu.CompilerParams(vmem_limit_bytes=32 * 2**20),
+        compiler_params=PARAMS,
         name="combine",
     )(*token_args, jnp.concatenate(returned, axis=0))
+    out_mine = tied(out_sum[units:], (input_grad, grad_in))
+    grad_out = (out_mine + out_other.astype(F32)).astype(BF16)[None]
     return (input_grad, grad_in, grad_out, grad_router, grad_gain)
 
 

time: 146 us -> 130 us (0.89); the launches traced: 144 us -> 129 us
  Pallas kernels: 2.35 us -> 20.1 us
  matrix products: 17.6 us -> 0 us
  waiting for transfers between devices: 77.5 us -> 66 us
  starting transfers between devices: 31.2 us -> 28 us
    pallas_call x0 -> x9, Pallas kernels: none -> 17.8 us  [the longest x2 7.86 us: front(): pl.pallas_call(functools.partial(front_kernel, tile), out_shape=[jax.Shap...]
    dot_general x12 -> x0, matrix products: 17.6 us -> none  [the longest x10 17 us: dot(): lax.dot_general(a, b, (((a_dim,), (b_dim,)), ((), ())), preferred_element...]
    ppermute x4, waiting for transfers between devices: 10.7 us -> 4.56 us  [over_half(): return lax.ppermute(value, 'expert', swap_half)]
    ppermute x4, waiting for transfers between devices: 20.5 us -> 15.7 us  [over_columns(): lax.ppermute(value, 'dp', turn_columns(step))]
    ppermute x6, starting transfers between devices: 12.9 us -> 10.3 us  [over_experts(): return lax.ppermute(value, 'expert', turn_experts(step))]
    unnamed x27 -> x32, local copies, waits for them, and re-layouts: 6.01 us -> 5.67 us
  transfers between devices with their start and end apart: 28 -> 26, of which waited for: 14 -> 16; matrix products, arithmetic and copies ran while one was open for 11% -> 5% of each run, Pallas kernels for 1% -> 12%
where the time goes in v4:
time: 130 us; the launch traced here: 129 us
  waiting for transfers between devices  66 us (51%)
  starting transfers between devices  28 us (22%)
  Pallas kernels  20.1 us (15%)
  other arithmetic  7.35 us (6%)
  local copies, waits for them, and re-layouts  6.78 us (5%)
    ppermute x6, waiting for transfers between devices, over_experts(): return lax.ppermute(value, 'expert', turn_experts(step))  29.9 us
    ppermute x4, waiting for transfers between devices, over_columns(): lax.ppermute(value, 'dp', turn_columns(step))  15.7 us
    ppermute x6, starting transfers between devices, over_experts(): return lax.ppermute(value, 'expert', turn_experts(step))  10.3 us
    ppermute x5, waiting for transfers between devices, pairwise(): lax.ppermute(value, name, [(i, i ^ bit) for i in range(size)])  8.23 us
    pallas_call x2, Pallas kernels, front(): pl.pallas_call(functools.partial(front_kernel, tile), out_shape=[jax.Shap...  7.86 us
    ppermute x1, waiting for transfers between devices, body(): lax.ppermute(leaving[turn - 1], 'dp', turn_columns(columns - turn))  6.86 us
    pallas_call x4, Pallas kernels, weight_half(): pl.pallas_call(functools.partial(weight_kernel, half, tile), out_shape=ja...  6.34 us
    ppermute x4, starting transfers between devices, over_columns(): lax.ppermute(value, 'dp', turn_columns(step))  5.76 us
  transfers between devices with their start and end apart: 26, of which 16 were waited for; matrix products, arithmetic and copies ran while one was open for 5% of the time, Pallas kernels for 12%

profile of v4, /device:TPU:0, one launch (start us, length us, event | category | flops | bytes accessed | tf_op | source)
XLA Modules:
  0.0 129.3 jit_solution(1721084295981376945)
XLA Ops:
  4.8 3.0 %collective-permute-start.2 = (bf16[2,80,1280]{2,1,0:T(8,128)(2,1)S(1)}, bf16[2,80,1280]{2,1,0:T(8,128)(2,1)S(1)}, u32[]{:S(2)}, u32[]{:S(2)}) collective-permute-start(bf16[2,80,1280]{2,1,0:T(8,128)(2,1)S(1)} %get-tuple-element.50), channel_id=1, source_target_pairs={{0,2},{1,3},{2,0},{3,1},{4,6},{5,7},{6,4},{7,5},{8,10},{9,11},{10,... | collective-permute-start | bytes 1228808 | tf_op jit(solution)/shard_map/ppermute | solution.py:186
  9.4 1.6 %collective-permute-start = (bf16[2,80,1280]{2,1,0:T(8,128)(2,1)S(1)}, bf16[2,80,1280]{2,1,0:T(8,128)(2,1)}, u32[]{:S(2)}, u32[]{:S(2)}) collective-permute-start(bf16[2,80,1280]{2,1,0:T(8,128)(2,1)S(1)} %get-tuple-element.51), channel_id=1, source_target_pairs={{0,8},{4,12},{8,16},{12,20},{16,24},{20,28},{24,0},{28,4},{1,9},{5... | collective-permute-start | bytes 1228808 | tf_op jit(solution)/shard_map/ppermute | solution.py:183
  10.9 2.2 %collective-permute-start.1 = (bf16[2,80,1280]{2,1,0:T(8,128)(2,1)S(1)}, bf16[2,80,1280]{2,1,0:T(8,128)(2,1)S(1)}, u32[]{:S(2)}, u32[]{:S(2)}) collective-permute-start(bf16[2,80,1280]{2,1,0:T(8,128)(2,1)S(1)} %get-tuple-element.52), channel_id=1, source_target_pairs={{0,24},{4,28},{8,0},{12,4},{16,8},{20,12},{24,16},{28,20},{1,25},{... | collective-permute-start | bytes 1228808 | tf_op jit(solution)/shard_map/ppermute | solution.py:183
  13.9 9.7 %collective-permute-done = bf16[2,80,1280]{2,1,0:T(8,128)(2,1)} collective-permute-done((bf16[2,80,1280]{2,1,0:T(8,128)(2,1)S(1)}, bf16[2,80,1280]{2,1,0:T(8,128)(2,1)}, u32[]{:S(2)}, u32[]{:S(2)}) %collective-permute-start) | collective-permute-done | bytes 409632 | tf_op jit(solution)/shard_map/ppermute | solution.py:183
  24.7 6.4 %collective-permute-done.1 = bf16[2,80,1280]{2,1,0:T(8,128)(2,1)S(1)} collective-permute-done((bf16[2,80,1280]{2,1,0:T(8,128)(2,1)S(1)}, bf16[2,80,1280]{2,1,0:T(8,128)(2,1)S(1)}, u32[]{:S(2)}, u32[]{:S(2)}) %collective-permute-start.1) | collective-permute-done | bytes 409632 | tf_op jit(solution)/shard_map/ppermute | solution.py:183
  32.3 1.6 %collective-permute-start.6 = (bf16[2,80,1280]{2,1,0:T(8,128)(2,1)S(1)}, bf16[2,80,1280]{2,1,0:T(8,128)(2,1)S(1)}, u32[]{:S(2)}, u32[]{:S(2)}) collective-permute-start(bf16[2,80,1280]{2,1,0:T(8,128)(2,1)S(1)} %collective-permute-done.1), channel_id=1, source_target_pairs={{0,2},{1,3},{2,0},{3,1},{4,6},{5,7},{6,4},{7,5},{8,10},{9,11},{10,... | collective-permute-start | bytes 1228808 | tf_op jit(solution)/shard_map/ppermute | solution.py:186
  33.8 2.5 %collective-permute-start.8 = (bf16[2,80,1280]{2,1,0:T(8,128)(2,1)S(1)}, bf16[2,80,1280]{2,1,0:T(8,128)(2,1)S(1)}, u32[]{:S(2)}, u32[]{:S(2)}) collective-permute-start(bf16[2,80,1280]{2,1,0:T(8,128)(2,1)S(1)} %get-tuple-element.59), channel_id=1, source_target_pairs={{0,16},{4,20},{8,24},{12,28},{16,0},{20,4},{24,8},{28,12},{1,17},{... | collective-permute-start | bytes 1228808 | tf_op jit(solution)/shard_map/ppermute | solution.py:183
  36.3 7.5 %collective-permute-done.5 = bf16[2,80,1280]{2,1,0:T(8,128)(2,1)S(1)} collective-permute-done((bf16[2,80,1280]{2,1,0:T(8,128)(2,1)}, bf16[2,80,1280]{2,1,0:T(8,128)(2,1)S(1)}, u32[]{:S(2)}, u32[]{:S(2)}) %collective-permute-start.5) | collective-permute-done | bytes 409632 | tf_op jit(solution)/shard_map/ppermute | solution.py:186
  43.8 7.1 %collective-permute-done.6 = bf16[2,80,1280]{2,1,0:T(8,128)(2,1)S(1)} collective-permute-done((bf16[2,80,1280]{2,1,0:T(8,128)(2,1)S(1)}, bf16[2,80,1280]{2,1,0:T(8,128)(2,1)S(1)}, u32[]{:S(2)}, u32[]{:S(2)}) %collective-permute-start.6) | collective-permute-done | bytes 409632 | tf_op jit(solution)/shard_map/ppermute | solution.py:186
  51.0 3.8 %collective-permute-done.8 = bf16[2,80,1280]{2,1,0:T(8,128)(2,1)S(1)} collective-permute-done((bf16[2,80,1280]{2,1,0:T(8,128)(2,1)S(1)}, bf16[2,80,1280]{2,1,0:T(8,128)(2,1)S(1)}, u32[]{:S(2)}, u32[]{:S(2)}) %collective-permute-start.8) | collective-permute-done | bytes 409632 | tf_op jit(solution)/shard_map/ppermute | solution.py:183
  58.8 5.2 %front.2 = (bf16[480,1280]{1,0:T(8,128)(2,1)S(1)}, bf16[480,1280]{1,0:T(8,128)(2,1)S(1)}, bf16[480,1280]{1,0:T(8,128)(2,1)S(1)}, f32[480,128]{1,0:T(8,128)S(1)}) custom-call(bf16[480,1280]{1,0:T(8,128)(2,1)S(1)} %get-tuple-element.101.m_ref, bf16[480,1280]{1,0:T(8,128)(2,1)S(1)} %get-tuple-element.100.d_ref, ...), custom_call_target="tpu_custom_call" | custom-call | flops 3145728000 | bytes 6553600 | tf_op jit(solution)/shard_map/front/pallas_call | solution.py:243
  64.0 1.8 %rows.2 = (f32[240,1280]{1,0:T(8,128)S(1)}, bf16[240,1280]{1,0:T(8,128)(2,1)S(1)}) custom-call(bf16[480,1280]{1,0:T(8,128)(2,1)S(1)} %get-tuple-element.62.pre_ref, f32[480,128]{1,0:T(8,128)S(1)} %get-tuple-element.63.logit_ref, bf16[1280,1280]{1,0:T(8,128)(2,1)S(1)} %pad_maximum_fusion.first_ref, f32[1,1280]{1,0:T(1,128)S(1)} %bitcast_convert_fusion.router_ref), custom_call_target="tpu_custom_call" | custom-call | flops 1572864000 | bytes 3276800 | tf_op jit(solution)/shard_map/rows/pallas_call | solution.py:263
  67.1 2.7 %front.3 = (bf16[160,1280]{1,0:T(8,128)(2,1)S(1)}, bf16[160,1280]{1,0:T(8,128)(2,1)S(1)}, bf16[160,1280]{1,0:T(8,128)(2,1)S(1)}, f32[160,128]{1,0:T(8,128)S(1)}) custom-call(bf16[160,1280]{1,0:T(8,128)(2,1)S(1)} %pad_maximum_fusion.4.m_ref, bf16[160,1280]{1,0:T(8,128)(2,1)S(1)} %pad_maximum_fusion.5.d_ref, bf16[1280,1280]{1,0:T(8,128)(2,1)S(1)} %pad_maximum_fusion.first_ref, ...), custom_call_target="tpu_custom_call" | custom-call | flops 1048576000 | bytes 6553600 | tf_op jit(solution)/shard_map/front/pallas_call | solution.py:243
  75.0 1.6 %collective-permute-start.14 = (f32[8,1280]{1,0:T(8,128)S(1)}, f32[8,1280]{1,0:T(8,128)S(1)}, u32[]{:S(2)}, u32[]{:S(2)}) collective-permute-start(f32[8,1280]{1,0:T(8,128)S(1)} %sums.1), channel_id=1, source_target_pairs={{0,4},{4,0},{8,12},{12,8},{16,20},{20,16},{24,28},{28,24},{1,5},{5... | collective-permute-start | bytes 122888 | tf_op jit(solution)/shard_map/ppermute | solution.py:310
  76.6 1.8 %weights.6 = bf16[640,1280]{1,0:T(8,128)(2,1)S(1)} custom-call(bf16[640,1280]{1,0:T(8,128)(2,1)S(1)} %constant_dynamic-update-slice_fusion.4.left_ref, bf16[640,1280]{1,0:T(8,128)(2,1)S(1)} %constant_dynamic-update-slice_fusion.6.right_ref), custom_call_target="tpu_custom_call" | custom-call | flops 1048576000 | bytes 3276800 | tf_op jit(solution)/shard_map/weights/pallas_call | solution.py:281
  84.0 3.4 %collective-permute-done.18 = f32[8,1280]{1,0:T(8,128)S(1)} collective-permute-done((f32[8,1280]{1,0:T(8,128)S(1)}, f32[8,1280]{1,0:T(8,128)S(1)}, u32[]{:S(2)}, u32[]{:S(2)}) %collective-permute-start.18) | collective-permute-done | bytes 40992 | tf_op jit(solution)/shard_map/ppermute | solution.py:310
  87.4 1.9 %collective-permute-start.19 = (f32[8,1280]{1,0:T(8,128)S(1)}, f32[8,1280]{1,0:T(8,128)S(1)}, u32[]{:S(2)}, u32[]{:S(2)}) collective-permute-start(f32[8,1280]{1,0:T(8,128)S(1)} %add.40), channel_id=1, source_target_pairs={{0,16},{4,20},{8,24},{12,28},{16,0},{20,4},{24,8},{28,12},{1,17},{... | collective-permute-start | bytes 122888 | tf_op jit(solution)/shard_map/ppermute | solution.py:310
  89.3 3.0 %collective-permute-done.19 = f32[8,1280]{1,0:T(8,128)S(1)} collective-permute-done((f32[8,1280]{1,0:T(8,128)S(1)}, f32[8,1280]{1,0:T(8,128)S(1)}, u32[]{:S(2)}, u32[]{:S(2)}) %collective-permute-start.19) | collective-permute-done | bytes 40992 | tf_op jit(solution)/shard_map/ppermute | solution.py:310
  93.5 6.9 %collective-permute-done.16 = bf16[320,1280]{1,0:T(8,128)(2,1)S(1)} collective-permute-done((bf16[320,1280]{1,0:T(8,128)(2,1)S(1)}, bf16[320,1280]{1,0:T(8,128)(2,1)S(1)}, u32[]{:S(2)}, u32[]{:S(2)}) %collective-permute-start.16) | collective-permute-done | bytes 819232 | tf_op jit(solution)/shard_map/ppermute | solution.py:343
  102.0 1.6 %collective-permute-start.25 = (f32[8,1280]{1,0:T(8,128)S(1)}, f32[8,1280]{1,0:T(8,128)S(1)}, u32[]{:S(2)}, u32[]{:S(2)}) collective-permute-start(f32[8,1280]{1,0:T(8,128)S(1)} %add.42), channel_id=1, source_target_pairs={{0,2},{1,3},{2,0},{3,1},{4,6},{5,7},{6,4},{7,5},{8,10},{9,11},{10,... | collective-permute-start | bytes 122888 | tf_op jit(solution)/shard_map/ppermute | solution.py:310
  106.2 3.4 %collective-permute-start.22 = (bf16[80,1280]{1,0:T(8,128)(2,1)S(1)}, bf16[80,1280]{1,0:T(8,128)(2,1)S(1)}, u32[]{:S(2)}, u32[]{:S(2)}) collective-permute-start(bf16[80,1280]{1,0:T(8,128)(2,1)S(1)} %get-tuple-element.97), channel_id=1, source_target_pairs={{0,16},{4,20},{8,24},{12,28},{16,0},{20,4},{24,8},{28,12},{1,17},{... | collective-permute-start | bytes 614408 | tf_op jit(solution)/shard_map/ppermute | solution.py:183
  112.4 3.1 %collective-permute-done.23 = bf16[80,1280]{1,0:T(8,128)(2,1)S(1)} collective-permute-done((bf16[80,1280]{1,0:T(8,128)(2,1)S(1)}, bf16[80,1280]{1,0:T(8,128)(2,1)S(1)}, u32[]{:S(2)}, u32[]{:S(2)}) %collective-permute-start.23) | collective-permute-done | bytes 204832 | tf_op jit(solution)/shard_map/ppermute | solution.py:183
  115.5 6.9 %collective-permute-done.22 = bf16[80,1280]{1,0:T(8,128)(2,1)S(1)} collective-permute-done((bf16[80,1280]{1,0:T(8,128)(2,1)S(1)}, bf16[80,1280]{1,0:T(8,128)(2,1)S(1)}, u32[]{:S(2)}, u32[]{:S(2)}) %collective-permute-start.22) | collective-permute-done | bytes 204832 | tf_op jit(solution)/shard_map/ppermute | solution.py:183
  124.0 4.3 %collective-permute-done.24 = bf16[320,1280]{1,0:T(8,128)(2,1)S(1)} collective-permute-done((bf16[320,1280]{1,0:T(8,128)(2,1)S(1)}, bf16[320,1280]{1,0:T(8,128)(2,1)S(1)}, u32[]{:S(2)}, u32[]{:S(2)}) %collective-permute-start.24) | collective-permute-done | bytes 819232 | tf_op jit(solution)/shard_map/ppermute | solution.py:189
  (103 shorter events, 35.5 us)
Async XLA Ops:
  4.8 26.3 %collective-permute-start.2 = (bf16[2,80,1280]{2,1,0:T(8,128)(2,1)S(1)}, bf16[2,80,1280]{2,1,0:T(8,128)(2,1)S(1)}, u32[]{:S(2)}, u32[]{:S(2)}) collective-permute-start(bf16[2,80,1280]{2,1,0:T(8,128)(2,1)S(1)} %get-tuple-element.50), channel_id=1, source_target_pairs={{0,2},{1,3},{2,0},{3,1},{4,6},{5,7},{6,4},{7,5},{8,10},{9,11},{10,... | collective-permute-start | bytes 1228808 | tf_op jit(solution)/shard_map/ppermute | solution.py:186
  7.8 23.3 %collective-permute-start.4 = (bf16[320,1280]{1,0:T(8,128)(2,1)}, bf16[320,1280]{1,0:T(8,128)(2,1)}, u32[]{:S(2)}, u32[]{:S(2)}) collective-permute-start(bf16[320,1280]{1,0:T(8,128)(2,1)} %bitcast.96), channel_id=1, source_target_pairs={{0,1},{1,0},{2,3},{3,2},{4,5},{5,4},{6,7},{7,6},{8,9},{9,8},{10,11... | collective-permute-start | bytes 2457608 | tf_op jit(solution)/shard_map/ppermute | solution.py:192
  7.8 23.3 %collective-permute-start.3 = (bf16[320,1280]{1,0:T(8,128)(2,1)}, bf16[320,1280]{1,0:T(8,128)(2,1)}, u32[]{:S(2)}, u32[]{:S(2)}) collective-permute-start(bf16[320,1280]{1,0:T(8,128)(2,1)} %bitcast.97), channel_id=1, source_target_pairs={{0,4},{4,0},{8,12},{12,8},{16,20},{20,16},{24,28},{28,24},{1,5},{5... | collective-permute-start | bytes 2457608 | tf_op jit(solution)/shard_map/ppermute | solution.py:189
  9.4 14.2 %collective-permute-start = (bf16[2,80,1280]{2,1,0:T(8,128)(2,1)S(1)}, bf16[2,80,1280]{2,1,0:T(8,128)(2,1)}, u32[]{:S(2)}, u32[]{:S(2)}) collective-permute-start(bf16[2,80,1280]{2,1,0:T(8,128)(2,1)S(1)} %get-tuple-element.51), channel_id=1, source_target_pairs={{0,8},{4,12},{8,16},{12,20},{16,24},{20,28},{24,0},{28,4},{1,9},{5... | collective-permute-start | bytes 1228808 | tf_op jit(solution)/shard_map/ppermute | solution.py:183
  10.9 20.1 %collective-permute-start.1 = (bf16[2,80,1280]{2,1,0:T(8,128)(2,1)S(1)}, bf16[2,80,1280]{2,1,0:T(8,128)(2,1)S(1)}, u32[]{:S(2)}, u32[]{:S(2)}) collective-permute-start(bf16[2,80,1280]{2,1,0:T(8,128)(2,1)S(1)} %get-tuple-element.52), channel_id=1, source_target_pairs={{0,24},{4,28},{8,0},{12,4},{16,8},{20,12},{24,16},{28,20},{1,25},{... | collective-permute-start | bytes 1228808 | tf_op jit(solution)/shard_map/ppermute | solution.py:183
  31.1 12.7 %collective-permute-start.5 = (bf16[2,80,1280]{2,1,0:T(8,128)(2,1)}, bf16[2,80,1280]{2,1,0:T(8,128)(2,1)S(1)}, u32[]{:S(2)}, u32[]{:S(2)}) collective-permute-start(bf16[2,80,1280]{2,1,0:T(8,128)(2,1)} %collective-permute-done), channel_id=1, source_target_pairs={{0,2},{1,3},{2,0},{3,1},{4,6},{5,7},{6,4},{7,5},{8,10},{9,11},{10,... | collective-permute-start | bytes 1228808 | tf_op jit(solution)/shard_map/ppermute | solution.py:186
  31.7 23.1 %collective-permute-start.7 = (bf16[320,1280]{1,0:T(8,128)(2,1)}, bf16[320,1280]{1,0:T(8,128)(2,1)S(1)}, u32[]{:S(2)}, u32[]{:S(2)}) collective-permute-start(bf16[320,1280]{1,0:T(8,128)(2,1)} %collective-permute-done.3), channel_id=1, source_target_pairs={{0,1},{1,0},{2,3},{3,2},{4,5},{5,4},{6,7},{7,6},{8,9},{9,8},{10,11... | collective-permute-start | bytes 2457608 | tf_op jit(solution)/shard_map/ppermute | solution.py:192
  31.7 23.1 %collective-permute-start.9 = (bf16[320,1280]{1,0:T(8,128)(2,1)S(1)}, bf16[320,1280]{1,0:T(8,128)(2,1)S(1)}, u32[]{:S(2)}, u32[]{:S(2)}) collective-permute-start(bf16[320,1280]{1,0:T(8,128)(2,1)S(1)} %bitcast.99), channel_id=1, source_target_pairs={{0,4},{4,0},{8,12},{12,8},{16,20},{20,16},{24,28},{28,24},{1,5},{5... | collective-permute-start | bytes 2457608 | tf_op jit(solution)/shard_map/ppermute | solution.py:189
  32.3 18.7 %collective-permute-start.6 = (bf16[2,80,1280]{2,1,0:T(8,128)(2,1)S(1)}, bf16[2,80,1280]{2,1,0:T(8,128)(2,1)S(1)}, u32[]{:S(2)}, u32[]{:S(2)}) collective-permute-start(bf16[2,80,1280]{2,1,0:T(8,128)(2,1)S(1)} %collective-permute-done.1), channel_id=1, source_target_pairs={{0,2},{1,3},{2,0},{3,1},{4,6},{5,7},{6,4},{7,5},{8,10},{9,11},{10,... | collective-permute-start | bytes 1228808 | tf_op jit(solution)/shard_map/ppermute | solution.py:186
  33.8 21.0 %collective-permute-start.8 = (bf16[2,80,1280]{2,1,0:T(8,128)(2,1)S(1)}, bf16[2,80,1280]{2,1,0:T(8,128)(2,1)S(1)}, u32[]{:S(2)}, u32[]{:S(2)}) collective-permute-start(bf16[2,80,1280]{2,1,0:T(8,128)(2,1)S(1)} %get-tuple-element.59), channel_id=1, source_target_pairs={{0,16},{4,20},{8,24},{12,28},{16,0},{20,4},{24,8},{28,12},{1,17},{... | collective-permute-start | bytes 1228808 | tf_op jit(solution)/shard_map/ppermute | solution.py:183
  54.8 3.5 %collective-permute-start.10 = (bf16[320,1280]{1,0:T(8,128)(2,1)S(1)}, bf16[320,1280]{1,0:T(8,128)(2,1)S(1)}, u32[]{:S(2)}, u32[]{:S(2)}) collective-permute-start(bf16[320,1280]{1,0:T(8,128)(2,1)S(1)} %collective-permute-done.9), channel_id=1, source_target_pairs={{0,1},{1,0},{2,3},{3,2},{4,5},{5,4},{6,7},{7,6},{8,9},{9,8},{10,11... | collective-permute-start | bytes 2457608 | tf_op jit(solution)/shard_map/ppermute | solution.py:192
  55.4 11.5 %collective-permute-start.12 = (bf16[2,80,1280]{2,1,0:T(8,128)(2,1)S(1)}, bf16[2,80,1280]{2,1,0:T(8,128)(2,1)S(1)}, u32[]{:S(2)}, u32[]{:S(2)}) collective-permute-start(bf16[2,80,1280]{2,1,0:T(8,128)(2,1)S(1)} %collective-permute-done.8), channel_id=1, source_target_pairs={{0,2},{1,3},{2,0},{3,1},{4,6},{5,7},{6,4},{7,5},{8,10},{9,11},{10,... | collective-permute-start | bytes 1228808 | tf_op jit(solution)/shard_map/ppermute | solution.py:186
  71.4 7.7 %collective-permute-start.13 = (bf16[640,1280]{1,0:T(8,128)(2,1)S(1)}, bf16[640,1280]{1,0:T(8,128)(2,1)S(1)}, u32[]{:S(2)}, u32[]{:S(2)}) collective-permute-start(bf16[640,1280]{1,0:T(8,128)(2,1)S(1)} %weights.4.leave_ref), channel_id=1, source_target_pairs={{0,1},{1,0},{2,3},{3,2},{4,5},{5,4},{6,7},{7,6},{8,9},{9,8},{10,11... | collective-permute-start | bytes 4915208 | tf_op jit(solution)/shard_map/ppermute | solution.py:192
  75.0 4.1 %collective-permute-start.14 = (f32[8,1280]{1,0:T(8,128)S(1)}, f32[8,1280]{1,0:T(8,128)S(1)}, u32[]{:S(2)}, u32[]{:S(2)}) collective-permute-start(f32[8,1280]{1,0:T(8,128)S(1)} %sums.1), channel_id=1, source_target_pairs={{0,4},{4,0},{8,12},{12,8},{16,20},{20,16},{24,28},{28,24},{1,5},{5... | collective-permute-start | bytes 122888 | tf_op jit(solution)/shard_map/ppermute | solution.py:310
  79.0 21.6 %collective-permute-start.17 = (bf16[640,1280]{1,0:T(8,128)(2,1)S(1)}, bf16[640,1280]{1,0:T(8,128)(2,1)S(1)}, u32[]{:S(2)}, u32[]{:S(2)}) collective-permute-start(bf16[640,1280]{1,0:T(8,128)(2,1)S(1)} %weights.6), channel_id=1, source_target_pairs={{0,1},{1,0},{2,3},{3,2},{4,5},{5,4},{6,7},{7,6},{8,9},{9,8},{10,11... | collective-permute-start | bytes 4915208 | tf_op jit(solution)/shard_map/ppermute | solution.py:192
  79.7 20.7 %collective-permute-start.16 = (bf16[320,1280]{1,0:T(8,128)(2,1)S(1)}, bf16[320,1280]{1,0:T(8,128)(2,1)S(1)}, u32[]{:S(2)}, u32[]{:S(2)}) collective-permute-start(bf16[320,1280]{1,0:T(8,128)(2,1)S(1)} %fusion.20), channel_id=1, source_target_pairs={{0,2},{1,3},{2,0},{3,1},{4,6},{5,7},{6,4},{7,5},{8,10},{9,11},{10,... | collective-permute-start | bytes 2457608 | tf_op jit(solution)/shard_map/ppermute | solution.py:343
  80.3 20.4 %collective-permute-start.15 = (bf16[320,1280]{1,0:T(8,128)(2,1)S(1)}, bf16[320,1280]{1,0:T(8,128)(2,1)S(1)}, u32[]{:S(2)}, u32[]{:S(2)}) collective-permute-start(bf16[320,1280]{1,0:T(8,128)(2,1)S(1)} %slice.192), channel_id=1, source_target_pairs={{0,4},{4,0},{8,12},{12,8},{16,20},{20,16},{24,28},{28,24},{1,5},{5... | collective-permute-start | bytes 2457608 | tf_op jit(solution)/shard_map/ppermute | solution.py:189
  83.3 4.1 %collective-permute-start.18 = (f32[8,1280]{1,0:T(8,128)S(1)}, f32[8,1280]{1,0:T(8,128)S(1)}, u32[]{:S(2)}, u32[]{:S(2)}) collective-permute-start(f32[8,1280]{1,0:T(8,128)S(1)} %add.38), channel_id=1, source_target_pairs={{0,8},{4,12},{8,0},{12,4},{16,24},{20,28},{24,16},{28,20},{1,9},{5... | collective-permute-start | bytes 122888 | tf_op jit(solution)/shard_map/ppermute | solution.py:310
  87.4 4.9 %collective-permute-start.19 = (f32[8,1280]{1,0:T(8,128)S(1)}, f32[8,1280]{1,0:T(8,128)S(1)}, u32[]{:S(2)}, u32[]{:S(2)}) collective-permute-start(f32[8,1280]{1,0:T(8,128)S(1)} %add.40), channel_id=1, source_target_pairs={{0,16},{4,20},{8,24},{12,28},{16,0},{20,4},{24,8},{28,12},{1,17},{... | collective-permute-start | bytes 122888 | tf_op jit(solution)/shard_map/ppermute | solution.py:310
  102.0 9.1 %collective-permute-start.25 = (f32[8,1280]{1,0:T(8,128)S(1)}, f32[8,1280]{1,0:T(8,128)S(1)}, u32[]{:S(2)}, u32[]{:S(2)}) collective-permute-start(f32[8,1280]{1,0:T(8,128)S(1)} %add.42), channel_id=1, source_target_pairs={{0,2},{1,3},{2,0},{3,1},{4,6},{5,7},{6,4},{7,5},{8,10},{9,11},{10,... | collective-permute-start | bytes 122888 | tf_op jit(solution)/shard_map/ppermute | solution.py:310
  105.6 9.9 %collective-permute-start.23 = (bf16[80,1280]{1,0:T(8,128)(2,1)S(1)}, bf16[80,1280]{1,0:T(8,128)(2,1)S(1)}, u32[]{:S(2)}, u32[]{:S(2)}) collective-permute-start(bf16[80,1280]{1,0:T(8,128)(2,1)S(1)} %get-tuple-element.96), channel_id=1, source_target_pairs={{0,8},{4,12},{8,16},{12,20},{16,24},{20,28},{24,0},{28,4},{1,9},{5... | collective-permute-start | bytes 614408 | tf_op jit(solution)/shard_map/ppermute | solution.py:183
  106.2 16.2 %collective-permute-start.22 = (bf16[80,1280]{1,0:T(8,128)(2,1)S(1)}, bf16[80,1280]{1,0:T(8,128)(2,1)S(1)}, u32[]{:S(2)}, u32[]{:S(2)}) collective-permute-start(bf16[80,1280]{1,0:T(8,128)(2,1)S(1)} %get-tuple-element.97), channel_id=1, source_target_pairs={{0,16},{4,20},{8,24},{12,28},{16,0},{20,4},{24,8},{28,12},{1,17},{... | collective-permute-start | bytes 614408 | tf_op jit(solution)/shard_map/ppermute | solution.py:183
  109.6 12.8 %collective-permute-start.21 = (bf16[80,1280]{1,0:T(8,128)(2,1)S(1)}, bf16[80,1280]{1,0:T(8,128)(2,1)S(1)}, u32[]{:S(2)}, u32[]{:S(2)}) collective-permute-start(bf16[80,1280]{1,0:T(8,128)(2,1)S(1)} %get-tuple-element.98), channel_id=1, source_target_pairs={{0,24},{4,28},{8,0},{12,4},{16,8},{20,12},{24,16},{28,20},{1,25},{... | collective-permute-start | bytes 614408 | tf_op jit(solution)/shard_map/ppermute | solution.py:183
  109.6 18.7 %collective-permute-start.24 = (bf16[320,1280]{1,0:T(8,128)(2,1)S(1)}, bf16[320,1280]{1,0:T(8,128)(2,1)S(1)}, u32[]{:S(2)}, u32[]{:S(2)}) collective-permute-start(bf16[320,1280]{1,0:T(8,128)(2,1)S(1)} %slice.191), channel_id=1, source_target_pairs={{0,4},{4,0},{8,12},{12,8},{16,20},{20,16},{24,28},{28,24},{1,5},{5... | collective-permute-start | bytes 2457608 | tf_op jit(solution)/shard_map/ppermute | solution.py:189
  (14 other events, 131.2 us)

commit v5 on v4

--- a/solution.py
+++ b/solution.py
@@ -106,15 +106,44 @@
     logit_ref[...] = jnp.broadcast_to(share * gate * (1.0 - gate), logit_ref.shape)
 
 
-def rows_kernel(tile, pre_ref, logit_ref, first_ref, router_ref, own_ref, side_ref):
+def first_kernel(tile, m_ref, d_ref, first_ref, router_ref, hidden_ref, slope_ref, y_ref, gate_ref):
+    rows_m = m_ref[...]
+    gate = jax.nn.sigmoid(jnp.sum(rows_m.astype(F32) * router_ref[...], axis=1, keepdims=True))
+    y_ref[...] = (gate * d_ref[...].astype(F32)).astype(BF16)
+    gate_ref[...] = jnp.broadcast_to(gate, gate_ref.shape)
+    for at in range(0, first_ref.shape[0], tile):
+        units = pl.ds(at, tile)
+        value, slope = gelu_parts(dot(rows_m, first_ref[units, :], 1, 1))
+        hidden_ref[:, units] = value.astype(BF16)
+        slope_ref[:, units] = gate * slope
+
+
+def second_kernel(tile, d_ref, second_ref, hidden_ref, slope_ref, gate_ref, pre_ref, logit_ref):
+    rows_d = d_ref[...]
+    gate = gate_ref[:, :1]
+    share = jnp.zeros_like(gate)
+    for at in range(0, second_ref.shape[0], tile):
+        units = pl.ds(at, tile)
+        back = dot(rows_d, second_ref[units, :], 1, 1)
+        pre_ref[:, units] = (back * slope_ref[:, units]).astype(BF16)
+        share = share + jnp.sum(hidden_ref[:, units].astype(F32) * back, axis=1, keepdims=True)
+    logit_ref[...] = jnp.broadcast_to(share * gate * (1.0 - gate), logit_ref.shape)
+
+
+def rows_kernel(tile, m_ref, pre_ref, logit_ref, first_ref, router_ref, own_ref, side_ref, sums_ref):
     count = own_ref.shape[0]
     pre = pre_ref[...]
     logit = logit_ref[:, :1]
+    row = lax.broadcasted_iota(jnp.int32, (sums_ref.shape[0], tile), 0)
     for at in range(0, first_ref.shape[1], tile):
         lanes = pl.ds(at, tile)
         rows = dot(pre, first_ref[:, lanes], 1, 0) + logit * router_ref[:, lanes]
         own_ref[:, lanes] = rows[:count]
         side_ref[:, lanes] = rows[count:].astype(BF16)
+        rows_m = m_ref[:, lanes].astype(F32)
+        router_part = jnp.sum(rows_m * logit, axis=0, keepdims=True)
+        gain_part = jnp.sum(rows_m * rows, axis=0, keepdims=True)
+        sums_ref[:, lanes] = jnp.where(row == 0, router_part, jnp.where(row == 1, gain_part, 0.0))
 
 
 def weight_kernel(half, tile, left_ref, right_ref, out_ref, turned):
@@ -123,18 +152,6 @@
     for at in range(0, right_ref.shape[1], tile):
         lanes = pl.ds(at, tile)
         out_ref[:, lanes] = dot(turned[...], right_ref[:, lanes], 1, 0).astype(out_ref.dtype)
-
-
-def sums_kernel(experts, own_ref, m_ref, logit_ref, first_ref, leave_ref, stay_ref, out_ref):
-    units = stay_ref.shape[0]
-    router_part = jnp.sum(m_ref[...].astype(F32) * logit_ref[:, :1], axis=0, keepdims=True)
-    gain_part = jnp.sum(
-        first_ref[:units, :].astype(F32) * leave_ref[...].astype(F32), axis=0, keepdims=True
-    ) + jnp.sum(first_ref[units:, :].astype(F32) * stay_ref[...], axis=0, keepdims=True)
-    row = lax.broadcasted_iota(jnp.int32, out_ref.shape, 0)
-    out_ref[...] = jnp.where(
-        row == own_ref[0], router_part, jnp.where(row == experts, gain_part, 0.0)
-    )
 
 
 VMEM = pl.BlockSpec(memory_space=pltpu.VMEM)
@@ -168,7 +185,24 @@
     def turn_experts(step):
         return [(i, (i + 2 * step) % halves) for i in range(halves)]
 
+    def over_experts(value, step):
+        return lax.ppermute(value, "expert", turn_experts(step))
+
+    def over_columns(value):
+        return [lax.ppermute(value, "dp", turn_columns(step)) for step in range(1, columns)]
+
+    def over_half(value):
+        return lax.ppermute(value, "expert", swap_half)
+
+    def over_pair(value):
+        return lax.ppermute(value, "dp", swap_pair)
+
     own_scalar = own.astype(jnp.int32).reshape(1)
+    first = w_in[0].T
+    second = w_out[0]
+    units = first.shape[0]
+    first_y = over_half(first)
+    first_c = over_pair(first)
     token_args = (own_scalar, prenorm_input, gain[None, :], routes.T, cotangent)
     send = pl.pallas_call(
         functools.partial(dispatch_kernel, experts, capacity),
@@ -176,49 +210,43 @@
         in_specs=[SMEM, VMEM, VMEM, VMEM, VMEM],
         out_specs=[VMEM] * experts,
         compiler_params=PARAMS,
+        cost_estimate=pl.CostEstimate(
+            flops=4 * experts * capacity * tokens * width,
+            bytes_accessed=8 * tokens * width,
+            transcendentals=0,
+        ),
         name="dispatch",
     )(*token_args)
 
-    def over_experts(value, step):
-        return lax.ppermute(value, "expert", turn_experts(step))
-
-    def over_columns(value):
-        return [lax.ppermute(value, "dp", turn_columns(step)) for step in range(1, columns)]
-
-    def over_half(value):
-        return lax.ppermute(value, "expert", swap_half)
-
-    def over_pair(value):
-        return lax.ppermute(value, "dp", swap_pair)
-
-    first = w_in[0].T
-    second = w_out[0]
-    units = first.shape[0]
     steps = sorted(range(experts), key=lambda step: min(step, experts - step))
     early, late = steps[: 3 * experts // 4], steps[3 * experts // 4 :]
     near = {0: send[0]}
     for step in early[1:]:
         near[step] = over_experts(send[step], step)
     side = {0: over_columns(send[0])}
-    first_y = over_half(tied(first, send[0]))
-    first_c = over_pair(tied(first, send[0]))
-
-    stage = (first_y, first_c, side[0], [near[step] for step in early[1:]])
-    second_held, late_held, early_held, first_y = tied(
-        (second, [send[step] for step in late], [near[step] for step in early[1:]], first_y), stage
+
+    stage = (first_y, first_c, [near[step] for step in early[1:]], side[0])
+    second_held, late_held, early_held, first_y, side[0] = tied(
+        (second, [send[step] for step in late], [near[step] for step in early[1:]], first_y, side[0]),
+        stage,
     )
     for step, value in zip(late, late_held):
         near[step] = over_experts(value, step)
     for step, value in zip(early[1:], early_held):
+        near[step] = value
         side[step] = over_columns(value)
     second_y = over_half(second_held)
     first_yc = over_pair(first_y)
 
     stage = (second_y, first_yc, [near[step] for step in late], [side[step] for step in early[1:]])
-    second_held, late_held, second_y = tied(
-        (second_held, [near[step] for step in late], second_y), stage
-    )
+    second_held, late_held, second_y, early_side_held = tied(
+        (second_held, [near[step] for step in late], second_y, [side[step] for step in early[1:]]),
+        stage,
+    )
+    for step, value in zip(early[1:], early_side_held):
+        side[step] = value
     for step, value in zip(late, late_held):
+        near[step] = value
         side[step] = over_columns(value)
     second_c = over_pair(second_held)
     second_yc = over_pair(second_y)
@@ -258,16 +286,57 @@
             name="front",
         )(rows_m, rows_d, all_first, all_second, router_row)
 
-    def row_gradients(grad_pre, logit_gradient):
+    def front_first(rows_m, rows_d):
+        count = rows_m.shape[0]
+        return pl.pallas_call(
+            functools.partial(first_kernel, tile),
+            out_shape=[
+                jax.ShapeDtypeStruct((count, hidden_units), BF16),
+                jax.ShapeDtypeStruct((count, hidden_units), F32),
+                jax.ShapeDtypeStruct((count, width), BF16),
+                jax.ShapeDtypeStruct((count, 128), F32),
+            ],
+            in_specs=[VMEM] * 4,
+            out_specs=[VMEM] * 4,
+            compiler_params=PARAMS,
+            cost_estimate=pl.CostEstimate(
+                flops=2 * count * width * hidden_units,
+                bytes_accessed=2 * width * hidden_units,
+                transcendentals=count * hidden_units,
+            ),
+            name="first",
+        )(rows_m, rows_d, all_first, router_row)
+
+    def front_second(rows_d, hidden, slope, gate):
+        count = rows_d.shape[0]
+        return pl.pallas_call(
+            functools.partial(second_kernel, tile),
+            out_shape=[
+                jax.ShapeDtypeStruct((count, hidden_units), BF16),
+                jax.ShapeDtypeStruct((count, 128), F32),
+            ],
+            in_specs=[VMEM] * 5,
+            out_specs=[VMEM] * 2,
+            compiler_params=PARAMS,
+            cost_estimate=pl.CostEstimate(
+                flops=2 * count * width * hidden_units,
+                bytes_accessed=2 * width * hidden_units,
+                transcendentals=0,
+            ),
+            name="second",
+        )(rows_d, all_second, hidden, slope, gate)
+
+    def row_gradients(rows_m, grad_pre, logit_gradient):
         count = grad_pre.shape[0] // columns
         return pl.pallas_call(
             functools.partial(rows_kernel, tile),
             out_shape=[
                 jax.ShapeDtypeStruct((count, width), F32),
                 jax.ShapeDtypeStruct((grad_pre.shape[0] - count, width), BF16),
+                jax.ShapeDtypeStruct((8, width), F32),
             ],
-            in_specs=[VMEM] * 4,
-            out_specs=[VMEM] * 2,
+            in_specs=[VMEM] * 5,
+            out_specs=[VMEM] * 3,
             compiler_params=PARAMS,
             cost_estimate=pl.CostEstimate(
                 flops=2 * grad_pre.shape[0] * width * hidden_units,
@@ -275,7 +344,7 @@
                 transcendentals=0,
             ),
             name="rows",
-        )(grad_pre, logit_gradient, all_first, router_row)
+        )(rows_m, grad_pre, logit_gradient, all_first, router_row)
 
     def weight_half(half, left, right, kind):
         return pl.pallas_call(
@@ -295,45 +364,40 @@
 
     early_m, early_d = gather_rows(early)
     early_hidden, early_pre, early_y, early_logit = front(early_m, early_d)
-    early_own, early_side = row_gradients(early_pre, early_logit)
+    early_own, early_side, early_sums = row_gradients(early_m, early_pre, early_logit)
     for step in late:
         near[step], side[step] = tied((near[step], side[step]), (early_own, early_side))
     late_m, late_d = gather_rows(late)
-    late_hidden, late_pre, late_y, late_logit = front(late_m, late_d)
-    rows_m = jnp.concatenate([early_m, late_m], axis=0)
-    logit_gradient = jnp.concatenate([early_logit, late_logit], axis=0)
-    grad_pre = jnp.concatenate([early_pre, late_pre], axis=0)
+
+    def pairwise(value, name, size, bit):
+        return value + lax.ppermute(value, name, [(i, i ^ bit) for i in range(size)])
+
+    late_hidden, late_slope, late_y, late_gate = front_first(late_m, late_d)
     hidden = jnp.concatenate([early_hidden, late_hidden], axis=0)
     grad_y = jnp.concatenate([early_y, late_y], axis=0)
-
-    def pairwise(value, name, size, bit):
-        return value + lax.ppermute(value, name, [(i, i ^ bit) for i in range(size)])
-
-    in_leave = weight_half(0, grad_pre, rows_m, BF16)
-    in_pair = over_pair(in_leave)
-    in_stay = weight_half(1, tied(grad_pre, in_leave), rows_m, F32)
-    total = pl.pallas_call(
-        functools.partial(sums_kernel, experts),
-        out_shape=jax.ShapeDtypeStruct((-(-(experts + 1) // 8) * 8, width), F32),
-        in_specs=[SMEM] + [VMEM] * 5,
-        out_specs=VMEM,
-        compiler_params=PARAMS,
-        cost_estimate=pl.CostEstimate(
-            flops=6 * width * hidden_units, bytes_accessed=6 * width * hidden_units, transcendentals=0
-        ),
-        name="sums",
-    )(own_scalar, rows_m, logit_gradient, all_first, in_leave, in_stay)
+    out_leave = weight_half(0, hidden, grad_y, BF16)
+    out_pair = over_pair(out_leave)
+    late_pre, late_logit = front_second(
+        tied(late_d, out_leave), late_hidden, late_slope, late_gate
+    )
+    late_own, late_side, late_sums = row_gradients(late_m, late_pre, late_logit)
+    sums = early_sums + late_sums
+    line = jnp.arange(-(-(experts + 1) // 8) * 8, dtype=jnp.int32)[:, None]
+    total = jnp.where(line == own, sums[:1], jnp.where(line == experts, sums[1:2], 0.0))
+    hidden = tied(hidden, total)
     total = pairwise(total, "expert", halves, 1)
-    late_own, late_side = row_gradients(tied(late_pre, in_stay), late_logit)
-    out_leave = weight_half(0, tied(hidden, late_own), grad_y, BF16)
-
-    stage = (in_pair, in_stay, total, late_own, late_side, out_leave)
-    in_pair, in_stay, total, late_side, early_side, out_leave, hidden = tied(
-        (in_pair, in_stay, total, late_side, early_side, out_leave, hidden), stage
-    )
-    in_sum = in_stay + in_pair.astype(F32)
-    in_half = in_sum[:units].astype(BF16)
-    in_other = over_half(in_half)
+    out_stay = weight_half(1, hidden, grad_y, F32)
+    rows_m = jnp.concatenate([early_m, late_m], axis=0)
+    grad_pre = jnp.concatenate([early_pre, late_pre], axis=0)
+    in_leave = weight_half(0, tied(grad_pre, out_stay), rows_m, BF16)
+
+    stage = (out_pair, out_stay, total, late_own, late_side, in_leave)
+    out_pair, out_stay, total, late_side, early_side, in_leave, grad_pre = tied(
+        (out_pair, out_stay, total, late_side, early_side, in_leave, grad_pre), stage
+    )
+    out_sum = out_stay + out_pair.astype(F32)
+    out_half = out_sum[:units].astype(BF16)
+    out_other = over_half(out_half)
 
     def by_turn(rows):
         return rows.reshape(columns - 1, -1, width)
@@ -343,19 +407,19 @@
         lax.ppermute(leaving[turn - 1], "dp", turn_columns(columns - turn))
         for turn in range(1, columns)
     ]
-    out_pair = over_pair(out_leave)
-    out_stay = weight_half(1, tied(hidden, (in_half, leaving)), grad_y, F32)
-    total = tied(total, out_stay)
+    in_pair = over_pair(in_leave)
+    in_stay = weight_half(1, tied(grad_pre, (out_half, leaving)), rows_m, F32)
+    total = tied(total, in_stay)
     bit = 2
     while bit < halves:
         total = pairwise(total, "expert", halves, bit)
         bit *= 2
     total = pairwise(total, "dp", groups, 1)
 
-    stage = (in_other, rows_back, out_pair, out_stay, total)
-    in_other, rows_back, out_pair, out_stay, total = tied(stage, stage)
-    out_sum = out_stay + out_pair.astype(F32)
-    out_other = over_half(out_sum[:units].astype(BF16))
+    stage = (out_other, rows_back, in_pair, in_stay, total)
+    out_other, rows_back, in_pair, in_stay, total = tied(stage, stage)
+    in_sum = in_stay + in_pair.astype(F32)
+    in_other = over_half(in_sum[:units].astype(BF16))
     own_rows = jnp.concatenate([early_own, late_own], axis=0)
     for piece in rows_back:
         own_rows = own_rows + piece.astype(F32)
@@ -368,10 +432,11 @@
     while bit < groups:
         total = pairwise(total, "dp", groups, bit)
         bit *= 2
-    router_t = total[:experts]
-    grad_router = router_t.T
-    grad_gain = (total[experts] + jnp.sum(router_t * router.astype(F32).T, axis=0)) / gain
+    grad_router = total[:experts].T
+    grad_gain = total[experts] / gain
+    grad_out = (out_sum[units:] + out_other.astype(F32)).astype(BF16)[None]
     grad_in = (in_sum[units:] + in_other.astype(F32)).astype(BF16).T[None]
+    returned = tied(returned, (in_other, grad_out))
 
     input_grad = pl.pallas_call(
         functools.partial(combine_kernel, experts, capacity),
@@ -381,8 +446,6 @@
         compiler_params=PARAMS,
         name="combine",
     )(*token_args, jnp.concatenate(returned, axis=0))
-    out_mine = tied(out_sum[units:], (input_grad, grad_in))
-    grad_out = (out_mine + out_other.astype(F32)).astype(BF16)[None]
     return (input_grad, grad_in, grad_out, grad_router, grad_gain)
 
 

time: 130 us -> 129 us (level)
  other arithmetic: 7.35 us -> 12 us
  waiting for transfers between devices: 66 us -> 61.9 us
  starting transfers between devices: 28 us -> 25.8 us
  local copies, waits for them, and re-layouts: 6.78 us -> 8.1 us
    ppermute x6, waiting for transfers between devices: 29.9 us -> 41.3 us  [over_experts(): return lax.ppermute(value, 'expert', turn_experts(step))]
    ppermute x4, waiting for transfers between devices: 15.7 us -> 5.89 us  [over_columns(): lax.ppermute(value, 'dp', turn_columns(step))]
    concatenate x1, other arithmetic: 1.53 us -> 5.48 us  [body(): all_first = jnp.concatenate([first_yc, first_c, first_y, first], axis=0)]
    ppermute x4, waiting for transfers between devices: 4.56 us -> 1.09 us  [over_half(): return lax.ppermute(value, 'expert', swap_half)]
    pallas_call x2 -> x1, Pallas kernels: 7.86 us -> 5.17 us  [front(): pl.pallas_call(functools.partial(front_kernel, tile), out_shape=[jax.Shap...]
    pallas_call x1 -> x2, Pallas kernels: 1.07 us -> 2.93 us  [the longest x1 1.51 us: front_first(): pl.pallas_call(functools.partial(first_kernel, tile), out_shape=[jax.Shap...]
    ppermute x4, starting transfers between devices: 5.76 us -> 4.11 us  [over_columns(): lax.ppermute(value, 'dp', turn_columns(step))]
    ppermute x6, starting transfers between devices: 10.3 us -> 8.82 us  [over_experts(): return lax.ppermute(value, 'expert', turn_experts(step))]
  transfers between devices with their start and end apart: 26 -> 26, of which waited for: 16 -> 12; matrix products, arithmetic and copies ran while one was open for 5% -> 12% of each run, Pallas kernels for 12% -> 12%
where the time goes in v5:
time: 129 us; the launch traced here: 128 us
  waiting for transfers between devices  61.9 us (48%)
  starting transfers between devices  25.8 us (20%)
  Pallas kernels  19.5 us (15%)
  other arithmetic  12 us (9%)
  local copies, waits for them, and re-layouts  8.1 us (6%)
    ppermute x6, waiting for transfers between devices, over_experts(): return lax.ppermute(value, 'expert', turn_experts(step))  41.3 us
    ppermute x6, starting transfers between devices, over_experts(): return lax.ppermute(value, 'expert', turn_experts(step))  8.82 us
    ppermute x5, waiting for transfers between devices, pairwise(): lax.ppermute(value, name, [(i, i ^ bit) for i in range(size)])  6.92 us
    ppermute x1, waiting for transfers between devices, body(): lax.ppermute(leaving[turn - 1], 'dp', turn_columns(columns - turn))  6.68 us
    unnamed x27, local copies, waits for them, and re-layouts  6.32 us
    pallas_call x4, Pallas kernels, weight_half(): pl.pallas_call(functools.partial(weight_kernel, half, tile), out_shape=ja...  6.3 us
    ppermute x4, waiting for transfers between devices, over_columns(): lax.ppermute(value, 'dp', turn_columns(step))  5.89 us
    ppermute x5, starting transfers between devices, pairwise(): lax.ppermute(value, name, [(i, i ^ bit) for i in range(size)])  5.51 us
  transfers between devices with their start and end apart: 26, of which 12 were waited for; matrix products, arithmetic and copies ran while one was open for 12% of the time, Pallas kernels for 12%

profile of v5, /device:TPU:0, one launch (start us, length us, event | category | flops | bytes accessed | tf_op | source)
XLA Modules:
  0.0 128.4 jit_solution(14966022644346806593)
XLA Ops:
  1.1 2.6 %collective-permute-start.2 = (bf16[320,1280]{1,0:T(8,128)(2,1)}, bf16[320,1280]{1,0:T(8,128)(2,1)}, u32[]{:S(2)}, u32[]{:S(2)}) collective-permute-start(bf16[320,1280]{1,0:T(8,128)(2,1)} %bitcast.68), channel_id=1, source_target_pairs={{0,4},{4,0},{8,12},{12,8},{16,20},{20,16},{24,28},{28,24},{1,5},{5... | collective-permute-start | bytes 2457608 | tf_op jit(solution)/shard_map/ppermute | solution.py:195
  7.9 1.5 %collective-permute-start.3 = (bf16[2,80,1280]{2,1,0:T(8,128)(2,1)S(1)}, bf16[2,80,1280]{2,1,0:T(8,128)(2,1)}, u32[]{:S(2)}, u32[]{:S(2)}) collective-permute-start(bf16[2,80,1280]{2,1,0:T(8,128)(2,1)S(1)} %get-tuple-element.59), channel_id=1, source_target_pairs={{0,2},{1,3},{2,0},{3,1},{4,6},{5,7},{6,4},{7,5},{8,10},{9,11},{10,... | collective-permute-start | bytes 1228808 | tf_op jit(solution)/shard_map/ppermute | solution.py:192
  9.5 1.6 %collective-permute-start = (bf16[2,80,1280]{2,1,0:T(8,128)(2,1)S(1)}, bf16[2,80,1280]{2,1,0:T(8,128)(2,1)}, u32[]{:S(2)}, u32[]{:S(2)}) collective-permute-start(bf16[2,80,1280]{2,1,0:T(8,128)(2,1)S(1)} %get-tuple-element.61), channel_id=1, source_target_pairs={{0,8},{4,12},{8,16},{12,20},{16,24},{20,28},{24,0},{28,4},{1,9},{5... | collective-permute-start | bytes 1228808 | tf_op jit(solution)/shard_map/ppermute | solution.py:189
  11.1 2.2 %collective-permute-start.1 = (bf16[2,80,1280]{2,1,0:T(8,128)(2,1)S(1)}, bf16[2,80,1280]{2,1,0:T(8,128)(2,1)}, u32[]{:S(2)}, u32[]{:S(2)}) collective-permute-start(bf16[2,80,1280]{2,1,0:T(8,128)(2,1)S(1)} %get-tuple-element.62), channel_id=1, source_target_pairs={{0,24},{4,28},{8,0},{12,4},{16,8},{20,12},{24,16},{28,20},{1,25},{... | collective-permute-start | bytes 1228808 | tf_op jit(solution)/shard_map/ppermute | solution.py:189
  14.1 5.6 %collective-permute-done.3 = bf16[2,80,1280]{2,1,0:T(8,128)(2,1)} collective-permute-done((bf16[2,80,1280]{2,1,0:T(8,128)(2,1)S(1)}, bf16[2,80,1280]{2,1,0:T(8,128)(2,1)}, u32[]{:S(2)}, u32[]{:S(2)}) %collective-permute-start.3) | collective-permute-done | bytes 409632 | tf_op jit(solution)/shard_map/ppermute | solution.py:192
  19.6 4.1 %collective-permute-done = bf16[2,80,1280]{2,1,0:T(8,128)(2,1)} collective-permute-done((bf16[2,80,1280]{2,1,0:T(8,128)(2,1)S(1)}, bf16[2,80,1280]{2,1,0:T(8,128)(2,1)}, u32[]{:S(2)}, u32[]{:S(2)}) %collective-permute-start) | collective-permute-done | bytes 409632 | tf_op jit(solution)/shard_map/ppermute | solution.py:189
  23.8 7.2 %collective-permute-done.1 = bf16[2,80,1280]{2,1,0:T(8,128)(2,1)} collective-permute-done((bf16[2,80,1280]{2,1,0:T(8,128)(2,1)S(1)}, bf16[2,80,1280]{2,1,0:T(8,128)(2,1)}, u32[]{:S(2)}, u32[]{:S(2)}) %collective-permute-start.1) | collective-permute-done | bytes 409632 | tf_op jit(solution)/shard_map/ppermute | solution.py:189
  38.1 14.9 %collective-permute-done.5 = bf16[2,80,1280]{2,1,0:T(8,128)(2,1)S(1)} collective-permute-done((bf16[2,80,1280]{2,1,0:T(8,128)(2,1)S(1)}, bf16[2,80,1280]{2,1,0:T(8,128)(2,1)S(1)}, u32[]{:S(2)}, u32[]{:S(2)}) %collective-permute-start.5) | collective-permute-done | bytes 409632 | tf_op jit(solution)/shard_map/ppermute | solution.py:189
  54.6 5.5 %pad_maximum_fusion.first_ref = bf16[1280,1280]{1,0:T(8,128)(2,1)S(1)} fusion(bf16[320,1280]{1,0:T(8,128)(2,1)S(1)} %bitcast.69, bf16[320,1280]{1,0:T(8,128)(2,1)} %collective-permute-done.2, bf16[320,1280]{1,0:T(8,128)(2,1)S(1)} %collective-permute-done.4, bf16[320,1280]{1,0:T(8,128)(2,1)S(1)} %collective-permute-done.9), kind=kLoop, calls=%fused_computation | loop fusion | flops 13107200 | bytes 6553600 | tf_op jit(solution)/shard_map/concatenate | solution.py:255
  60.6 5.2 %front.1 = (bf16[480,1280]{1,0:T(8,128)(2,1)S(1)}, bf16[480,1280]{1,0:T(8,128)(2,1)S(1)}, bf16[480,1280]{1,0:T(8,128)(2,1)S(1)}, f32[480,128]{1,0:T(8,128)S(1)}) custom-call(bf16[480,1280]{1,0:T(8,128)(2,1)S(1)} %get-tuple-element.121.m_ref, bf16[480,1280]{1,0:T(8,128)(2,1)S(1)} %get-tuple-element.120.d_ref, ...), custom_call_target="tpu_custom_call" | custom-call | flops 3145728000 | bytes 6553600 | tf_op jit(solution)/shard_map/front/pallas_call | solution.py:271
  65.8 1.9 %rows.2 = (f32[240,1280]{1,0:T(8,128)S(1)}, bf16[240,1280]{1,0:T(8,128)(2,1)S(1)}, f32[8,1280]{1,0:T(8,128)S(1)}) custom-call(bf16[480,1280]{1,0:T(8,128)(2,1)S(1)} %get-tuple-element.121.m_ref, bf16[480,1280]{1,0:T(8,128)(2,1)S(1)} %get-tuple-element.73.pre_ref, f32[480,128]{1,0:T(8,128)S(1)} %get-tuple-element.74.logit_ref, ...), custom_call_target="tpu_custom_call" | custom-call | flops 1572864000 | bytes 3276800 | tf_op jit(solution)/shard_map/rows/pallas_call | solution.py:331
  68.0 1.5 %first.1 = (bf16[160,1280]{1,0:T(8,128)(2,1)S(1)}, f32[160,1280]{1,0:T(8,128)S(1)}, bf16[160,1280]{1,0:T(8,128)(2,1)S(1)}, f32[160,128]{1,0:T(8,128)S(1)}) custom-call(bf16[160,1280]{1,0:T(8,128)(2,1)S(1)} %pad_maximum_fusion.4.m_ref, bf16[160,1280]{1,0:T(8,128)(2,1)S(1)} %pad_maximum_fusion.5.d_ref, bf16[1280,1280]{1,0:T(8,128)(2,1)S(1)} %pad_maximum_fusion.first_ref, ...), custom_call_target="tpu_custom_call" | custom-call | flops 524288000 | bytes 3276800 | tf_op jit(solution)/shard_map/first/pallas_call | solution.py:291
  73.7 1.6 %collective-permute-start.14 = (f32[8,1280]{1,0:T(8,128)S(1)}, f32[8,1280]{1,0:T(8,128)S(1)}, u32[]{:S(2)}, u32[]{:S(2)}) collective-permute-start(f32[8,1280]{1,0:T(8,128)S(1)} %select_select_fusion), channel_id=1, source_target_pairs={{0,4},{4,0},{8,12},{12,8},{16,20},{20,16},{24,28},{28,24},{1,5},{5... | collective-permute-start | bytes 122888 | tf_op jit(solution)/shard_map/ppermute | solution.py:373
  76.8 1.8 %weights.6 = bf16[640,1280]{1,0:T(8,128)(2,1)S(1)} custom-call(bf16[640,1280]{1,0:T(8,128)(2,1)S(1)} %constant_dynamic-update-slice_fusion.4.left_ref, bf16[640,1280]{1,0:T(8,128)(2,1)S(1)} %constant_dynamic-update-slice_fusion.6.right_ref), custom_call_target="tpu_custom_call" | custom-call | flops 1048576000 | bytes 3276800 | tf_op jit(solution)/shard_map/weights/pallas_call | solution.py:350
  79.0 1.7 %convert_add_fusion.1 = f32[640,1280]{1,0:T(8,128)S(1)} fusion(f32[640,1280]{1,0:T(8,128)S(1)} %weights.5, bf16[640,1280]{1,0:T(8,128)(2,1)} %collective-permute-done.13), kind=kLoop, calls=%fused_computation.3 | loop fusion | flops 1638400 | bytes 8192000 | tf_op jit(solution)/shard_map/add | solution.py:398
  82.9 1.5 %weights.7 = f32[640,1280]{1,0:T(8,128)S(1)} custom-call(bf16[640,1280]{1,0:T(8,128)(2,1)S(1)} %constant_dynamic-update-slice_fusion.4.left_ref, bf16[640,1280]{1,0:T(8,128)(2,1)S(1)} %constant_dynamic-update-slice_fusion.6.right_ref), custom_call_target="tpu_custom_call" | custom-call | flops 1048576000 | bytes 3276800 | tf_op jit(solution)/shard_map/weights/pallas_call | solution.py:350
  84.5 1.6 %collective-permute-start.18 = (f32[8,1280]{1,0:T(8,128)S(1)}, f32[8,1280]{1,0:T(8,128)S(1)}, u32[]{:S(2)}, u32[]{:S(2)}) collective-permute-start(f32[8,1280]{1,0:T(8,128)S(1)} %fusion.5), channel_id=1, source_target_pairs={{0,8},{4,12},{8,0},{12,4},{16,24},{20,28},{24,16},{28,20},{1,9},{5... | collective-permute-start | bytes 122888 | tf_op jit(solution)/shard_map/ppermute | solution.py:373
  86.1 2.4 %collective-permute-done.18 = f32[8,1280]{1,0:T(8,128)S(1)} collective-permute-done((f32[8,1280]{1,0:T(8,128)S(1)}, f32[8,1280]{1,0:T(8,128)S(1)}, u32[]{:S(2)}, u32[]{:S(2)}) %collective-permute-start.18) | collective-permute-done | bytes 40992 | tf_op jit(solution)/shard_map/ppermute | solution.py:373
  88.6 1.6 %collective-permute-start.19 = (f32[8,1280]{1,0:T(8,128)S(1)}, f32[8,1280]{1,0:T(8,128)S(1)}, u32[]{:S(2)}, u32[]{:S(2)}) collective-permute-start(f32[8,1280]{1,0:T(8,128)S(1)} %add.41), channel_id=1, source_target_pairs={{0,16},{4,20},{8,24},{12,28},{16,0},{20,4},{24,8},{28,12},{1,17},{... | collective-permute-start | bytes 122888 | tf_op jit(solution)/shard_map/ppermute | solution.py:373
  90.2 3.3 %collective-permute-done.19 = f32[8,1280]{1,0:T(8,128)S(1)} collective-permute-done((f32[8,1280]{1,0:T(8,128)S(1)}, f32[8,1280]{1,0:T(8,128)S(1)}, u32[]{:S(2)}, u32[]{:S(2)}) %collective-permute-start.19) | collective-permute-done | bytes 40992 | tf_op jit(solution)/shard_map/ppermute | solution.py:373
  94.7 6.7 %collective-permute-done.16 = bf16[320,1280]{1,0:T(8,128)(2,1)S(1)} collective-permute-done((bf16[320,1280]{1,0:T(8,128)(2,1)S(1)}, bf16[320,1280]{1,0:T(8,128)(2,1)S(1)}, u32[]{:S(2)}, u32[]{:S(2)}) %collective-permute-start.16) | collective-permute-done | bytes 819232 | tf_op jit(solution)/shard_map/ppermute | solution.py:407
  105.6 2.2 %collective-permute-start.21 = (bf16[80,1280]{1,0:T(8,128)(2,1)S(1)}, bf16[80,1280]{1,0:T(8,128)(2,1)S(1)}, u32[]{:S(2)}, u32[]{:S(2)}) collective-permute-start(bf16[80,1280]{1,0:T(8,128)(2,1)S(1)} %get-tuple-element.117), channel_id=1, source_target_pairs={{0,24},{4,28},{8,0},{12,4},{16,8},{20,12},{24,16},{28,20},{1,25},{... | collective-permute-start | bytes 614408 | tf_op jit(solution)/shard_map/ppermute | solution.py:189
  110.6 2.8 %collective-permute-done.21 = bf16[80,1280]{1,0:T(8,128)(2,1)S(1)} collective-permute-done((bf16[80,1280]{1,0:T(8,128)(2,1)S(1)}, bf16[80,1280]{1,0:T(8,128)(2,1)S(1)}, u32[]{:S(2)}, u32[]{:S(2)}) %collective-permute-start.21) | collective-permute-done | bytes 204832 | tf_op jit(solution)/shard_map/ppermute | solution.py:189
  113.4 12.3 %collective-permute-done.22 = bf16[80,1280]{1,0:T(8,128)(2,1)S(1)} collective-permute-done((bf16[80,1280]{1,0:T(8,128)(2,1)S(1)}, bf16[80,1280]{1,0:T(8,128)(2,1)S(1)}, u32[]{:S(2)}, u32[]{:S(2)}) %collective-permute-start.22) | collective-permute-done | bytes 204832 | tf_op jit(solution)/shard_map/ppermute | solution.py:189
  (99 shorter events, 33.9 us)
Async XLA Ops:
  0.6 30.3 %collective-permute-start.4 = (bf16[320,1280]{1,0:T(8,128)(2,1)}, bf16[320,1280]{1,0:T(8,128)(2,1)S(1)}, u32[]{:S(2)}, u32[]{:S(2)}) collective-permute-start(bf16[320,1280]{1,0:T(8,128)(2,1)} %bitcast.67), channel_id=1, source_target_pairs={{0,1},{1,0},{2,3},{3,2},{4,5},{5,4},{6,7},{7,6},{8,9},{9,8},{10,11... | collective-permute-start | bytes 2457608 | tf_op jit(solution)/shard_map/ppermute | solution.py:198
  1.1 29.8 %collective-permute-start.2 = (bf16[320,1280]{1,0:T(8,128)(2,1)}, bf16[320,1280]{1,0:T(8,128)(2,1)}, u32[]{:S(2)}, u32[]{:S(2)}) collective-permute-start(bf16[320,1280]{1,0:T(8,128)(2,1)} %bitcast.68), channel_id=1, source_target_pairs={{0,4},{4,0},{8,12},{12,8},{16,20},{20,16},{24,28},{28,24},{1,5},{5... | collective-permute-start | bytes 2457608 | tf_op jit(solution)/shard_map/ppermute | solution.py:195
  7.9 11.7 %collective-permute-start.3 = (bf16[2,80,1280]{2,1,0:T(8,128)(2,1)S(1)}, bf16[2,80,1280]{2,1,0:T(8,128)(2,1)}, u32[]{:S(2)}, u32[]{:S(2)}) collective-permute-start(bf16[2,80,1280]{2,1,0:T(8,128)(2,1)S(1)} %get-tuple-element.59), channel_id=1, source_target_pairs={{0,2},{1,3},{2,0},{3,1},{4,6},{5,7},{6,4},{7,5},{8,10},{9,11},{10,... | collective-permute-start | bytes 1228808 | tf_op jit(solution)/shard_map/ppermute | solution.py:192
  9.5 14.3 %collective-permute-start = (bf16[2,80,1280]{2,1,0:T(8,128)(2,1)S(1)}, bf16[2,80,1280]{2,1,0:T(8,128)(2,1)}, u32[]{:S(2)}, u32[]{:S(2)}) collective-permute-start(bf16[2,80,1280]{2,1,0:T(8,128)(2,1)S(1)} %get-tuple-element.61), channel_id=1, source_target_pairs={{0,8},{4,12},{8,16},{12,20},{16,24},{20,28},{24,0},{28,4},{1,9},{5... | collective-permute-start | bytes 1228808 | tf_op jit(solution)/shard_map/ppermute | solution.py:189
  11.1 19.9 %collective-permute-start.1 = (bf16[2,80,1280]{2,1,0:T(8,128)(2,1)S(1)}, bf16[2,80,1280]{2,1,0:T(8,128)(2,1)}, u32[]{:S(2)}, u32[]{:S(2)}) collective-permute-start(bf16[2,80,1280]{2,1,0:T(8,128)(2,1)S(1)} %get-tuple-element.62), channel_id=1, source_target_pairs={{0,24},{4,28},{8,0},{12,4},{16,8},{20,12},{24,16},{28,20},{1,25},{... | collective-permute-start | bytes 1228808 | tf_op jit(solution)/shard_map/ppermute | solution.py:189
  30.9 22.4 %collective-permute-start.6 = (bf16[320,1280]{1,0:T(8,128)(2,1)S(1)}, bf16[320,1280]{1,0:T(8,128)(2,1)S(1)}, u32[]{:S(2)}, u32[]{:S(2)}) collective-permute-start(bf16[320,1280]{1,0:T(8,128)(2,1)S(1)} %bitcast.70), channel_id=1, source_target_pairs={{0,4},{4,0},{8,12},{12,8},{16,20},{20,16},{24,28},{28,24},{1,5},{5... | collective-permute-start | bytes 2457608 | tf_op jit(solution)/shard_map/ppermute | solution.py:195
  31.5 21.9 %collective-permute-start.9 = (bf16[320,1280]{1,0:T(8,128)(2,1)}, bf16[320,1280]{1,0:T(8,128)(2,1)S(1)}, u32[]{:S(2)}, u32[]{:S(2)}) collective-permute-start(bf16[320,1280]{1,0:T(8,128)(2,1)} %collective-permute-done.2), channel_id=1, source_target_pairs={{0,1},{1,0},{2,3},{3,2},{4,5},{5,4},{6,7},{7,6},{8,9},{9,8},{10,11... | collective-permute-start | bytes 2457608 | tf_op jit(solution)/shard_map/ppermute | solution.py:198
  31.5 21.6 %collective-permute-start.5 = (bf16[2,80,1280]{2,1,0:T(8,128)(2,1)S(1)}, bf16[2,80,1280]{2,1,0:T(8,128)(2,1)S(1)}, u32[]{:S(2)}, u32[]{:S(2)}) collective-permute-start(bf16[2,80,1280]{2,1,0:T(8,128)(2,1)S(1)} %get-tuple-element.67), channel_id=1, source_target_pairs={{0,16},{4,20},{8,24},{12,28},{16,0},{20,4},{24,8},{28,12},{1,17},{... | collective-permute-start | bytes 1228808 | tf_op jit(solution)/shard_map/ppermute | solution.py:189
  32.8 20.3 %collective-permute-start.7 = (bf16[2,80,1280]{2,1,0:T(8,128)(2,1)}, bf16[2,80,1280]{2,1,0:T(8,128)(2,1)S(1)}, u32[]{:S(2)}, u32[]{:S(2)}) collective-permute-start(bf16[2,80,1280]{2,1,0:T(8,128)(2,1)} %collective-permute-done), channel_id=1, source_target_pairs={{0,2},{1,3},{2,0},{3,1},{4,6},{5,7},{6,4},{7,5},{8,10},{9,11},{10,... | collective-permute-start | bytes 1228808 | tf_op jit(solution)/shard_map/ppermute | solution.py:192
  33.3 20.0 %collective-permute-start.8 = (bf16[2,80,1280]{2,1,0:T(8,128)(2,1)}, bf16[2,80,1280]{2,1,0:T(8,128)(2,1)S(1)}, u32[]{:S(2)}, u32[]{:S(2)}) collective-permute-start(bf16[2,80,1280]{2,1,0:T(8,128)(2,1)} %collective-permute-done.1), channel_id=1, source_target_pairs={{0,2},{1,3},{2,0},{3,1},{4,6},{5,7},{6,4},{7,5},{8,10},{9,11},{10,... | collective-permute-start | bytes 1228808 | tf_op jit(solution)/shard_map/ppermute | solution.py:192
  53.4 6.7 %collective-permute-start.10 = (bf16[320,1280]{1,0:T(8,128)(2,1)S(1)}, bf16[320,1280]{1,0:T(8,128)(2,1)S(1)}, u32[]{:S(2)}, u32[]{:S(2)}) collective-permute-start(bf16[320,1280]{1,0:T(8,128)(2,1)S(1)} %collective-permute-done.6), channel_id=1, source_target_pairs={{0,1},{1,0},{2,3},{3,2},{4,5},{5,4},{6,7},{7,6},{8,9},{9,8},{10,11... | collective-permute-start | bytes 2457608 | tf_op jit(solution)/shard_map/ppermute | solution.py:198
  53.4 6.7 %collective-permute-start.11 = (bf16[320,1280]{1,0:T(8,128)(2,1)S(1)}, bf16[320,1280]{1,0:T(8,128)(2,1)S(1)}, u32[]{:S(2)}, u32[]{:S(2)}) collective-permute-start(bf16[320,1280]{1,0:T(8,128)(2,1)S(1)} %bitcast.71), channel_id=1, source_target_pairs={{0,1},{1,0},{2,3},{3,2},{4,5},{5,4},{6,7},{7,6},{8,9},{9,8},{10,11... | collective-permute-start | bytes 2457608 | tf_op jit(solution)/shard_map/ppermute | solution.py:198
  53.9 13.9 %collective-permute-start.12 = (bf16[2,80,1280]{2,1,0:T(8,128)(2,1)S(1)}, bf16[2,80,1280]{2,1,0:T(8,128)(2,1)S(1)}, u32[]{:S(2)}, u32[]{:S(2)}) collective-permute-start(bf16[2,80,1280]{2,1,0:T(8,128)(2,1)S(1)} %collective-permute-done.5), channel_id=1, source_target_pairs={{0,2},{1,3},{2,0},{3,1},{4,6},{5,7},{6,4},{7,5},{8,10},{9,11},{10,... | collective-permute-start | bytes 1228808 | tf_op jit(solution)/shard_map/ppermute | solution.py:192
  71.2 7.4 %collective-permute-start.13 = (bf16[640,1280]{1,0:T(8,128)(2,1)S(1)}, bf16[640,1280]{1,0:T(8,128)(2,1)}, u32[]{:S(2)}, u32[]{:S(2)}) collective-permute-start(bf16[640,1280]{1,0:T(8,128)(2,1)S(1)} %weights.4), channel_id=1, source_target_pairs={{0,1},{1,0},{2,3},{3,2},{4,5},{5,4},{6,7},{7,6},{8,9},{9,8},{10,11... | collective-permute-start | bytes 4915208 | tf_op jit(solution)/shard_map/ppermute | solution.py:198
  73.7 4.9 %collective-permute-start.14 = (f32[8,1280]{1,0:T(8,128)S(1)}, f32[8,1280]{1,0:T(8,128)S(1)}, u32[]{:S(2)}, u32[]{:S(2)}) collective-permute-start(f32[8,1280]{1,0:T(8,128)S(1)} %select_select_fusion), channel_id=1, source_target_pairs={{0,4},{4,0},{8,12},{12,8},{16,20},{20,16},{24,28},{28,24},{1,5},{5... | collective-permute-start | bytes 122888 | tf_op jit(solution)/shard_map/ppermute | solution.py:373
  78.7 23.8 %collective-permute-start.17 = (bf16[640,1280]{1,0:T(8,128)(2,1)S(1)}, bf16[640,1280]{1,0:T(8,128)(2,1)S(1)}, u32[]{:S(2)}, u32[]{:S(2)}) collective-permute-start(bf16[640,1280]{1,0:T(8,128)(2,1)S(1)} %weights.6), channel_id=1, source_target_pairs={{0,1},{1,0},{2,3},{3,2},{4,5},{5,4},{6,7},{7,6},{8,9},{9,8},{10,11... | collective-permute-start | bytes 4915208 | tf_op jit(solution)/shard_map/ppermute | solution.py:198
  80.9 20.5 %collective-permute-start.16 = (bf16[320,1280]{1,0:T(8,128)(2,1)S(1)}, bf16[320,1280]{1,0:T(8,128)(2,1)S(1)}, u32[]{:S(2)}, u32[]{:S(2)}) collective-permute-start(bf16[320,1280]{1,0:T(8,128)(2,1)S(1)} %fusion.6), channel_id=1, source_target_pairs={{0,2},{1,3},{2,0},{3,1},{4,6},{5,7},{6,4},{7,5},{8,10},{9,11},{10,... | collective-permute-start | bytes 2457608 | tf_op jit(solution)/shard_map/ppermute | solution.py:407
  82.3 20.1 %collective-permute-start.15 = (bf16[320,1280]{1,0:T(8,128)(2,1)S(1)}, bf16[320,1280]{1,0:T(8,128)(2,1)S(1)}, u32[]{:S(2)}, u32[]{:S(2)}) collective-permute-start(bf16[320,1280]{1,0:T(8,128)(2,1)S(1)} %slice.173), channel_id=1, source_target_pairs={{0,4},{4,0},{8,12},{12,8},{16,20},{20,16},{24,28},{28,24},{1,5},{5... | collective-permute-start | bytes 2457608 | tf_op jit(solution)/shard_map/ppermute | solution.py:195
  88.6 4.9 %collective-permute-start.19 = (f32[8,1280]{1,0:T(8,128)S(1)}, f32[8,1280]{1,0:T(8,128)S(1)}, u32[]{:S(2)}, u32[]{:S(2)}) collective-permute-start(f32[8,1280]{1,0:T(8,128)S(1)} %add.41), channel_id=1, source_target_pairs={{0,16},{4,20},{8,24},{12,28},{16,0},{20,4},{24,8},{28,12},{1,17},{... | collective-permute-start | bytes 122888 | tf_op jit(solution)/shard_map/ppermute | solution.py:373
  102.5 6.8 %collective-permute-start.25 = (f32[8,1280]{1,0:T(8,128)S(1)}, f32[8,1280]{1,0:T(8,128)S(1)}, u32[]{:S(2)}, u32[]{:S(2)}) collective-permute-start(f32[8,1280]{1,0:T(8,128)S(1)} %add.43), channel_id=1, source_target_pairs={{0,2},{1,3},{2,0},{3,1},{4,6},{5,7},{6,4},{7,5},{8,10},{9,11},{10,... | collective-permute-start | bytes 122888 | tf_op jit(solution)/shard_map/ppermute | solution.py:373
  103.5 22.2 %collective-permute-start.24 = (bf16[320,1280]{1,0:T(8,128)(2,1)S(1)}, bf16[320,1280]{1,0:T(8,128)(2,1)S(1)}, u32[]{:S(2)}, u32[]{:S(2)}) collective-permute-start(bf16[320,1280]{1,0:T(8,128)(2,1)S(1)} %slice.172), channel_id=1, source_target_pairs={{0,4},{4,0},{8,12},{12,8},{16,20},{20,16},{24,28},{28,24},{1,5},{5... | collective-permute-start | bytes 2457608 | tf_op jit(solution)/shard_map/ppermute | solution.py:195
  105.6 7.8 %collective-permute-start.21 = (bf16[80,1280]{1,0:T(8,128)(2,1)S(1)}, bf16[80,1280]{1,0:T(8,128)(2,1)S(1)}, u32[]{:S(2)}, u32[]{:S(2)}) collective-permute-start(bf16[80,1280]{1,0:T(8,128)(2,1)S(1)} %get-tuple-element.117), channel_id=1, source_target_pairs={{0,24},{4,28},{8,0},{12,4},{16,8},{20,12},{24,16},{28,20},{1,25},{... | collective-permute-start | bytes 614408 | tf_op jit(solution)/shard_map/ppermute | solution.py:189
  107.8 17.8 %collective-permute-start.22 = (bf16[80,1280]{1,0:T(8,128)(2,1)S(1)}, bf16[80,1280]{1,0:T(8,128)(2,1)S(1)}, u32[]{:S(2)}, u32[]{:S(2)}) collective-permute-start(bf16[80,1280]{1,0:T(8,128)(2,1)S(1)} %get-tuple-element.116), channel_id=1, source_target_pairs={{0,16},{4,20},{8,24},{12,28},{16,0},{20,4},{24,8},{28,12},{1,17},{... | collective-permute-start | bytes 614408 | tf_op jit(solution)/shard_map/ppermute | solution.py:189
  108.7 17.0 %collective-permute-start.23 = (bf16[80,1280]{1,0:T(8,128)(2,1)S(1)}, bf16[80,1280]{1,0:T(8,128)(2,1)S(1)}, u32[]{:S(2)}, u32[]{:S(2)}) collective-permute-start(bf16[80,1280]{1,0:T(8,128)(2,1)S(1)} %get-tuple-element.115), channel_id=1, source_target_pairs={{0,8},{4,12},{8,16},{12,20},{16,24},{20,28},{24,0},{28,4},{1,9},{5... | collective-permute-start | bytes 614408 | tf_op jit(solution)/shard_map/ppermute | solution.py:189
  (11 other events, 114.6 us)

commit v6 on v3

v6 whole, which is shorter than its diff:
```python
import functools
import math

import jax
import jax.numpy as jnp
from jax import lax
from jax.experimental import pallas as pl
from jax.experimental.pallas import tpu as pltpu
from jax.sharding import PartitionSpec as P

F32 = jnp.float32
BF16 = jnp.bfloat16
VMEM = pl.BlockSpec(memory_space=pltpu.VMEM)
SMEM = pl.BlockSpec(memory_space=pltpu.SMEM)
ANY = pl.BlockSpec(memory_space=pl.ANY)
PARAMS = pltpu.CompilerParams(vmem_limit_bytes=40 * 2**20)


def gelu_parts(pre):
    coeff = math.sqrt(2.0 / math.pi)
    inner = coeff * (pre + 0.044715 * pre * pre * pre)
    tanh_val = jnp.tanh(inner)
    value = 0.5 * pre * (1.0 + tanh_val)
    slope = 0.5 * (1.0 + tanh_val) + 0.5 * pre * (1.0 - tanh_val * tanh_val) * coeff * (
        1.0 + 3.0 * 0.044715 * pre * pre
    )
    return (value, slope)


def dot(a, b, a_dim, b_dim):
    return lax.dot_general(a, b, (((a_dim,), (b_dim,)), ((), ())), preferred_element_type=F32)


def spans(total, size=256):
    return [(at, min(size, total - at)) for at in range(0, total, size)]


def norm_pieces(block):
    values = block.astype(F32)
    centred_rows = values - jnp.mean(values, axis=1, keepdims=True)
    inverse_deviation = lax.rsqrt(
        jnp.mean(centred_rows * centred_rows, axis=1, keepdims=True) + 1e-06
    )
    return centred_rows * inverse_deviation, inverse_deviation


def slot_of(own, routes, experts, capacity):
    top, tokens = routes.shape
    relative = routes - own
    relative = jnp.where(relative < 0, relative + experts, relative)
    lanes = max(16, experts)
    expert = lax.broadcasted_iota(jnp.int32, (lanes, tokens), 0)
    picks = [expert == relative[j : j + 1, :] for j in range(top)]
    chosen = sum(jnp.where(pick, 1.0, 0.0) for pick in picks)
    earlier = lax.broadcasted_iota(jnp.int32, (tokens, tokens), 0) < lax.broadcasted_iota(
        jnp.int32, (tokens, tokens), 1
    )
    before = dot(chosen.astype(BF16), jnp.where(earlier, 1.0, 0.0).astype(BF16), 1, 0)
    return [
        relative[j : j + 1, :] * capacity
        + jnp.sum(jnp.where(pick, before, 0.0), axis=0, keepdims=True).astype(jnp.int32)
        for j, pick in enumerate(picks)
    ]


def place_matrix(slots, first, count, tokens):
    row = lax.broadcasted_iota(jnp.int32, (count, tokens), 0) + first
    hit = slots[0] == row
    for slot in slots[1:]:
        hit = hit | (slot == row)
    return jnp.where(hit, 1.0, 0.0).astype(BF16)


def dispatch_kernel(experts, capacity, own_ref, x_hbm, gain_ref, routes_ref, d_hbm, *refs):
    send_refs, (x_ref, d_ref, sems) = refs[:experts], refs[experts:]
    x_copy = pltpu.make_async_copy(x_hbm, x_ref, sems.at[0])
    d_copy = pltpu.make_async_copy(d_hbm, d_ref, sems.at[1])
    x_copy.start()
    d_copy.start()
    tokens = x_ref.shape[0]
    slots = slot_of(own_ref[0], routes_ref[...], experts, capacity)
    x_copy.wait()
    normalized_rows, _ = norm_pieces(x_ref[...])
    mixed_rows = (normalized_rows * gain_ref[...]).astype(BF16)
    d_copy.wait()
    cotangent = d_ref[...]
    for step in range(experts):
        places = place_matrix(slots, step * capacity, capacity, tokens)
        send_refs[step][0] = dot(places, mixed_rows, 1, 0).astype(BF16)
        send_refs[step][1] = dot(places, cotangent, 1, 0).astype(BF16)


def prepare_kernel(experts, capacity, own_ref, x_ref, routes_ref, norm_ref, deviation_ref, places_ref):
    normalized_rows, inverse_deviation = norm_pieces(x_ref[...])
    norm_ref[...] = normalized_rows
    deviation_ref[...] = jnp.broadcast_to(inverse_deviation, deviation_ref.shape)
    slots = slot_of(own_ref[0], routes_ref[...], experts, capacity)
    places_ref[...] = place_matrix(slots, 0, experts * capacity, x_ref.shape[0])


def finish_kernel(
    norm_ref, deviation_ref, places_ref, gain_ref, d_ref, rows_ref, stay_ref, pair_ref, other_ref, *refs
):
    out_ref, sum_ref, router_ref, gain_grad_ref = refs[-4:]
    sum_ref[...] = (
        stay_ref[...] + pair_ref[...].astype(F32) + other_ref[...].astype(F32)
    ).astype(BF16)
    normalized_rows = norm_ref[...]
    scaled_rows = dot(places_ref[...], rows_ref[...], 0, 0) * gain_ref[...]
    mean_first_term = jnp.mean(scaled_rows, axis=1, keepdims=True)
    mean_second_term = jnp.mean(scaled_rows * normalized_rows, axis=1, keepdims=True)
    norm_backward = deviation_ref[:, :1] * (
        scaled_rows - mean_first_term - normalized_rows * mean_second_term
    )
    out_ref[...] = (d_ref[...].astype(F32) + norm_backward).astype(BF16)
    parts = [ref[...] for ref in refs[:-4]]
    while len(parts) > 1:
        parts = [parts[i] + parts[i + 1] for i in range(0, len(parts), 2)]
    experts = router_ref.shape[0]
    router_ref[...] = parts[0][:experts]
    gain_grad_ref[...] = jnp.sum(parts[0][experts:], axis=0, keepdims=True) / gain_ref[...]


def first_kernel(m_ref, d_ref, first_ref, router_ref, hidden_ref, slope_ref, y_ref, gate_ref):
    rows_m = m_ref[...]
    gate = jax.nn.sigmoid(jnp.sum(rows_m.astype(F32) * router_ref[...], axis=1, keepdims=True))
    y_ref[...] = (gate * d_ref[...].astype(F32)).astype(BF16)
    gate_ref[...] = jnp.broadcast_to(gate, gate_ref.shape)
    for at, size in spans(first_ref.shape[0]):
        units = pl.ds(at, size)
        value, slope = gelu_parts(dot(rows_m, first_ref[units, :], 1, 1))
        hidden_ref[:, units] = value.astype(BF16)
        slope_ref[:, units] = gate * slope


def second_kernel(d_ref, second_ref, hidden_ref, slope_ref, gate_ref, pre_ref, logit_ref):
    rows_d = d_ref[...]
    gate = gate_ref[:, :1]
    share = jnp.zeros_like(gate)
    for at, size in spans(second_ref.shape[0]):
        units = pl.ds(at, size)
        back = dot(rows_d, second_ref[units, :], 1, 1)
        pre_ref[:, units] = (back * slope_ref[:, units]).astype(BF16)
        share = share + jnp.sum(hidden_ref[:, units].astype(F32) * back, axis=1, keepdims=True)
    logit_ref[...] = jnp.broadcast_to(share * gate * (1.0 - gate), logit_ref.shape)


def rows_kernel(m_ref, pre_ref, logit_ref, first_ref, router_ref, own_ref, side_ref, sums_ref):
    count = own_ref.shape[0]
    pre = pre_ref[...]
    logit = logit_ref[:, :1]
    for at, size in spans(first_ref.shape[1]):
        lanes = pl.ds(at, size)
        rows = dot(pre, first_ref[:, lanes], 1, 0) + logit * router_ref[:, lanes]
        own_ref[:, lanes] = rows[:count]
        side_ref[:, lanes] = rows[count:].astype(BF16)
        rows_m = m_ref[:, lanes].astype(F32)
        router_part = jnp.sum(rows_m * logit, axis=0, keepdims=True)
        gain_part = jnp.sum(rows_m * rows, axis=0, keepdims=True)
        row = lax.broadcasted_iota(jnp.int32, (sums_ref.shape[0], size), 0)
        sums_ref[:, lanes] = jnp.where(row == 0, router_part, jnp.where(row == 1, gain_part, 0.0))


def weight_kernel(first, left_ref, right_ref, out_ref, turned):
    units = out_ref.shape[0]
    low = first // 128 * 128
    high = -(-(first + units) // 128) * 128
    turned[...] = left_ref[:, low:high].T
    for at, size in spans(right_ref.shape[1]):
        lanes = pl.ds(at, size)
        out_ref[:, lanes] = dot(
            turned[first - low : first - low + units, :], right_ref[:, lanes], 1, 0
        ).astype(out_ref.dtype)


def join_kernel(*refs):
    at = 0
    for ref in refs[:-1]:
        refs[-1][at : at + ref.shape[0], :] = ref[...]
        at += ref.shape[0]


def half_kernel(stay_ref, pair_ref, out_ref):
    out_ref[...] = (stay_ref[...] + pair_ref[...].astype(F32)).astype(BF16)


def tied(values, after):
    held, _ = lax.optimization_barrier((values, after))
    return held


def shape(kind, *sizes):
    return jax.ShapeDtypeStruct(sizes, kind)


def call(kernel, name, outs, args, flops=0, specs=None, scratch=()):
    return pl.pallas_call(
        kernel,
        out_shape=outs,
        in_specs=specs or [VMEM] * len(args),
        out_specs=jax.tree.map(lambda _: VMEM, outs),
        scratch_shapes=list(scratch),
        compiler_params=PARAMS,
        cost_estimate=pl.CostEstimate(flops=flops, bytes_accessed=flops // 512, transcendentals=0),
        name=name,
    )(*args)


def body(prenorm_input, gain, router, routes, w_in, w_out, cotangent):
    halves = lax.axis_size("expert")
    experts = halves // 2
    groups = lax.axis_size("dp")
    columns = groups // 2
    tokens, width = prenorm_input.shape
    top = routes.shape[1]
    capacity = max(2, 5 * tokens * top // (4 * experts))
    slots = experts * capacity
    own = lax.axis_index("expert") // 2

    def over_half(value):
        return lax.ppermute(value, "expert", [(i, i ^ 1) for i in range(halves)])

    def over_pair(value):
        return lax.ppermute(value, "dp", [(i, i ^ 1) for i in range(groups)])

    def over_columns(value):
        return [
            lax.ppermute(value, "dp", [(i, (i + 2 * step) % groups) for i in range(groups)])
            for step in range(1, columns)
        ]

    def back_over_columns(values):
        return [
            lax.ppermute(value, "dp", [(i, (i - 2 * step) % groups) for i in range(groups)])
            for step, value in enumerate(values, 1)
        ]

    def over_experts(value, step):
        return lax.ppermute(value, "expert", [(i, (i + 2 * step) % halves) for i in range(halves)])

    def over_groups(value):
        return [value] + [
            lax.ppermute(value, "dp", [(i, i ^ bit) for i in range(groups)]) for bit in range(1, groups)
        ]

    first = w_in[0].T
    second = w_out[0]
    units = first.shape[0]
    hidden_units = 4 * units

    own_scalar = own.astype(jnp.int32).reshape(1)
    gain_row = gain[None, :]
    routes_t = routes.T
    send = call(
        functools.partial(dispatch_kernel, experts, capacity),
        "dispatch",
        [shape(BF16, 2, capacity, width)] * experts,
        (own_scalar, prenorm_input, gain_row, routes_t, cotangent),
        flops=4 * slots * tokens * width,
        specs=[SMEM, ANY, VMEM, VMEM, ANY],
        scratch=[
            pltpu.VMEM((tokens, width), BF16),
            pltpu.VMEM((tokens, width), BF16),
            pltpu.SemaphoreType.DMA((2,)),
        ],
    )

    steps = sorted(range(experts), key=lambda step: min(step, experts - step))
    quarter = experts // 4
    early, late = steps[: 3 * quarter], steps[3 * quarter :]
    near = {0: send[0]}
    for step in early[1:]:
        near[step] = over_experts(send[step], step)
    side = {0: over_columns(send[0])}
    first_y = over_half(tied(first, send[0]))
    first_c = over_pair(tied(first, send[0]))

    stage = (first_y, first_c, [near[step] for step in early], side[0])
    second_held, late_held, early_held, first_y, side[0] = tied(
        (second, [send[step] for step in late], [near[step] for step in early], first_y, side[0]),
        stage,
    )
    for step, value in zip(late, late_held):
        near[step] = over_experts(value, step)
    for step, value in zip(early, early_held):
        near[step] = value
        if step:
            side[step] = over_columns(value)
    second_y = over_half(second_held)
    first_yc = over_pair(first_y)
    prepared = call(
        functools.partial(prepare_kernel, experts, capacity),
        "prepare",
        [shape(F32, tokens, width), shape(F32, tokens, 128), shape(BF16, slots, tokens)],
        (own_scalar, prenorm_input, routes_t),
        specs=[SMEM, VMEM, VMEM],
    )

    stage = (
        second_y,
        first_yc,
        [near[step] for step in late],
        [side[step] for step in early[1:]],
        prepared,
    )
    late_held, second_held, second_y, early_held, first_yc, prepared = tied(
        (
            [near[step] for step in late],
            second_held,
            second_y,
            [side[step] for step in early[1:]],
            first_yc,
            prepared,
        ),
        stage,
    )
    for step, value in zip(early[1:], early_held):
        side[step] = value
    for step, value in zip(late, late_held):
        near[step] = value
        side[step] = over_columns(value)
    second_c = over_pair(second_held)
    second_yc = over_pair(second_y)

    def join(*parts):
        return call(join_kernel, "join", shape(BF16, hidden_units, width), parts)

    all_first = join(first_yc, first_c, first_y, first)
    all_second = join(second_yc, second_c, second_y, second_held)

    router_row = lax.dynamic_slice_in_dim(router, own, 1, 1).astype(F32).T

    def gather_rows(chosen):
        pieces = [near[step] for step in chosen]
        for turn in range(columns - 1):
            pieces = pieces + [side[step][turn] for step in chosen]
        return (
            jnp.concatenate([piece[0] for piece in pieces], axis=0),
            jnp.concatenate([piece[1] for piece in pieces], axis=0),
        )

    def first_product(rows_m, rows_d):
        count = rows_m.shape[0]
        return call(
            first_kernel,
            "first",
            [
                shape(BF16, count, hidden_units),
                shape(F32, count, hidden_units),
                shape(BF16, count, width),
                shape(F32, count, 128),
            ],
            (rows_m, rows_d, all_first, router_row),
            flops=2 * count * width * hidden_units,
        )

    def second_product(rows_d, hidden, slope, gate):
        count = rows_d.shape[0]
        return call(
            second_kernel,
            "second",
            [shape(BF16, count, hidden_units), shape(F32, count, 128)],
            (rows_d, all_second, hidden, slope, gate),
            flops=2 * count * width * hidden_units,
        )

    def row_gradients(rows_m, grad_pre, logit_gradient):
        count = grad_pre.shape[0]
        return call(
            rows_kernel,
            "rows",
            [
                shape(F32, count // columns, width),
                shape(BF16, count - count // columns, width),
                shape(F32, 8, width),
            ],
            (rows_m, grad_pre, logit_gradient, all_first, router_row),
            flops=2 * count * width * hidden_units,
        )

    def weight_gradient(at, blocks, left, right, kind):
        low = at * units // 128 * 128
        high = -(-(at + blocks) * units // 128) * 128
        return call(
            functools.partial(weight_kernel, at * units),
            "weights",
            shape(kind, blocks * units, width),
            (left, right),
            flops=2 * left.shape[0] * width * blocks * units,
            scratch=[pltpu.VMEM((high - low, left.shape[0]), BF16)],
        )

    def half_sum(stay, pair):
        return call(half_kernel, "half", shape(BF16, units, width), (stay, pair))

    early_m, early_d = gather_rows(early)
    early_hidden, early_slope, early_y, early_gate = first_product(early_m, early_d)
    early_pre, early_logit = second_product(early_d, early_hidden, early_slope, early_gate)
    early_own, early_side, early_sums = row_gradients(early_m, early_pre, early_logit)
    for step in late:
        near[step], side[step] = tied((near[step], side[step]), (early_own, early_side))
    late_m, late_d = gather_rows(late)

    block = quarter * capacity

    def by_turn(rows):
        return rows.reshape(columns - 1, -1, width)

    early_side = by_turn(early_side)

    moved = back_over_columns(list(early_side[:, block : 2 * block]))
    late_hidden, late_slope, late_y, late_gate = first_product(late_m, late_d)
    hidden = jnp.concatenate([early_hidden, late_hidden], axis=0)
    grad_y = jnp.concatenate([early_y, late_y], axis=0)
    out_leave = weight_gradient(0, 1, hidden, grad_y, BF16)
    out_pair = over_pair(out_leave)
    hidden = tied(hidden, out_leave)
    out_stay = weight_gradient(2, 1, hidden, grad_y, F32)
    late_pre, late_logit = second_product(tied(late_d, out_stay), late_hidden, late_slope, late_gate)
    late_own, late_side, late_sums = row_gradients(late_m, late_pre, late_logit)
    sums = early_sums + late_sums
    line = jnp.arange(2 * experts, dtype=jnp.int32)[:, None]
    total = jnp.where(line == own, sums[:1], jnp.where(line == experts + own, sums[1:2], 0.0))
    total = total + over_half(total)
    out_half = half_sum(out_stay, out_pair)

    stage = (out_half, total, late_own, late_side, moved)
    out_half, total, late_side, moved, hidden = tied((out_half, total, late_side, moved, hidden), stage)
    out_other = over_half(out_half)
    late_side = by_turn(late_side)
    leaving = jnp.concatenate([early_side[:, :block], early_side[:, 2 * block :], late_side], axis=1)
    rows_back = back_over_columns(list(leaving))

    def add_rows(own_rows, pieces):
        for piece in pieces:
            own_rows = own_rows + piece.astype(F32)
        return own_rows.astype(BF16).reshape(-1, capacity, width)

    returned = [None] * experts

    def send_back(chosen, rows):
        for step, value in zip(chosen, rows):
            returned[step] = over_experts(value, experts - step) if step else value

    moved_steps = steps[quarter : 2 * quarter]
    other_steps = steps[:quarter] + steps[2 * quarter :]
    send_back(moved_steps, add_rows(early_own[block : 2 * block], moved))
    rows_m = jnp.concatenate([early_m, late_m], axis=0)
    grad_pre = jnp.concatenate([early_pre, late_pre], axis=0)
    total = tied(total, (out_half, leaving))
    totals = [total] + [over_experts(total, step) for step in range(1, experts)]
    grad_pre = tied(grad_pre, (out_half, leaving))
    in_leave = weight_gradient(0, 1, grad_pre, rows_m, BF16)
    in_pair = over_pair(in_leave)
    in_stay = weight_gradient(2, 1, tied(grad_pre, in_leave), rows_m, F32)
    hidden, grad_pre = tied((hidden, grad_pre), in_stay)
    out_rest = over_pair(weight_gradient(1, 1, hidden, grad_y, BF16))
    out_mine = weight_gradient(3, 1, hidden, grad_y, F32)
    in_rest = over_pair(weight_gradient(1, 1, grad_pre, rows_m, BF16))
    in_mine = weight_gradient(3, 1, grad_pre, rows_m, F32)

    moved_back = [returned[step] for step in moved_steps]
    stage = (out_other, rows_back, in_pair, in_stay, totals, moved_back)
    out_other, rows_back, in_pair, in_stay, totals, moved_back = tied(stage, stage)
    for step, value in zip(moved_steps, moved_back):
        returned[step] = value
    in_other = over_half(half_sum(in_stay, in_pair))
    own_rows = jnp.concatenate([early_own[:block], early_own[2 * block :], late_own], axis=0)
    send_back(other_steps, add_rows(own_rows, rows_back))
    totals = over_groups(sum(totals[1:], totals[0]))
    grad_out = (out_mine + out_rest.astype(F32) + out_other.astype(F32)).astype(BF16)[None]

    returned = tied(returned, (in_other, grad_out))
    norm, deviation, places = prepared
    input_grad, grad_in, grad_router, grad_gain = call(
        finish_kernel,
        "finish",
        [
            shape(BF16, tokens, width),
            shape(BF16, units, width),
            shape(F32, experts, width),
            shape(F32, 1, width),
        ],
        (
            norm,
            deviation,
            places,
            gain_row,
            cotangent,
            jnp.concatenate(returned, axis=0),
            in_mine,
            in_rest,
            in_other,
            *totals,
        ),
    )
    return (input_grad, grad_in.T[None], grad_out, grad_router.T, grad_gain[0])


def solution(mesh):
    in_specs = (
        P(("expert", "dp"), None),
        P(),
        P(),
        P(("expert", "dp"), None),
        P("expert", None, "dp"),
        P("expert", "dp", None),
        P(("expert", "dp"), None),
    )
    out_specs = (
        P(("expert", "dp"), None),
        P("expert", None, "dp"),
        P("expert", "dp", None),
        P(),
        P(),
    )
    return jax.shard_map(body, mesh=mesh, in_specs=in_specs, out_specs=out_specs, check_vma=False)
```

time: 146 us -> 133 us (0.911); the launches traced: 144 us -> 133 us
  Pallas kernels: 2.35 us -> 23.3 us
  matrix products: 17.6 us -> 0 us
  waiting for transfers between devices: 77.5 us -> 60 us
  local copies, waits for them, and re-layouts: 7.95 us -> 16.5 us
  other arithmetic: 6.14 us -> 3.12 us
  starting transfers between devices: 31.2 us -> 28.6 us
    pallas_call x2 -> x21, Pallas kernels: 2.35 us -> 23.3 us  [call(): pl.pallas_call(kernel, out_shape=outs, in_specs=specs or [VMEM] * len(arg...]
    dot_general x12 -> x0, matrix products: 17.6 us -> none  [the longest x10 17 us: dot(): lax.dot_general(a, b, (((a_dim,), (b_dim,)), ((), ())), preferred_element...]
    ppermute x28 -> x31, waiting for transfers between devices: 77.5 us -> 60 us  [the longest x9 49.9 us: over_experts(): lax.ppermute(value, 'expert', [(i, (i + 2 * step) % halves) for i in rang...]
    unnamed x27 -> x48, local copies, waits for them, and re-layouts: 6.01 us -> 13.6 us
    ppermute x28 -> x31, starting transfers between devices: 31.2 us -> 28.6 us  [the longest x9 12.6 us: over_experts(): lax.ppermute(value, 'expert', [(i, (i + 2 * step) % halves) for i in rang...]
  transfers between devices with their start and end apart: 28 -> 31, of which waited for: 14 -> 13; matrix products, arithmetic and copies ran while one was open for 11% -> 5% of each run, Pallas kernels for 1% -> 13%
where the time goes in v6:
time: 133 us
  waiting for transfers between devices  60 us (45%)
  starting transfers between devices  28.6 us (22%)
  Pallas kernels  23.3 us (18%)
  local copies, waits for them, and re-layouts  16.5 us (12%)
  other arithmetic  3.12 us (2%)
    ppermute x9, waiting for transfers between devices, over_experts(): lax.ppermute(value, 'expert', [(i, (i + 2 * step) % halves) for i in rang...  49.9 us
    pallas_call x21, Pallas kernels, call(): pl.pallas_call(kernel, out_shape=outs, in_specs=specs or [VMEM] * len(arg...  23.3 us
    unnamed x48, local copies, waits for them, and re-layouts  13.6 us
    ppermute x9, starting transfers between devices, over_experts(): lax.ppermute(value, 'expert', [(i, (i + 2 * step) % halves) for i in rang...  12.6 us
    ppermute x5, starting transfers between devices, over_half(): return lax.ppermute(value, 'expert', [(i, i ^ 1) for i in range(halves)])  5.95 us
    ppermute x5, waiting for transfers between devices, over_half(): return lax.ppermute(value, 'expert', [(i, i ^ 1) for i in range(halves)])  4.31 us
    ppermute x4, starting transfers between devices, over_columns(): lax.ppermute(value, 'dp', [(i, (i + 2 * step) % groups) for i in range(gr...  4.06 us
    ppermute x2, waiting for transfers between devices, back_over_columns(): lax.ppermute(value, 'dp', [(i, (i - 2 * step) % groups) for i in range(gr...  3.85 us
  transfers between devices with their start and end apart: 31, of which 13 were waited for; matrix products, arithmetic and copies ran while one was open for 5% of the time, Pallas kernels for 13%

profile of v6, /device:TPU:0, one launch (start us, length us, event | category | flops | bytes accessed | tf_op | source)
XLA Modules:
  0.0 132.6 jit_solution(2529785338019988943)
XLA Ops:
  5.7 2.6 %collective-permute-start.2 = (bf16[320,1280]{1,0:T(8,128)(2,1)}, bf16[320,1280]{1,0:T(8,128)(2,1)}, u32[]{:S(2)}, u32[]{:S(2)}) collective-permute-start(bf16[320,1280]{1,0:T(8,128)(2,1)} %bitcast.64), channel_id=1, source_target_pairs={{0,4},{4,0},{8,12},{12,8},{16,20},{20,16},{24,28},{28,24},{1,5},{5... | collective-permute-start | bytes 2457608 | tf_op jit(solution)/shard_map/ppermute | solution.py:221
  8.3 1.5 %collective-permute-start.3 = (bf16[2,80,1280]{2,1,0:T(8,128)(2,1)S(1)}, bf16[2,80,1280]{2,1,0:T(8,128)(2,1)S(1)}, u32[]{:S(2)}, u32[]{:S(2)}) collective-permute-start(bf16[2,80,1280]{2,1,0:T(8,128)(2,1)S(1)} %get-tuple-element.94), channel_id=1, source_target_pairs={{0,2},{1,3},{2,0},{3,1},{4,6},{5,7},{6,4},{7,5},{8,10},{9,11},{10,... | collective-permute-start | bytes 1228808 | tf_op jit(solution)/shard_map/ppermute | solution.py:228
  9.8 1.6 %collective-permute-start = (bf16[2,80,1280]{2,1,0:T(8,128)(2,1)S(1)}, bf16[2,80,1280]{2,1,0:T(8,128)(2,1)}, u32[]{:S(2)}, u32[]{:S(2)}) collective-permute-start(bf16[2,80,1280]{2,1,0:T(8,128)(2,1)S(1)} %get-tuple-element.80), channel_id=1, source_target_pairs={{0,8},{4,12},{8,16},{12,20},{16,24},{20,28},{24,0},{28,4},{1,9},{5... | collective-permute-start | bytes 1228808 | tf_op jit(solution)/shard_map/ppermute | solution.py:239
  11.4 2.3 %collective-permute-start.1 = (bf16[2,80,1280]{2,1,0:T(8,128)(2,1)S(1)}, bf16[2,80,1280]{2,1,0:T(8,128)(2,1)}, u32[]{:S(2)}, u32[]{:S(2)}) collective-permute-start(bf16[2,80,1280]{2,1,0:T(8,128)(2,1)S(1)} %get-tuple-element.81), channel_id=1, source_target_pairs={{0,24},{4,28},{8,0},{12,4},{16,8},{20,12},{24,16},{28,20},{1,25},{... | collective-permute-start | bytes 1228808 | tf_op jit(solution)/shard_map/ppermute | solution.py:239
  17.1 6.9 %collective-permute-done = bf16[2,80,1280]{2,1,0:T(8,128)(2,1)} collective-permute-done((bf16[2,80,1280]{2,1,0:T(8,128)(2,1)S(1)}, bf16[2,80,1280]{2,1,0:T(8,128)(2,1)}, u32[]{:S(2)}, u32[]{:S(2)}) %collective-permute-start) | collective-permute-done | bytes 409632 | tf_op jit(solution)/shard_map/ppermute | solution.py:239
  24.1 7.1 %collective-permute-done.1 = bf16[2,80,1280]{2,1,0:T(8,128)(2,1)} collective-permute-done((bf16[2,80,1280]{2,1,0:T(8,128)(2,1)S(1)}, bf16[2,80,1280]{2,1,0:T(8,128)(2,1)}, u32[]{:S(2)}, u32[]{:S(2)}) %collective-permute-start.1) | collective-permute-done | bytes 409632 | tf_op jit(solution)/shard_map/ppermute | solution.py:239
  34.0 1.5 %collective-permute-start.8 = (bf16[2,80,1280]{2,1,0:T(8,128)(2,1)}, bf16[2,80,1280]{2,1,0:T(8,128)(2,1)S(1)}, u32[]{:S(2)}, u32[]{:S(2)}) collective-permute-start(bf16[2,80,1280]{2,1,0:T(8,128)(2,1)} %collective-permute-done.1), channel_id=1, source_target_pairs={{0,2},{1,3},{2,0},{3,1},{4,6},{5,7},{6,4},{7,5},{8,10},{9,11},{10,... | collective-permute-start | bytes 1228808 | tf_op jit(solution)/shard_map/ppermute | solution.py:228
  38.5 14.1 %collective-permute-done.5 = bf16[2,80,1280]{2,1,0:T(8,128)(2,1)S(1)} collective-permute-done((bf16[2,80,1280]{2,1,0:T(8,128)(2,1)S(1)}, bf16[2,80,1280]{2,1,0:T(8,128)(2,1)S(1)}, u32[]{:S(2)}, u32[]{:S(2)}) %collective-permute-start.5) | collective-permute-done | bytes 409632 | tf_op jit(solution)/shard_map/ppermute | solution.py:239
  56.5 3.3 %first.2 = (bf16[480,1280]{1,0:T(8,128)(2,1)S(1)}, f32[480,1280]{1,0:T(8,128)S(1)}, bf16[480,1280]{1,0:T(8,128)(2,1)S(1)}, f32[480,128]{1,0:T(8,128)S(1)}) custom-call(bf16[480,1280]{1,0:T(8,128)(2,1)S(1)} %get-tuple-element.166.m_ref, bf16[480,1280]{1,0:T(8,128)(2,1)S(1)} %get-tuple-element.165.d_ref, bf16[1280,1280]{1,0:T(8,128)(2,1)S(1)} %join.3.first_ref, ...), custom_call_target="tpu_custom_call" | custom-call | flops 1572864000 | bytes 3072000 | tf_op jit(solution)/shard_map/first/pallas_call | solution.py:197
  65.0 2.1 %second.2 = (bf16[480,1280]{1,0:T(8,128)(2,1)S(1)}, f32[480,128]{1,0:T(8,128)S(1)}) custom-call(bf16[480,1280]{1,0:T(8,128)(2,1)S(1)} %get-tuple-element.165.d_ref, bf16[1280,1280]{1,0:T(8,128)(2,1)S(1)} %join.2.second_ref, bf16[480,1280]{1,0:T(8,128)(2,1)S(1)} %get-tuple-element.101.hidden_ref, f32[480,1280]{1,0:T(8,128)S(1)} %copy-done.1, ...), custom_call_target="tpu_custom_call" | custom-call | flops 1572864000 | bytes 3072000 | tf_op jit(solution)/shard_map/second/pallas_call | solution.py:197
  67.0 1.9 %rows.2 = (f32[240,1280]{1,0:T(8,128)S(1)}, bf16[240,1280]{1,0:T(8,128)(2,1)S(1)}, f32[8,1280]{1,0:T(8,128)S(1)}) custom-call(bf16[480,1280]{1,0:T(8,128)(2,1)S(1)} %get-tuple-element.166.m_ref, bf16[480,1280]{1,0:T(8,128)(2,1)S(1)} %get-tuple-element.104.pre_ref, f32[480,128]{1,0:T(8,128)S(1)} %get-tuple-element.105.logit_ref, ...), custom_call_target="tpu_custom_call" | custom-call | flops 1572864000 | bytes 3072000 | tf_op jit(solution)/shard_map/rows/pallas_call | solution.py:197
  70.2 1.5 %first.3 = (bf16[160,1280]{1,0:T(8,128)(2,1)S(1)}, f32[160,1280]{1,0:T(8,128)S(1)}, bf16[160,1280]{1,0:T(8,128)(2,1)S(1)}, f32[160,128]{1,0:T(8,128)S(1)}) custom-call(bf16[160,1280]{1,0:T(8,128)(2,1)S(1)} %pad_maximum_fusion.3.m_ref, bf16[160,1280]{1,0:T(8,128)(2,1)S(1)} %pad_maximum_fusion.4.d_ref, bf16[1280,1280]{1,0:T(8,128)(2,1)S(1)} %join.3.first_ref, ...), custom_call_target="tpu_custom_call" | custom-call | flops 524288000 | bytes 1024000 | tf_op jit(solution)/shard_map/first/pallas_call | solution.py:197
  79.4 1.8 %collective-permute-done.14 = f32[8,1280]{1,0:T(8,128)S(1)} collective-permute-done((f32[8,1280]{1,0:T(8,128)S(1)}, f32[8,1280]{1,0:T(8,128)S(1)}, u32[]{:S(2)}, u32[]{:S(2)}) %collective-permute-start.14) | collective-permute-done | bytes 40992 | tf_op jit(solution)/shard_map/ppermute | solution.py:221
  81.5 3.9 %collective-permute-done.15 = bf16[80,1280]{1,0:T(8,128)(2,1)S(1)} collective-permute-done((bf16[80,1280]{1,0:T(8,128)(2,1)S(1)}, bf16[80,1280]{1,0:T(8,128)(2,1)S(1)}, u32[]{:S(2)}, u32[]{:S(2)}) %collective-permute-start.15) | collective-permute-done | bytes 204832 | tf_op jit(solution)/shard_map/ppermute | solution.py:234
  87.6 1.5 %collective-permute-start.17 = (bf16[240,1280]{1,0:T(8,128)(2,1)S(1)}, bf16[240,1280]{1,0:T(8,128)(2,1)S(1)}, u32[]{:S(2)}, u32[]{:S(2)}) collective-permute-start(bf16[240,1280]{1,0:T(8,128)(2,1)S(1)} %pad_maximum_fusion.2), channel_id=1, source_target_pairs={{0,2},{1,3},{2,0},{3,1},{4,6},{5,7},{6,4},{7,5},{8,10},{9,11},{10,... | collective-permute-start | bytes 1843208 | tf_op jit(solution)/shard_map/ppermute | solution.py:234
  89.2 3.3 %collective-permute-start.22 = (bf16[80,1280]{1,0:T(8,128)(2,1)S(1)}, bf16[80,1280]{1,0:T(8,128)(2,1)S(1)}, u32[]{:S(2)}, u32[]{:S(2)}) collective-permute-start(bf16[80,1280]{1,0:T(8,128)(2,1)S(1)} %get-tuple-element.153), channel_id=1, source_target_pairs={{0,24},{4,28},{8,0},{12,4},{16,8},{20,12},{24,16},{28,20},{1,25},{... | collective-permute-start | bytes 614408 | tf_op jit(solution)/shard_map/ppermute | solution.py:239
  95.5 2.4 %collective-permute-done.21 = f32[8,1280]{1,0:T(8,128)S(1)} collective-permute-done((f32[8,1280]{1,0:T(8,128)S(1)}, f32[8,1280]{1,0:T(8,128)S(1)}, u32[]{:S(2)}, u32[]{:S(2)}) %collective-permute-start.21) | collective-permute-done | bytes 40992 | tf_op jit(solution)/shard_map/ppermute | solution.py:239
  100.0 2.8 %collective-permute-done.20 = f32[8,1280]{1,0:T(8,128)S(1)} collective-permute-done((f32[8,1280]{1,0:T(8,128)S(1)}, f32[8,1280]{1,0:T(8,128)S(1)}, u32[]{:S(2)}, u32[]{:S(2)}) %collective-permute-start.20) | collective-permute-done | bytes 40992 | tf_op jit(solution)/shard_map/ppermute | solution.py:239
  102.8 1.8 %collective-permute-start.19 = (f32[8,1280]{1,0:T(8,128)S(1)}, f32[8,1280]{1,0:T(8,128)S(1)}, u32[]{:S(2)}, u32[]{:S(2)}) collective-permute-start(f32[8,1280]{1,0:T(8,128)S(1)} %fusion.2), channel_id=1, source_target_pairs={{0,8},{4,12},{8,16},{12,20},{16,24},{20,28},{24,0},{28,4},{1,9},{5... | collective-permute-start | bytes 122888 | tf_op jit(solution)/shard_map/ppermute | solution.py:239
  105.5 3.5 %collective-permute-done.19 = f32[8,1280]{1,0:T(8,128)S(1)} collective-permute-done((f32[8,1280]{1,0:T(8,128)S(1)}, f32[8,1280]{1,0:T(8,128)S(1)}, u32[]{:S(2)}, u32[]{:S(2)}) %collective-permute-start.19) | collective-permute-done | bytes 40992 | tf_op jit(solution)/shard_map/ppermute | solution.py:239
  110.6 1.9 %collective-permute-done.26 = bf16[320,1280]{1,0:T(8,128)(2,1)S(1)} collective-permute-done((bf16[320,1280]{1,0:T(8,128)(2,1)S(1)}, bf16[320,1280]{1,0:T(8,128)(2,1)S(1)}, u32[]{:S(2)}, u32[]{:S(2)}) %collective-permute-start.26) | collective-permute-done | bytes 819232 | tf_op jit(solution)/shard_map/ppermute | solution.py:224
  114.3 6.0 %collective-permute-done.24 = bf16[80,1280]{1,0:T(8,128)(2,1)S(1)} collective-permute-done((bf16[80,1280]{1,0:T(8,128)(2,1)S(1)}, bf16[80,1280]{1,0:T(8,128)(2,1)S(1)}, u32[]{:S(2)}, u32[]{:S(2)}) %collective-permute-start.24) | collective-permute-done | bytes 204832 | tf_op jit(solution)/shard_map/ppermute | solution.py:239
  121.7 7.0 %collective-permute-done.23 = bf16[80,1280]{1,0:T(8,128)(2,1)S(1)} collective-permute-done((bf16[80,1280]{1,0:T(8,128)(2,1)S(1)}, bf16[80,1280]{1,0:T(8,128)(2,1)S(1)}, u32[]{:S(2)}, u32[]{:S(2)}) %collective-permute-start.23) | collective-permute-done | bytes 204832 | tf_op jit(solution)/shard_map/ppermute | solution.py:239
  130.0 2.0 %finish.1 = (bf16[128,1280]{1,0:T(8,128)(2,1)}, bf16[320,1280]{1,0:T(8,128)(2,1)}, f32[4,1280]{1,0:T(4,128)}, f32[1,1280]{1,0:T(1,128)S(1)}) custom-call(f32[128,1280]{1,0:T(8,128)S(1)} %copy-done.9, f32[128,128]{1,0:T(8,128)S(1)} %get-tuple-element.92.deviation_ref, bf16[320,128]{1,0:T(8,128)(2,1)S(1)} %get-tuple-element.93.places_ref, ...), custom_call_target="tpu_custom_call" | custom-call | tf_op jit(solution)/shard_map/finish/pallas_call | solution.py:197
  (131 shorter events, 47.3 us)
Async XLA Ops:
  5.2 26.1 %collective-permute-start.4 = (bf16[320,1280]{1,0:T(8,128)(2,1)}, bf16[320,1280]{1,0:T(8,128)(2,1)S(1)}, u32[]{:S(2)}, u32[]{:S(2)}) collective-permute-start(bf16[320,1280]{1,0:T(8,128)(2,1)} %bitcast.63), channel_id=1, source_target_pairs={{0,1},{1,0},{2,3},{3,2},{4,5},{5,4},{6,7},{7,6},{8,9},{9,8},{10,11... | collective-permute-start | bytes 2457608 | tf_op jit(solution)/shard_map/ppermute | solution.py:224
  5.7 26.5 %collective-permute-start.2 = (bf16[320,1280]{1,0:T(8,128)(2,1)}, bf16[320,1280]{1,0:T(8,128)(2,1)}, u32[]{:S(2)}, u32[]{:S(2)}) collective-permute-start(bf16[320,1280]{1,0:T(8,128)(2,1)} %bitcast.64), channel_id=1, source_target_pairs={{0,4},{4,0},{8,12},{12,8},{16,20},{20,16},{24,28},{28,24},{1,5},{5... | collective-permute-start | bytes 2457608 | tf_op jit(solution)/shard_map/ppermute | solution.py:221
  8.3 22.9 %collective-permute-start.3 = (bf16[2,80,1280]{2,1,0:T(8,128)(2,1)S(1)}, bf16[2,80,1280]{2,1,0:T(8,128)(2,1)S(1)}, u32[]{:S(2)}, u32[]{:S(2)}) collective-permute-start(bf16[2,80,1280]{2,1,0:T(8,128)(2,1)S(1)} %get-tuple-element.94), channel_id=1, source_target_pairs={{0,2},{1,3},{2,0},{3,1},{4,6},{5,7},{6,4},{7,5},{8,10},{9,11},{10,... | collective-permute-start | bytes 1228808 | tf_op jit(solution)/shard_map/ppermute | solution.py:228
  9.8 14.3 %collective-permute-start = (bf16[2,80,1280]{2,1,0:T(8,128)(2,1)S(1)}, bf16[2,80,1280]{2,1,0:T(8,128)(2,1)}, u32[]{:S(2)}, u32[]{:S(2)}) collective-permute-start(bf16[2,80,1280]{2,1,0:T(8,128)(2,1)S(1)} %get-tuple-element.80), channel_id=1, source_target_pairs={{0,8},{4,12},{8,16},{12,20},{16,24},{20,28},{24,0},{28,4},{1,9},{5... | collective-permute-start | bytes 1228808 | tf_op jit(solution)/shard_map/ppermute | solution.py:239
  11.4 19.9 %collective-permute-start.1 = (bf16[2,80,1280]{2,1,0:T(8,128)(2,1)S(1)}, bf16[2,80,1280]{2,1,0:T(8,128)(2,1)}, u32[]{:S(2)}, u32[]{:S(2)}) collective-permute-start(bf16[2,80,1280]{2,1,0:T(8,128)(2,1)S(1)} %get-tuple-element.81), channel_id=1, source_target_pairs={{0,24},{4,28},{8,0},{12,4},{16,8},{20,12},{24,16},{28,20},{1,25},{... | collective-permute-start | bytes 1228808 | tf_op jit(solution)/shard_map/ppermute | solution.py:239
  32.2 20.5 %collective-permute-start.5 = (bf16[2,80,1280]{2,1,0:T(8,128)(2,1)S(1)}, bf16[2,80,1280]{2,1,0:T(8,128)(2,1)S(1)}, u32[]{:S(2)}, u32[]{:S(2)}) collective-permute-start(bf16[2,80,1280]{2,1,0:T(8,128)(2,1)S(1)} %get-tuple-element.83), channel_id=1, source_target_pairs={{0,16},{4,20},{8,24},{12,28},{16,0},{20,4},{24,8},{28,12},{1,17},{... | collective-permute-start | bytes 1228808 | tf_op jit(solution)/shard_map/ppermute | solution.py:239
  33.5 19.2 %collective-permute-start.7 = (bf16[2,80,1280]{2,1,0:T(8,128)(2,1)}, bf16[2,80,1280]{2,1,0:T(8,128)(2,1)S(1)}, u32[]{:S(2)}, u32[]{:S(2)}) collective-permute-start(bf16[2,80,1280]{2,1,0:T(8,128)(2,1)} %collective-permute-done), channel_id=1, source_target_pairs={{0,2},{1,3},{2,0},{3,1},{4,6},{5,7},{6,4},{7,5},{8,10},{9,11},{10,... | collective-permute-start | bytes 1228808 | tf_op jit(solution)/shard_map/ppermute | solution.py:228
  34.0 18.6 %collective-permute-start.8 = (bf16[2,80,1280]{2,1,0:T(8,128)(2,1)}, bf16[2,80,1280]{2,1,0:T(8,128)(2,1)S(1)}, u32[]{:S(2)}, u32[]{:S(2)}) collective-permute-start(bf16[2,80,1280]{2,1,0:T(8,128)(2,1)} %collective-permute-done.1), channel_id=1, source_target_pairs={{0,2},{1,3},{2,0},{3,1},{4,6},{5,7},{6,4},{7,5},{8,10},{9,11},{10,... | collective-permute-start | bytes 1228808 | tf_op jit(solution)/shard_map/ppermute | solution.py:228
  35.5 18.5 %collective-permute-start.6 = (bf16[320,1280]{1,0:T(8,128)(2,1)}, bf16[320,1280]{1,0:T(8,128)(2,1)S(1)}, u32[]{:S(2)}, u32[]{:S(2)}) collective-permute-start(bf16[320,1280]{1,0:T(8,128)(2,1)} %bitcast.66), channel_id=1, source_target_pairs={{0,4},{4,0},{8,12},{12,8},{16,20},{20,16},{24,28},{28,24},{1,5},{5... | collective-permute-start | bytes 2457608 | tf_op jit(solution)/shard_map/ppermute | solution.py:221
  36.0 18.0 %collective-permute-start.9 = (bf16[320,1280]{1,0:T(8,128)(2,1)}, bf16[320,1280]{1,0:T(8,128)(2,1)S(1)}, u32[]{:S(2)}, u32[]{:S(2)}) collective-permute-start(bf16[320,1280]{1,0:T(8,128)(2,1)} %collective-permute-done.2.refs_2_), channel_id=1, source_target_pairs={{0,1},{1,0},{2,3},{3,2},{4,5},{5,4},{6,7},{7,6},{8,9},{9,8},{10,11... | collective-permute-start | bytes 2457608 | tf_op jit(solution)/shard_map/ppermute | solution.py:224
  54.0 15.0 %collective-permute-start.12 = (bf16[2,80,1280]{2,1,0:T(8,128)(2,1)S(1)}, bf16[2,80,1280]{2,1,0:T(8,128)(2,1)}, u32[]{:S(2)}, u32[]{:S(2)}) collective-permute-start(bf16[2,80,1280]{2,1,0:T(8,128)(2,1)S(1)} %collective-permute-done.5), channel_id=1, source_target_pairs={{0,2},{1,3},{2,0},{3,1},{4,6},{5,7},{6,4},{7,5},{8,10},{9,11},{10,... | collective-permute-start | bytes 1228808 | tf_op jit(solution)/shard_map/ppermute | solution.py:228
  54.5 6.7 %collective-permute-start.10 = (bf16[320,1280]{1,0:T(8,128)(2,1)S(1)}, bf16[320,1280]{1,0:T(8,128)(2,1)S(1)}, u32[]{:S(2)}, u32[]{:S(2)}) collective-permute-start(bf16[320,1280]{1,0:T(8,128)(2,1)S(1)} %collective-permute-done.6.refs_2_), channel_id=1, source_target_pairs={{0,1},{1,0},{2,3},{3,2},{4,5},{5,4},{6,7},{7,6},{8,9},{9,8},{10,11... | collective-permute-start | bytes 2457608 | tf_op jit(solution)/shard_map/ppermute | solution.py:224
  72.7 8.6 %collective-permute-start.13 = (bf16[320,1280]{1,0:T(8,128)(2,1)S(1)}, bf16[320,1280]{1,0:T(8,128)(2,1)S(1)}, u32[]{:S(2)}, u32[]{:S(2)}) collective-permute-start(bf16[320,1280]{1,0:T(8,128)(2,1)S(1)} %weights.8), channel_id=1, source_target_pairs={{0,1},{1,0},{2,3},{3,2},{4,5},{5,4},{6,7},{7,6},{8,9},{9,8},{10,11... | collective-permute-start | bytes 2457608 | tf_op jit(solution)/shard_map/ppermute | solution.py:224
  78.1 7.2 %collective-permute-start.15 = (bf16[80,1280]{1,0:T(8,128)(2,1)S(1)}, bf16[80,1280]{1,0:T(8,128)(2,1)S(1)}, u32[]{:S(2)}, u32[]{:S(2)}) collective-permute-start(bf16[80,1280]{1,0:T(8,128)(2,1)S(1)} %get-tuple-element.163), channel_id=1, source_target_pairs={{0,2},{1,3},{2,0},{3,1},{4,6},{5,7},{6,4},{7,5},{8,10},{9,11},{10,... | collective-permute-start | bytes 614408 | tf_op jit(solution)/shard_map/ppermute | solution.py:234
  86.2 23.2 %collective-permute-start.18 = (bf16[320,1280]{1,0:T(8,128)(2,1)S(1)}, bf16[320,1280]{1,0:T(8,128)(2,1)S(1)}, u32[]{:S(2)}, u32[]{:S(2)}) collective-permute-start(bf16[320,1280]{1,0:T(8,128)(2,1)S(1)} %weights.10), channel_id=1, source_target_pairs={{0,1},{1,0},{2,3},{3,2},{4,5},{5,4},{6,7},{7,6},{8,9},{9,8},{10,11... | collective-permute-start | bytes 2457608 | tf_op jit(solution)/shard_map/ppermute | solution.py:224
  86.3 23.2 %collective-permute-start.16 = (bf16[320,1280]{1,0:T(8,128)(2,1)S(1)}, bf16[320,1280]{1,0:T(8,128)(2,1)S(1)}, u32[]{:S(2)}, u32[]{:S(2)}) collective-permute-start(bf16[320,1280]{1,0:T(8,128)(2,1)S(1)} %half.2), channel_id=1, source_target_pairs={{0,4},{4,0},{8,12},{12,8},{16,20},{20,16},{24,28},{28,24},{1,5},{5... | collective-permute-start | bytes 2457608 | tf_op jit(solution)/shard_map/ppermute | solution.py:221
  87.6 21.9 %collective-permute-start.17 = (bf16[240,1280]{1,0:T(8,128)(2,1)S(1)}, bf16[240,1280]{1,0:T(8,128)(2,1)S(1)}, u32[]{:S(2)}, u32[]{:S(2)}) collective-permute-start(bf16[240,1280]{1,0:T(8,128)(2,1)S(1)} %pad_maximum_fusion.2), channel_id=1, source_target_pairs={{0,2},{1,3},{2,0},{3,1},{4,6},{5,7},{6,4},{7,5},{8,10},{9,11},{10,... | collective-permute-start | bytes 1843208 | tf_op jit(solution)/shard_map/ppermute | solution.py:234
  89.2 19.7 %collective-permute-start.22 = (bf16[80,1280]{1,0:T(8,128)(2,1)S(1)}, bf16[80,1280]{1,0:T(8,128)(2,1)S(1)}, u32[]{:S(2)}, u32[]{:S(2)}) collective-permute-start(bf16[80,1280]{1,0:T(8,128)(2,1)S(1)} %get-tuple-element.153), channel_id=1, source_target_pairs={{0,24},{4,28},{8,0},{12,4},{16,8},{20,12},{24,16},{28,20},{1,25},{... | collective-permute-start | bytes 614408 | tf_op jit(solution)/shard_map/ppermute | solution.py:239
  109.0 21.0 %collective-permute-start.27 = (bf16[320,1280]{1,0:T(8,128)(2,1)S(1)}, bf16[320,1280]{1,0:T(8,128)(2,1)S(1)}, u32[]{:S(2)}, u32[]{:S(2)}) collective-permute-start(bf16[320,1280]{1,0:T(8,128)(2,1)S(1)} %weights.15), channel_id=1, source_target_pairs={{0,1},{1,0},{2,3},{3,2},{4,5},{5,4},{6,7},{7,6},{8,9},{9,8},{10,11... | collective-permute-start | bytes 2457608 | tf_op jit(solution)/shard_map/ppermute | solution.py:224
  109.6 20.2 %collective-permute-start.25 = (bf16[320,1280]{1,0:T(8,128)(2,1)S(1)}, bf16[320,1280]{1,0:T(8,128)(2,1)S(1)}, u32[]{:S(2)}, u32[]{:S(2)}) collective-permute-start(bf16[320,1280]{1,0:T(8,128)(2,1)S(1)} %half.3), channel_id=1, source_target_pairs={{0,4},{4,0},{8,12},{12,8},{16,20},{20,16},{24,28},{28,24},{1,5},{5... | collective-permute-start | bytes 2457608 | tf_op jit(solution)/shard_map/ppermute | solution.py:221
  110.4 19.5 %collective-permute-start.30 = (f32[8,1280]{1,0:T(8,128)S(1)}, f32[8,1280]{1,0:T(8,128)S(1)}, u32[]{:S(2)}, u32[]{:S(2)}) collective-permute-start(f32[8,1280]{1,0:T(8,128)S(1)} %add_add_fusion.refs_0_), channel_id=1, source_target_pairs={{0,3},{1,2},{2,1},{3,0},{4,7},{5,6},{6,5},{7,4},{8,11},{9,10},{10,... | collective-permute-start | bytes 122888 | tf_op jit(solution)/shard_map/ppermute | solution.py:243
  110.5 9.8 %collective-permute-start.24 = (bf16[80,1280]{1,0:T(8,128)(2,1)S(1)}, bf16[80,1280]{1,0:T(8,128)(2,1)S(1)}, u32[]{:S(2)}, u32[]{:S(2)}) collective-permute-start(bf16[80,1280]{1,0:T(8,128)(2,1)S(1)} %get-tuple-element.156), channel_id=1, source_target_pairs={{0,8},{4,12},{8,16},{12,20},{16,24},{20,28},{24,0},{28,4},{1,9},{5... | collective-permute-start | bytes 614408 | tf_op jit(solution)/shard_map/ppermute | solution.py:239
  112.5 16.2 %collective-permute-start.23 = (bf16[80,1280]{1,0:T(8,128)(2,1)S(1)}, bf16[80,1280]{1,0:T(8,128)(2,1)S(1)}, u32[]{:S(2)}, u32[]{:S(2)}) collective-permute-start(bf16[80,1280]{1,0:T(8,128)(2,1)S(1)} %get-tuple-element.157), channel_id=1, source_target_pairs={{0,16},{4,20},{8,24},{12,28},{16,0},{20,4},{24,8},{28,12},{1,17},{... | collective-permute-start | bytes 614408 | tf_op jit(solution)/shard_map/ppermute | solution.py:239
  120.3 9.7 %collective-permute-start.29 = (f32[8,1280]{1,0:T(8,128)S(1)}, f32[8,1280]{1,0:T(8,128)S(1)}, u32[]{:S(2)}, u32[]{:S(2)}) collective-permute-start(f32[8,1280]{1,0:T(8,128)S(1)} %add_add_fusion.refs_0_), channel_id=1, source_target_pairs={{0,2},{1,3},{2,0},{3,1},{4,6},{5,7},{6,4},{7,5},{8,10},{9,11},{10,... | collective-permute-start | bytes 122888 | tf_op jit(solution)/shard_map/ppermute | solution.py:243
  (27 other events, 153.5 us)

commit v7 on v6

--- a/solution.py
+++ b/solution.py
@@ -13,7 +13,6 @@
 VMEM = pl.BlockSpec(memory_space=pltpu.VMEM)
 SMEM = pl.BlockSpec(memory_space=pltpu.SMEM)
 ANY = pl.BlockSpec(memory_space=pl.ANY)
-PARAMS = pltpu.CompilerParams(vmem_limit_bytes=40 * 2**20)
 
 
 def gelu_parts(pre):
@@ -81,7 +80,7 @@
     slots = slot_of(own_ref[0], routes_ref[...], experts, capacity)
     x_copy.wait()
     normalized_rows, _ = norm_pieces(x_ref[...])
-    mixed_rows = (normalized_rows * gain_ref[...]).astype(BF16)
+    mixed_rows = (normalized_rows * gain_ref[...][None, :]).astype(BF16)
     d_copy.wait()
     cotangent = d_ref[...]
     for step in range(experts):
@@ -99,26 +98,24 @@
 
 
 def finish_kernel(
-    norm_ref, deviation_ref, places_ref, gain_ref, d_ref, rows_ref, stay_ref, pair_ref, other_ref, *refs
+    norm_ref, deviation_ref, places_ref, gain_ref, d_ref, rows_ref, stay_ref, pair_ref, other_ref,
+    total_ref, last_ref, out_ref, sum_ref, router_ref, gain_grad_ref
 ):
-    out_ref, sum_ref, router_ref, gain_grad_ref = refs[-4:]
     sum_ref[...] = (
         stay_ref[...] + pair_ref[...].astype(F32) + other_ref[...].astype(F32)
     ).astype(BF16)
     normalized_rows = norm_ref[...]
-    scaled_rows = dot(places_ref[...], rows_ref[...], 0, 0) * gain_ref[...]
+    scaled_rows = dot(places_ref[...], rows_ref[...], 0, 0) * gain_ref[...][None, :]
     mean_first_term = jnp.mean(scaled_rows, axis=1, keepdims=True)
     mean_second_term = jnp.mean(scaled_rows * normalized_rows, axis=1, keepdims=True)
     norm_backward = deviation_ref[:, :1] * (
         scaled_rows - mean_first_term - normalized_rows * mean_second_term
     )
     out_ref[...] = (d_ref[...].astype(F32) + norm_backward).astype(BF16)
-    parts = [ref[...] for ref in refs[:-4]]
-    while len(parts) > 1:
-        parts = [parts[i] + parts[i + 1] for i in range(0, len(parts), 2)]
     experts = router_ref.shape[0]
-    router_ref[...] = parts[0][:experts]
-    gain_grad_ref[...] = jnp.sum(parts[0][experts:], axis=0, keepdims=True) / gain_ref[...]
+    total = total_ref[...] + last_ref[...]
+    router_ref[...] = total[:experts]
+    gain_grad_ref[...] = jnp.sum(total[experts:], axis=0) / gain_ref[...]
 
 
 def first_kernel(m_ref, d_ref, first_ref, router_ref, hidden_ref, slope_ref, y_ref, gate_ref):
@@ -193,14 +190,14 @@
     return jax.ShapeDtypeStruct(sizes, kind)
 
 
-def call(kernel, name, outs, args, flops=0, specs=None, scratch=()):
+def call(kernel, name, outs, args, flops=0, specs=None, scratch=(), mebibytes=18):
     return pl.pallas_call(
         kernel,
         out_shape=outs,
         in_specs=specs or [VMEM] * len(args),
         out_specs=jax.tree.map(lambda _: VMEM, outs),
         scratch_shapes=list(scratch),
-        compiler_params=PARAMS,
+        compiler_params=pltpu.CompilerParams(vmem_limit_bytes=mebibytes * 2**20),
         cost_estimate=pl.CostEstimate(flops=flops, bytes_accessed=flops // 512, transcendentals=0),
         name=name,
     )(*args)
@@ -238,10 +235,8 @@
     def over_experts(value, step):
         return lax.ppermute(value, "expert", [(i, (i + 2 * step) % halves) for i in range(halves)])
 
-    def over_groups(value):
-        return [value] + [
-            lax.ppermute(value, "dp", [(i, i ^ bit) for i in range(groups)]) for bit in range(1, groups)
-        ]
+    def pairwise(value, name, size, bit):
+        return value + lax.ppermute(value, name, [(i, i ^ bit) for i in range(size)])
 
     first = w_in[0].T
     second = w_out[0]
@@ -249,13 +244,12 @@
     hidden_units = 4 * units
 
     own_scalar = own.astype(jnp.int32).reshape(1)
-    gain_row = gain[None, :]
     routes_t = routes.T
     send = call(
         functools.partial(dispatch_kernel, experts, capacity),
         "dispatch",
         [shape(BF16, 2, capacity, width)] * experts,
-        (own_scalar, prenorm_input, gain_row, routes_t, cotangent),
+        (own_scalar, prenorm_input, gain, routes_t, cotangent),
         flops=4 * slots * tokens * width,
         specs=[SMEM, ANY, VMEM, VMEM, ANY],
         scratch=[
@@ -263,6 +257,7 @@
             pltpu.VMEM((tokens, width), BF16),
             pltpu.SemaphoreType.DMA((2,)),
         ],
+        mebibytes=60,
     )
 
     steps = sorted(range(experts), key=lambda step: min(step, experts - step))
@@ -401,14 +396,6 @@
         near[step], side[step] = tied((near[step], side[step]), (early_own, early_side))
     late_m, late_d = gather_rows(late)
 
-    block = quarter * capacity
-
-    def by_turn(rows):
-        return rows.reshape(columns - 1, -1, width)
-
-    early_side = by_turn(early_side)
-
-    moved = back_over_columns(list(early_side[:, block : 2 * block]))
     late_hidden, late_slope, late_y, late_gate = first_product(late_m, late_d)
     hidden = jnp.concatenate([early_hidden, late_hidden], axis=0)
     grad_y = jnp.concatenate([early_y, late_y], axis=0)
@@ -419,16 +406,18 @@
     late_pre, late_logit = second_product(tied(late_d, out_stay), late_hidden, late_slope, late_gate)
     late_own, late_side, late_sums = row_gradients(late_m, late_pre, late_logit)
     sums = early_sums + late_sums
-    line = jnp.arange(2 * experts, dtype=jnp.int32)[:, None]
-    total = jnp.where(line == own, sums[:1], jnp.where(line == experts + own, sums[1:2], 0.0))
-    total = total + over_half(total)
+    line = jnp.arange(-(-(experts + 1) // 8) * 8, dtype=jnp.int32)[:, None]
+    total = jnp.where(line == own, sums[:1], jnp.where(line == experts, sums[1:2], 0.0))
+    total = pairwise(total, "expert", halves, 1)
     out_half = half_sum(out_stay, out_pair)
 
-    stage = (out_half, total, late_own, late_side, moved)
-    out_half, total, late_side, moved, hidden = tied((out_half, total, late_side, moved, hidden), stage)
+    def by_turn(rows):
+        return rows.reshape(columns - 1, -1, width)
+
+    leaving = jnp.concatenate([by_turn(early_side), by_turn(late_side)], axis=1)
+    stage = (out_half, total, late_own, leaving)
+    out_half, total, leaving, hidden = tied((out_half, total, leaving, hidden), stage)
     out_other = over_half(out_half)
-    late_side = by_turn(late_side)
-    leaving = jnp.concatenate([early_side[:, :block], early_side[:, 2 * block :], late_side], axis=1)
     rows_back = back_over_columns(list(leaving))
 
     def add_rows(own_rows, pieces):
@@ -442,32 +431,33 @@
         for step, value in zip(chosen, rows):
             returned[step] = over_experts(value, experts - step) if step else value
 
-    moved_steps = steps[quarter : 2 * quarter]
-    other_steps = steps[:quarter] + steps[2 * quarter :]
-    send_back(moved_steps, add_rows(early_own[block : 2 * block], moved))
     rows_m = jnp.concatenate([early_m, late_m], axis=0)
     grad_pre = jnp.concatenate([early_pre, late_pre], axis=0)
-    total = tied(total, (out_half, leaving))
-    totals = [total] + [over_experts(total, step) for step in range(1, experts)]
     grad_pre = tied(grad_pre, (out_half, leaving))
     in_leave = weight_gradient(0, 1, grad_pre, rows_m, BF16)
     in_pair = over_pair(in_leave)
     in_stay = weight_gradient(2, 1, tied(grad_pre, in_leave), rows_m, F32)
+    total = tied(total, in_stay)
+    bit = 2
+    while bit < halves:
+        total = pairwise(total, "expert", halves, bit)
+        bit *= 2
+    total = pairwise(total, "dp", groups, 1)
     hidden, grad_pre = tied((hidden, grad_pre), in_stay)
     out_rest = over_pair(weight_gradient(1, 1, hidden, grad_y, BF16))
     out_mine = weight_gradient(3, 1, hidden, grad_y, F32)
     in_rest = over_pair(weight_gradient(1, 1, grad_pre, rows_m, BF16))
     in_mine = weight_gradient(3, 1, grad_pre, rows_m, F32)
 
-    moved_back = [returned[step] for step in moved_steps]
-    stage = (out_other, rows_back, in_pair, in_stay, totals, moved_back)
-    out_other, rows_back, in_pair, in_stay, totals, moved_back = tied(stage, stage)
-    for step, value in zip(moved_steps, moved_back):
-        returned[step] = value
+    stage = (out_other, rows_back, in_pair, in_stay, total)
+    out_other, rows_back, in_pair, in_stay, total = tied(stage, stage)
     in_other = over_half(half_sum(in_stay, in_pair))
-    own_rows = jnp.concatenate([early_own[:block], early_own[2 * block :], late_own], axis=0)
-    send_back(other_steps, add_rows(own_rows, rows_back))
-    totals = over_groups(sum(totals[1:], totals[0]))
+    send_back(steps, add_rows(jnp.concatenate([early_own, late_own], axis=0), rows_back))
+    bit = 2
+    while bit < groups // 2:
+        total = pairwise(total, "dp", groups, bit)
+        bit *= 2
+    last = lax.ppermute(total, "dp", [(i, i ^ bit) for i in range(groups)])
     grad_out = (out_mine + out_rest.astype(F32) + out_other.astype(F32)).astype(BF16)[None]
 
     returned = tied(returned, (in_other, grad_out))
@@ -479,22 +469,23 @@
             shape(BF16, tokens, width),
             shape(BF16, units, width),
             shape(F32, experts, width),
-            shape(F32, 1, width),
+            shape(F32, width),
         ],
         (
             norm,
             deviation,
             places,
-            gain_row,
+            gain,
             cotangent,
             jnp.concatenate(returned, axis=0),
             in_mine,
             in_rest,
             in_other,
-            *totals,
+            total,
+            last,
         ),
     )
-    return (input_grad, grad_in.T[None], grad_out, grad_router.T, grad_gain[0])
+    return (input_grad, grad_in.T[None], grad_out, grad_router.T, grad_gain)
 
 
 def solution(mesh):

time: 133 us -> 123 us (0.925)
  local copies, waits for them, and re-layouts: 16.5 us -> 6.5 us
  starting transfers between devices: 28.6 us -> 25.7 us
  waiting for transfers between devices: 60 us -> 62.9 us
    ppermute x9 -> x6, waiting for transfers between devices: 49.9 us -> 41.5 us  [over_experts(): lax.ppermute(value, 'expert', [(i, (i + 2 * step) % halves) for i in rang...]
    unnamed x48 -> x20, local copies, waits for them, and re-layouts: 13.6 us -> 6.28 us
    ppermute x4, waiting for transfers between devices: 0.01 us -> 6.92 us  [over_columns(): lax.ppermute(value, 'dp', [(i, (i + 2 * step) % groups) for i in range(gr...]
    ppermute x3 -> x5, waiting for transfers between devices: 0.01 us -> 6.76 us  [the longest x4 6.75 us: pairwise(): lax.ppermute(value, name, [(i, i ^ bit) for i in range(size)])]
    ppermute x3 -> x5, starting transfers between devices: 1.5 us -> 5.28 us  [the longest x4 4.75 us: pairwise(): lax.ppermute(value, name, [(i, i ^ bit) for i in range(size)])]
    ppermute x9 -> x6, starting transfers between devices: 12.6 us -> 8.81 us  [over_experts(): lax.ppermute(value, 'expert', [(i, (i + 2 * step) % halves) for i in rang...]
    ppermute x2 -> x1, starting transfers between devices: 2.8 us -> 0.59 us  [back_over_columns(): lax.ppermute(value, 'dp', [(i, (i - 2 * step) % groups) for i in range(gr...]
    ppermute x8, waiting for transfers between devices: 1.88 us -> 0.02 us  [over_pair(): return lax.ppermute(value, 'dp', [(i, i ^ 1) for i in range(groups)])]
  transfers between devices with their start and end apart: 31 -> 28, of which waited for: 13 -> 14; matrix products, arithmetic and copies ran while one was open for 5% -> 5% of each run, Pallas kernels for 13% -> 13%
where the time goes in v7:
time: 123 us
  waiting for transfers between devices  62.9 us (51%)
  starting transfers between devices  25.7 us (21%)
  Pallas kernels  24.4 us (20%)
  local copies, waits for them, and re-layouts  6.5 us (5%)
  other arithmetic  2.55 us (2%)
    ppermute x6, waiting for transfers between devices, over_experts(): lax.ppermute(value, 'expert', [(i, (i + 2 * step) % halves) for i in rang...  41.5 us
    pallas_call x21, Pallas kernels, call(): pl.pallas_call(kernel, out_shape=outs, in_specs=specs or [VMEM] * len(arg...  24.4 us
    ppermute x6, starting transfers between devices, over_experts(): lax.ppermute(value, 'expert', [(i, (i + 2 * step) % halves) for i in rang...  8.81 us
    ppermute x4, waiting for transfers between devices, over_columns(): lax.ppermute(value, 'dp', [(i, (i + 2 * step) % groups) for i in range(gr...  6.92 us
    ppermute x4, waiting for transfers between devices, pairwise(): lax.ppermute(value, name, [(i, i ^ bit) for i in range(size)])  6.75 us
    unnamed x20, local copies, waits for them, and re-layouts  6.28 us
    ppermute x4, starting transfers between devices, over_half(): return lax.ppermute(value, 'expert', [(i, i ^ 1) for i in range(halves)])  5.32 us
    ppermute x4, starting transfers between devices, pairwise(): lax.ppermute(value, name, [(i, i ^ bit) for i in range(size)])  4.75 us
  transfers between devices with their start and end apart: 28, of which 14 were waited for; matrix products, arithmetic and copies ran while one was open for 5% of the time, Pallas kernels for 13%

profile of v7, /device:TPU:0, one launch (start us, length us, event | category | flops | bytes accessed | tf_op | source)
XLA Modules:
  0.0 123.2 jit_solution(4356695969107849908)
XLA Ops:
  0.7 3.5 %dispatch.1 = (bf16[2,80,1280]{2,1,0:T(8,128)(2,1)}, bf16[2,80,1280]{2,1,0:T(8,128)(2,1)}, bf16[2,80,1280]{2,1,0:T(8,128)(2,1)}, bf16[2,80,1280]{2,1,0:T(8,128)(2,1)}) custom-call(s32[1]{0:T(128)} %bitcast.1.own_ref, bf16[128,1280]{1,0:T(8,128)(2,1)} %x_ref.1, f32[1280]{0:T(1024)} %gain_ref.3, s32[2,128]{1,0:T(2,128)} %bitcast.68, bf16[128,1280]{1,0:T(8,128)(2,1)} %d_ref.1), custom_call_target="tpu_custom_call" | custom-call | flops 209715200 | bytes 409600 | tf_op jit(solution)/shard_map/dispatch/pallas_call | solution.py:194
  4.6 2.6 %collective-permute-start.2 = (bf16[320,1280]{1,0:T(8,128)(2,1)}, bf16[320,1280]{1,0:T(8,128)(2,1)S(1)}, u32[]{:S(2)}, u32[]{:S(2)}) collective-permute-start(bf16[320,1280]{1,0:T(8,128)(2,1)} %bitcast.61), channel_id=1, source_target_pairs={{0,4},{4,0},{8,12},{12,8},{16,20},{20,16},{24,28},{28,24},{1,5},{5... | collective-permute-start | bytes 2457608 | tf_op jit(solution)/shard_map/ppermute | solution.py:218
  8.7 1.6 %collective-permute-start = (bf16[2,80,1280]{2,1,0:T(8,128)(2,1)}, bf16[2,80,1280]{2,1,0:T(8,128)(2,1)}, u32[]{:S(2)}, u32[]{:S(2)}) collective-permute-start(bf16[2,80,1280]{2,1,0:T(8,128)(2,1)} %get-tuple-element.75), channel_id=1, source_target_pairs={{0,8},{4,12},{8,16},{12,20},{16,24},{20,28},{24,0},{28,4},{1,9},{5... | collective-permute-start | bytes 1228808 | tf_op jit(solution)/shard_map/ppermute | solution.py:236
  10.3 2.2 %collective-permute-start.1 = (bf16[2,80,1280]{2,1,0:T(8,128)(2,1)}, bf16[2,80,1280]{2,1,0:T(8,128)(2,1)}, u32[]{:S(2)}, u32[]{:S(2)}) collective-permute-start(bf16[2,80,1280]{2,1,0:T(8,128)(2,1)} %get-tuple-element.76), channel_id=1, source_target_pairs={{0,24},{4,28},{8,0},{12,4},{16,8},{20,12},{24,16},{28,20},{1,25},{... | collective-permute-start | bytes 1228808 | tf_op jit(solution)/shard_map/ppermute | solution.py:236
  15.2 3.9 %collective-permute-done.3 = bf16[2,80,1280]{2,1,0:T(8,128)(2,1)} collective-permute-done((bf16[2,80,1280]{2,1,0:T(8,128)(2,1)}, bf16[2,80,1280]{2,1,0:T(8,128)(2,1)}, u32[]{:S(2)}, u32[]{:S(2)}) %collective-permute-start.3) | collective-permute-done | bytes 409632 | tf_op jit(solution)/shard_map/ppermute | solution.py:225
  19.1 4.1 %collective-permute-done = bf16[2,80,1280]{2,1,0:T(8,128)(2,1)} collective-permute-done((bf16[2,80,1280]{2,1,0:T(8,128)(2,1)}, bf16[2,80,1280]{2,1,0:T(8,128)(2,1)}, u32[]{:S(2)}, u32[]{:S(2)}) %collective-permute-start) | collective-permute-done | bytes 409632 | tf_op jit(solution)/shard_map/ppermute | solution.py:236
  23.2 7.2 %collective-permute-done.1 = bf16[2,80,1280]{2,1,0:T(8,128)(2,1)} collective-permute-done((bf16[2,80,1280]{2,1,0:T(8,128)(2,1)}, bf16[2,80,1280]{2,1,0:T(8,128)(2,1)}, u32[]{:S(2)}, u32[]{:S(2)}) %collective-permute-start.1) | collective-permute-done | bytes 409632 | tf_op jit(solution)/shard_map/ppermute | solution.py:236
  38.7 15.1 %collective-permute-done.5 = bf16[2,80,1280]{2,1,0:T(8,128)(2,1)S(1)} collective-permute-done((bf16[2,80,1280]{2,1,0:T(8,128)(2,1)}, bf16[2,80,1280]{2,1,0:T(8,128)(2,1)S(1)}, u32[]{:S(2)}, u32[]{:S(2)}) %collective-permute-start.5) | collective-permute-done | bytes 409632 | tf_op jit(solution)/shard_map/ppermute | solution.py:236
  55.3 3.3 %first.2 = (bf16[480,1280]{1,0:T(8,128)(2,1)S(1)}, f32[480,1280]{1,0:T(8,128)S(1)}, bf16[480,1280]{1,0:T(8,128)(2,1)S(1)}, f32[480,128]{1,0:T(8,128)S(1)}) custom-call(bf16[480,1280]{1,0:T(8,128)(2,1)S(1)} %get-tuple-element.149.m_ref, bf16[480,1280]{1,0:T(8,128)(2,1)S(1)} %get-tuple-element.148.d_ref, bf16[1280,1280]{1,0:T(8,128)(2,1)S(1)} %join.3.first_ref, ...), custom_call_target="tpu_custom_call" | custom-call | flops 1572864000 | bytes 3072000 | tf_op jit(solution)/shard_map/first/pallas_call | solution.py:194
  59.0 2.0 %second.2 = (bf16[480,1280]{1,0:T(8,128)(2,1)S(1)}, f32[480,128]{1,0:T(8,128)S(1)}) custom-call(bf16[480,1280]{1,0:T(8,128)(2,1)S(1)} %get-tuple-element.148.d_ref, bf16[1280,1280]{1,0:T(8,128)(2,1)S(1)} %join.2.second_ref, bf16[480,1280]{1,0:T(8,128)(2,1)S(1)} %get-tuple-element.96.hidden_ref, f32[480,1280]{1,0:T(8,128)S(1)} %get-tuple-element.97.slope_ref, ...), custom_call_target="tpu_custom_call" | custom-call | flops 1572864000 | bytes 3072000 | tf_op jit(solution)/shard_map/second/pallas_call | solution.py:194
  61.0 1.9 %rows.2 = (f32[240,1280]{1,0:T(8,128)S(1)}, bf16[240,1280]{1,0:T(8,128)(2,1)S(1)}, f32[8,1280]{1,0:T(8,128)S(1)}) custom-call(bf16[480,1280]{1,0:T(8,128)(2,1)S(1)} %get-tuple-element.149.m_ref, bf16[480,1280]{1,0:T(8,128)(2,1)S(1)} %get-tuple-element.99.pre_ref, f32[480,128]{1,0:T(8,128)S(1)} %get-tuple-element.100.logit_ref, ...), custom_call_target="tpu_custom_call" | custom-call | flops 1572864000 | bytes 3072000 | tf_op jit(solution)/shard_map/rows/pallas_call | solution.py:194
  63.0 2.9 %collective-permute-done.12 = bf16[2,80,1280]{2,1,0:T(8,128)(2,1)S(1)} collective-permute-done((bf16[2,80,1280]{2,1,0:T(8,128)(2,1)S(1)}, bf16[2,80,1280]{2,1,0:T(8,128)(2,1)S(1)}, u32[]{:S(2)}, u32[]{:S(2)}) %collective-permute-start.12) | collective-permute-done | bytes 409632 | tf_op jit(solution)/shard_map/ppermute | solution.py:225
  72.0 1.6 %collective-permute-start.14 = (f32[8,1280]{1,0:T(8,128)S(1)}, f32[8,1280]{1,0:T(8,128)S(1)}, u32[]{:S(2)}, u32[]{:S(2)}) collective-permute-start(f32[8,1280]{1,0:T(8,128)S(1)} %select_select_fusion), channel_id=1, source_target_pairs={{0,4},{4,0},{8,12},{12,8},{16,20},{20,16},{24,28},{28,24},{1,5},{5... | collective-permute-start | bytes 122888 | tf_op jit(solution)/shard_map/ppermute | solution.py:239
  73.6 2.4 %collective-permute-done.14 = f32[8,1280]{1,0:T(8,128)S(1)} collective-permute-done((f32[8,1280]{1,0:T(8,128)S(1)}, f32[8,1280]{1,0:T(8,128)S(1)}, u32[]{:S(2)}, u32[]{:S(2)}) %collective-permute-start.14) | collective-permute-done | bytes 40992 | tf_op jit(solution)/shard_map/ppermute | solution.py:239
  76.3 1.6 %collective-permute-start.15 = (bf16[320,1280]{1,0:T(8,128)(2,1)S(1)}, bf16[320,1280]{1,0:T(8,128)(2,1)S(1)}, u32[]{:S(2)}, u32[]{:S(2)}) collective-permute-start(bf16[320,1280]{1,0:T(8,128)(2,1)S(1)} %half.2), channel_id=1, source_target_pairs={{0,4},{4,0},{8,12},{12,8},{16,20},{20,16},{24,28},{28,24},{1,5},{5... | collective-permute-start | bytes 2457608 | tf_op jit(solution)/shard_map/ppermute | solution.py:218
  83.8 1.6 %collective-permute-done.18 = f32[8,1280]{1,0:T(8,128)S(1)} collective-permute-done((f32[8,1280]{1,0:T(8,128)S(1)}, f32[8,1280]{1,0:T(8,128)S(1)}, u32[]{:S(2)}, u32[]{:S(2)}) %collective-permute-start.18) | collective-permute-done | bytes 40992 | tf_op jit(solution)/shard_map/ppermute | solution.py:239
  85.4 1.6 %collective-permute-start.19 = (f32[8,1280]{1,0:T(8,128)S(1)}, f32[8,1280]{1,0:T(8,128)S(1)}, u32[]{:S(2)}, u32[]{:S(2)}) collective-permute-start(f32[8,1280]{1,0:T(8,128)S(1)} %add.31), channel_id=1, source_target_pairs={{0,16},{4,20},{8,24},{12,28},{16,0},{20,4},{24,8},{28,12},{1,17},{... | collective-permute-start | bytes 122888 | tf_op jit(solution)/shard_map/ppermute | solution.py:239
  87.9 2.4 %collective-permute-done.19 = f32[8,1280]{1,0:T(8,128)S(1)} collective-permute-done((f32[8,1280]{1,0:T(8,128)S(1)}, f32[8,1280]{1,0:T(8,128)S(1)}, u32[]{:S(2)}, u32[]{:S(2)}) %collective-permute-start.19) | collective-permute-done | bytes 40992 | tf_op jit(solution)/shard_map/ppermute | solution.py:239
  91.8 4.0 %collective-permute-done.15 = bf16[320,1280]{1,0:T(8,128)(2,1)S(1)} collective-permute-done((bf16[320,1280]{1,0:T(8,128)(2,1)S(1)}, bf16[320,1280]{1,0:T(8,128)(2,1)S(1)}, u32[]{:S(2)}, u32[]{:S(2)}) %collective-permute-start.15) | collective-permute-done | bytes 819232 | tf_op jit(solution)/shard_map/ppermute | solution.py:218
  95.9 3.7 %collective-permute-done.16 = bf16[320,1280]{1,0:T(8,128)(2,1)S(1)} collective-permute-done((bf16[320,1280]{1,0:T(8,128)(2,1)S(1)}, bf16[320,1280]{1,0:T(8,128)(2,1)S(1)}, u32[]{:S(2)}, u32[]{:S(2)}) %collective-permute-start.16) | collective-permute-done | bytes 819232 | tf_op jit(solution)/shard_map/ppermute | solution.py:231
  100.5 2.2 %collective-permute-start.21 = (bf16[80,1280]{1,0:T(8,128)(2,1)S(1)}, bf16[80,1280]{1,0:T(8,128)(2,1)S(1)}, u32[]{:S(2)}, u32[]{:S(2)}) collective-permute-start(bf16[80,1280]{1,0:T(8,128)(2,1)S(1)} %get-tuple-element.145), channel_id=1, source_target_pairs={{0,24},{4,28},{8,0},{12,4},{16,8},{20,12},{24,16},{28,20},{1,25},{... | collective-permute-start | bytes 614408 | tf_op jit(solution)/shard_map/ppermute | solution.py:236
  105.4 2.9 %collective-permute-done.21 = bf16[80,1280]{1,0:T(8,128)(2,1)S(1)} collective-permute-done((bf16[80,1280]{1,0:T(8,128)(2,1)S(1)}, bf16[80,1280]{1,0:T(8,128)(2,1)S(1)}, u32[]{:S(2)}, u32[]{:S(2)}) %collective-permute-start.21) | collective-permute-done | bytes 204832 | tf_op jit(solution)/shard_map/ppermute | solution.py:236
  108.9 12.2 %collective-permute-done.22 = bf16[80,1280]{1,0:T(8,128)(2,1)S(1)} collective-permute-done((bf16[80,1280]{1,0:T(8,128)(2,1)S(1)}, bf16[80,1280]{1,0:T(8,128)(2,1)S(1)}, u32[]{:S(2)}, u32[]{:S(2)}) %collective-permute-start.22) | collective-permute-done | bytes 204832 | tf_op jit(solution)/shard_map/ppermute | solution.py:236
  121.2 2.0 %finish.1 = (bf16[128,1280]{1,0:T(8,128)(2,1)}, bf16[320,1280]{1,0:T(8,128)(2,1)}, f32[4,1280]{1,0:T(4,128)}, f32[1280]{0:T(1024)}) custom-call(f32[128,1280]{1,0:T(8,128)S(1)} %get-tuple-element.86.norm_ref, f32[128,128]{1,0:T(8,128)S(1)} %get-tuple-element.87.deviation_ref, bf16[320,128]{1,0:T(8,128)(2,1)S(1)} %get-tuple-element.88.places_ref, ...), custom_call_target="tpu_custom_call" | custom-call | tf_op jit(solution)/shard_map/finish/pallas_call | solution.py:194
  (94 shorter events, 33.5 us)
Async XLA Ops:
  4.1 26.3 %collective-permute-start.4 = (bf16[320,1280]{1,0:T(8,128)(2,1)}, bf16[320,1280]{1,0:T(8,128)(2,1)S(1)}, u32[]{:S(2)}, u32[]{:S(2)}) collective-permute-start(bf16[320,1280]{1,0:T(8,128)(2,1)} %bitcast.60), channel_id=1, source_target_pairs={{0,1},{1,0},{2,3},{3,2},{4,5},{5,4},{6,7},{7,6},{8,9},{9,8},{10,11... | collective-permute-start | bytes 2457608 | tf_op jit(solution)/shard_map/ppermute | solution.py:221
  4.6 25.7 %collective-permute-start.2 = (bf16[320,1280]{1,0:T(8,128)(2,1)}, bf16[320,1280]{1,0:T(8,128)(2,1)S(1)}, u32[]{:S(2)}, u32[]{:S(2)}) collective-permute-start(bf16[320,1280]{1,0:T(8,128)(2,1)} %bitcast.61), channel_id=1, source_target_pairs={{0,4},{4,0},{8,12},{12,8},{16,20},{20,16},{24,28},{28,24},{1,5},{5... | collective-permute-start | bytes 2457608 | tf_op jit(solution)/shard_map/ppermute | solution.py:218
  7.2 11.9 %collective-permute-start.3 = (bf16[2,80,1280]{2,1,0:T(8,128)(2,1)}, bf16[2,80,1280]{2,1,0:T(8,128)(2,1)}, u32[]{:S(2)}, u32[]{:S(2)}) collective-permute-start(bf16[2,80,1280]{2,1,0:T(8,128)(2,1)} %get-tuple-element.89), channel_id=1, source_target_pairs={{0,2},{1,3},{2,0},{3,1},{4,6},{5,7},{6,4},{7,5},{8,10},{9,11},{10,... | collective-permute-start | bytes 1228808 | tf_op jit(solution)/shard_map/ppermute | solution.py:225
  8.7 14.5 %collective-permute-start = (bf16[2,80,1280]{2,1,0:T(8,128)(2,1)}, bf16[2,80,1280]{2,1,0:T(8,128)(2,1)}, u32[]{:S(2)}, u32[]{:S(2)}) collective-permute-start(bf16[2,80,1280]{2,1,0:T(8,128)(2,1)} %get-tuple-element.75), channel_id=1, source_target_pairs={{0,8},{4,12},{8,16},{12,20},{16,24},{20,28},{24,0},{28,4},{1,9},{5... | collective-permute-start | bytes 1228808 | tf_op jit(solution)/shard_map/ppermute | solution.py:236
  10.3 20.1 %collective-permute-start.1 = (bf16[2,80,1280]{2,1,0:T(8,128)(2,1)}, bf16[2,80,1280]{2,1,0:T(8,128)(2,1)}, u32[]{:S(2)}, u32[]{:S(2)}) collective-permute-start(bf16[2,80,1280]{2,1,0:T(8,128)(2,1)} %get-tuple-element.76), channel_id=1, source_target_pairs={{0,24},{4,28},{8,0},{12,4},{16,8},{20,12},{24,16},{28,20},{1,25},{... | collective-permute-start | bytes 1228808 | tf_op jit(solution)/shard_map/ppermute | solution.py:236
  31.5 22.5 %collective-permute-start.6 = (bf16[320,1280]{1,0:T(8,128)(2,1)S(1)}, bf16[320,1280]{1,0:T(8,128)(2,1)S(1)}, u32[]{:S(2)}, u32[]{:S(2)}) collective-permute-start(bf16[320,1280]{1,0:T(8,128)(2,1)S(1)} %bitcast.63), channel_id=1, source_target_pairs={{0,4},{4,0},{8,12},{12,8},{16,20},{20,16},{24,28},{28,24},{1,5},{5... | collective-permute-start | bytes 2457608 | tf_op jit(solution)/shard_map/ppermute | solution.py:218
  32.0 21.9 %collective-permute-start.9 = (bf16[320,1280]{1,0:T(8,128)(2,1)S(1)}, bf16[320,1280]{1,0:T(8,128)(2,1)S(1)}, u32[]{:S(2)}, u32[]{:S(2)}) collective-permute-start(bf16[320,1280]{1,0:T(8,128)(2,1)S(1)} %collective-permute-done.2.refs_2_), channel_id=1, source_target_pairs={{0,1},{1,0},{2,3},{3,2},{4,5},{5,4},{6,7},{7,6},{8,9},{9,8},{10,11... | collective-permute-start | bytes 2457608 | tf_op jit(solution)/shard_map/ppermute | solution.py:221
  32.0 21.8 %collective-permute-start.5 = (bf16[2,80,1280]{2,1,0:T(8,128)(2,1)}, bf16[2,80,1280]{2,1,0:T(8,128)(2,1)S(1)}, u32[]{:S(2)}, u32[]{:S(2)}) collective-permute-start(bf16[2,80,1280]{2,1,0:T(8,128)(2,1)} %get-tuple-element.78), channel_id=1, source_target_pairs={{0,16},{4,20},{8,24},{12,28},{16,0},{20,4},{24,8},{28,12},{1,17},{... | collective-permute-start | bytes 1228808 | tf_op jit(solution)/shard_map/ppermute | solution.py:236
  33.3 20.5 %collective-permute-start.7 = (bf16[2,80,1280]{2,1,0:T(8,128)(2,1)}, bf16[2,80,1280]{2,1,0:T(8,128)(2,1)S(1)}, u32[]{:S(2)}, u32[]{:S(2)}) collective-permute-start(bf16[2,80,1280]{2,1,0:T(8,128)(2,1)} %collective-permute-done), channel_id=1, source_target_pairs={{0,2},{1,3},{2,0},{3,1},{4,6},{5,7},{6,4},{7,5},{8,10},{9,11},{10,... | collective-permute-start | bytes 1228808 | tf_op jit(solution)/shard_map/ppermute | solution.py:225
  33.9 20.1 %collective-permute-start.8 = (bf16[2,80,1280]{2,1,0:T(8,128)(2,1)}, bf16[2,80,1280]{2,1,0:T(8,128)(2,1)S(1)}, u32[]{:S(2)}, u32[]{:S(2)}) collective-permute-start(bf16[2,80,1280]{2,1,0:T(8,128)(2,1)} %collective-permute-done.1), channel_id=1, source_target_pairs={{0,2},{1,3},{2,0},{3,1},{4,6},{5,7},{6,4},{7,5},{8,10},{9,11},{10,... | collective-permute-start | bytes 1228808 | tf_op jit(solution)/shard_map/ppermute | solution.py:225
  53.9 4.8 %collective-permute-start.10 = (bf16[320,1280]{1,0:T(8,128)(2,1)S(1)}, bf16[320,1280]{1,0:T(8,128)(2,1)S(1)}, u32[]{:S(2)}, u32[]{:S(2)}) collective-permute-start(bf16[320,1280]{1,0:T(8,128)(2,1)S(1)} %collective-permute-done.6.refs_2_), channel_id=1, source_target_pairs={{0,1},{1,0},{2,3},{3,2},{4,5},{5,4},{6,7},{7,6},{8,9},{9,8},{10,11... | collective-permute-start | bytes 2457608 | tf_op jit(solution)/shard_map/ppermute | solution.py:221
  54.4 11.4 %collective-permute-start.12 = (bf16[2,80,1280]{2,1,0:T(8,128)(2,1)S(1)}, bf16[2,80,1280]{2,1,0:T(8,128)(2,1)S(1)}, u32[]{:S(2)}, u32[]{:S(2)}) collective-permute-start(bf16[2,80,1280]{2,1,0:T(8,128)(2,1)S(1)} %collective-permute-done.5), channel_id=1, source_target_pairs={{0,2},{1,3},{2,0},{3,1},{4,6},{5,7},{6,4},{7,5},{8,10},{9,11},{10,... | collective-permute-start | bytes 1228808 | tf_op jit(solution)/shard_map/ppermute | solution.py:225
  68.5 7.6 %collective-permute-start.13 = (bf16[320,1280]{1,0:T(8,128)(2,1)S(1)}, bf16[320,1280]{1,0:T(8,128)(2,1)S(1)}, u32[]{:S(2)}, u32[]{:S(2)}) collective-permute-start(bf16[320,1280]{1,0:T(8,128)(2,1)S(1)} %weights.8), channel_id=1, source_target_pairs={{0,1},{1,0},{2,3},{3,2},{4,5},{5,4},{6,7},{7,6},{8,9},{9,8},{10,11... | collective-permute-start | bytes 2457608 | tf_op jit(solution)/shard_map/ppermute | solution.py:221
  76.3 19.6 %collective-permute-start.15 = (bf16[320,1280]{1,0:T(8,128)(2,1)S(1)}, bf16[320,1280]{1,0:T(8,128)(2,1)S(1)}, u32[]{:S(2)}, u32[]{:S(2)}) collective-permute-start(bf16[320,1280]{1,0:T(8,128)(2,1)S(1)} %half.2), channel_id=1, source_target_pairs={{0,4},{4,0},{8,12},{12,8},{16,20},{20,16},{24,28},{28,24},{1,5},{5... | collective-permute-start | bytes 2457608 | tf_op jit(solution)/shard_map/ppermute | solution.py:218
  78.8 13.0 %collective-permute-start.17 = (bf16[320,1280]{1,0:T(8,128)(2,1)S(1)}, bf16[320,1280]{1,0:T(8,128)(2,1)S(1)}, u32[]{:S(2)}, u32[]{:S(2)}) collective-permute-start(bf16[320,1280]{1,0:T(8,128)(2,1)S(1)} %weights.10), channel_id=1, source_target_pairs={{0,1},{1,0},{2,3},{3,2},{4,5},{5,4},{6,7},{7,6},{8,9},{9,8},{10,11... | collective-permute-start | bytes 2457608 | tf_op jit(solution)/shard_map/ppermute | solution.py:221
  78.9 20.7 %collective-permute-start.16 = (bf16[320,1280]{1,0:T(8,128)(2,1)S(1)}, bf16[320,1280]{1,0:T(8,128)(2,1)S(1)}, u32[]{:S(2)}, u32[]{:S(2)}) collective-permute-start(bf16[320,1280]{1,0:T(8,128)(2,1)S(1)} %bitcast.70), channel_id=1, source_target_pairs={{0,2},{1,3},{2,0},{3,1},{4,6},{5,7},{6,4},{7,5},{8,10},{9,11},{10,... | collective-permute-start | bytes 2457608 | tf_op jit(solution)/shard_map/ppermute | solution.py:231
  81.2 39.9 %collective-permute-start.26 = (bf16[320,1280]{1,0:T(8,128)(2,1)S(1)}, bf16[320,1280]{1,0:T(8,128)(2,1)S(1)}, u32[]{:S(2)}, u32[]{:S(2)}) collective-permute-start(bf16[320,1280]{1,0:T(8,128)(2,1)S(1)} %weights.15), channel_id=1, source_target_pairs={{0,1},{1,0},{2,3},{3,2},{4,5},{5,4},{6,7},{7,6},{8,9},{9,8},{10,11... | collective-permute-start | bytes 2457608 | tf_op jit(solution)/shard_map/ppermute | solution.py:221
  85.4 4.9 %collective-permute-start.19 = (f32[8,1280]{1,0:T(8,128)S(1)}, f32[8,1280]{1,0:T(8,128)S(1)}, u32[]{:S(2)}, u32[]{:S(2)}) collective-permute-start(f32[8,1280]{1,0:T(8,128)S(1)} %add.31), channel_id=1, source_target_pairs={{0,16},{4,20},{8,24},{12,28},{16,0},{20,4},{24,8},{28,12},{1,17},{... | collective-permute-start | bytes 122888 | tf_op jit(solution)/shard_map/ppermute | solution.py:239
  91.6 12.0 %collective-permute-start.25 = (bf16[320,1280]{1,0:T(8,128)(2,1)S(1)}, bf16[320,1280]{1,0:T(8,128)(2,1)S(1)}, u32[]{:S(2)}, u32[]{:S(2)}) collective-permute-start(bf16[320,1280]{1,0:T(8,128)(2,1)S(1)} %weights.13), channel_id=1, source_target_pairs={{0,1},{1,0},{2,3},{3,2},{4,5},{5,4},{6,7},{7,6},{8,9},{9,8},{10,11... | collective-permute-start | bytes 2457608 | tf_op jit(solution)/shard_map/ppermute | solution.py:221
  99.7 21.4 %collective-permute-start.24 = (bf16[320,1280]{1,0:T(8,128)(2,1)S(1)}, bf16[320,1280]{1,0:T(8,128)(2,1)S(1)}, u32[]{:S(2)}, u32[]{:S(2)}) collective-permute-start(bf16[320,1280]{1,0:T(8,128)(2,1)S(1)} %half.3), channel_id=1, source_target_pairs={{0,4},{4,0},{8,12},{12,8},{16,20},{20,16},{24,28},{28,24},{1,5},{5... | collective-permute-start | bytes 2457608 | tf_op jit(solution)/shard_map/ppermute | solution.py:218
  100.5 7.8 %collective-permute-start.21 = (bf16[80,1280]{1,0:T(8,128)(2,1)S(1)}, bf16[80,1280]{1,0:T(8,128)(2,1)S(1)}, u32[]{:S(2)}, u32[]{:S(2)}) collective-permute-start(bf16[80,1280]{1,0:T(8,128)(2,1)S(1)} %get-tuple-element.145), channel_id=1, source_target_pairs={{0,24},{4,28},{8,0},{12,4},{16,8},{20,12},{24,16},{28,20},{1,25},{... | collective-permute-start | bytes 614408 | tf_op jit(solution)/shard_map/ppermute | solution.py:236
  102.7 18.3 %collective-permute-start.22 = (bf16[80,1280]{1,0:T(8,128)(2,1)S(1)}, bf16[80,1280]{1,0:T(8,128)(2,1)S(1)}, u32[]{:S(2)}, u32[]{:S(2)}) collective-permute-start(bf16[80,1280]{1,0:T(8,128)(2,1)S(1)} %get-tuple-element.144), channel_id=1, source_target_pairs={{0,16},{4,20},{8,24},{12,28},{16,0},{20,4},{24,8},{28,12},{1,17},{... | collective-permute-start | bytes 614408 | tf_op jit(solution)/shard_map/ppermute | solution.py:236
  103.6 17.5 %collective-permute-start.23 = (bf16[80,1280]{1,0:T(8,128)(2,1)S(1)}, bf16[80,1280]{1,0:T(8,128)(2,1)S(1)}, u32[]{:S(2)}, u32[]{:S(2)}) collective-permute-start(bf16[80,1280]{1,0:T(8,128)(2,1)S(1)} %get-tuple-element.143), channel_id=1, source_target_pairs={{0,8},{4,12},{8,16},{12,20},{16,24},{20,28},{24,0},{28,4},{1,9},{5... | collective-permute-start | bytes 614408 | tf_op jit(solution)/shard_map/ppermute | solution.py:236
  108.3 12.8 %collective-permute-start.27 = (f32[8,1280]{1,0:T(8,128)S(1)}, f32[8,1280]{1,0:T(8,128)S(1)}, u32[]{:S(2)}, u32[]{:S(2)}) collective-permute-start(f32[8,1280]{1,0:T(8,128)S(1)} %add.33.total_ref), channel_id=1, source_target_pairs={{0,2},{1,3},{2,0},{3,1},{4,6},{5,7},{6,4},{7,5},{8,10},{9,11},{10,... | collective-permute-start | bytes 122888 | tf_op jit(solution)/shard_map/ppermute | solution.py:460
  (10 other events, 96.7 us)

commit v8 on v7

--- a/solution.py
+++ b/solution.py
@@ -11,7 +11,6 @@
 F32 = jnp.float32
 BF16 = jnp.bfloat16
 VMEM = pl.BlockSpec(memory_space=pltpu.VMEM)
-SMEM = pl.BlockSpec(memory_space=pltpu.SMEM)
 ANY = pl.BlockSpec(memory_space=pl.ANY)
 
 
@@ -70,18 +69,24 @@
     return jnp.where(hit, 1.0, 0.0).astype(BF16)
 
 
-def dispatch_kernel(experts, capacity, own_ref, x_hbm, gain_ref, routes_ref, d_hbm, *refs):
-    send_refs, (x_ref, d_ref, sems) = refs[:experts], refs[experts:]
-    x_copy = pltpu.make_async_copy(x_hbm, x_ref, sems.at[0])
-    d_copy = pltpu.make_async_copy(d_hbm, d_ref, sems.at[1])
-    x_copy.start()
-    d_copy.start()
+def dispatch_kernel(experts, capacity, x_hbm, gain_hbm, routes_hbm, d_hbm, *refs):
+    send_refs, (x_ref, gain_ref, routes_ref, d_ref, sems) = refs[:experts], refs[experts:]
+    copies = [
+        pltpu.make_async_copy(source, target, sems.at[at])
+        for at, (source, target) in enumerate(
+            ((routes_hbm, routes_ref), (x_hbm, x_ref), (gain_hbm, gain_ref), (d_hbm, d_ref))
+        )
+    ]
+    for copy in copies:
+        copy.start()
     tokens = x_ref.shape[0]
-    slots = slot_of(own_ref[0], routes_ref[...], experts, capacity)
-    x_copy.wait()
+    copies[0].wait()
+    slots = slot_of(lax.axis_index("expert") // 2, routes_ref[...], experts, capacity)
+    copies[1].wait()
     normalized_rows, _ = norm_pieces(x_ref[...])
+    copies[2].wait()
     mixed_rows = (normalized_rows * gain_ref[...][None, :]).astype(BF16)
-    d_copy.wait()
+    copies[3].wait()
     cotangent = d_ref[...]
     for step in range(experts):
         places = place_matrix(slots, step * capacity, capacity, tokens)
@@ -89,11 +94,11 @@
         send_refs[step][1] = dot(places, cotangent, 1, 0).astype(BF16)
 
 
-def prepare_kernel(experts, capacity, own_ref, x_ref, routes_ref, norm_ref, deviation_ref, places_ref):
+def prepare_kernel(experts, capacity, x_ref, routes_ref, norm_ref, deviation_ref, places_ref):
     normalized_rows, inverse_deviation = norm_pieces(x_ref[...])
     norm_ref[...] = normalized_rows
     deviation_ref[...] = jnp.broadcast_to(inverse_deviation, deviation_ref.shape)
-    slots = slot_of(own_ref[0], routes_ref[...], experts, capacity)
+    slots = slot_of(lax.axis_index("expert") // 2, routes_ref[...], experts, capacity)
     places_ref[...] = place_matrix(slots, 0, experts * capacity, x_ref.shape[0])
 
 
@@ -177,6 +182,13 @@
         at += ref.shape[0]
 
 
+def gather_kernel(*refs):
+    rows = refs[0].shape[1]
+    for at, ref in enumerate(refs[:-2]):
+        refs[-2][at * rows : (at + 1) * rows, :] = ref[0]
+        refs[-1][at * rows : (at + 1) * rows, :] = ref[1]
+
+
 def half_kernel(stay_ref, pair_ref, out_ref):
     out_ref[...] = (stay_ref[...] + pair_ref[...].astype(F32)).astype(BF16)
 
@@ -243,19 +255,20 @@
     units = first.shape[0]
     hidden_units = 4 * units
 
-    own_scalar = own.astype(jnp.int32).reshape(1)
     routes_t = routes.T
     send = call(
         functools.partial(dispatch_kernel, experts, capacity),
         "dispatch",
         [shape(BF16, 2, capacity, width)] * experts,
-        (own_scalar, prenorm_input, gain, routes_t, cotangent),
+        (prenorm_input, gain, routes_t, cotangent),
         flops=4 * slots * tokens * width,
-        specs=[SMEM, ANY, VMEM, VMEM, ANY],
+        specs=[ANY] * 4,
         scratch=[
             pltpu.VMEM((tokens, width), BF16),
+            pltpu.VMEM((width,), F32),
+            pltpu.VMEM((top, tokens), jnp.int32),
             pltpu.VMEM((tokens, width), BF16),
-            pltpu.SemaphoreType.DMA((2,)),
+            pltpu.SemaphoreType.DMA((4,)),
         ],
         mebibytes=60,
     )
@@ -287,8 +300,7 @@
         functools.partial(prepare_kernel, experts, capacity),
         "prepare",
         [shape(F32, tokens, width), shape(F32, tokens, 128), shape(BF16, slots, tokens)],
-        (own_scalar, prenorm_input, routes_t),
-        specs=[SMEM, VMEM, VMEM],
+        (prenorm_input, routes_t),
     )
 
     stage = (
@@ -329,6 +341,9 @@
         pieces = [near[step] for step in chosen]
         for turn in range(columns - 1):
             pieces = pieces + [side[step][turn] for step in chosen]
+        if capacity % 16 == 0:
+            outs = [shape(BF16, len(pieces) * capacity, width)] * 2
+            return call(gather_kernel, "gather", outs, pieces)
         return (
             jnp.concatenate([piece[0] for piece in pieces], axis=0),
             jnp.concatenate([piece[1] for piece in pieces], axis=0),
@@ -396,6 +411,21 @@
         near[step], side[step] = tied((near[step], side[step]), (early_own, early_side))
     late_m, late_d = gather_rows(late)
 
+    def by_turn(rows):
+        return list(rows.reshape(columns - 1, -1, width))
+
+    def add_rows(own_rows, pieces):
+        for piece in pieces:
+            own_rows = own_rows + piece.astype(F32)
+        return own_rows.astype(BF16).reshape(-1, capacity, width)
+
+    returned = [None] * experts
+
+    def send_back(chosen, rows):
+        for step, value in zip(chosen, rows):
+            returned[step] = over_experts(value, experts - step) if step else value
+
+    early_back = back_over_columns(by_turn(early_side))
     late_hidden, late_slope, late_y, late_gate = first_product(late_m, late_d)
     hidden = jnp.concatenate([early_hidden, late_hidden], axis=0)
     grad_y = jnp.concatenate([early_y, late_y], axis=0)
@@ -408,32 +438,15 @@
     sums = early_sums + late_sums
     line = jnp.arange(-(-(experts + 1) // 8) * 8, dtype=jnp.int32)[:, None]
     total = jnp.where(line == own, sums[:1], jnp.where(line == experts, sums[1:2], 0.0))
-    total = pairwise(total, "expert", halves, 1)
     out_half = half_sum(out_stay, out_pair)
 
-    def by_turn(rows):
-        return rows.reshape(columns - 1, -1, width)
-
-    leaving = jnp.concatenate([by_turn(early_side), by_turn(late_side)], axis=1)
-    stage = (out_half, total, late_own, leaving)
-    out_half, total, leaving, hidden = tied((out_half, total, leaving, hidden), stage)
+    stage = (out_half, total, late_own, late_side)
+    out_half, total, late_side, hidden = tied((out_half, total, late_side, hidden), stage)
     out_other = over_half(out_half)
-    rows_back = back_over_columns(list(leaving))
-
-    def add_rows(own_rows, pieces):
-        for piece in pieces:
-            own_rows = own_rows + piece.astype(F32)
-        return own_rows.astype(BF16).reshape(-1, capacity, width)
-
-    returned = [None] * experts
-
-    def send_back(chosen, rows):
-        for step, value in zip(chosen, rows):
-            returned[step] = over_experts(value, experts - step) if step else value
-
+    late_back = back_over_columns(by_turn(late_side))
     rows_m = jnp.concatenate([early_m, late_m], axis=0)
     grad_pre = jnp.concatenate([early_pre, late_pre], axis=0)
-    grad_pre = tied(grad_pre, (out_half, leaving))
+    grad_pre = tied(grad_pre, (out_half, late_side))
     in_leave = weight_gradient(0, 1, grad_pre, rows_m, BF16)
     in_pair = over_pair(in_leave)
     in_stay = weight_gradient(2, 1, tied(grad_pre, in_leave), rows_m, F32)
@@ -443,16 +456,22 @@
         total = pairwise(total, "expert", halves, bit)
         bit *= 2
     total = pairwise(total, "dp", groups, 1)
+    early_back, late_back = tied((early_back, late_back), total)
+    early_rows = add_rows(early_own, early_back)
+    late_rows = add_rows(late_own, late_back)
+    total = tied(total, (early_rows, late_rows))
+    total = pairwise(total, "expert", halves, 1)
     hidden, grad_pre = tied((hidden, grad_pre), in_stay)
     out_rest = over_pair(weight_gradient(1, 1, hidden, grad_y, BF16))
     out_mine = weight_gradient(3, 1, hidden, grad_y, F32)
     in_rest = over_pair(weight_gradient(1, 1, grad_pre, rows_m, BF16))
     in_mine = weight_gradient(3, 1, grad_pre, rows_m, F32)
 
-    stage = (out_other, rows_back, in_pair, in_stay, total)
-    out_other, rows_back, in_pair, in_stay, total = tied(stage, stage)
+    stage = (out_other, early_rows, late_rows, in_pair, in_stay, total)
+    out_other, early_rows, late_rows, in_pair, in_stay, total = tied(stage, stage)
     in_other = over_half(half_sum(in_stay, in_pair))
-    send_back(steps, add_rows(jnp.concatenate([early_own, late_own], axis=0), rows_back))
+    send_back(early, early_rows)
+    send_back(late, late_rows)
     bit = 2
     while bit < groups // 2:
         total = pairwise(total, "dp", groups, bit)

time: 123 us -> 122 us (level)
  waiting for transfers between devices: 62.9 us -> 53.2 us
  starting transfers between devices: 25.7 us -> 30.2 us
  Pallas kernels: 24.4 us -> 27.4 us
    ppermute x4, waiting for transfers between devices: 6.92 us -> 0.13 us  [over_columns(): lax.ppermute(value, 'dp', [(i, (i + 2 * step) % groups) for i in range(gr...]
    ppermute x6, waiting for transfers between devices: 41.5 us -> 45.8 us  [over_experts(): lax.ppermute(value, 'expert', [(i, (i + 2 * step) % halves) for i in rang...]
    ppermute x4, waiting for transfers between devices: 4.04 us -> 0.01 us  [over_half(): return lax.ppermute(value, 'expert', [(i, i ^ 1) for i in range(halves)])]
    ppermute x1 -> x2, waiting for transfers between devices: 3.66 us -> 0.52 us  [back_over_columns(): lax.ppermute(value, 'dp', [(i, (i - 2 * step) % groups) for i in range(gr...]
    pallas_call x21 -> x23, Pallas kernels: 24.4 us -> 27.4 us  [call(): pl.pallas_call(kernel, out_shape=outs, in_specs=specs or [VMEM] * len(arg...]
    ppermute x1 -> x2, starting transfers between devices: 0.59 us -> 2.16 us  [back_over_columns(): lax.ppermute(value, 'dp', [(i, (i - 2 * step) % groups) for i in range(gr...]
    ppermute x4, starting transfers between devices: 5.32 us -> 6.63 us  [over_half(): return lax.ppermute(value, 'expert', [(i, i ^ 1) for i in range(halves)])]
    unnamed x20 -> x24, local copies, waits for them, and re-layouts: 6.28 us -> 6.52 us
  transfers between devices with their start and end apart: 28 -> 29, of which waited for: 14 -> 11; matrix products, arithmetic and copies ran while one was open for 5% -> 2% of each run, Pallas kernels for 13% -> 16%
where the time goes in v8:
time: 122 us; the launch traced here: 121 us
  waiting for transfers between devices  53.2 us (44%)
  starting transfers between devices  30.2 us (25%)
  Pallas kernels  27.4 us (22%)
  local copies, waits for them, and re-layouts  6.68 us (5%)
  other arithmetic  2.57 us (2%)
    ppermute x6, waiting for transfers between devices, over_experts(): lax.ppermute(value, 'expert', [(i, (i + 2 * step) % halves) for i in rang...  45.8 us
    pallas_call x23, Pallas kernels, call(): pl.pallas_call(kernel, out_shape=outs, in_specs=specs or [VMEM] * len(arg...  27.4 us
    ppermute x6, starting transfers between devices, over_experts(): lax.ppermute(value, 'expert', [(i, (i + 2 * step) % halves) for i in rang...  8.87 us
    ppermute x4, waiting for transfers between devices, pairwise(): lax.ppermute(value, name, [(i, i ^ bit) for i in range(size)])  6.66 us
    ppermute x4, starting transfers between devices, over_half(): return lax.ppermute(value, 'expert', [(i, i ^ 1) for i in range(halves)])  6.63 us
    unnamed x24, local copies, waits for them, and re-layouts  6.52 us
    ppermute x4, starting transfers between devices, over_columns(): lax.ppermute(value, 'dp', [(i, (i + 2 * step) % groups) for i in range(gr...  5.01 us
    ppermute x4, starting transfers between devices, pairwise(): lax.ppermute(value, name, [(i, i ^ bit) for i in range(size)])  4.84 us
  transfers between devices with their start and end apart: 29, of which 11 were waited for; matrix products, arithmetic and copies ran while one was open for 2% of the time, Pallas kernels for 16%

profile of v8, /device:TPU:0, one launch (start us, length us, event | category | flops | bytes accessed | tf_op | source)
XLA Modules:
  0.0 121.1 jit_solution(15695512858745549930)
XLA Ops:
  0.6 2.9 %dispatch.1 = (bf16[2,80,1280]{2,1,0:T(8,128)(2,1)}, bf16[2,80,1280]{2,1,0:T(8,128)(2,1)}, bf16[2,80,1280]{2,1,0:T(8,128)(2,1)}, bf16[2,80,1280]{2,1,0:T(8,128)(2,1)}) custom-call(bf16[128,1280]{1,0:T(8,128)(2,1)} %x_ref.1, f32[1280]{0:T(1024)} %gain_ref.1, s32[2,128]{1,0:T(2,128)} %bitcast.30, bf16[128,1280]{1,0:T(8,128)(2,1)} %d_ref.1), custom_call_target="tpu_custom_call" | custom-call | flops 209715200 | bytes 409600 | tf_op jit(solution)/shard_map/dispatch/pallas_call | solution.py:206
  3.5 3.0 %collective-permute-start.2 = (bf16[320,1280]{1,0:T(8,128)(2,1)}, bf16[320,1280]{1,0:T(8,128)(2,1)S(1)}, u32[]{:S(2)}, u32[]{:S(2)}) collective-permute-start(bf16[320,1280]{1,0:T(8,128)(2,1)} %bitcast.24), channel_id=1, source_target_pairs={{0,4},{4,0},{8,12},{12,8},{16,20},{20,16},{24,28},{28,24},{1,5},{5... | collective-permute-start | bytes 2457608 | tf_op jit(solution)/shard_map/ppermute | solution.py:230
  6.5 1.6 %collective-permute-start = (bf16[2,80,1280]{2,1,0:T(8,128)(2,1)}, bf16[2,80,1280]{2,1,0:T(8,128)(2,1)}, u32[]{:S(2)}, u32[]{:S(2)}) collective-permute-start(bf16[2,80,1280]{2,1,0:T(8,128)(2,1)} %get-tuple-element.83), channel_id=1, source_target_pairs={{0,8},{4,12},{8,16},{12,20},{16,24},{20,28},{24,0},{28,4},{1,9},{5... | collective-permute-start | bytes 1228808 | tf_op jit(solution)/shard_map/ppermute | solution.py:248
  8.1 2.2 %collective-permute-start.1 = (bf16[2,80,1280]{2,1,0:T(8,128)(2,1)}, bf16[2,80,1280]{2,1,0:T(8,128)(2,1)}, u32[]{:S(2)}, u32[]{:S(2)}) collective-permute-start(bf16[2,80,1280]{2,1,0:T(8,128)(2,1)} %get-tuple-element.84), channel_id=1, source_target_pairs={{0,24},{4,28},{8,0},{12,4},{16,8},{20,12},{24,16},{28,20},{1,25},{... | collective-permute-start | bytes 1228808 | tf_op jit(solution)/shard_map/ppermute | solution.py:248
  11.9 9.1 %collective-permute-done.refs_1_ = bf16[2,80,1280]{2,1,0:T(8,128)(2,1)} collective-permute-done((bf16[2,80,1280]{2,1,0:T(8,128)(2,1)}, bf16[2,80,1280]{2,1,0:T(8,128)(2,1)}, u32[]{:S(2)}, u32[]{:S(2)}) %collective-permute-start) | collective-permute-done | bytes 409632 | tf_op jit(solution)/shard_map/ppermute | solution.py:248
  21.0 7.9 %collective-permute-done.1.refs_2_ = bf16[2,80,1280]{2,1,0:T(8,128)(2,1)} collective-permute-done((bf16[2,80,1280]{2,1,0:T(8,128)(2,1)}, bf16[2,80,1280]{2,1,0:T(8,128)(2,1)}, u32[]{:S(2)}, u32[]{:S(2)}) %collective-permute-start.1) | collective-permute-done | bytes 409632 | tf_op jit(solution)/shard_map/ppermute | solution.py:248
  36.9 15.0 %collective-permute-done.5.refs_0_ = bf16[2,80,1280]{2,1,0:T(8,128)(2,1)} collective-permute-done((bf16[2,80,1280]{2,1,0:T(8,128)(2,1)}, bf16[2,80,1280]{2,1,0:T(8,128)(2,1)}, u32[]{:S(2)}, u32[]{:S(2)}) %collective-permute-start.5) | collective-permute-done | bytes 409632 | tf_op jit(solution)/shard_map/ppermute | solution.py:248
  56.1 1.5 %gather.2 = (bf16[480,1280]{1,0:T(8,128)(2,1)S(1)}, bf16[480,1280]{1,0:T(8,128)(2,1)S(1)}) custom-call(bf16[2,80,1280]{2,1,0:T(8,128)(2,1)S(1)} %copy-done.4, bf16[2,80,1280]{2,1,0:T(8,128)(2,1)} %collective-permute-done.refs_1_, bf16[2,80,1280]{2,1,0:T(8,128)(2,1)} %collective-permute-done.1.refs_2_, bf16[2,80,1280]{2,1,0:T(8,128)(2,1)S(1)} %copy-done.6, ...), custom_call_target="tpu_custom_call" | custom-call | tf_op jit(solution)/shard_map/gather/pallas_call | solution.py:206
  59.0 3.3 %first.2 = (bf16[480,1280]{1,0:T(8,128)(2,1)S(1)}, f32[480,1280]{1,0:T(8,128)S(1)}, bf16[480,1280]{1,0:T(8,128)(2,1)S(1)}, f32[480,128]{1,0:T(8,128)S(1)}) custom-call(bf16[480,1280]{1,0:T(8,128)(2,1)S(1)} %get-tuple-element.101.m_ref, bf16[480,1280]{1,0:T(8,128)(2,1)S(1)} %get-tuple-element.102.d_ref, bf16[1280,1280]{1,0:T(8,128)(2,1)S(1)} %join.2.first_ref, ...), custom_call_target="tpu_custom_call" | custom-call | flops 1572864000 | bytes 3072000 | tf_op jit(solution)/shard_map/first/pallas_call | solution.py:206
  63.8 2.0 %second.2 = (bf16[480,1280]{1,0:T(8,128)(2,1)S(1)}, f32[480,128]{1,0:T(8,128)S(1)}) custom-call(bf16[480,1280]{1,0:T(8,128)(2,1)S(1)} %get-tuple-element.102.d_ref, bf16[1280,1280]{1,0:T(8,128)(2,1)S(1)} %join.3.second_ref, bf16[480,1280]{1,0:T(8,128)(2,1)S(1)} %get-tuple-element.104.hidden_ref, f32[480,1280]{1,0:T(8,128)S(1)} %get-tuple-element.108.slope_ref, ...), custom_call_target="tpu_custom_call" | custom-call | flops 1572864000 | bytes 3072000 | tf_op jit(solution)/shard_map/second/pallas_call | solution.py:206
  65.8 1.9 %rows.2 = (f32[240,1280]{1,0:T(8,128)S(1)}, bf16[240,1280]{1,0:T(8,128)(2,1)S(1)}, f32[8,1280]{1,0:T(8,128)S(1)}) custom-call(bf16[480,1280]{1,0:T(8,128)(2,1)S(1)} %get-tuple-element.101.m_ref, bf16[480,1280]{1,0:T(8,128)(2,1)S(1)} %get-tuple-element.110.pre_ref, f32[480,128]{1,0:T(8,128)S(1)} %get-tuple-element.111.logit_ref, ...), custom_call_target="tpu_custom_call" | custom-call | flops 1572864000 | bytes 3072000 | tf_op jit(solution)/shard_map/rows/pallas_call | solution.py:206
  75.7 1.6 %collective-permute-start.14 = (bf16[320,1280]{1,0:T(8,128)(2,1)S(1)}, bf16[320,1280]{1,0:T(8,128)(2,1)S(1)}, u32[]{:S(2)}, u32[]{:S(2)}) collective-permute-start(bf16[320,1280]{1,0:T(8,128)(2,1)S(1)} %half.2), channel_id=1, source_target_pairs={{0,4},{4,0},{8,12},{12,8},{16,20},{20,16},{24,28},{28,24},{1,5},{5... | collective-permute-start | bytes 2457608 | tf_op jit(solution)/shard_map/ppermute | solution.py:230
  77.2 1.6 %collective-permute-start.16 = (bf16[80,1280]{1,0:T(8,128)(2,1)S(1)}, bf16[80,1280]{1,0:T(8,128)(2,1)S(1)}, u32[]{:S(2)}, u32[]{:S(2)}) collective-permute-start(bf16[80,1280]{1,0:T(8,128)(2,1)S(1)} %get-tuple-element.132), channel_id=1, source_target_pairs={{0,2},{1,3},{2,0},{3,1},{4,6},{5,7},{6,4},{7,5},{8,10},{9,11},{10,... | collective-permute-start | bytes 614408 | tf_op jit(solution)/shard_map/ppermute | solution.py:243
  80.6 1.6 %collective-permute-start.17 = (f32[8,1280]{1,0:T(8,128)S(1)}, f32[8,1280]{1,0:T(8,128)S(1)}, u32[]{:S(2)}, u32[]{:S(2)}) collective-permute-start(f32[8,1280]{1,0:T(8,128)S(1)} %select_select_fusion), channel_id=1, source_target_pairs={{0,8},{4,12},{8,0},{12,4},{16,24},{20,28},{24,16},{28,20},{1,9},{5... | collective-permute-start | bytes 122888 | tf_op jit(solution)/shard_map/ppermute | solution.py:251
  83.1 1.6 %collective-permute-done.17 = f32[8,1280]{1,0:T(8,128)S(1)} collective-permute-done((f32[8,1280]{1,0:T(8,128)S(1)}, f32[8,1280]{1,0:T(8,128)S(1)}, u32[]{:S(2)}, u32[]{:S(2)}) %collective-permute-start.17) | collective-permute-done | bytes 40992 | tf_op jit(solution)/shard_map/ppermute | solution.py:251
  84.7 1.6 %collective-permute-start.18 = (f32[8,1280]{1,0:T(8,128)S(1)}, f32[8,1280]{1,0:T(8,128)S(1)}, u32[]{:S(2)}, u32[]{:S(2)}) collective-permute-start(f32[8,1280]{1,0:T(8,128)S(1)} %add.33), channel_id=1, source_target_pairs={{0,16},{4,20},{8,24},{12,28},{16,0},{20,4},{24,8},{28,12},{1,17},{... | collective-permute-start | bytes 122888 | tf_op jit(solution)/shard_map/ppermute | solution.py:251
  87.2 2.5 %collective-permute-done.18 = f32[8,1280]{1,0:T(8,128)S(1)} collective-permute-done((f32[8,1280]{1,0:T(8,128)S(1)}, f32[8,1280]{1,0:T(8,128)S(1)}, u32[]{:S(2)}, u32[]{:S(2)}) %collective-permute-start.18) | collective-permute-done | bytes 40992 | tf_op jit(solution)/shard_map/ppermute | solution.py:251
  92.2 1.6 %collective-permute-start.21 = (f32[8,1280]{1,0:T(8,128)S(1)}, f32[8,1280]{1,0:T(8,128)S(1)}, u32[]{:S(2)}, u32[]{:S(2)}) collective-permute-start(f32[8,1280]{1,0:T(8,128)S(1)} %add.35), channel_id=1, source_target_pairs={{0,4},{4,0},{8,12},{12,8},{16,20},{20,16},{24,28},{28,24},{1,5},{5... | collective-permute-start | bytes 122888 | tf_op jit(solution)/shard_map/ppermute | solution.py:251
  94.7 2.2 %collective-permute-done.21 = f32[8,1280]{1,0:T(8,128)S(1)} collective-permute-done((f32[8,1280]{1,0:T(8,128)S(1)}, f32[8,1280]{1,0:T(8,128)S(1)}, u32[]{:S(2)}, u32[]{:S(2)}) %collective-permute-start.21) | collective-permute-done | bytes 40992 | tf_op jit(solution)/shard_map/ppermute | solution.py:251
  97.1 1.6 %collective-permute-start.25 = (bf16[320,1280]{1,0:T(8,128)(2,1)S(1)}, bf16[320,1280]{1,0:T(8,128)(2,1)S(1)}, u32[]{:S(2)}, u32[]{:S(2)}) collective-permute-start(bf16[320,1280]{1,0:T(8,128)(2,1)S(1)} %half.3), channel_id=1, source_target_pairs={{0,4},{4,0},{8,12},{12,8},{16,20},{20,16},{24,28},{28,24},{1,5},{5... | collective-permute-start | bytes 2457608 | tf_op jit(solution)/shard_map/ppermute | solution.py:230
  98.7 2.3 %collective-permute-start.22 = (bf16[80,1280]{1,0:T(8,128)(2,1)S(1)}, bf16[80,1280]{1,0:T(8,128)(2,1)S(1)}, u32[]{:S(2)}, u32[]{:S(2)}) collective-permute-start(bf16[80,1280]{1,0:T(8,128)(2,1)S(1)} %get-tuple-element.160), channel_id=1, source_target_pairs={{0,24},{4,28},{8,0},{12,4},{16,8},{20,12},{24,16},{28,20},{1,25},{... | collective-permute-start | bytes 614408 | tf_op jit(solution)/shard_map/ppermute | solution.py:248
  103.7 2.9 %collective-permute-done.22 = bf16[80,1280]{1,0:T(8,128)(2,1)S(1)} collective-permute-done((bf16[80,1280]{1,0:T(8,128)(2,1)S(1)}, bf16[80,1280]{1,0:T(8,128)(2,1)S(1)}, u32[]{:S(2)}, u32[]{:S(2)}) %collective-permute-start.22) | collective-permute-done | bytes 204832 | tf_op jit(solution)/shard_map/ppermute | solution.py:248
  108.0 11.0 %collective-permute-done.23 = bf16[80,1280]{1,0:T(8,128)(2,1)S(1)} collective-permute-done((bf16[80,1280]{1,0:T(8,128)(2,1)S(1)}, bf16[80,1280]{1,0:T(8,128)(2,1)S(1)}, u32[]{:S(2)}, u32[]{:S(2)}) %collective-permute-start.23) | collective-permute-done | bytes 204832 | tf_op jit(solution)/shard_map/ppermute | solution.py:248
  119.1 1.9 %finish.1 = (bf16[128,1280]{1,0:T(8,128)(2,1)}, bf16[320,1280]{1,0:T(8,128)(2,1)}, f32[4,1280]{1,0:T(4,128)}, f32[1280]{0:T(1024)}) custom-call(f32[128,1280]{1,0:T(8,128)S(1)} %copy-done.3, f32[128,128]{1,0:T(8,128)S(1)} %get-tuple-element.95.deviation_ref, bf16[320,128]{1,0:T(8,128)(2,1)S(1)} %get-tuple-element.96.places_ref, f32[1280]{0:T(1024)S(1)} %copy-done.9, ...), custom_call_target="tpu_custom_call" | custom-call | tf_op jit(solution)/shard_map/finish/pallas_call | solution.py:206
  (99 shorter events, 35.7 us)
Async XLA Ops:
  3.5 26.1 %collective-permute-start.2 = (bf16[320,1280]{1,0:T(8,128)(2,1)}, bf16[320,1280]{1,0:T(8,128)(2,1)S(1)}, u32[]{:S(2)}, u32[]{:S(2)}) collective-permute-start(bf16[320,1280]{1,0:T(8,128)(2,1)} %bitcast.24), channel_id=1, source_target_pairs={{0,4},{4,0},{8,12},{12,8},{16,20},{20,16},{24,28},{28,24},{1,5},{5... | collective-permute-start | bytes 2457608 | tf_op jit(solution)/shard_map/ppermute | solution.py:230
  6.5 23.0 %collective-permute-start.4 = (bf16[320,1280]{1,0:T(8,128)(2,1)}, bf16[320,1280]{1,0:T(8,128)(2,1)S(1)}, u32[]{:S(2)}, u32[]{:S(2)}) collective-permute-start(bf16[320,1280]{1,0:T(8,128)(2,1)} %bitcast.25), channel_id=1, source_target_pairs={{0,1},{1,0},{2,3},{3,2},{4,5},{5,4},{6,7},{7,6},{8,9},{9,8},{10,11... | collective-permute-start | bytes 2457608 | tf_op jit(solution)/shard_map/ppermute | solution.py:233
  6.5 14.4 %collective-permute-start = (bf16[2,80,1280]{2,1,0:T(8,128)(2,1)}, bf16[2,80,1280]{2,1,0:T(8,128)(2,1)}, u32[]{:S(2)}, u32[]{:S(2)}) collective-permute-start(bf16[2,80,1280]{2,1,0:T(8,128)(2,1)} %get-tuple-element.83), channel_id=1, source_target_pairs={{0,8},{4,12},{8,16},{12,20},{16,24},{20,28},{24,0},{28,4},{1,9},{5... | collective-permute-start | bytes 1228808 | tf_op jit(solution)/shard_map/ppermute | solution.py:248
  8.1 20.7 %collective-permute-start.1 = (bf16[2,80,1280]{2,1,0:T(8,128)(2,1)}, bf16[2,80,1280]{2,1,0:T(8,128)(2,1)}, u32[]{:S(2)}, u32[]{:S(2)}) collective-permute-start(bf16[2,80,1280]{2,1,0:T(8,128)(2,1)} %get-tuple-element.84), channel_id=1, source_target_pairs={{0,24},{4,28},{8,0},{12,4},{16,8},{20,12},{24,16},{28,20},{1,25},{... | collective-permute-start | bytes 1228808 | tf_op jit(solution)/shard_map/ppermute | solution.py:248
  10.4 18.4 %collective-permute-start.3 = (bf16[2,80,1280]{2,1,0:T(8,128)(2,1)}, bf16[2,80,1280]{2,1,0:T(8,128)(2,1)S(1)}, u32[]{:S(2)}, u32[]{:S(2)}) collective-permute-start(bf16[2,80,1280]{2,1,0:T(8,128)(2,1)} %get-tuple-element.97.refs_0_), channel_id=1, source_target_pairs={{0,2},{1,3},{2,0},{3,1},{4,6},{5,7},{6,4},{7,5},{8,10},{9,11},{10,... | collective-permute-start | bytes 1228808 | tf_op jit(solution)/shard_map/ppermute | solution.py:237
  29.6 22.5 %collective-permute-start.6 = (bf16[320,1280]{1,0:T(8,128)(2,1)}, bf16[320,1280]{1,0:T(8,128)(2,1)S(1)}, u32[]{:S(2)}, u32[]{:S(2)}) collective-permute-start(bf16[320,1280]{1,0:T(8,128)(2,1)} %bitcast.27), channel_id=1, source_target_pairs={{0,4},{4,0},{8,12},{12,8},{16,20},{20,16},{24,28},{28,24},{1,5},{5... | collective-permute-start | bytes 2457608 | tf_op jit(solution)/shard_map/ppermute | solution.py:230
  30.1 22.0 %collective-permute-start.9 = (bf16[320,1280]{1,0:T(8,128)(2,1)S(1)}, bf16[320,1280]{1,0:T(8,128)(2,1)}, u32[]{:S(2)}, u32[]{:S(2)}) collective-permute-start(bf16[320,1280]{1,0:T(8,128)(2,1)S(1)} %collective-permute-done.2.refs_2_), channel_id=1, source_target_pairs={{0,1},{1,0},{2,3},{3,2},{4,5},{5,4},{6,7},{7,6},{8,9},{9,8},{10,11... | collective-permute-start | bytes 2457608 | tf_op jit(solution)/shard_map/ppermute | solution.py:233
  30.1 21.9 %collective-permute-start.5 = (bf16[2,80,1280]{2,1,0:T(8,128)(2,1)}, bf16[2,80,1280]{2,1,0:T(8,128)(2,1)}, u32[]{:S(2)}, u32[]{:S(2)}) collective-permute-start(bf16[2,80,1280]{2,1,0:T(8,128)(2,1)} %get-tuple-element.86), channel_id=1, source_target_pairs={{0,16},{4,20},{8,24},{12,28},{16,0},{20,4},{24,8},{28,12},{1,17},{... | collective-permute-start | bytes 1228808 | tf_op jit(solution)/shard_map/ppermute | solution.py:248
  31.4 20.6 %collective-permute-start.7 = (bf16[2,80,1280]{2,1,0:T(8,128)(2,1)}, bf16[2,80,1280]{2,1,0:T(8,128)(2,1)}, u32[]{:S(2)}, u32[]{:S(2)}) collective-permute-start(bf16[2,80,1280]{2,1,0:T(8,128)(2,1)} %collective-permute-done.refs_1_), channel_id=1, source_target_pairs={{0,2},{1,3},{2,0},{3,1},{4,6},{5,7},{6,4},{7,5},{8,10},{9,11},{10,... | collective-permute-start | bytes 1228808 | tf_op jit(solution)/shard_map/ppermute | solution.py:237
  32.9 19.2 %collective-permute-start.8 = (bf16[2,80,1280]{2,1,0:T(8,128)(2,1)}, bf16[2,80,1280]{2,1,0:T(8,128)(2,1)}, u32[]{:S(2)}, u32[]{:S(2)}) collective-permute-start(bf16[2,80,1280]{2,1,0:T(8,128)(2,1)} %collective-permute-done.1.refs_2_), channel_id=1, source_target_pairs={{0,2},{1,3},{2,0},{3,1},{4,6},{5,7},{6,4},{7,5},{8,10},{9,11},{10,... | collective-permute-start | bytes 1228808 | tf_op jit(solution)/shard_map/ppermute | solution.py:237
  52.1 10.5 %collective-permute-start.11 = (bf16[320,1280]{1,0:T(8,128)(2,1)S(1)}, bf16[320,1280]{1,0:T(8,128)(2,1)S(1)}, u32[]{:S(2)}, u32[]{:S(2)}) collective-permute-start(bf16[320,1280]{1,0:T(8,128)(2,1)S(1)} %collective-permute-done.6.refs_2_), channel_id=1, source_target_pairs={{0,1},{1,0},{2,3},{3,2},{4,5},{5,4},{6,7},{7,6},{8,9},{9,8},{10,11... | collective-permute-start | bytes 2457608 | tf_op jit(solution)/shard_map/ppermute | solution.py:233
  52.1 10.5 %collective-permute-start.12 = (bf16[320,1280]{1,0:T(8,128)(2,1)}, bf16[320,1280]{1,0:T(8,128)(2,1)S(1)}, u32[]{:S(2)}, u32[]{:S(2)}) collective-permute-start(bf16[320,1280]{1,0:T(8,128)(2,1)} %bitcast.28), channel_id=1, source_target_pairs={{0,1},{1,0},{2,3},{3,2},{4,5},{5,4},{6,7},{7,6},{8,9},{9,8},{10,11... | collective-permute-start | bytes 2457608 | tf_op jit(solution)/shard_map/ppermute | solution.py:233
  52.6 15.2 %collective-permute-start.10 = (bf16[2,80,1280]{2,1,0:T(8,128)(2,1)}, bf16[2,80,1280]{2,1,0:T(8,128)(2,1)S(1)}, u32[]{:S(2)}, u32[]{:S(2)}) collective-permute-start(bf16[2,80,1280]{2,1,0:T(8,128)(2,1)} %collective-permute-done.5.refs_0_), channel_id=1, source_target_pairs={{0,2},{1,3},{2,0},{3,1},{4,6},{5,7},{6,4},{7,5},{8,10},{9,11},{10,... | collective-permute-start | bytes 1228808 | tf_op jit(solution)/shard_map/ppermute | solution.py:237
  71.4 19.8 %collective-permute-start.15 = (bf16[240,1280]{1,0:T(8,128)(2,1)S(1)}, bf16[240,1280]{1,0:T(8,128)(2,1)S(1)}, u32[]{:S(2)}, u32[]{:S(2)}) collective-permute-start(bf16[240,1280]{1,0:T(8,128)(2,1)S(1)} %get-tuple-element.113), channel_id=1, source_target_pairs={{0,2},{1,3},{2,0},{3,1},{4,6},{5,7},{6,4},{7,5},{8,10},{9,11},{10,... | collective-permute-start | bytes 1843208 | tf_op jit(solution)/shard_map/ppermute | solution.py:243
  75.7 21.3 %collective-permute-start.14 = (bf16[320,1280]{1,0:T(8,128)(2,1)S(1)}, bf16[320,1280]{1,0:T(8,128)(2,1)S(1)}, u32[]{:S(2)}, u32[]{:S(2)}) collective-permute-start(bf16[320,1280]{1,0:T(8,128)(2,1)S(1)} %half.2), channel_id=1, source_target_pairs={{0,4},{4,0},{8,12},{12,8},{16,20},{20,16},{24,28},{28,24},{1,5},{5... | collective-permute-start | bytes 2457608 | tf_op jit(solution)/shard_map/ppermute | solution.py:230
  77.2 14.8 %collective-permute-start.16 = (bf16[80,1280]{1,0:T(8,128)(2,1)S(1)}, bf16[80,1280]{1,0:T(8,128)(2,1)S(1)}, u32[]{:S(2)}, u32[]{:S(2)}) collective-permute-start(bf16[80,1280]{1,0:T(8,128)(2,1)S(1)} %get-tuple-element.132), channel_id=1, source_target_pairs={{0,2},{1,3},{2,0},{3,1},{4,6},{5,7},{6,4},{7,5},{8,10},{9,11},{10,... | collective-permute-start | bytes 614408 | tf_op jit(solution)/shard_map/ppermute | solution.py:243
  79.7 17.3 %collective-permute-start.20 = (bf16[320,1280]{1,0:T(8,128)(2,1)S(1)}, bf16[320,1280]{1,0:T(8,128)(2,1)S(1)}, u32[]{:S(2)}, u32[]{:S(2)}) collective-permute-start(bf16[320,1280]{1,0:T(8,128)(2,1)S(1)} %weights.10), channel_id=1, source_target_pairs={{0,1},{1,0},{2,3},{3,2},{4,5},{5,4},{6,7},{7,6},{8,9},{9,8},{10,11... | collective-permute-start | bytes 2457608 | tf_op jit(solution)/shard_map/ppermute | solution.py:233
  90.9 10.9 %collective-permute-start.26 = (bf16[320,1280]{1,0:T(8,128)(2,1)S(1)}, bf16[320,1280]{1,0:T(8,128)(2,1)S(1)}, u32[]{:S(2)}, u32[]{:S(2)}) collective-permute-start(bf16[320,1280]{1,0:T(8,128)(2,1)S(1)} %weights.13), channel_id=1, source_target_pairs={{0,1},{1,0},{2,3},{3,2},{4,5},{5,4},{6,7},{7,6},{8,9},{9,8},{10,11... | collective-permute-start | bytes 2457608 | tf_op jit(solution)/shard_map/ppermute | solution.py:233
  91.2 27.9 %collective-permute-start.27 = (bf16[320,1280]{1,0:T(8,128)(2,1)S(1)}, bf16[320,1280]{1,0:T(8,128)(2,1)S(1)}, u32[]{:S(2)}, u32[]{:S(2)}) collective-permute-start(bf16[320,1280]{1,0:T(8,128)(2,1)S(1)} %weights.15), channel_id=1, source_target_pairs={{0,1},{1,0},{2,3},{3,2},{4,5},{5,4},{6,7},{7,6},{8,9},{9,8},{10,11... | collective-permute-start | bytes 2457608 | tf_op jit(solution)/shard_map/ppermute | solution.py:233
  97.1 21.9 %collective-permute-start.25 = (bf16[320,1280]{1,0:T(8,128)(2,1)S(1)}, bf16[320,1280]{1,0:T(8,128)(2,1)S(1)}, u32[]{:S(2)}, u32[]{:S(2)}) collective-permute-start(bf16[320,1280]{1,0:T(8,128)(2,1)S(1)} %half.3), channel_id=1, source_target_pairs={{0,4},{4,0},{8,12},{12,8},{16,20},{20,16},{24,28},{28,24},{1,5},{5... | collective-permute-start | bytes 2457608 | tf_op jit(solution)/shard_map/ppermute | solution.py:230
  98.7 7.9 %collective-permute-start.22 = (bf16[80,1280]{1,0:T(8,128)(2,1)S(1)}, bf16[80,1280]{1,0:T(8,128)(2,1)S(1)}, u32[]{:S(2)}, u32[]{:S(2)}) collective-permute-start(bf16[80,1280]{1,0:T(8,128)(2,1)S(1)} %get-tuple-element.160), channel_id=1, source_target_pairs={{0,24},{4,28},{8,0},{12,4},{16,8},{20,12},{24,16},{28,20},{1,25},{... | collective-permute-start | bytes 614408 | tf_op jit(solution)/shard_map/ppermute | solution.py:248
  101.0 18.0 %collective-permute-start.23 = (bf16[80,1280]{1,0:T(8,128)(2,1)S(1)}, bf16[80,1280]{1,0:T(8,128)(2,1)S(1)}, u32[]{:S(2)}, u32[]{:S(2)}) collective-permute-start(bf16[80,1280]{1,0:T(8,128)(2,1)S(1)} %bitcast.33), channel_id=1, source_target_pairs={{0,16},{4,20},{8,24},{12,28},{16,0},{20,4},{24,8},{28,12},{1,17},{... | collective-permute-start | bytes 614408 | tf_op jit(solution)/shard_map/ppermute | solution.py:248
  101.8 17.2 %collective-permute-start.24 = (bf16[80,1280]{1,0:T(8,128)(2,1)S(1)}, bf16[80,1280]{1,0:T(8,128)(2,1)S(1)}, u32[]{:S(2)}, u32[]{:S(2)}) collective-permute-start(bf16[80,1280]{1,0:T(8,128)(2,1)S(1)} %get-tuple-element.159), channel_id=1, source_target_pairs={{0,8},{4,12},{8,16},{12,20},{16,24},{20,28},{24,0},{28,4},{1,9},{5... | collective-permute-start | bytes 614408 | tf_op jit(solution)/shard_map/ppermute | solution.py:248
  106.6 12.5 %collective-permute-start.28 = (f32[8,1280]{1,0:T(8,128)S(1)}, f32[8,1280]{1,0:T(8,128)S(1)}, u32[]{:S(2)}, u32[]{:S(2)}) collective-permute-start(f32[8,1280]{1,0:T(8,128)S(1)} %add.38.total_ref), channel_id=1, source_target_pairs={{0,2},{1,3},{2,0},{3,1},{4,6},{5,7},{6,4},{7,5},{8,10},{9,11},{10,... | collective-permute-start | bytes 122888 | tf_op jit(solution)/shard_map/ppermute | solution.py:479
  (16 other events, 128.9 us)

commit v9 on v8

--- a/solution.py
+++ b/solution.py
@@ -147,15 +147,16 @@
     logit_ref[...] = jnp.broadcast_to(share * gate * (1.0 - gate), logit_ref.shape)
 
 
-def rows_kernel(m_ref, pre_ref, logit_ref, first_ref, router_ref, own_ref, side_ref, sums_ref):
-    count = own_ref.shape[0]
+def rows_kernel(count, m_ref, pre_ref, logit_ref, first_ref, router_ref, sums_ref, *refs):
     pre = pre_ref[...]
     logit = logit_ref[:, :1]
     for at, size in spans(first_ref.shape[1]):
         lanes = pl.ds(at, size)
         rows = dot(pre, first_ref[:, lanes], 1, 0) + logit * router_ref[:, lanes]
-        own_ref[:, lanes] = rows[:count]
-        side_ref[:, lanes] = rows[count:].astype(BF16)
+        if count:
+            refs[0][:, lanes] = rows[:count]
+        if count < pre.shape[0]:
+            refs[-1][:, lanes] = rows[count:].astype(BF16)
         rows_m = m_ref[:, lanes].astype(F32)
         router_part = jnp.sum(rows_m * logit, axis=0, keepdims=True)
         gain_part = jnp.sum(rows_m * rows, axis=0, keepdims=True)
@@ -175,18 +176,33 @@
         ).astype(out_ref.dtype)
 
 
+def copy_all(pairs, sems):
+    copies = [
+        pltpu.make_async_copy(source, target, sems.at[at]) for at, (source, target) in enumerate(pairs)
+    ]
+    for copy in copies:
+        copy.start()
+    for copy in copies:
+        copy.wait()
+
+
 def join_kernel(*refs):
-    at = 0
-    for ref in refs[:-1]:
-        refs[-1][at : at + ref.shape[0], :] = ref[...]
-        at += ref.shape[0]
+    parts, (out_ref, sems) = refs[:-2], refs[-2:]
+    rows = parts[0].shape[0]
+    copy_all([(ref, out_ref.at[pl.ds(at * rows, rows)]) for at, ref in enumerate(parts)], sems)
 
 
 def gather_kernel(*refs):
-    rows = refs[0].shape[1]
-    for at, ref in enumerate(refs[:-2]):
-        refs[-2][at * rows : (at + 1) * rows, :] = ref[0]
-        refs[-1][at * rows : (at + 1) * rows, :] = ref[1]
+    parts, (m_ref, d_ref, sems) = refs[:-3], refs[-3:]
+    rows = parts[0].shape[1]
+    copy_all(
+        [
+            (ref.at[kind], out_ref.at[pl.ds(at * rows, rows)])
+            for at, ref in enumerate(parts)
+            for kind, out_ref in enumerate((m_ref, d_ref))
+        ],
+        sems,
+    )
 
 
 def half_kernel(stay_ref, pair_ref, out_ref):
@@ -303,51 +319,32 @@
         (prenorm_input, routes_t),
     )
 
-    stage = (
-        second_y,
-        first_yc,
-        [near[step] for step in late],
-        [side[step] for step in early[1:]],
-        prepared,
-    )
-    late_held, second_held, second_y, early_held, first_yc, prepared = tied(
-        (
-            [near[step] for step in late],
-            second_held,
-            second_y,
-            [side[step] for step in early[1:]],
-            first_yc,
-            prepared,
-        ),
-        stage,
-    )
-    for step, value in zip(early[1:], early_held):
-        side[step] = value
-    for step, value in zip(late, late_held):
-        near[step] = value
-        side[step] = over_columns(value)
-    second_c = over_pair(second_held)
-    second_yc = over_pair(second_y)
-
     def join(*parts):
-        return call(join_kernel, "join", shape(BF16, hidden_units, width), parts)
-
-    all_first = join(first_yc, first_c, first_y, first)
-    all_second = join(second_yc, second_c, second_y, second_held)
+        return call(
+            join_kernel,
+            "join",
+            shape(BF16, hidden_units, width),
+            parts,
+            specs=[ANY] * len(parts),
+            scratch=[pltpu.SemaphoreType.DMA((len(parts),))],
+        )
+
+    def gather_rows(pieces):
+        if capacity % 16 == 0:
+            return call(
+                gather_kernel,
+                "gather",
+                [shape(BF16, len(pieces) * capacity, width)] * 2,
+                pieces,
+                specs=[ANY] * len(pieces),
+                scratch=[pltpu.SemaphoreType.DMA((2 * len(pieces),))],
+            )
+        return [jnp.concatenate([piece[kind] for piece in pieces], axis=0) for kind in range(2)]
+
+    def side_pieces(chosen):
+        return [side[step][turn] for turn in range(columns - 1) for step in chosen]
 
     router_row = lax.dynamic_slice_in_dim(router, own, 1, 1).astype(F32).T
-
-    def gather_rows(chosen):
-        pieces = [near[step] for step in chosen]
-        for turn in range(columns - 1):
-            pieces = pieces + [side[step][turn] for step in chosen]
-        if capacity % 16 == 0:
-            outs = [shape(BF16, len(pieces) * capacity, width)] * 2
-            return call(gather_kernel, "gather", outs, pieces)
-        return (
-            jnp.concatenate([piece[0] for piece in pieces], axis=0),
-            jnp.concatenate([piece[1] for piece in pieces], axis=0),
-        )
 
     def first_product(rows_m, rows_d):
         count = rows_m.shape[0]
@@ -374,16 +371,17 @@
             flops=2 * count * width * hidden_units,
         )
 
-    def row_gradients(rows_m, grad_pre, logit_gradient):
+    def row_gradients(stay, rows_m, grad_pre, logit_gradient):
         count = grad_pre.shape[0]
+        outs = [shape(F32, 8, width)]
+        if stay:
+            outs.append(shape(F32, stay, width))
+        if stay < count:
+            outs.append(shape(BF16, count - stay, width))
         return call(
-            rows_kernel,
+            functools.partial(rows_kernel, stay),
             "rows",
-            [
-                shape(F32, count // columns, width),
-                shape(BF16, count - count // columns, width),
-                shape(F32, 8, width),
-            ],
+            outs,
             (rows_m, grad_pre, logit_gradient, all_first, router_row),
             flops=2 * count * width * hidden_units,
         )
@@ -403,13 +401,47 @@
     def half_sum(stay, pair):
         return call(half_kernel, "half", shape(BF16, units, width), (stay, pair))
 
-    early_m, early_d = gather_rows(early)
-    early_hidden, early_slope, early_y, early_gate = first_product(early_m, early_d)
-    early_pre, early_logit = second_product(early_d, early_hidden, early_slope, early_gate)
-    early_own, early_side, early_sums = row_gradients(early_m, early_pre, early_logit)
+    all_first = join(first_yc, first_c, first_y, first)
+    near_m, near_d = gather_rows([near[step] for step in early])
+    near_first = first_product(near_m, near_d)
+
+    stage = (
+        second_y,
+        near_first,
+        [near[step] for step in late],
+        [side[step] for step in early[1:]],
+        prepared,
+    )
+    late_held, second_held, second_y, early_held, near_first, prepared = tied(
+        (
+            [near[step] for step in late],
+            second_held,
+            second_y,
+            [side[step] for step in early[1:]],
+            near_first,
+            prepared,
+        ),
+        stage,
+    )
+    for step, value in zip(early[1:], early_held):
+        side[step] = value
+    for step, value in zip(late, late_held):
+        near[step] = value
+        side[step] = over_columns(value)
+    second_c = over_pair(second_held)
+    second_yc = over_pair(second_y)
+
+    side_m, side_d = gather_rows(side_pieces(early))
+    side_hidden, side_slope, side_y, side_gate = first_product(side_m, side_d)
+    all_second = join(second_yc, second_c, second_y, second_held)
+    side_pre, side_logit = second_product(side_d, side_hidden, side_slope, side_gate)
+    side_sums, side_rows = row_gradients(0, side_m, side_pre, side_logit)
+    near_hidden, near_slope, near_y, near_gate = near_first
+    near_pre, near_logit = second_product(tied(near_d, side_rows), near_hidden, near_slope, near_gate)
+    near_sums, near_rows = row_gradients(near_m.shape[0], near_m, near_pre, near_logit)
     for step in late:
-        near[step], side[step] = tied((near[step], side[step]), (early_own, early_side))
-    late_m, late_d = gather_rows(late)
+        near[step], side[step] = tied((near[step], side[step]), near_rows)
+    late_m, late_d = gather_rows([near[step] for step in late] + side_pieces(late))
 
     def by_turn(rows):
         return list(rows.reshape(columns - 1, -1, width))
@@ -425,52 +457,59 @@
         for step, value in zip(chosen, rows):
             returned[step] = over_experts(value, experts - step) if step else value
 
-    early_back = back_over_columns(by_turn(early_side))
+    early_back = back_over_columns(by_turn(side_rows))
     late_hidden, late_slope, late_y, late_gate = first_product(late_m, late_d)
-    hidden = jnp.concatenate([early_hidden, late_hidden], axis=0)
-    grad_y = jnp.concatenate([early_y, late_y], axis=0)
+    hidden = jnp.concatenate([near_hidden, side_hidden, late_hidden], axis=0)
+    grad_y = jnp.concatenate([near_y, side_y, late_y], axis=0)
     out_leave = weight_gradient(0, 1, hidden, grad_y, BF16)
     out_pair = over_pair(out_leave)
     hidden = tied(hidden, out_leave)
     out_stay = weight_gradient(2, 1, hidden, grad_y, F32)
     late_pre, late_logit = second_product(tied(late_d, out_stay), late_hidden, late_slope, late_gate)
-    late_own, late_side, late_sums = row_gradients(late_m, late_pre, late_logit)
-    sums = early_sums + late_sums
+    late_sums, late_rows, late_side = row_gradients(
+        late_m.shape[0] // columns, late_m, late_pre, late_logit
+    )
+    sums = near_sums + side_sums + late_sums
     line = jnp.arange(-(-(experts + 1) // 8) * 8, dtype=jnp.int32)[:, None]
     total = jnp.where(line == own, sums[:1], jnp.where(line == experts, sums[1:2], 0.0))
     out_half = half_sum(out_stay, out_pair)
 
-    stage = (out_half, total, late_own, late_side)
-    out_half, total, late_side, hidden = tied((out_half, total, late_side, hidden), stage)
+    stage = (out_half, late_rows, late_side, total)
+    out_half, late_side, total, hidden = tied((out_half, late_side, total, hidden), stage)
     out_other = over_half(out_half)
     late_back = back_over_columns(by_turn(late_side))
-    rows_m = jnp.concatenate([early_m, late_m], axis=0)
-    grad_pre = jnp.concatenate([early_pre, late_pre], axis=0)
-    grad_pre = tied(grad_pre, (out_half, late_side))
-    in_leave = weight_gradient(0, 1, grad_pre, rows_m, BF16)
-    in_pair = over_pair(in_leave)
-    in_stay = weight_gradient(2, 1, tied(grad_pre, in_leave), rows_m, F32)
-    total = tied(total, in_stay)
+    total = pairwise(total, "dp", groups, 1)
+    pair_total = total
     bit = 2
     while bit < halves:
         total = pairwise(total, "expert", halves, bit)
         bit *= 2
-    total = pairwise(total, "dp", groups, 1)
     early_back, late_back = tied((early_back, late_back), total)
-    early_rows = add_rows(early_own, early_back)
-    late_rows = add_rows(late_own, late_back)
-    total = tied(total, (early_rows, late_rows))
-    total = pairwise(total, "expert", halves, 1)
+    early_rows = add_rows(near_rows, early_back)
+    moved = range(quarter, 2 * quarter)
+    send_back([steps[at] for at in moved], [early_rows[at] for at in moved])
+    late_rows = add_rows(late_rows, late_back)
+    total = pairwise(tied(total, (early_rows, late_rows)), "expert", halves, 1)
+    rows_m = jnp.concatenate([near_m, side_m, late_m], axis=0)
+    grad_pre = jnp.concatenate([near_pre, side_pre, late_pre], axis=0)
+    grad_pre = tied(grad_pre, pair_total)
+    in_leave = weight_gradient(0, 1, grad_pre, rows_m, BF16)
+    in_pair = over_pair(in_leave)
+    in_stay = weight_gradient(2, 1, tied(grad_pre, in_leave), rows_m, F32)
     hidden, grad_pre = tied((hidden, grad_pre), in_stay)
     out_rest = over_pair(weight_gradient(1, 1, hidden, grad_y, BF16))
     out_mine = weight_gradient(3, 1, hidden, grad_y, F32)
     in_rest = over_pair(weight_gradient(1, 1, grad_pre, rows_m, BF16))
     in_mine = weight_gradient(3, 1, grad_pre, rows_m, F32)
 
-    stage = (out_other, early_rows, late_rows, in_pair, in_stay, total)
-    out_other, early_rows, late_rows, in_pair, in_stay, total = tied(stage, stage)
+    moved_rows = [returned[steps[at]] for at in moved]
+    stage = (out_other, early_rows, late_rows, moved_rows, in_pair, in_stay, total)
+    out_other, early_rows, late_rows, moved_rows, in_pair, in_stay, total = tied(stage, stage)
+    for at, value in zip(moved, moved_rows):
+        returned[steps[at]] = value
     in_other = over_half(half_sum(in_stay, in_pair))
-    send_back(early, early_rows)
+    rest = [at for at in range(len(early)) if at not in moved]
+    send_back([steps[at] for at in rest], [early_rows[at] for at in rest])
     send_back(late, late_rows)
     bit = 2
     while bit < groups // 2:

time: 122 us -> 124 us (1.016)
  waiting for transfers between devices: 53.2 us -> 50.2 us
  Pallas kernels: 27.4 us -> 30.3 us
  starting transfers between devices: 30.2 us -> 32.2 us
    ppermute x6, waiting for transfers between devices: 45.8 us -> 23.6 us  [over_experts(): lax.ppermute(value, 'expert', [(i, (i + 2 * step) % halves) for i in rang...]
    ppermute x4, waiting for transfers between devices: 0.13 us -> 17.5 us  [over_columns(): lax.ppermute(value, 'dp', [(i, (i + 2 * step) % groups) for i in range(gr...]
    ppermute x6, starting transfers between devices: 8.87 us -> 13.1 us  [over_experts(): lax.ppermute(value, 'expert', [(i, (i + 2 * step) % halves) for i in rang...]
    pallas_call x23 -> x27, Pallas kernels: 27.4 us -> 30.3 us  [call(): pl.pallas_call(kernel, out_shape=outs, in_specs=specs or [VMEM] * len(arg...]
    ppermute x4, waiting for transfers between devices: 6.66 us -> 4.14 us  [pairwise(): lax.ppermute(value, name, [(i, i ^ bit) for i in range(size)])]
    ppermute x2, waiting for transfers between devices: 0.52 us -> 2.94 us  [back_over_columns(): lax.ppermute(value, 'dp', [(i, (i - 2 * step) % groups) for i in range(gr...]
    ppermute x4, waiting for transfers between devices: 0.01 us -> 1.98 us  [over_half(): return lax.ppermute(value, 'expert', [(i, i ^ 1) for i in range(halves)])]
    unnamed x24 -> x35, local copies, waits for them, and re-layouts: 6.52 us -> 7.19 us
  transfers between devices with their start and end apart: 29 -> 29, of which waited for: 11 -> 14; matrix products, arithmetic and copies ran while one was open for 2% -> 2% of each run, Pallas kernels for 16% -> 18%
where the time goes in v9:
time: 124 us; the launch traced here: 123 us
  waiting for transfers between devices  50.2 us (40%)
  starting transfers between devices  32.2 us (26%)
  Pallas kernels  30.3 us (24%)
  local copies, waits for them, and re-layouts  7.35 us (6%)
  other arithmetic  2.31 us (2%)
    pallas_call x27, Pallas kernels, call(): pl.pallas_call(kernel, out_shape=outs, in_specs=specs or [VMEM] * len(arg...  30.3 us
    ppermute x6, waiting for transfers between devices, over_experts(): lax.ppermute(value, 'expert', [(i, (i + 2 * step) % halves) for i in rang...  23.6 us
    ppermute x4, waiting for transfers between devices, over_columns(): lax.ppermute(value, 'dp', [(i, (i + 2 * step) % groups) for i in range(gr...  17.5 us
    ppermute x6, starting transfers between devices, over_experts(): lax.ppermute(value, 'expert', [(i, (i + 2 * step) % halves) for i in rang...  13.1 us
    unnamed x35, local copies, waits for them, and re-layouts  7.19 us
    ppermute x4, starting transfers between devices, over_half(): return lax.ppermute(value, 'expert', [(i, i ^ 1) for i in range(halves)])  6.21 us
    ppermute x4, starting transfers between devices, pairwise(): lax.ppermute(value, name, [(i, i ^ bit) for i in range(size)])  5.1 us
    ppermute x4, waiting for transfers between devices, pairwise(): lax.ppermute(value, name, [(i, i ^ bit) for i in range(size)])  4.14 us
  transfers between devices with their start and end apart: 29, of which 14 were waited for; matrix products, arithmetic and copies ran while one was open for 2% of the time, Pallas kernels for 18%

profile of v9, /device:TPU:0, one launch (start us, length us, event | category | flops | bytes accessed | tf_op | source)
XLA Modules:
  0.0 123.4 jit_solution(14648986623060217766)
XLA Ops:
  0.6 2.9 %dispatch.1 = (bf16[2,80,1280]{2,1,0:T(8,128)(2,1)}, bf16[2,80,1280]{2,1,0:T(8,128)(2,1)}, bf16[2,80,1280]{2,1,0:T(8,128)(2,1)}, bf16[2,80,1280]{2,1,0:T(8,128)(2,1)}) custom-call(bf16[128,1280]{1,0:T(8,128)(2,1)} %x_ref.1, f32[1280]{0:T(1024)} %gain_ref.1, s32[2,128]{1,0:T(2,128)} %bitcast.28, bf16[128,1280]{1,0:T(8,128)(2,1)} %d_ref.1), custom_call_target="tpu_custom_call" | custom-call | flops 209715200 | bytes 409600 | tf_op jit(solution)/shard_map/dispatch/pallas_call | solution.py:222
  4.0 2.6 %collective-permute-start.2 = (bf16[320,1280]{1,0:T(8,128)(2,1)}, bf16[320,1280]{1,0:T(8,128)(2,1)S(1)}, u32[]{:S(2)}, u32[]{:S(2)}) collective-permute-start(bf16[320,1280]{1,0:T(8,128)(2,1)} %bitcast.23), channel_id=1, source_target_pairs={{0,4},{4,0},{8,12},{12,8},{16,20},{20,16},{24,28},{28,24},{1,5},{5... | collective-permute-start | bytes 2457608 | tf_op jit(solution)/shard_map/ppermute | solution.py:246
  9.7 2.2 %collective-permute-start.1 = (bf16[2,80,1280]{2,1,0:T(8,128)(2,1)}, bf16[2,80,1280]{2,1,0:T(8,128)(2,1)S(1)}, u32[]{:S(2)}, u32[]{:S(2)}) collective-permute-start(bf16[2,80,1280]{2,1,0:T(8,128)(2,1)} %get-tuple-element.97), channel_id=1, source_target_pairs={{0,24},{4,28},{8,0},{12,4},{16,8},{20,12},{24,16},{28,20},{1,25},{... | collective-permute-start | bytes 1228808 | tf_op jit(solution)/shard_map/ppermute | solution.py:264
  12.0 6.4 %collective-permute-done.3.refs_0_ = bf16[2,80,1280]{2,1,0:T(8,128)(2,1)S(1)} collective-permute-done((bf16[2,80,1280]{2,1,0:T(8,128)(2,1)}, bf16[2,80,1280]{2,1,0:T(8,128)(2,1)S(1)}, u32[]{:S(2)}, u32[]{:S(2)}) %collective-permute-start.3) | collective-permute-done | bytes 409632 | tf_op jit(solution)/shard_map/ppermute | solution.py:253
  19.1 3.4 %collective-permute-done.refs_1_ = bf16[2,80,1280]{2,1,0:T(8,128)(2,1)S(1)} collective-permute-done((bf16[2,80,1280]{2,1,0:T(8,128)(2,1)}, bf16[2,80,1280]{2,1,0:T(8,128)(2,1)S(1)}, u32[]{:S(2)}, u32[]{:S(2)}) %collective-permute-start) | collective-permute-done | bytes 409632 | tf_op jit(solution)/shard_map/ppermute | solution.py:264
  22.5 7.1 %collective-permute-done.1.refs_2_ = bf16[2,80,1280]{2,1,0:T(8,128)(2,1)S(1)} collective-permute-done((bf16[2,80,1280]{2,1,0:T(8,128)(2,1)}, bf16[2,80,1280]{2,1,0:T(8,128)(2,1)S(1)}, u32[]{:S(2)}, u32[]{:S(2)}) %collective-permute-start.1) | collective-permute-done | bytes 409632 | tf_op jit(solution)/shard_map/ppermute | solution.py:264
  40.9 1.6 %gather.3 = (bf16[240,1280]{1,0:T(8,128)(2,1)S(1)}, bf16[240,1280]{1,0:T(8,128)(2,1)S(1)}) custom-call(bf16[2,80,1280]{2,1,0:T(8,128)(2,1)S(1)} %copy-done.6, bf16[2,80,1280]{2,1,0:T(8,128)(2,1)S(1)} %copy-done.8, bf16[2,80,1280]{2,1,0:T(8,128)(2,1)S(1)} %copy-done.10), custom_call_target="tpu_custom_call" | custom-call | tf_op jit(solution)/shard_map/gather/pallas_call | solution.py:222
  43.8 1.7 %first.3 = (bf16[240,1280]{1,0:T(8,128)(2,1)S(1)}, f32[240,1280]{1,0:T(8,128)S(1)}, bf16[240,1280]{1,0:T(8,128)(2,1)S(1)}, f32[240,128]{1,0:T(8,128)S(1)}) custom-call(bf16[240,1280]{1,0:T(8,128)(2,1)S(1)} %get-tuple-element.104.m_ref, bf16[240,1280]{1,0:T(8,128)(2,1)S(1)} %get-tuple-element.132.d_ref, bf16[1280,1280]{1,0:T(8,128)(2,1)S(1)} %join.2.first_ref, ...), custom_call_target="tpu_custom_call" | custom-call | flops 786432000 | bytes 1536000 | tf_op jit(solution)/shard_map/first/pallas_call | solution.py:222
  47.1 7.3 %collective-permute-done.8.refs_2_ = bf16[2,80,1280]{2,1,0:T(8,128)(2,1)S(1)} collective-permute-done((bf16[2,80,1280]{2,1,0:T(8,128)(2,1)}, bf16[2,80,1280]{2,1,0:T(8,128)(2,1)S(1)}, u32[]{:S(2)}, u32[]{:S(2)}) %collective-permute-start.8) | collective-permute-done | bytes 409632 | tf_op jit(solution)/shard_map/ppermute | solution.py:253
  54.3 2.4 %collective-permute-done.5.refs_0_ = bf16[2,80,1280]{2,1,0:T(8,128)(2,1)S(1)} collective-permute-done((bf16[2,80,1280]{2,1,0:T(8,128)(2,1)}, bf16[2,80,1280]{2,1,0:T(8,128)(2,1)S(1)}, u32[]{:S(2)}, u32[]{:S(2)}) %collective-permute-start.5) | collective-permute-done | bytes 409632 | tf_op jit(solution)/shard_map/ppermute | solution.py:264
  57.8 1.6 %gather.4 = (bf16[240,1280]{1,0:T(8,128)(2,1)S(1)}, bf16[240,1280]{1,0:T(8,128)(2,1)S(1)}) custom-call(bf16[2,80,1280]{2,1,0:T(8,128)(2,1)S(1)} %copy-done.5, bf16[2,80,1280]{2,1,0:T(8,128)(2,1)S(1)} %collective-permute-done.7.refs_1_, bf16[2,80,1280]{2,1,0:T(8,128)(2,1)S(1)} %collective-permute-done.8.refs_2_), custom_call_target="tpu_custom_call" | custom-call | tf_op jit(solution)/shard_map/gather/pallas_call | solution.py:222
  59.4 1.7 %first.4 = (bf16[240,1280]{1,0:T(8,128)(2,1)S(1)}, f32[240,1280]{1,0:T(8,128)S(1)}, bf16[240,1280]{1,0:T(8,128)(2,1)S(1)}, f32[240,128]{1,0:T(8,128)S(1)}) custom-call(bf16[240,1280]{1,0:T(8,128)(2,1)S(1)} %get-tuple-element.121.m_ref, bf16[240,1280]{1,0:T(8,128)(2,1)S(1)} %get-tuple-element.122.d_ref, bf16[1280,1280]{1,0:T(8,128)(2,1)S(1)} %join.2.first_ref, ...), custom_call_target="tpu_custom_call" | custom-call | flops 786432000 | bytes 1536000 | tf_op jit(solution)/shard_map/first/pallas_call | solution.py:222
  66.5 2.2 %collective-permute-done.10.refs_1_ = bf16[2,80,1280]{2,1,0:T(8,128)(2,1)S(1)} collective-permute-done((bf16[2,80,1280]{2,1,0:T(8,128)(2,1)S(1)}, bf16[2,80,1280]{2,1,0:T(8,128)(2,1)S(1)}, u32[]{:S(2)}, u32[]{:S(2)}) %collective-permute-start.10) | collective-permute-done | bytes 409632 | tf_op jit(solution)/shard_map/ppermute | solution.py:253
  84.0 3.1 %collective-permute-start.19 = (f32[8,1280]{1,0:T(8,128)S(1)}, f32[8,1280]{1,0:T(8,128)S(1)}, u32[]{:S(2)}, u32[]{:S(2)}) collective-permute-start(f32[8,1280]{1,0:T(8,128)S(1)} %add.38), channel_id=1, source_target_pairs={{0,16},{4,20},{8,24},{12,28},{16,0},{20,4},{24,8},{28,12},{1,17},{... | collective-permute-start | bytes 122888 | tf_op jit(solution)/shard_map/ppermute | solution.py:267
  87.9 2.2 %collective-permute-done.19 = f32[8,1280]{1,0:T(8,128)S(1)} collective-permute-done((f32[8,1280]{1,0:T(8,128)S(1)}, f32[8,1280]{1,0:T(8,128)S(1)}, u32[]{:S(2)}, u32[]{:S(2)}) %collective-permute-start.19) | collective-permute-done | bytes 40992 | tf_op jit(solution)/shard_map/ppermute | solution.py:267
  90.2 2.9 %collective-permute-done.16 = bf16[80,1280]{1,0:T(8,128)(2,1)S(1)} collective-permute-done((bf16[80,1280]{1,0:T(8,128)(2,1)S(1)}, bf16[80,1280]{1,0:T(8,128)(2,1)S(1)}, u32[]{:S(2)}, u32[]{:S(2)}) %collective-permute-start.16) | collective-permute-done | bytes 204832 | tf_op jit(solution)/shard_map/ppermute | solution.py:259
  93.2 2.9 %collective-permute-start.20 = (bf16[80,1280]{1,0:T(8,128)(2,1)S(1)}, bf16[80,1280]{1,0:T(8,128)(2,1)S(1)}, u32[]{:S(2)}, u32[]{:S(2)}) collective-permute-start(bf16[80,1280]{1,0:T(8,128)(2,1)S(1)} %slice.23), channel_id=1, source_target_pairs={{0,24},{4,28},{8,0},{12,4},{16,8},{20,12},{24,16},{28,20},{1,25},{... | collective-permute-start | bytes 614408 | tf_op jit(solution)/shard_map/ppermute | solution.py:264
  96.2 1.6 %collective-permute-start.22 = (f32[8,1280]{1,0:T(8,128)S(1)}, f32[8,1280]{1,0:T(8,128)S(1)}, u32[]{:S(2)}, u32[]{:S(2)}) collective-permute-start(f32[8,1280]{1,0:T(8,128)S(1)} %add.39), channel_id=1, source_target_pairs={{0,4},{4,0},{8,12},{12,8},{16,20},{20,16},{24,28},{28,24},{1,5},{5... | collective-permute-start | bytes 122888 | tf_op jit(solution)/shard_map/ppermute | solution.py:267
  98.7 1.6 %collective-permute-done.22 = f32[8,1280]{1,0:T(8,128)S(1)} collective-permute-done((f32[8,1280]{1,0:T(8,128)S(1)}, f32[8,1280]{1,0:T(8,128)S(1)}, u32[]{:S(2)}, u32[]{:S(2)}) %collective-permute-start.22) | collective-permute-done | bytes 40992 | tf_op jit(solution)/shard_map/ppermute | solution.py:267
  102.2 4.8 %collective-permute-start.23 = (bf16[80,1280]{1,0:T(8,128)(2,1)S(1)}, bf16[80,1280]{1,0:T(8,128)(2,1)S(1)}, u32[]{:S(2)}, u32[]{:S(2)}) collective-permute-start(bf16[80,1280]{1,0:T(8,128)(2,1)S(1)} %bitcast.31), channel_id=1, source_target_pairs={{0,16},{4,20},{8,24},{12,28},{16,0},{20,4},{24,8},{28,12},{1,17},{... | collective-permute-start | bytes 614408 | tf_op jit(solution)/shard_map/ppermute | solution.py:264
  108.6 3.9 %collective-permute-done.24 = bf16[80,1280]{1,0:T(8,128)(2,1)S(1)} collective-permute-done((bf16[80,1280]{1,0:T(8,128)(2,1)S(1)}, bf16[80,1280]{1,0:T(8,128)(2,1)S(1)}, u32[]{:S(2)}, u32[]{:S(2)}) %collective-permute-start.24) | collective-permute-done | bytes 204832 | tf_op jit(solution)/shard_map/ppermute | solution.py:264
  112.5 6.8 %collective-permute-done.23 = bf16[80,1280]{1,0:T(8,128)(2,1)S(1)} collective-permute-done((bf16[80,1280]{1,0:T(8,128)(2,1)S(1)}, bf16[80,1280]{1,0:T(8,128)(2,1)S(1)}, u32[]{:S(2)}, u32[]{:S(2)}) %collective-permute-start.23) | collective-permute-done | bytes 204832 | tf_op jit(solution)/shard_map/ppermute | solution.py:264
  119.3 2.0 %collective-permute-done.25.other_ref = bf16[320,1280]{1,0:T(8,128)(2,1)S(1)} collective-permute-done((bf16[320,1280]{1,0:T(8,128)(2,1)S(1)}, bf16[320,1280]{1,0:T(8,128)(2,1)S(1)}, u32[]{:S(2)}, u32[]{:S(2)}) %collective-permute-start.25) | collective-permute-done | bytes 819232 | tf_op jit(solution)/shard_map/ppermute | solution.py:246
  121.4 2.0 %finish.1 = (bf16[128,1280]{1,0:T(8,128)(2,1)}, bf16[320,1280]{1,0:T(8,128)(2,1)}, f32[4,1280]{1,0:T(4,128)}, f32[1280]{0:T(1024)}) custom-call(f32[128,1280]{1,0:T(8,128)S(1)} %copy-done.3, f32[128,128]{1,0:T(8,128)S(1)} %get-tuple-element.115.deviation_ref, bf16[320,128]{1,0:T(8,128)(2,1)S(1)} %get-tuple-element.116.places_ref, f32[1280]{0:T(1024)S(1)} %copy-done.13, ...), custom_call_target="tpu_custom_call" | custom-call | tf_op jit(solution)/shard_map/finish/pallas_call | solution.py:222
  (115 shorter events, 45.3 us)
Async XLA Ops:
  3.5 26.2 %collective-permute-start.4 = (bf16[320,1280]{1,0:T(8,128)(2,1)}, bf16[320,1280]{1,0:T(8,128)(2,1)S(1)}, u32[]{:S(2)}, u32[]{:S(2)}) collective-permute-start(bf16[320,1280]{1,0:T(8,128)(2,1)} %bitcast.22), channel_id=1, source_target_pairs={{0,1},{1,0},{2,3},{3,2},{4,5},{5,4},{6,7},{7,6},{8,9},{9,8},{10,11... | collective-permute-start | bytes 2457608 | tf_op jit(solution)/shard_map/ppermute | solution.py:249
  4.0 25.6 %collective-permute-start.2 = (bf16[320,1280]{1,0:T(8,128)(2,1)}, bf16[320,1280]{1,0:T(8,128)(2,1)S(1)}, u32[]{:S(2)}, u32[]{:S(2)}) collective-permute-start(bf16[320,1280]{1,0:T(8,128)(2,1)} %bitcast.23), channel_id=1, source_target_pairs={{0,4},{4,0},{8,12},{12,8},{16,20},{20,16},{24,28},{28,24},{1,5},{5... | collective-permute-start | bytes 2457608 | tf_op jit(solution)/shard_map/ppermute | solution.py:246
  6.6 11.7 %collective-permute-start.3 = (bf16[2,80,1280]{2,1,0:T(8,128)(2,1)}, bf16[2,80,1280]{2,1,0:T(8,128)(2,1)S(1)}, u32[]{:S(2)}, u32[]{:S(2)}) collective-permute-start(bf16[2,80,1280]{2,1,0:T(8,128)(2,1)} %get-tuple-element.103.refs_0_), channel_id=1, source_target_pairs={{0,2},{1,3},{2,0},{3,1},{4,6},{5,7},{6,4},{7,5},{8,10},{9,11},{10,... | collective-permute-start | bytes 1228808 | tf_op jit(solution)/shard_map/ppermute | solution.py:253
  8.1 14.4 %collective-permute-start = (bf16[2,80,1280]{2,1,0:T(8,128)(2,1)}, bf16[2,80,1280]{2,1,0:T(8,128)(2,1)S(1)}, u32[]{:S(2)}, u32[]{:S(2)}) collective-permute-start(bf16[2,80,1280]{2,1,0:T(8,128)(2,1)} %get-tuple-element.96), channel_id=1, source_target_pairs={{0,8},{4,12},{8,16},{12,20},{16,24},{20,28},{24,0},{28,4},{1,9},{5... | collective-permute-start | bytes 1228808 | tf_op jit(solution)/shard_map/ppermute | solution.py:264
  9.7 20.0 %collective-permute-start.1 = (bf16[2,80,1280]{2,1,0:T(8,128)(2,1)}, bf16[2,80,1280]{2,1,0:T(8,128)(2,1)S(1)}, u32[]{:S(2)}, u32[]{:S(2)}) collective-permute-start(bf16[2,80,1280]{2,1,0:T(8,128)(2,1)} %get-tuple-element.97), channel_id=1, source_target_pairs={{0,24},{4,28},{8,0},{12,4},{16,8},{20,12},{24,16},{28,20},{1,25},{... | collective-permute-start | bytes 1228808 | tf_op jit(solution)/shard_map/ppermute | solution.py:264
  29.7 12.9 %collective-permute-start.9 = (bf16[320,1280]{1,0:T(8,128)(2,1)S(1)}, bf16[320,1280]{1,0:T(8,128)(2,1)}, u32[]{:S(2)}, u32[]{:S(2)}) collective-permute-start(bf16[320,1280]{1,0:T(8,128)(2,1)S(1)} %collective-permute-done.2.refs_2_), channel_id=1, source_target_pairs={{0,1},{1,0},{2,3},{3,2},{4,5},{5,4},{6,7},{7,6},{8,9},{9,8},{10,11... | collective-permute-start | bytes 2457608 | tf_op jit(solution)/shard_map/ppermute | solution.py:249
  30.4 26.3 %collective-permute-start.6 = (bf16[320,1280]{1,0:T(8,128)(2,1)}, bf16[320,1280]{1,0:T(8,128)(2,1)S(1)}, u32[]{:S(2)}, u32[]{:S(2)}) collective-permute-start(bf16[320,1280]{1,0:T(8,128)(2,1)} %bitcast.25), channel_id=1, source_target_pairs={{0,4},{4,0},{8,12},{12,8},{16,20},{20,16},{24,28},{28,24},{1,5},{5... | collective-permute-start | bytes 2457608 | tf_op jit(solution)/shard_map/ppermute | solution.py:246
  34.4 12.6 %collective-permute-start.7 = (bf16[2,80,1280]{2,1,0:T(8,128)(2,1)}, bf16[2,80,1280]{2,1,0:T(8,128)(2,1)S(1)}, u32[]{:S(2)}, u32[]{:S(2)}) collective-permute-start(bf16[2,80,1280]{2,1,0:T(8,128)(2,1)} %copy-done.7), channel_id=1, source_target_pairs={{0,2},{1,3},{2,0},{3,1},{4,6},{5,7},{6,4},{7,5},{8,10},{9,11},{10,... | collective-permute-start | bytes 1228808 | tf_op jit(solution)/shard_map/ppermute | solution.py:253
  35.0 19.4 %collective-permute-start.8 = (bf16[2,80,1280]{2,1,0:T(8,128)(2,1)}, bf16[2,80,1280]{2,1,0:T(8,128)(2,1)S(1)}, u32[]{:S(2)}, u32[]{:S(2)}) collective-permute-start(bf16[2,80,1280]{2,1,0:T(8,128)(2,1)} %copy-done.9), channel_id=1, source_target_pairs={{0,2},{1,3},{2,0},{3,1},{4,6},{5,7},{6,4},{7,5},{8,10},{9,11},{10,... | collective-permute-start | bytes 1228808 | tf_op jit(solution)/shard_map/ppermute | solution.py:253
  36.5 20.2 %collective-permute-start.5 = (bf16[2,80,1280]{2,1,0:T(8,128)(2,1)}, bf16[2,80,1280]{2,1,0:T(8,128)(2,1)S(1)}, u32[]{:S(2)}, u32[]{:S(2)}) collective-permute-start(bf16[2,80,1280]{2,1,0:T(8,128)(2,1)} %get-tuple-element.99), channel_id=1, source_target_pairs={{0,16},{4,20},{8,24},{12,28},{16,0},{20,4},{24,8},{28,12},{1,17},{... | collective-permute-start | bytes 1228808 | tf_op jit(solution)/shard_map/ppermute | solution.py:264
  56.7 4.6 %collective-permute-start.12 = (bf16[320,1280]{1,0:T(8,128)(2,1)S(1)}, bf16[320,1280]{1,0:T(8,128)(2,1)S(1)}, u32[]{:S(2)}, u32[]{:S(2)}) collective-permute-start(bf16[320,1280]{1,0:T(8,128)(2,1)S(1)} %bitcast.26), channel_id=1, source_target_pairs={{0,1},{1,0},{2,3},{3,2},{4,5},{5,4},{6,7},{7,6},{8,9},{9,8},{10,11... | collective-permute-start | bytes 2457608 | tf_op jit(solution)/shard_map/ppermute | solution.py:249
  57.2 11.4 %collective-permute-start.10 = (bf16[2,80,1280]{2,1,0:T(8,128)(2,1)S(1)}, bf16[2,80,1280]{2,1,0:T(8,128)(2,1)S(1)}, u32[]{:S(2)}, u32[]{:S(2)}) collective-permute-start(bf16[2,80,1280]{2,1,0:T(8,128)(2,1)S(1)} %collective-permute-done.5.refs_0_), channel_id=1, source_target_pairs={{0,2},{1,3},{2,0},{3,1},{4,6},{5,7},{6,4},{7,5},{8,10},{9,11},{10,... | collective-permute-start | bytes 1228808 | tf_op jit(solution)/shard_map/ppermute | solution.py:253
  72.5 17.7 %collective-permute-start.15 = (bf16[240,1280]{1,0:T(8,128)(2,1)S(1)}, bf16[240,1280]{1,0:T(8,128)(2,1)S(1)}, u32[]{:S(2)}, u32[]{:S(2)}) collective-permute-start(bf16[240,1280]{1,0:T(8,128)(2,1)S(1)} %get-tuple-element.131), channel_id=1, source_target_pairs={{0,2},{1,3},{2,0},{3,1},{4,6},{5,7},{6,4},{7,5},{8,10},{9,11},{10,... | collective-permute-start | bytes 1843208 | tf_op jit(solution)/shard_map/ppermute | solution.py:259
  76.8 16.3 %collective-permute-start.16 = (bf16[80,1280]{1,0:T(8,128)(2,1)S(1)}, bf16[80,1280]{1,0:T(8,128)(2,1)S(1)}, u32[]{:S(2)}, u32[]{:S(2)}) collective-permute-start(bf16[80,1280]{1,0:T(8,128)(2,1)S(1)} %get-tuple-element.158), channel_id=1, source_target_pairs={{0,2},{1,3},{2,0},{3,1},{4,6},{5,7},{6,4},{7,5},{8,10},{9,11},{10,... | collective-permute-start | bytes 614408 | tf_op jit(solution)/shard_map/ppermute | solution.py:259
  78.4 22.0 %collective-permute-start.14 = (bf16[320,1280]{1,0:T(8,128)(2,1)S(1)}, bf16[320,1280]{1,0:T(8,128)(2,1)S(1)}, u32[]{:S(2)}, u32[]{:S(2)}) collective-permute-start(bf16[320,1280]{1,0:T(8,128)(2,1)S(1)} %half.2), channel_id=1, source_target_pairs={{0,4},{4,0},{8,12},{12,8},{16,20},{20,16},{24,28},{28,24},{1,5},{5... | collective-permute-start | bytes 2457608 | tf_op jit(solution)/shard_map/ppermute | solution.py:246
  81.0 19.3 %collective-permute-start.21 = (bf16[320,1280]{1,0:T(8,128)(2,1)S(1)}, bf16[320,1280]{1,0:T(8,128)(2,1)S(1)}, u32[]{:S(2)}, u32[]{:S(2)}) collective-permute-start(bf16[320,1280]{1,0:T(8,128)(2,1)S(1)} %weights.10), channel_id=1, source_target_pairs={{0,1},{1,0},{2,3},{3,2},{4,5},{5,4},{6,7},{7,6},{8,9},{9,8},{10,11... | collective-permute-start | bytes 2457608 | tf_op jit(solution)/shard_map/ppermute | solution.py:249
  84.0 6.2 %collective-permute-start.19 = (f32[8,1280]{1,0:T(8,128)S(1)}, f32[8,1280]{1,0:T(8,128)S(1)}, u32[]{:S(2)}, u32[]{:S(2)}) collective-permute-start(f32[8,1280]{1,0:T(8,128)S(1)} %add.38), channel_id=1, source_target_pairs={{0,16},{4,20},{8,24},{12,28},{16,0},{20,4},{24,8},{28,12},{1,17},{... | collective-permute-start | bytes 122888 | tf_op jit(solution)/shard_map/ppermute | solution.py:267
  90.2 16.9 %collective-permute-start.26 = (bf16[320,1280]{1,0:T(8,128)(2,1)S(1)}, bf16[320,1280]{1,0:T(8,128)(2,1)S(1)}, u32[]{:S(2)}, u32[]{:S(2)}) collective-permute-start(bf16[320,1280]{1,0:T(8,128)(2,1)S(1)} %weights.13), channel_id=1, source_target_pairs={{0,1},{1,0},{2,3},{3,2},{4,5},{5,4},{6,7},{7,6},{8,9},{9,8},{10,11... | collective-permute-start | bytes 2457608 | tf_op jit(solution)/shard_map/ppermute | solution.py:249
  93.2 7.1 %collective-permute-start.20 = (bf16[80,1280]{1,0:T(8,128)(2,1)S(1)}, bf16[80,1280]{1,0:T(8,128)(2,1)S(1)}, u32[]{:S(2)}, u32[]{:S(2)}) collective-permute-start(bf16[80,1280]{1,0:T(8,128)(2,1)S(1)} %slice.23), channel_id=1, source_target_pairs={{0,24},{4,28},{8,0},{12,4},{16,8},{20,12},{24,16},{28,20},{1,25},{... | collective-permute-start | bytes 614408 | tf_op jit(solution)/shard_map/ppermute | solution.py:264
  100.3 21.1 %collective-permute-start.27 = (bf16[320,1280]{1,0:T(8,128)(2,1)S(1)}, bf16[320,1280]{1,0:T(8,128)(2,1)S(1)}, u32[]{:S(2)}, u32[]{:S(2)}) collective-permute-start(bf16[320,1280]{1,0:T(8,128)(2,1)S(1)} %weights.15), channel_id=1, source_target_pairs={{0,1},{1,0},{2,3},{3,2},{4,5},{5,4},{6,7},{7,6},{8,9},{9,8},{10,11... | collective-permute-start | bytes 2457608 | tf_op jit(solution)/shard_map/ppermute | solution.py:249
  100.6 20.7 %collective-permute-start.25 = (bf16[320,1280]{1,0:T(8,128)(2,1)S(1)}, bf16[320,1280]{1,0:T(8,128)(2,1)S(1)}, u32[]{:S(2)}, u32[]{:S(2)}) collective-permute-start(bf16[320,1280]{1,0:T(8,128)(2,1)S(1)} %half.3), channel_id=1, source_target_pairs={{0,4},{4,0},{8,12},{12,8},{16,20},{20,16},{24,28},{28,24},{1,5},{5... | collective-permute-start | bytes 2457608 | tf_op jit(solution)/shard_map/ppermute | solution.py:246
  102.2 10.3 %collective-permute-start.24 = (bf16[80,1280]{1,0:T(8,128)(2,1)S(1)}, bf16[80,1280]{1,0:T(8,128)(2,1)S(1)}, u32[]{:S(2)}, u32[]{:S(2)}) collective-permute-start(bf16[80,1280]{1,0:T(8,128)(2,1)S(1)} %get-tuple-element.185), channel_id=1, source_target_pairs={{0,8},{4,12},{8,16},{12,20},{16,24},{20,28},{24,0},{28,4},{1,9},{5... | collective-permute-start | bytes 614408 | tf_op jit(solution)/shard_map/ppermute | solution.py:264
  102.2 17.0 %collective-permute-start.23 = (bf16[80,1280]{1,0:T(8,128)(2,1)S(1)}, bf16[80,1280]{1,0:T(8,128)(2,1)S(1)}, u32[]{:S(2)}, u32[]{:S(2)}) collective-permute-start(bf16[80,1280]{1,0:T(8,128)(2,1)S(1)} %bitcast.31), channel_id=1, source_target_pairs={{0,16},{4,20},{8,24},{12,28},{16,0},{20,4},{24,8},{28,12},{1,17},{... | collective-permute-start | bytes 614408 | tf_op jit(solution)/shard_map/ppermute | solution.py:264
  107.1 14.3 %collective-permute-start.28 = (f32[8,1280]{1,0:T(8,128)S(1)}, f32[8,1280]{1,0:T(8,128)S(1)}, u32[]{:S(2)}, u32[]{:S(2)}) collective-permute-start(f32[8,1280]{1,0:T(8,128)S(1)} %add.42.total_ref), channel_id=1, source_target_pairs={{0,2},{1,3},{2,0},{3,1},{4,6},{5,7},{6,4},{7,5},{8,10},{9,11},{10,... | collective-permute-start | bytes 122888 | tf_op jit(solution)/shard_map/ppermute | solution.py:518
  (20 other events, 141.4 us)

commit v10 on v8

--- a/solution.py
+++ b/solution.py
@@ -1,5 +1,6 @@
 import functools
 import math
+import random
 
 import jax
 import jax.numpy as jnp
@@ -9,6 +10,7 @@
 from jax.sharding import PartitionSpec as P
 
 F32 = jnp.float32
+ORDER = 14
 BF16 = jnp.bfloat16
 VMEM = pl.BlockSpec(memory_space=pltpu.VMEM)
 ANY = pl.BlockSpec(memory_space=pl.ANY)
@@ -104,11 +106,13 @@
 
 def finish_kernel(
     norm_ref, deviation_ref, places_ref, gain_ref, d_ref, rows_ref, stay_ref, pair_ref, other_ref,
-    total_ref, last_ref, out_ref, sum_ref, router_ref, gain_grad_ref
+    total_ref, last_ref, out_hbm, sum_hbm, router_ref, gain_grad_ref, out_ref, sum_ref, sems
 ):
     sum_ref[...] = (
         stay_ref[...] + pair_ref[...].astype(F32) + other_ref[...].astype(F32)
     ).astype(BF16)
+    sum_copy = pltpu.make_async_copy(sum_ref, sum_hbm, sems.at[0])
+    sum_copy.start()
     normalized_rows = norm_ref[...]
     scaled_rows = dot(places_ref[...], rows_ref[...], 0, 0) * gain_ref[...][None, :]
     mean_first_term = jnp.mean(scaled_rows, axis=1, keepdims=True)
@@ -117,10 +121,14 @@
         scaled_rows - mean_first_term - normalized_rows * mean_second_term
     )
     out_ref[...] = (d_ref[...].astype(F32) + norm_backward).astype(BF16)
+    out_copy = pltpu.make_async_copy(out_ref, out_hbm, sems.at[1])
+    out_copy.start()
     experts = router_ref.shape[0]
     total = total_ref[...] + last_ref[...]
     router_ref[...] = total[:experts]
     gain_grad_ref[...] = jnp.sum(total[experts:], axis=0) / gain_ref[...]
+    sum_copy.wait()
+    out_copy.wait()
 
 
 def first_kernel(m_ref, d_ref, first_ref, router_ref, hidden_ref, slope_ref, y_ref, gate_ref):
@@ -182,32 +190,29 @@
         at += ref.shape[0]
 
 
-def gather_kernel(*refs):
-    rows = refs[0].shape[1]
-    for at, ref in enumerate(refs[:-2]):
-        refs[-2][at * rows : (at + 1) * rows, :] = ref[0]
-        refs[-1][at * rows : (at + 1) * rows, :] = ref[1]
-
-
 def half_kernel(stay_ref, pair_ref, out_ref):
     out_ref[...] = (stay_ref[...] + pair_ref[...].astype(F32)).astype(BF16)
 
 
 def tied(values, after):
-    held, _ = lax.optimization_barrier((values, after))
-    return held
+    leaves, tree = jax.tree.flatten(values)
+    operands = {id(leaf): leaf for leaf in leaves + jax.tree.leaves(after)}
+    keys = list(operands)
+    random.Random(ORDER + len(keys)).shuffle(keys)
+    held = dict(zip(keys, lax.optimization_barrier([operands[key] for key in keys])))
+    return jax.tree.unflatten(tree, [held[id(leaf)] for leaf in leaves])
 
 
 def shape(kind, *sizes):
     return jax.ShapeDtypeStruct(sizes, kind)
 
 
-def call(kernel, name, outs, args, flops=0, specs=None, scratch=(), mebibytes=18):
+def call(kernel, name, outs, args, flops=0, specs=None, out_specs=None, scratch=(), mebibytes=18):
     return pl.pallas_call(
         kernel,
         out_shape=outs,
         in_specs=specs or [VMEM] * len(args),
-        out_specs=jax.tree.map(lambda _: VMEM, outs),
+        out_specs=out_specs or jax.tree.map(lambda _: VMEM, outs),
         scratch_shapes=list(scratch),
         compiler_params=pltpu.CompilerParams(vmem_limit_bytes=mebibytes * 2**20),
         cost_estimate=pl.CostEstimate(flops=flops, bytes_accessed=flops // 512, transcendentals=0),
@@ -341,9 +346,6 @@
         pieces = [near[step] for step in chosen]
         for turn in range(columns - 1):
             pieces = pieces + [side[step][turn] for step in chosen]
-        if capacity % 16 == 0:
-            outs = [shape(BF16, len(pieces) * capacity, width)] * 2
-            return call(gather_kernel, "gather", outs, pieces)
         return (
             jnp.concatenate([piece[0] for piece in pieces], axis=0),
             jnp.concatenate([piece[1] for piece in pieces], axis=0),
@@ -443,19 +445,18 @@
     stage = (out_half, total, late_own, late_side)
     out_half, total, late_side, hidden = tied((out_half, total, late_side, hidden), stage)
     out_other = over_half(out_half)
-    late_back = back_over_columns(by_turn(late_side))
     rows_m = jnp.concatenate([early_m, late_m], axis=0)
     grad_pre = jnp.concatenate([early_pre, late_pre], axis=0)
-    grad_pre = tied(grad_pre, (out_half, late_side))
-    in_leave = weight_gradient(0, 1, grad_pre, rows_m, BF16)
-    in_pair = over_pair(in_leave)
-    in_stay = weight_gradient(2, 1, tied(grad_pre, in_leave), rows_m, F32)
-    total = tied(total, in_stay)
+    total = pairwise(total, "dp", groups, 1)
+    grad_pre, late_side = tied((grad_pre, late_side), total)
     bit = 2
     while bit < halves:
         total = pairwise(total, "expert", halves, bit)
         bit *= 2
-    total = pairwise(total, "dp", groups, 1)
+    late_back = back_over_columns(by_turn(late_side))
+    in_leave = weight_gradient(0, 1, grad_pre, rows_m, BF16)
+    in_pair = over_pair(in_leave)
+    in_stay = weight_gradient(2, 1, tied(grad_pre, in_leave), rows_m, F32)
     early_back, late_back = tied((early_back, late_back), total)
     early_rows = add_rows(early_own, early_back)
     late_rows = add_rows(late_own, late_back)
@@ -503,6 +504,12 @@
             total,
             last,
         ),
+        out_specs=[ANY, ANY, VMEM, VMEM],
+        scratch=[
+            pltpu.VMEM((tokens, width), BF16),
+            pltpu.VMEM((units, width), BF16),
+            pltpu.SemaphoreType.DMA((2,)),
+        ],
     )
     return (input_grad, grad_in.T[None], grad_out, grad_router.T, grad_gain)
 

time: 122 us -> 116 us (0.951)
  Pallas kernels: 27.4 us -> 24.6 us
  local copies, waits for them, and re-layouts: 6.68 us -> 4.46 us
  waiting for transfers between devices: 53.2 us -> 54.9 us
  starting transfers between devices: 30.2 us -> 28.6 us
    ppermute x6, waiting for transfers between devices: 45.8 us -> 39.8 us  [over_experts(): lax.ppermute(value, 'expert', [(i, (i + 2 * step) % halves) for i in rang...]
    ppermute x4, waiting for transfers between devices: 0.01 us -> 5.73 us  [over_half(): return lax.ppermute(value, 'expert', [(i, i ^ 1) for i in range(halves)])]
    pallas_call x23 -> x21, Pallas kernels: 27.4 us -> 24.6 us  [call(): pl.pallas_call(kernel, out_shape=outs, in_specs=specs or [VMEM] * len(arg...]
    unnamed x24 -> x20, local copies, waits for them, and re-layouts: 6.52 us -> 4.26 us
    ppermute x4, waiting for transfers between devices: 6.66 us -> 8.61 us  [pairwise(): lax.ppermute(value, name, [(i, i ^ bit) for i in range(size)])]
    ppermute x4, starting transfers between devices: 6.63 us -> 4.69 us  [over_half(): return lax.ppermute(value, 'expert', [(i, i ^ 1) for i in range(halves)])]
  transfers between devices with their start and end apart: 29 -> 29, of which waited for: 11 -> 12; matrix products, arithmetic and copies ran while one was open for 2% -> 4% of each run, Pallas kernels for 16% -> 16%
where the time goes in v10:
time: 116 us
  waiting for transfers between devices  54.9 us (47%)
  starting transfers between devices  28.6 us (25%)
  Pallas kernels  24.6 us (21%)
  local copies, waits for them, and re-layouts  4.46 us (4%)
  other arithmetic  2.37 us (2%)
  between operations  1.2 us (1%)
    ppermute x6, waiting for transfers between devices, over_experts(): lax.ppermute(value, 'expert', [(i, (i + 2 * step) % halves) for i in rang...  39.8 us
    pallas_call x21, Pallas kernels, call(): pl.pallas_call(kernel, out_shape=outs, in_specs=specs or [VMEM] * len(arg...  24.6 us
    ppermute x6, starting transfers between devices, over_experts(): lax.ppermute(value, 'expert', [(i, (i + 2 * step) % halves) for i in rang...  9.25 us
    ppermute x4, waiting for transfers between devices, pairwise(): lax.ppermute(value, name, [(i, i ^ bit) for i in range(size)])  8.61 us
    ppermute x4, waiting for transfers between devices, over_half(): return lax.ppermute(value, 'expert', [(i, i ^ 1) for i in range(halves)])  5.73 us
    ppermute x4, starting transfers between devices, over_columns(): lax.ppermute(value, 'dp', [(i, (i + 2 * step) % groups) for i in range(gr...  5.01 us
    ppermute x4, starting transfers between devices, pairwise(): lax.ppermute(value, name, [(i, i ^ bit) for i in range(size)])  4.85 us
    ppermute x4, starting transfers between devices, over_half(): return lax.ppermute(value, 'expert', [(i, i ^ 1) for i in range(halves)])  4.69 us
  transfers between devices with their start and end apart: 29, of which 12 were waited for; matrix products, arithmetic and copies ran while one was open for 4% of the time, Pallas kernels for 16%

profile of v10, /device:TPU:0, one launch (start us, length us, event | category | flops | bytes accessed | tf_op | source)
XLA Modules:
  0.0 116.1 jit_solution(6970775143896774364)
XLA Ops:
  0.6 2.8 %dispatch.1 = (bf16[2,80,1280]{2,1,0:T(8,128)(2,1)}, bf16[2,80,1280]{2,1,0:T(8,128)(2,1)}, bf16[2,80,1280]{2,1,0:T(8,128)(2,1)}, bf16[2,80,1280]{2,1,0:T(8,128)(2,1)}) custom-call(bf16[128,1280]{1,0:T(8,128)(2,1)} %x_hbm.1, f32[1280]{0:T(1024)} %gain_ref.1, s32[2,128]{1,0:T(2,128)} %bitcast.72, bf16[128,1280]{1,0:T(8,128)(2,1)} %d_ref.1), custom_call_target="tpu_custom_call" | custom-call | flops 209715200 | bytes 409600 | tf_op jit(solution)/shard_map/dispatch/pallas_call | solution.py:211
  3.4 3.0 %collective-permute-start.2 = (bf16[320,1280]{1,0:T(8,128)(2,1)}, bf16[320,1280]{1,0:T(8,128)(2,1)S(1)}, u32[]{:S(2)}, u32[]{:S(2)}) collective-permute-start(bf16[320,1280]{1,0:T(8,128)(2,1)} %bitcast.66), channel_id=1, source_target_pairs={{0,4},{4,0},{8,12},{12,8},{16,20},{20,16},{24,28},{28,24},{1,5},{5... | collective-permute-start | bytes 2457608 | tf_op jit(solution)/shard_map/ppermute | solution.py:235
  6.5 1.6 %collective-permute-start.3 = (bf16[2,80,1280]{2,1,0:T(8,128)(2,1)}, bf16[2,80,1280]{2,1,0:T(8,128)(2,1)S(1)}, u32[]{:S(2)}, u32[]{:S(2)}) collective-permute-start(bf16[2,80,1280]{2,1,0:T(8,128)(2,1)} %get-tuple-element.80), channel_id=1, source_target_pairs={{0,8},{4,12},{8,16},{12,20},{16,24},{20,28},{24,0},{28,4},{1,9},{5... | collective-permute-start | bytes 1228808 | tf_op jit(solution)/shard_map/ppermute | solution.py:253
  8.0 2.2 %collective-permute-start.4 = (bf16[2,80,1280]{2,1,0:T(8,128)(2,1)}, bf16[2,80,1280]{2,1,0:T(8,128)(2,1)S(1)}, u32[]{:S(2)}, u32[]{:S(2)}) collective-permute-start(bf16[2,80,1280]{2,1,0:T(8,128)(2,1)} %get-tuple-element.81), channel_id=1, source_target_pairs={{0,24},{4,28},{8,0},{12,4},{16,8},{20,12},{24,16},{28,20},{1,25},{... | collective-permute-start | bytes 1228808 | tf_op jit(solution)/shard_map/ppermute | solution.py:253
  10.3 1.5 %collective-permute-start = (bf16[2,80,1280]{2,1,0:T(8,128)(2,1)}, bf16[2,80,1280]{2,1,0:T(8,128)(2,1)}, u32[]{:S(2)}, u32[]{:S(2)}) collective-permute-start(bf16[2,80,1280]{2,1,0:T(8,128)(2,1)} %get-tuple-element.93), channel_id=1, source_target_pairs={{0,2},{1,3},{2,0},{3,1},{4,6},{5,7},{6,4},{7,5},{8,10},{9,11},{10,... | collective-permute-start | bytes 1228808 | tf_op jit(solution)/shard_map/ppermute | solution.py:242
  14.5 6.3 %collective-permute-done.3 = bf16[2,80,1280]{2,1,0:T(8,128)(2,1)S(1)} collective-permute-done((bf16[2,80,1280]{2,1,0:T(8,128)(2,1)}, bf16[2,80,1280]{2,1,0:T(8,128)(2,1)S(1)}, u32[]{:S(2)}, u32[]{:S(2)}) %collective-permute-start.3) | collective-permute-done | bytes 409632 | tf_op jit(solution)/shard_map/ppermute | solution.py:253
  20.8 7.9 %collective-permute-done.4 = bf16[2,80,1280]{2,1,0:T(8,128)(2,1)S(1)} collective-permute-done((bf16[2,80,1280]{2,1,0:T(8,128)(2,1)}, bf16[2,80,1280]{2,1,0:T(8,128)(2,1)S(1)}, u32[]{:S(2)}, u32[]{:S(2)}) %collective-permute-start.4) | collective-permute-done | bytes 409632 | tf_op jit(solution)/shard_map/ppermute | solution.py:253
  30.0 1.5 %collective-permute-start.6 = (bf16[2,80,1280]{2,1,0:T(8,128)(2,1)S(1)}, bf16[2,80,1280]{2,1,0:T(8,128)(2,1)S(1)}, u32[]{:S(2)}, u32[]{:S(2)}) collective-permute-start(bf16[2,80,1280]{2,1,0:T(8,128)(2,1)S(1)} %collective-permute-done.3), channel_id=1, source_target_pairs={{0,2},{1,3},{2,0},{3,1},{4,6},{5,7},{6,4},{7,5},{8,10},{9,11},{10,... | collective-permute-start | bytes 1228808 | tf_op jit(solution)/shard_map/ppermute | solution.py:242
  34.9 14.5 %collective-permute-done.8 = bf16[2,80,1280]{2,1,0:T(8,128)(2,1)S(1)} collective-permute-done((bf16[2,80,1280]{2,1,0:T(8,128)(2,1)}, bf16[2,80,1280]{2,1,0:T(8,128)(2,1)S(1)}, u32[]{:S(2)}, u32[]{:S(2)}) %collective-permute-start.8) | collective-permute-done | bytes 409632 | tf_op jit(solution)/shard_map/ppermute | solution.py:253
  49.6 3.4 %collective-permute-done.7.refs_2_ = bf16[320,1280]{1,0:T(8,128)(2,1)S(1)} collective-permute-done((bf16[320,1280]{1,0:T(8,128)(2,1)}, bf16[320,1280]{1,0:T(8,128)(2,1)S(1)}, u32[]{:S(2)}, u32[]{:S(2)}) %collective-permute-start.7) | collective-permute-done | bytes 819232 | tf_op jit(solution)/shard_map/ppermute | solution.py:235
  55.2 3.3 %first.2 = (bf16[480,1280]{1,0:T(8,128)(2,1)S(1)}, f32[480,1280]{1,0:T(8,128)S(1)}, bf16[480,1280]{1,0:T(8,128)(2,1)S(1)}, f32[480,128]{1,0:T(8,128)S(1)}) custom-call(bf16[480,1280]{1,0:T(8,128)(2,1)S(1)} %get-tuple-element.155.m_ref, bf16[480,1280]{1,0:T(8,128)(2,1)S(1)} %get-tuple-element.156.d_ref, bf16[1280,1280]{1,0:T(8,128)(2,1)S(1)} %join.3.first_ref, ...), custom_call_target="tpu_custom_call" | custom-call | flops 1572864000 | bytes 3072000 | tf_op jit(solution)/shard_map/first/pallas_call | solution.py:211
  58.9 2.0 %second.2 = (bf16[480,1280]{1,0:T(8,128)(2,1)S(1)}, f32[480,128]{1,0:T(8,128)S(1)}) custom-call(bf16[480,1280]{1,0:T(8,128)(2,1)S(1)} %get-tuple-element.156.d_ref, bf16[1280,1280]{1,0:T(8,128)(2,1)S(1)} %join.2.second_ref, bf16[480,1280]{1,0:T(8,128)(2,1)S(1)} %get-tuple-element.100.hidden_ref, f32[480,1280]{1,0:T(8,128)S(1)} %get-tuple-element.101.slope_ref, ...), custom_call_target="tpu_custom_call" | custom-call | flops 1572864000 | bytes 3072000 | tf_op jit(solution)/shard_map/second/pallas_call | solution.py:211
  60.9 1.9 %rows.2 = (f32[240,1280]{1,0:T(8,128)S(1)}, bf16[240,1280]{1,0:T(8,128)(2,1)S(1)}, f32[8,1280]{1,0:T(8,128)S(1)}) custom-call(bf16[480,1280]{1,0:T(8,128)(2,1)S(1)} %get-tuple-element.155.m_ref, bf16[480,1280]{1,0:T(8,128)(2,1)S(1)} %get-tuple-element.103.pre_ref, f32[480,128]{1,0:T(8,128)S(1)} %get-tuple-element.104.logit_ref, ...), custom_call_target="tpu_custom_call" | custom-call | flops 1572864000 | bytes 3072000 | tf_op jit(solution)/shard_map/rows/pallas_call | solution.py:211
  64.1 1.5 %first.3 = (bf16[160,1280]{1,0:T(8,128)(2,1)S(1)}, f32[160,1280]{1,0:T(8,128)S(1)}, bf16[160,1280]{1,0:T(8,128)(2,1)S(1)}, f32[160,128]{1,0:T(8,128)S(1)}) custom-call(bf16[160,1280]{1,0:T(8,128)(2,1)S(1)} %pad_maximum_fusion.3.m_ref, bf16[160,1280]{1,0:T(8,128)(2,1)S(1)} %pad_maximum_fusion.2.d_ref, bf16[1280,1280]{1,0:T(8,128)(2,1)S(1)} %join.3.first_ref, ...), custom_call_target="tpu_custom_call" | custom-call | flops 524288000 | bytes 1024000 | tf_op jit(solution)/shard_map/first/pallas_call | solution.py:211
  71.7 1.6 %collective-permute-start.19 = (f32[8,1280]{1,0:T(8,128)S(1)}, f32[8,1280]{1,0:T(8,128)S(1)}, u32[]{:S(2)}, u32[]{:S(2)}) collective-permute-start(f32[8,1280]{1,0:T(8,128)S(1)} %add.33), channel_id=1, source_target_pairs={{0,8},{4,12},{8,0},{12,4},{16,24},{20,28},{24,16},{28,20},{1,9},{5... | collective-permute-start | bytes 122888 | tf_op jit(solution)/shard_map/ppermute | solution.py:256
  73.3 1.5 %collective-permute-start.18 = (bf16[80,1280]{1,0:T(8,128)(2,1)S(1)}, bf16[80,1280]{1,0:T(8,128)(2,1)S(1)}, u32[]{:S(2)}, u32[]{:S(2)}) collective-permute-start(bf16[80,1280]{1,0:T(8,128)(2,1)S(1)} %get-tuple-element.128), channel_id=1, source_target_pairs={{0,2},{1,3},{2,0},{3,1},{4,6},{5,7},{6,4},{7,5},{8,10},{9,11},{10,... | collective-permute-start | bytes 614408 | tf_op jit(solution)/shard_map/ppermute | solution.py:248
  80.5 3.6 %collective-permute-done.20 = f32[8,1280]{1,0:T(8,128)S(1)} collective-permute-done((f32[8,1280]{1,0:T(8,128)S(1)}, f32[8,1280]{1,0:T(8,128)S(1)}, u32[]{:S(2)}, u32[]{:S(2)}) %collective-permute-start.20) | collective-permute-done | bytes 40992 | tf_op jit(solution)/shard_map/ppermute | solution.py:256
  87.2 4.9 %collective-permute-done.21 = f32[8,1280]{1,0:T(8,128)S(1)} collective-permute-done((f32[8,1280]{1,0:T(8,128)S(1)}, f32[8,1280]{1,0:T(8,128)S(1)}, u32[]{:S(2)}, u32[]{:S(2)}) %collective-permute-start.21) | collective-permute-done | bytes 40992 | tf_op jit(solution)/shard_map/ppermute | solution.py:256
  92.1 1.7 %collective-permute-start.24 = (bf16[80,1280]{1,0:T(8,128)(2,1)S(1)}, bf16[80,1280]{1,0:T(8,128)(2,1)S(1)}, u32[]{:S(2)}, u32[]{:S(2)}) collective-permute-start(bf16[80,1280]{1,0:T(8,128)(2,1)S(1)} %bitcast.75), channel_id=1, source_target_pairs={{0,16},{4,20},{8,24},{12,28},{16,0},{20,4},{24,8},{28,12},{1,17},{... | collective-permute-start | bytes 614408 | tf_op jit(solution)/shard_map/ppermute | solution.py:253
  94.5 2.4 %collective-permute-start.25 = (bf16[80,1280]{1,0:T(8,128)(2,1)S(1)}, bf16[80,1280]{1,0:T(8,128)(2,1)S(1)}, u32[]{:S(2)}, u32[]{:S(2)}) collective-permute-start(bf16[80,1280]{1,0:T(8,128)(2,1)S(1)} %get-tuple-element.151), channel_id=1, source_target_pairs={{0,24},{4,28},{8,0},{12,4},{16,8},{20,12},{24,16},{28,20},{1,25},{... | collective-permute-start | bytes 614408 | tf_op jit(solution)/shard_map/ppermute | solution.py:253
  98.1 11.1 %collective-permute-done.24 = bf16[80,1280]{1,0:T(8,128)(2,1)S(1)} collective-permute-done((bf16[80,1280]{1,0:T(8,128)(2,1)S(1)}, bf16[80,1280]{1,0:T(8,128)(2,1)S(1)}, u32[]{:S(2)}, u32[]{:S(2)}) %collective-permute-start.24) | collective-permute-done | bytes 204832 | tf_op jit(solution)/shard_map/ppermute | solution.py:253
  109.2 1.5 %collective-permute-start.28 = (f32[8,1280]{1,0:T(8,128)S(1)}, f32[8,1280]{1,0:T(8,128)S(1)}, u32[]{:S(2)}, u32[]{:S(2)}) collective-permute-start(f32[8,1280]{1,0:T(8,128)S(1)} %add.38.total_ref), channel_id=1, source_target_pairs={{0,2},{1,3},{2,0},{3,1},{4,6},{5,7},{6,4},{7,5},{8,10},{9,11},{10,... | collective-permute-start | bytes 122888 | tf_op jit(solution)/shard_map/ppermute | solution.py:480
  110.7 2.4 %collective-permute-done.22.other_ref = bf16[320,1280]{1,0:T(8,128)(2,1)S(1)} collective-permute-done((bf16[320,1280]{1,0:T(8,128)(2,1)S(1)}, bf16[320,1280]{1,0:T(8,128)(2,1)S(1)}, u32[]{:S(2)}, u32[]{:S(2)}) %collective-permute-start.22) | collective-permute-done | bytes 819232 | tf_op jit(solution)/shard_map/ppermute | solution.py:235
  113.2 2.7 %finish.1 = (bf16[128,1280]{1,0:T(8,128)(2,1)}, bf16[320,1280]{1,0:T(8,128)(2,1)}, f32[4,1280]{1,0:T(4,128)}, f32[1280]{0:T(1024)}) custom-call(f32[128,1280]{1,0:T(8,128)S(1)} %get-tuple-element.90.norm_ref, f32[128,128]{1,0:T(8,128)S(1)} %get-tuple-element.91.deviation_ref, bf16[320,128]{1,0:T(8,128)(2,1)S(1)} %get-tuple-element.92.places_ref, ...), custom_call_target="tpu_custom_call" | custom-call | tf_op jit(solution)/shard_map/finish/pallas_call | solution.py:211
  (96 shorter events, 28.3 us)
Async XLA Ops:
  3.4 25.2 %collective-permute-start.2 = (bf16[320,1280]{1,0:T(8,128)(2,1)}, bf16[320,1280]{1,0:T(8,128)(2,1)S(1)}, u32[]{:S(2)}, u32[]{:S(2)}) collective-permute-start(bf16[320,1280]{1,0:T(8,128)(2,1)} %bitcast.66), channel_id=1, source_target_pairs={{0,4},{4,0},{8,12},{12,8},{16,20},{20,16},{24,28},{28,24},{1,5},{5... | collective-permute-start | bytes 2457608 | tf_op jit(solution)/shard_map/ppermute | solution.py:235
  6.5 22.2 %collective-permute-start.1 = (bf16[320,1280]{1,0:T(8,128)(2,1)}, bf16[320,1280]{1,0:T(8,128)(2,1)S(1)}, u32[]{:S(2)}, u32[]{:S(2)}) collective-permute-start(bf16[320,1280]{1,0:T(8,128)(2,1)} %bitcast.67), channel_id=1, source_target_pairs={{0,1},{1,0},{2,3},{3,2},{4,5},{5,4},{6,7},{7,6},{8,9},{9,8},{10,11... | collective-permute-start | bytes 2457608 | tf_op jit(solution)/shard_map/ppermute | solution.py:238
  6.5 14.3 %collective-permute-start.3 = (bf16[2,80,1280]{2,1,0:T(8,128)(2,1)}, bf16[2,80,1280]{2,1,0:T(8,128)(2,1)S(1)}, u32[]{:S(2)}, u32[]{:S(2)}) collective-permute-start(bf16[2,80,1280]{2,1,0:T(8,128)(2,1)} %get-tuple-element.80), channel_id=1, source_target_pairs={{0,8},{4,12},{8,16},{12,20},{16,24},{20,28},{24,0},{28,4},{1,9},{5... | collective-permute-start | bytes 1228808 | tf_op jit(solution)/shard_map/ppermute | solution.py:253
  8.0 20.6 %collective-permute-start.4 = (bf16[2,80,1280]{2,1,0:T(8,128)(2,1)}, bf16[2,80,1280]{2,1,0:T(8,128)(2,1)S(1)}, u32[]{:S(2)}, u32[]{:S(2)}) collective-permute-start(bf16[2,80,1280]{2,1,0:T(8,128)(2,1)} %get-tuple-element.81), channel_id=1, source_target_pairs={{0,24},{4,28},{8,0},{12,4},{16,8},{20,12},{24,16},{28,20},{1,25},{... | collective-permute-start | bytes 1228808 | tf_op jit(solution)/shard_map/ppermute | solution.py:253
  10.3 18.3 %collective-permute-start = (bf16[2,80,1280]{2,1,0:T(8,128)(2,1)}, bf16[2,80,1280]{2,1,0:T(8,128)(2,1)}, u32[]{:S(2)}, u32[]{:S(2)}) collective-permute-start(bf16[2,80,1280]{2,1,0:T(8,128)(2,1)} %get-tuple-element.93), channel_id=1, source_target_pairs={{0,2},{1,3},{2,0},{3,1},{4,6},{5,7},{6,4},{7,5},{8,10},{9,11},{10,... | collective-permute-start | bytes 1228808 | tf_op jit(solution)/shard_map/ppermute | solution.py:242
  28.6 20.8 %collective-permute-start.8 = (bf16[2,80,1280]{2,1,0:T(8,128)(2,1)}, bf16[2,80,1280]{2,1,0:T(8,128)(2,1)S(1)}, u32[]{:S(2)}, u32[]{:S(2)}) collective-permute-start(bf16[2,80,1280]{2,1,0:T(8,128)(2,1)} %get-tuple-element.88), channel_id=1, source_target_pairs={{0,16},{4,20},{8,24},{12,28},{16,0},{20,4},{24,8},{28,12},{1,17},{... | collective-permute-start | bytes 1228808 | tf_op jit(solution)/shard_map/ppermute | solution.py:253
  30.0 19.4 %collective-permute-start.6 = (bf16[2,80,1280]{2,1,0:T(8,128)(2,1)S(1)}, bf16[2,80,1280]{2,1,0:T(8,128)(2,1)S(1)}, u32[]{:S(2)}, u32[]{:S(2)}) collective-permute-start(bf16[2,80,1280]{2,1,0:T(8,128)(2,1)S(1)} %collective-permute-done.3), channel_id=1, source_target_pairs={{0,2},{1,3},{2,0},{3,1},{4,6},{5,7},{6,4},{7,5},{8,10},{9,11},{10,... | collective-permute-start | bytes 1228808 | tf_op jit(solution)/shard_map/ppermute | solution.py:242
  31.5 18.1 %collective-permute-start.9 = (bf16[2,80,1280]{2,1,0:T(8,128)(2,1)S(1)}, bf16[2,80,1280]{2,1,0:T(8,128)(2,1)S(1)}, u32[]{:S(2)}, u32[]{:S(2)}) collective-permute-start(bf16[2,80,1280]{2,1,0:T(8,128)(2,1)S(1)} %collective-permute-done.4), channel_id=1, source_target_pairs={{0,2},{1,3},{2,0},{3,1},{4,6},{5,7},{6,4},{7,5},{8,10},{9,11},{10,... | collective-permute-start | bytes 1228808 | tf_op jit(solution)/shard_map/ppermute | solution.py:242
  32.0 17.5 %collective-permute-start.5 = (bf16[320,1280]{1,0:T(8,128)(2,1)S(1)}, bf16[320,1280]{1,0:T(8,128)(2,1)S(1)}, u32[]{:S(2)}, u32[]{:S(2)}) collective-permute-start(bf16[320,1280]{1,0:T(8,128)(2,1)S(1)} %collective-permute-done.2.refs_2_), channel_id=1, source_target_pairs={{0,1},{1,0},{2,3},{3,2},{4,5},{5,4},{6,7},{7,6},{8,9},{9,8},{10,11... | collective-permute-start | bytes 2457608 | tf_op jit(solution)/shard_map/ppermute | solution.py:238
  32.1 20.9 %collective-permute-start.7 = (bf16[320,1280]{1,0:T(8,128)(2,1)}, bf16[320,1280]{1,0:T(8,128)(2,1)S(1)}, u32[]{:S(2)}, u32[]{:S(2)}) collective-permute-start(bf16[320,1280]{1,0:T(8,128)(2,1)} %bitcast.69), channel_id=1, source_target_pairs={{0,4},{4,0},{8,12},{12,8},{16,20},{20,16},{24,28},{28,24},{1,5},{5... | collective-permute-start | bytes 2457608 | tf_op jit(solution)/shard_map/ppermute | solution.py:235
  52.9 11.1 %collective-permute-start.12 = (bf16[2,80,1280]{2,1,0:T(8,128)(2,1)S(1)}, bf16[2,80,1280]{2,1,0:T(8,128)(2,1)S(1)}, u32[]{:S(2)}, u32[]{:S(2)}) collective-permute-start(bf16[2,80,1280]{2,1,0:T(8,128)(2,1)S(1)} %collective-permute-done.8), channel_id=1, source_target_pairs={{0,2},{1,3},{2,0},{3,1},{4,6},{5,7},{6,4},{7,5},{8,10},{9,11},{10,... | collective-permute-start | bytes 1228808 | tf_op jit(solution)/shard_map/ppermute | solution.py:242
  62.9 21.3 %collective-permute-start.17 = (bf16[240,1280]{1,0:T(8,128)(2,1)S(1)}, bf16[240,1280]{1,0:T(8,128)(2,1)S(1)}, u32[]{:S(2)}, u32[]{:S(2)}) collective-permute-start(bf16[240,1280]{1,0:T(8,128)(2,1)S(1)} %get-tuple-element.106), channel_id=1, source_target_pairs={{0,2},{1,3},{2,0},{3,1},{4,6},{5,7},{6,4},{7,5},{8,10},{9,11},{10,... | collective-permute-start | bytes 1843208 | tf_op jit(solution)/shard_map/ppermute | solution.py:248
  71.0 21.1 %collective-permute-start.15 = (bf16[320,1280]{1,0:T(8,128)(2,1)S(1)}, bf16[320,1280]{1,0:T(8,128)(2,1)S(1)}, u32[]{:S(2)}, u32[]{:S(2)}) collective-permute-start(bf16[320,1280]{1,0:T(8,128)(2,1)S(1)} %half.2), channel_id=1, source_target_pairs={{0,4},{4,0},{8,12},{12,8},{16,20},{20,16},{24,28},{28,24},{1,5},{5... | collective-permute-start | bytes 2457608 | tf_op jit(solution)/shard_map/ppermute | solution.py:235
  71.7 6.7 %collective-permute-start.19 = (f32[8,1280]{1,0:T(8,128)S(1)}, f32[8,1280]{1,0:T(8,128)S(1)}, u32[]{:S(2)}, u32[]{:S(2)}) collective-permute-start(f32[8,1280]{1,0:T(8,128)S(1)} %add.33), channel_id=1, source_target_pairs={{0,8},{4,12},{8,0},{12,4},{16,24},{20,28},{24,16},{28,20},{1,9},{5... | collective-permute-start | bytes 122888 | tf_op jit(solution)/shard_map/ppermute | solution.py:256
  73.3 11.4 %collective-permute-start.18 = (bf16[80,1280]{1,0:T(8,128)(2,1)S(1)}, bf16[80,1280]{1,0:T(8,128)(2,1)S(1)}, u32[]{:S(2)}, u32[]{:S(2)}) collective-permute-start(bf16[80,1280]{1,0:T(8,128)(2,1)S(1)} %get-tuple-element.128), channel_id=1, source_target_pairs={{0,2},{1,3},{2,0},{3,1},{4,6},{5,7},{6,4},{7,5},{8,10},{9,11},{10,... | collective-permute-start | bytes 614408 | tf_op jit(solution)/shard_map/ppermute | solution.py:248
  75.7 16.4 %collective-permute-start.16 = (bf16[320,1280]{1,0:T(8,128)(2,1)S(1)}, bf16[320,1280]{1,0:T(8,128)(2,1)S(1)}, u32[]{:S(2)}, u32[]{:S(2)}) collective-permute-start(bf16[320,1280]{1,0:T(8,128)(2,1)S(1)} %weights.10), channel_id=1, source_target_pairs={{0,1},{1,0},{2,3},{3,2},{4,5},{5,4},{6,7},{7,6},{8,9},{9,8},{10,11... | collective-permute-start | bytes 2457608 | tf_op jit(solution)/shard_map/ppermute | solution.py:238
  78.4 5.7 %collective-permute-start.20 = (f32[8,1280]{1,0:T(8,128)S(1)}, f32[8,1280]{1,0:T(8,128)S(1)}, u32[]{:S(2)}, u32[]{:S(2)}) collective-permute-start(f32[8,1280]{1,0:T(8,128)S(1)} %add.34), channel_id=1, source_target_pairs={{0,16},{4,20},{8,24},{12,28},{16,0},{20,4},{24,8},{28,12},{1,17},{... | collective-permute-start | bytes 122888 | tf_op jit(solution)/shard_map/ppermute | solution.py:256
  84.1 29.0 %collective-permute-start.27 = (bf16[320,1280]{1,0:T(8,128)(2,1)S(1)}, bf16[320,1280]{1,0:T(8,128)(2,1)S(1)}, u32[]{:S(2)}, u32[]{:S(2)}) collective-permute-start(bf16[320,1280]{1,0:T(8,128)(2,1)S(1)} %weights.15), channel_id=1, source_target_pairs={{0,1},{1,0},{2,3},{3,2},{4,5},{5,4},{6,7},{7,6},{8,9},{9,8},{10,11... | collective-permute-start | bytes 2457608 | tf_op jit(solution)/shard_map/ppermute | solution.py:238
  84.2 12.8 %collective-permute-start.26 = (bf16[320,1280]{1,0:T(8,128)(2,1)S(1)}, bf16[320,1280]{1,0:T(8,128)(2,1)S(1)}, u32[]{:S(2)}, u32[]{:S(2)}) collective-permute-start(bf16[320,1280]{1,0:T(8,128)(2,1)S(1)} %weights.13), channel_id=1, source_target_pairs={{0,1},{1,0},{2,3},{3,2},{4,5},{5,4},{6,7},{7,6},{8,9},{9,8},{10,11... | collective-permute-start | bytes 2457608 | tf_op jit(solution)/shard_map/ppermute | solution.py:238
  84.9 7.2 %collective-permute-start.21 = (f32[8,1280]{1,0:T(8,128)S(1)}, f32[8,1280]{1,0:T(8,128)S(1)}, u32[]{:S(2)}, u32[]{:S(2)}) collective-permute-start(f32[8,1280]{1,0:T(8,128)S(1)} %add.35), channel_id=1, source_target_pairs={{0,4},{4,0},{8,12},{12,8},{16,20},{20,16},{24,28},{28,24},{1,5},{5... | collective-permute-start | bytes 122888 | tf_op jit(solution)/shard_map/ppermute | solution.py:256
  92.1 17.1 %collective-permute-start.24 = (bf16[80,1280]{1,0:T(8,128)(2,1)S(1)}, bf16[80,1280]{1,0:T(8,128)(2,1)S(1)}, u32[]{:S(2)}, u32[]{:S(2)}) collective-permute-start(bf16[80,1280]{1,0:T(8,128)(2,1)S(1)} %bitcast.75), channel_id=1, source_target_pairs={{0,16},{4,20},{8,24},{12,28},{16,0},{20,4},{24,8},{28,12},{1,17},{... | collective-permute-start | bytes 614408 | tf_op jit(solution)/shard_map/ppermute | solution.py:253
  93.9 19.1 %collective-permute-start.22 = (bf16[320,1280]{1,0:T(8,128)(2,1)S(1)}, bf16[320,1280]{1,0:T(8,128)(2,1)S(1)}, u32[]{:S(2)}, u32[]{:S(2)}) collective-permute-start(bf16[320,1280]{1,0:T(8,128)(2,1)S(1)} %half.3), channel_id=1, source_target_pairs={{0,4},{4,0},{8,12},{12,8},{16,20},{20,16},{24,28},{28,24},{1,5},{5... | collective-permute-start | bytes 2457608 | tf_op jit(solution)/shard_map/ppermute | solution.py:235
  94.5 16.1 %collective-permute-start.25 = (bf16[80,1280]{1,0:T(8,128)(2,1)S(1)}, bf16[80,1280]{1,0:T(8,128)(2,1)S(1)}, u32[]{:S(2)}, u32[]{:S(2)}) collective-permute-start(bf16[80,1280]{1,0:T(8,128)(2,1)S(1)} %get-tuple-element.151), channel_id=1, source_target_pairs={{0,24},{4,28},{8,0},{12,4},{16,8},{20,12},{24,16},{28,20},{1,25},{... | collective-permute-start | bytes 614408 | tf_op jit(solution)/shard_map/ppermute | solution.py:253
  96.9 13.7 %collective-permute-start.23 = (bf16[80,1280]{1,0:T(8,128)(2,1)S(1)}, bf16[80,1280]{1,0:T(8,128)(2,1)S(1)}, u32[]{:S(2)}, u32[]{:S(2)}) collective-permute-start(bf16[80,1280]{1,0:T(8,128)(2,1)S(1)} %get-tuple-element.152), channel_id=1, source_target_pairs={{0,8},{4,12},{8,16},{12,20},{16,24},{20,28},{24,0},{28,4},{1,9},{5... | collective-permute-start | bytes 614408 | tf_op jit(solution)/shard_map/ppermute | solution.py:253
  (11 other events, 91.3 us)

commit v11 on v10

--- a/solution.py
+++ b/solution.py
@@ -10,7 +10,7 @@
 from jax.sharding import PartitionSpec as P
 
 F32 = jnp.float32
-ORDER = 14
+ORDER = 24
 BF16 = jnp.bfloat16
 VMEM = pl.BlockSpec(memory_space=pltpu.VMEM)
 ANY = pl.BlockSpec(memory_space=pl.ANY)
@@ -106,13 +106,11 @@
 
 def finish_kernel(
     norm_ref, deviation_ref, places_ref, gain_ref, d_ref, rows_ref, stay_ref, pair_ref, other_ref,
-    total_ref, last_ref, out_hbm, sum_hbm, router_ref, gain_grad_ref, out_ref, sum_ref, sems
+    total_ref, last_ref, out_ref, sum_ref, router_ref, gain_grad_ref
 ):
     sum_ref[...] = (
         stay_ref[...] + pair_ref[...].astype(F32) + other_ref[...].astype(F32)
     ).astype(BF16)
-    sum_copy = pltpu.make_async_copy(sum_ref, sum_hbm, sems.at[0])
-    sum_copy.start()
     normalized_rows = norm_ref[...]
     scaled_rows = dot(places_ref[...], rows_ref[...], 0, 0) * gain_ref[...][None, :]
     mean_first_term = jnp.mean(scaled_rows, axis=1, keepdims=True)
@@ -121,14 +119,10 @@
         scaled_rows - mean_first_term - normalized_rows * mean_second_term
     )
     out_ref[...] = (d_ref[...].astype(F32) + norm_backward).astype(BF16)
-    out_copy = pltpu.make_async_copy(out_ref, out_hbm, sems.at[1])
-    out_copy.start()
     experts = router_ref.shape[0]
     total = total_ref[...] + last_ref[...]
     router_ref[...] = total[:experts]
     gain_grad_ref[...] = jnp.sum(total[experts:], axis=0) / gain_ref[...]
-    sum_copy.wait()
-    out_copy.wait()
 
 
 def first_kernel(m_ref, d_ref, first_ref, router_ref, hidden_ref, slope_ref, y_ref, gate_ref):
@@ -309,17 +303,15 @@
     )
 
     stage = (
-        second_y,
         first_yc,
         [near[step] for step in late],
         [side[step] for step in early[1:]],
         prepared,
     )
-    late_held, second_held, second_y, early_held, first_yc, prepared = tied(
+    late_held, second_held, early_held, first_yc, prepared = tied(
         (
             [near[step] for step in late],
             second_held,
-            second_y,
             [side[step] for step in early[1:]],
             first_yc,
             prepared,
@@ -504,12 +496,6 @@
             total,
             last,
         ),
-        out_specs=[ANY, ANY, VMEM, VMEM],
-        scratch=[
-            pltpu.VMEM((tokens, width), BF16),
-            pltpu.VMEM((units, width), BF16),
-            pltpu.SemaphoreType.DMA((2,)),
-        ],
     )
     return (input_grad, grad_in.T[None], grad_out, grad_router.T, grad_gain)
 

time: 116 us -> 115 us (level)
    ppermute x6, waiting for transfers between devices: 39.8 us -> 44.9 us  [over_experts(): lax.ppermute(value, 'expert', [(i, (i + 2 * step) % halves) for i in rang...]
    ppermute x4, waiting for transfers between devices: 5.73 us -> 1.42 us  [over_half(): return lax.ppermute(value, 'expert', [(i, i ^ 1) for i in range(halves)])]
  transfers between devices with their start and end apart: 29 -> 29, of which waited for: 12 -> 10; matrix products, arithmetic and copies ran while one was open for 4% -> 4% of each run, Pallas kernels for 16% -> 17%
where the time goes in v11:
time: 115 us
  waiting for transfers between devices  55.2 us (48%)
  starting transfers between devices  27.7 us (24%)
  Pallas kernels  23.8 us (21%)
  local copies, waits for them, and re-layouts  4.45 us (4%)
  other arithmetic  2.37 us (2%)
    ppermute x6, waiting for transfers between devices, over_experts(): lax.ppermute(value, 'expert', [(i, (i + 2 * step) % halves) for i in rang...  44.9 us
    pallas_call x21, Pallas kernels, call(): pl.pallas_call(kernel, out_shape=outs, in_specs=specs or [VMEM] * len(arg...  23.8 us
    ppermute x4, waiting for transfers between devices, pairwise(): lax.ppermute(value, name, [(i, i ^ bit) for i in range(size)])  8.82 us
    ppermute x6, starting transfers between devices, over_experts(): lax.ppermute(value, 'expert', [(i, (i + 2 * step) % halves) for i in rang...  8.68 us
    ppermute x4, starting transfers between devices, pairwise(): lax.ppermute(value, name, [(i, i ^ bit) for i in range(size)])  5.6 us
    ppermute x4, starting transfers between devices, over_columns(): lax.ppermute(value, 'dp', [(i, (i + 2 * step) % groups) for i in range(gr...  5.06 us
    unnamed x20, local copies, waits for them, and re-layouts  4.25 us
    ppermute x4, starting transfers between devices, over_half(): return lax.ppermute(value, 'expert', [(i, i ^ 1) for i in range(halves)])  4.22 us
  transfers between devices with their start and end apart: 29, of which 10 were waited for; matrix products, arithmetic and copies ran while one was open for 4% of the time, Pallas kernels for 17%

profile of v11, /device:TPU:0, one launch (start us, length us, event | category | flops | bytes accessed | tf_op | source)
XLA Modules:
  0.0 114.6 jit_solution(3026837438266409369)
XLA Ops:
  0.6 2.8 %dispatch.1 = (bf16[2,80,1280]{2,1,0:T(8,128)(2,1)}, bf16[2,80,1280]{2,1,0:T(8,128)(2,1)}, bf16[2,80,1280]{2,1,0:T(8,128)(2,1)}, bf16[2,80,1280]{2,1,0:T(8,128)(2,1)}) custom-call(bf16[128,1280]{1,0:T(8,128)(2,1)} %x_ref.1, f32[1280]{0:T(1024)} %gain_ref.1, s32[2,128]{1,0:T(2,128)} %bitcast.72, bf16[128,1280]{1,0:T(8,128)(2,1)} %d_ref.1), custom_call_target="tpu_custom_call" | custom-call | flops 209715200 | bytes 409600 | tf_op jit(solution)/shard_map/dispatch/pallas_call | solution.py:205
  4.0 2.6 %collective-permute-start.2 = (bf16[320,1280]{1,0:T(8,128)(2,1)}, bf16[320,1280]{1,0:T(8,128)(2,1)S(1)}, u32[]{:S(2)}, u32[]{:S(2)}) collective-permute-start(bf16[320,1280]{1,0:T(8,128)(2,1)} %bitcast.67), channel_id=1, source_target_pairs={{0,4},{4,0},{8,12},{12,8},{16,20},{20,16},{24,28},{28,24},{1,5},{5... | collective-permute-start | bytes 2457608 | tf_op jit(solution)/shard_map/ppermute | solution.py:229
  6.5 3.6 %collective-permute-start = (bf16[2,80,1280]{2,1,0:T(8,128)(2,1)}, bf16[2,80,1280]{2,1,0:T(8,128)(2,1)S(1)}, u32[]{:S(2)}, u32[]{:S(2)}) collective-permute-start(bf16[2,80,1280]{2,1,0:T(8,128)(2,1)} %get-tuple-element.76), channel_id=1, source_target_pairs={{0,24},{4,28},{8,0},{12,4},{16,8},{20,12},{24,16},{28,20},{1,25},{... | collective-permute-start | bytes 1228808 | tf_op jit(solution)/shard_map/ppermute | solution.py:247
  10.2 1.5 %collective-permute-start.3 = (bf16[2,80,1280]{2,1,0:T(8,128)(2,1)}, bf16[2,80,1280]{2,1,0:T(8,128)(2,1)}, u32[]{:S(2)}, u32[]{:S(2)}) collective-permute-start(bf16[2,80,1280]{2,1,0:T(8,128)(2,1)} %get-tuple-element.92), channel_id=1, source_target_pairs={{0,2},{1,3},{2,0},{3,1},{4,6},{5,7},{6,4},{7,5},{8,10},{9,11},{10,... | collective-permute-start | bytes 1228808 | tf_op jit(solution)/shard_map/ppermute | solution.py:236
  14.3 6.0 %collective-permute-done = bf16[2,80,1280]{2,1,0:T(8,128)(2,1)S(1)} collective-permute-done((bf16[2,80,1280]{2,1,0:T(8,128)(2,1)}, bf16[2,80,1280]{2,1,0:T(8,128)(2,1)S(1)}, u32[]{:S(2)}, u32[]{:S(2)}) %collective-permute-start) | collective-permute-done | bytes 409632 | tf_op jit(solution)/shard_map/ppermute | solution.py:247
  20.3 8.8 %collective-permute-done.1 = bf16[2,80,1280]{2,1,0:T(8,128)(2,1)S(1)} collective-permute-done((bf16[2,80,1280]{2,1,0:T(8,128)(2,1)}, bf16[2,80,1280]{2,1,0:T(8,128)(2,1)S(1)}, u32[]{:S(2)}, u32[]{:S(2)}) %collective-permute-start.1) | collective-permute-done | bytes 409632 | tf_op jit(solution)/shard_map/ppermute | solution.py:247
  29.9 1.5 %collective-permute-start.7 = (bf16[2,80,1280]{2,1,0:T(8,128)(2,1)S(1)}, bf16[2,80,1280]{2,1,0:T(8,128)(2,1)S(1)}, u32[]{:S(2)}, u32[]{:S(2)}) collective-permute-start(bf16[2,80,1280]{2,1,0:T(8,128)(2,1)S(1)} %collective-permute-done), channel_id=1, source_target_pairs={{0,2},{1,3},{2,0},{3,1},{4,6},{5,7},{6,4},{7,5},{8,10},{9,11},{10,... | collective-permute-start | bytes 1228808 | tf_op jit(solution)/shard_map/ppermute | solution.py:236
  34.8 14.9 %collective-permute-done.6 = bf16[2,80,1280]{2,1,0:T(8,128)(2,1)S(1)} collective-permute-done((bf16[2,80,1280]{2,1,0:T(8,128)(2,1)}, bf16[2,80,1280]{2,1,0:T(8,128)(2,1)S(1)}, u32[]{:S(2)}, u32[]{:S(2)}) %collective-permute-start.6) | collective-permute-done | bytes 409632 | tf_op jit(solution)/shard_map/ppermute | solution.py:247
  49.8 1.6 %collective-permute-start.13 = (bf16[2,80,1280]{2,1,0:T(8,128)(2,1)S(1)}, bf16[2,80,1280]{2,1,0:T(8,128)(2,1)S(1)}, u32[]{:S(2)}, u32[]{:S(2)}) collective-permute-start(bf16[2,80,1280]{2,1,0:T(8,128)(2,1)S(1)} %collective-permute-done.6), channel_id=1, source_target_pairs={{0,2},{1,3},{2,0},{3,1},{4,6},{5,7},{6,4},{7,5},{8,10},{9,11},{10,... | collective-permute-start | bytes 1228808 | tf_op jit(solution)/shard_map/ppermute | solution.py:236
  53.1 3.3 %first.2 = (bf16[480,1280]{1,0:T(8,128)(2,1)S(1)}, f32[480,1280]{1,0:T(8,128)S(1)}, bf16[480,1280]{1,0:T(8,128)(2,1)S(1)}, f32[480,128]{1,0:T(8,128)S(1)}) custom-call(bf16[480,1280]{1,0:T(8,128)(2,1)S(1)} %get-tuple-element.154.m_ref, bf16[480,1280]{1,0:T(8,128)(2,1)S(1)} %get-tuple-element.153.d_ref, bf16[1280,1280]{1,0:T(8,128)(2,1)S(1)} %join.3.first_ref, ...), custom_call_target="tpu_custom_call" | custom-call | flops 1572864000 | bytes 3072000 | tf_op jit(solution)/shard_map/first/pallas_call | solution.py:205
  56.8 2.0 %second.2 = (bf16[480,1280]{1,0:T(8,128)(2,1)S(1)}, f32[480,128]{1,0:T(8,128)S(1)}) custom-call(bf16[480,1280]{1,0:T(8,128)(2,1)S(1)} %get-tuple-element.153.d_ref, bf16[1280,1280]{1,0:T(8,128)(2,1)S(1)} %join.2.second_ref, bf16[480,1280]{1,0:T(8,128)(2,1)S(1)} %get-tuple-element.98.hidden_ref, f32[480,1280]{1,0:T(8,128)S(1)} %get-tuple-element.99.slope_ref, ...), custom_call_target="tpu_custom_call" | custom-call | flops 1572864000 | bytes 3072000 | tf_op jit(solution)/shard_map/second/pallas_call | solution.py:205
  58.8 1.9 %rows.2 = (f32[240,1280]{1,0:T(8,128)S(1)}, bf16[240,1280]{1,0:T(8,128)(2,1)S(1)}, f32[8,1280]{1,0:T(8,128)S(1)}) custom-call(bf16[480,1280]{1,0:T(8,128)(2,1)S(1)} %get-tuple-element.154.m_ref, bf16[480,1280]{1,0:T(8,128)(2,1)S(1)} %get-tuple-element.101.pre_ref, f32[480,128]{1,0:T(8,128)S(1)} %get-tuple-element.102.logit_ref, ...), custom_call_target="tpu_custom_call" | custom-call | flops 1572864000 | bytes 3072000 | tf_op jit(solution)/shard_map/rows/pallas_call | solution.py:205
  60.7 1.5 %collective-permute-start.12 = (bf16[240,1280]{1,0:T(8,128)(2,1)S(1)}, bf16[240,1280]{1,0:T(8,128)(2,1)S(1)}, u32[]{:S(2)}, u32[]{:S(2)}) collective-permute-start(bf16[240,1280]{1,0:T(8,128)(2,1)S(1)} %get-tuple-element.104), channel_id=1, source_target_pairs={{0,2},{1,3},{2,0},{3,1},{4,6},{5,7},{6,4},{7,5},{8,10},{9,11},{10,... | collective-permute-start | bytes 1843208 | tf_op jit(solution)/shard_map/ppermute | solution.py:242
  62.4 1.5 %first.3 = (bf16[160,1280]{1,0:T(8,128)(2,1)S(1)}, f32[160,1280]{1,0:T(8,128)S(1)}, bf16[160,1280]{1,0:T(8,128)(2,1)S(1)}, f32[160,128]{1,0:T(8,128)S(1)}) custom-call(bf16[160,1280]{1,0:T(8,128)(2,1)S(1)} %pad_maximum_fusion.2.m_ref, bf16[160,1280]{1,0:T(8,128)(2,1)S(1)} %pad_maximum_fusion.3.d_ref, bf16[1280,1280]{1,0:T(8,128)(2,1)S(1)} %join.3.first_ref, ...), custom_call_target="tpu_custom_call" | custom-call | flops 524288000 | bytes 1024000 | tf_op jit(solution)/shard_map/first/pallas_call | solution.py:205
  70.1 1.6 %collective-permute-start.17 = (f32[8,1280]{1,0:T(8,128)S(1)}, f32[8,1280]{1,0:T(8,128)S(1)}, u32[]{:S(2)}, u32[]{:S(2)}) collective-permute-start(f32[8,1280]{1,0:T(8,128)S(1)} %add.33), channel_id=1, source_target_pairs={{0,8},{4,12},{8,0},{12,4},{16,24},{20,28},{24,16},{28,20},{1,9},{5... | collective-permute-start | bytes 122888 | tf_op jit(solution)/shard_map/ppermute | solution.py:250
  75.8 2.3 %collective-permute-start.18 = (f32[8,1280]{1,0:T(8,128)S(1)}, f32[8,1280]{1,0:T(8,128)S(1)}, u32[]{:S(2)}, u32[]{:S(2)}) collective-permute-start(f32[8,1280]{1,0:T(8,128)S(1)} %add.34), channel_id=1, source_target_pairs={{0,16},{4,20},{8,24},{12,28},{16,0},{20,4},{24,8},{28,12},{1,17},{... | collective-permute-start | bytes 122888 | tf_op jit(solution)/shard_map/ppermute | solution.py:250
  79.0 2.5 %collective-permute-done.18 = f32[8,1280]{1,0:T(8,128)S(1)} collective-permute-done((f32[8,1280]{1,0:T(8,128)S(1)}, f32[8,1280]{1,0:T(8,128)S(1)}, u32[]{:S(2)}, u32[]{:S(2)}) %collective-permute-start.18) | collective-permute-done | bytes 40992 | tf_op jit(solution)/shard_map/ppermute | solution.py:250
  84.5 6.0 %collective-permute-done.20 = f32[8,1280]{1,0:T(8,128)S(1)} collective-permute-done((f32[8,1280]{1,0:T(8,128)S(1)}, f32[8,1280]{1,0:T(8,128)S(1)}, u32[]{:S(2)}, u32[]{:S(2)}) %collective-permute-start.20) | collective-permute-done | bytes 40992 | tf_op jit(solution)/shard_map/ppermute | solution.py:250
  91.3 1.6 %collective-permute-start.23 = (bf16[80,1280]{1,0:T(8,128)(2,1)S(1)}, bf16[80,1280]{1,0:T(8,128)(2,1)S(1)}, u32[]{:S(2)}, u32[]{:S(2)}) collective-permute-start(bf16[80,1280]{1,0:T(8,128)(2,1)S(1)} %get-tuple-element.150), channel_id=1, source_target_pairs={{0,8},{4,12},{8,16},{12,20},{16,24},{20,28},{24,0},{28,4},{1,9},{5... | collective-permute-start | bytes 614408 | tf_op jit(solution)/shard_map/ppermute | solution.py:247
  93.0 2.2 %collective-permute-start.22 = (bf16[80,1280]{1,0:T(8,128)(2,1)S(1)}, bf16[80,1280]{1,0:T(8,128)(2,1)S(1)}, u32[]{:S(2)}, u32[]{:S(2)}) collective-permute-start(bf16[80,1280]{1,0:T(8,128)(2,1)S(1)} %get-tuple-element.151), channel_id=1, source_target_pairs={{0,24},{4,28},{8,0},{12,4},{16,8},{20,12},{24,16},{28,20},{1,25},{... | collective-permute-start | bytes 614408 | tf_op jit(solution)/shard_map/ppermute | solution.py:247
  96.7 4.5 %collective-permute-done.23 = bf16[80,1280]{1,0:T(8,128)(2,1)S(1)} collective-permute-done((bf16[80,1280]{1,0:T(8,128)(2,1)S(1)}, bf16[80,1280]{1,0:T(8,128)(2,1)S(1)}, u32[]{:S(2)}, u32[]{:S(2)}) %collective-permute-start.23) | collective-permute-done | bytes 204832 | tf_op jit(solution)/shard_map/ppermute | solution.py:247
  101.7 1.4 %collective-permute-done.22 = bf16[80,1280]{1,0:T(8,128)(2,1)S(1)} collective-permute-done((bf16[80,1280]{1,0:T(8,128)(2,1)S(1)}, bf16[80,1280]{1,0:T(8,128)(2,1)S(1)}, u32[]{:S(2)}, u32[]{:S(2)}) %collective-permute-start.22) | collective-permute-done | bytes 204832 | tf_op jit(solution)/shard_map/ppermute | solution.py:247
  103.2 9.3 %collective-permute-done.25 = bf16[80,1280]{1,0:T(8,128)(2,1)S(1)} collective-permute-done((bf16[80,1280]{1,0:T(8,128)(2,1)S(1)}, bf16[80,1280]{1,0:T(8,128)(2,1)S(1)}, u32[]{:S(2)}, u32[]{:S(2)}) %collective-permute-start.25) | collective-permute-done | bytes 204832 | tf_op jit(solution)/shard_map/ppermute | solution.py:247
  112.6 2.0 %finish.1 = (bf16[128,1280]{1,0:T(8,128)(2,1)}, bf16[320,1280]{1,0:T(8,128)(2,1)}, f32[4,1280]{1,0:T(4,128)}, f32[1280]{0:T(1024)}) custom-call(f32[128,1280]{1,0:T(8,128)S(1)} %get-tuple-element.89.norm_ref, f32[128,128]{1,0:T(8,128)S(1)} %get-tuple-element.90.deviation_ref, bf16[320,128]{1,0:T(8,128)(2,1)S(1)} %get-tuple-element.91.places_ref, ...), custom_call_target="tpu_custom_call" | custom-call | tf_op jit(solution)/shard_map/finish/pallas_call | solution.py:205
  (96 shorter events, 26.5 us)
Async XLA Ops:
  3.4 25.7 %collective-permute-start.4 = (bf16[320,1280]{1,0:T(8,128)(2,1)}, bf16[320,1280]{1,0:T(8,128)(2,1)S(1)}, u32[]{:S(2)}, u32[]{:S(2)}) collective-permute-start(bf16[320,1280]{1,0:T(8,128)(2,1)} %bitcast.66), channel_id=1, source_target_pairs={{0,1},{1,0},{2,3},{3,2},{4,5},{5,4},{6,7},{7,6},{8,9},{9,8},{10,11... | collective-permute-start | bytes 2457608 | tf_op jit(solution)/shard_map/ppermute | solution.py:232
  4.0 25.1 %collective-permute-start.2 = (bf16[320,1280]{1,0:T(8,128)(2,1)}, bf16[320,1280]{1,0:T(8,128)(2,1)S(1)}, u32[]{:S(2)}, u32[]{:S(2)}) collective-permute-start(bf16[320,1280]{1,0:T(8,128)(2,1)} %bitcast.67), channel_id=1, source_target_pairs={{0,4},{4,0},{8,12},{12,8},{16,20},{20,16},{24,28},{28,24},{1,5},{5... | collective-permute-start | bytes 2457608 | tf_op jit(solution)/shard_map/ppermute | solution.py:229
  6.5 13.8 %collective-permute-start = (bf16[2,80,1280]{2,1,0:T(8,128)(2,1)}, bf16[2,80,1280]{2,1,0:T(8,128)(2,1)S(1)}, u32[]{:S(2)}, u32[]{:S(2)}) collective-permute-start(bf16[2,80,1280]{2,1,0:T(8,128)(2,1)} %get-tuple-element.76), channel_id=1, source_target_pairs={{0,24},{4,28},{8,0},{12,4},{16,8},{20,12},{24,16},{28,20},{1,25},{... | collective-permute-start | bytes 1228808 | tf_op jit(solution)/shard_map/ppermute | solution.py:247
  10.2 18.9 %collective-permute-start.1 = (bf16[2,80,1280]{2,1,0:T(8,128)(2,1)}, bf16[2,80,1280]{2,1,0:T(8,128)(2,1)S(1)}, u32[]{:S(2)}, u32[]{:S(2)}) collective-permute-start(bf16[2,80,1280]{2,1,0:T(8,128)(2,1)} %get-tuple-element.77), channel_id=1, source_target_pairs={{0,8},{4,12},{8,16},{12,20},{16,24},{20,28},{24,0},{28,4},{1,9},{5... | collective-permute-start | bytes 1228808 | tf_op jit(solution)/shard_map/ppermute | solution.py:247
  10.2 18.9 %collective-permute-start.3 = (bf16[2,80,1280]{2,1,0:T(8,128)(2,1)}, bf16[2,80,1280]{2,1,0:T(8,128)(2,1)}, u32[]{:S(2)}, u32[]{:S(2)}) collective-permute-start(bf16[2,80,1280]{2,1,0:T(8,128)(2,1)} %get-tuple-element.92), channel_id=1, source_target_pairs={{0,2},{1,3},{2,0},{3,1},{4,6},{5,7},{6,4},{7,5},{8,10},{9,11},{10,... | collective-permute-start | bytes 1228808 | tf_op jit(solution)/shard_map/ppermute | solution.py:236
  29.1 20.7 %collective-permute-start.6 = (bf16[2,80,1280]{2,1,0:T(8,128)(2,1)}, bf16[2,80,1280]{2,1,0:T(8,128)(2,1)S(1)}, u32[]{:S(2)}, u32[]{:S(2)}) collective-permute-start(bf16[2,80,1280]{2,1,0:T(8,128)(2,1)} %get-tuple-element.82), channel_id=1, source_target_pairs={{0,16},{4,20},{8,24},{12,28},{16,0},{20,4},{24,8},{28,12},{1,17},{... | collective-permute-start | bytes 1228808 | tf_op jit(solution)/shard_map/ppermute | solution.py:247
  29.9 19.9 %collective-permute-start.7 = (bf16[2,80,1280]{2,1,0:T(8,128)(2,1)S(1)}, bf16[2,80,1280]{2,1,0:T(8,128)(2,1)S(1)}, u32[]{:S(2)}, u32[]{:S(2)}) collective-permute-start(bf16[2,80,1280]{2,1,0:T(8,128)(2,1)S(1)} %collective-permute-done), channel_id=1, source_target_pairs={{0,2},{1,3},{2,0},{3,1},{4,6},{5,7},{6,4},{7,5},{8,10},{9,11},{10,... | collective-permute-start | bytes 1228808 | tf_op jit(solution)/shard_map/ppermute | solution.py:236
  31.4 18.4 %collective-permute-start.8 = (bf16[2,80,1280]{2,1,0:T(8,128)(2,1)S(1)}, bf16[2,80,1280]{2,1,0:T(8,128)(2,1)S(1)}, u32[]{:S(2)}, u32[]{:S(2)}) collective-permute-start(bf16[2,80,1280]{2,1,0:T(8,128)(2,1)S(1)} %collective-permute-done.1), channel_id=1, source_target_pairs={{0,2},{1,3},{2,0},{3,1},{4,6},{5,7},{6,4},{7,5},{8,10},{9,11},{10,... | collective-permute-start | bytes 1228808 | tf_op jit(solution)/shard_map/ppermute | solution.py:236
  31.9 17.8 %collective-permute-start.5 = (bf16[320,1280]{1,0:T(8,128)(2,1)S(1)}, bf16[320,1280]{1,0:T(8,128)(2,1)S(1)}, u32[]{:S(2)}, u32[]{:S(2)}) collective-permute-start(bf16[320,1280]{1,0:T(8,128)(2,1)S(1)} %collective-permute-done.2.refs_2_), channel_id=1, source_target_pairs={{0,1},{1,0},{2,3},{3,2},{4,5},{5,4},{6,7},{7,6},{8,9},{9,8},{10,11... | collective-permute-start | bytes 2457608 | tf_op jit(solution)/shard_map/ppermute | solution.py:232
  31.9 20.9 %collective-permute-start.9 = (bf16[320,1280]{1,0:T(8,128)(2,1)}, bf16[320,1280]{1,0:T(8,128)(2,1)S(1)}, u32[]{:S(2)}, u32[]{:S(2)}) collective-permute-start(bf16[320,1280]{1,0:T(8,128)(2,1)} %bitcast.69), channel_id=1, source_target_pairs={{0,4},{4,0},{8,12},{12,8},{16,20},{20,16},{24,28},{28,24},{1,5},{5... | collective-permute-start | bytes 2457608 | tf_op jit(solution)/shard_map/ppermute | solution.py:229
  49.8 12.5 %collective-permute-start.13 = (bf16[2,80,1280]{2,1,0:T(8,128)(2,1)S(1)}, bf16[2,80,1280]{2,1,0:T(8,128)(2,1)S(1)}, u32[]{:S(2)}, u32[]{:S(2)}) collective-permute-start(bf16[2,80,1280]{2,1,0:T(8,128)(2,1)S(1)} %collective-permute-done.6), channel_id=1, source_target_pairs={{0,2},{1,3},{2,0},{3,1},{4,6},{5,7},{6,4},{7,5},{8,10},{9,11},{10,... | collective-permute-start | bytes 1228808 | tf_op jit(solution)/shard_map/ppermute | solution.py:236
  60.7 20.9 %collective-permute-start.12 = (bf16[240,1280]{1,0:T(8,128)(2,1)S(1)}, bf16[240,1280]{1,0:T(8,128)(2,1)S(1)}, u32[]{:S(2)}, u32[]{:S(2)}) collective-permute-start(bf16[240,1280]{1,0:T(8,128)(2,1)S(1)} %get-tuple-element.104), channel_id=1, source_target_pairs={{0,2},{1,3},{2,0},{3,1},{4,6},{5,7},{6,4},{7,5},{8,10},{9,11},{10,... | collective-permute-start | bytes 1843208 | tf_op jit(solution)/shard_map/ppermute | solution.py:242
  69.2 21.4 %collective-permute-start.21 = (bf16[320,1280]{1,0:T(8,128)(2,1)S(1)}, bf16[320,1280]{1,0:T(8,128)(2,1)S(1)}, u32[]{:S(2)}, u32[]{:S(2)}) collective-permute-start(bf16[320,1280]{1,0:T(8,128)(2,1)S(1)} %half.2), channel_id=1, source_target_pairs={{0,4},{4,0},{8,12},{12,8},{16,20},{20,16},{24,28},{28,24},{1,5},{5... | collective-permute-start | bytes 2457608 | tf_op jit(solution)/shard_map/ppermute | solution.py:229
  71.6 10.4 %collective-permute-start.16 = (bf16[80,1280]{1,0:T(8,128)(2,1)S(1)}, bf16[80,1280]{1,0:T(8,128)(2,1)S(1)}, u32[]{:S(2)}, u32[]{:S(2)}) collective-permute-start(bf16[80,1280]{1,0:T(8,128)(2,1)S(1)} %get-tuple-element.123), channel_id=1, source_target_pairs={{0,2},{1,3},{2,0},{3,1},{4,6},{5,7},{6,4},{7,5},{8,10},{9,11},{10,... | collective-permute-start | bytes 614408 | tf_op jit(solution)/shard_map/ppermute | solution.py:242
  73.1 17.5 %collective-permute-start.19 = (bf16[320,1280]{1,0:T(8,128)(2,1)S(1)}, bf16[320,1280]{1,0:T(8,128)(2,1)S(1)}, u32[]{:S(2)}, u32[]{:S(2)}) collective-permute-start(bf16[320,1280]{1,0:T(8,128)(2,1)S(1)} %weights.10), channel_id=1, source_target_pairs={{0,1},{1,0},{2,3},{3,2},{4,5},{5,4},{6,7},{7,6},{8,9},{9,8},{10,11... | collective-permute-start | bytes 2457608 | tf_op jit(solution)/shard_map/ppermute | solution.py:232
  75.8 5.7 %collective-permute-start.18 = (f32[8,1280]{1,0:T(8,128)S(1)}, f32[8,1280]{1,0:T(8,128)S(1)}, u32[]{:S(2)}, u32[]{:S(2)}) collective-permute-start(f32[8,1280]{1,0:T(8,128)S(1)} %add.34), channel_id=1, source_target_pairs={{0,16},{4,20},{8,24},{12,28},{16,0},{20,4},{24,8},{28,12},{1,17},{... | collective-permute-start | bytes 122888 | tf_op jit(solution)/shard_map/ppermute | solution.py:250
  81.5 31.0 %collective-permute-start.27 = (bf16[320,1280]{1,0:T(8,128)(2,1)S(1)}, bf16[320,1280]{1,0:T(8,128)(2,1)S(1)}, u32[]{:S(2)}, u32[]{:S(2)}) collective-permute-start(bf16[320,1280]{1,0:T(8,128)(2,1)S(1)} %weights.15), channel_id=1, source_target_pairs={{0,1},{1,0},{2,3},{3,2},{4,5},{5,4},{6,7},{7,6},{8,9},{9,8},{10,11... | collective-permute-start | bytes 2457608 | tf_op jit(solution)/shard_map/ppermute | solution.py:232
  81.6 13.6 %collective-permute-start.24 = (bf16[320,1280]{1,0:T(8,128)(2,1)S(1)}, bf16[320,1280]{1,0:T(8,128)(2,1)S(1)}, u32[]{:S(2)}, u32[]{:S(2)}) collective-permute-start(bf16[320,1280]{1,0:T(8,128)(2,1)S(1)} %weights.13), channel_id=1, source_target_pairs={{0,1},{1,0},{2,3},{3,2},{4,5},{5,4},{6,7},{7,6},{8,9},{9,8},{10,11... | collective-permute-start | bytes 2457608 | tf_op jit(solution)/shard_map/ppermute | solution.py:232
  82.3 8.3 %collective-permute-start.20 = (f32[8,1280]{1,0:T(8,128)S(1)}, f32[8,1280]{1,0:T(8,128)S(1)}, u32[]{:S(2)}, u32[]{:S(2)}) collective-permute-start(f32[8,1280]{1,0:T(8,128)S(1)} %add.35), channel_id=1, source_target_pairs={{0,4},{4,0},{8,12},{12,8},{16,20},{20,16},{24,28},{28,24},{1,5},{5... | collective-permute-start | bytes 122888 | tf_op jit(solution)/shard_map/ppermute | solution.py:250
  90.7 21.7 %collective-permute-start.26 = (bf16[320,1280]{1,0:T(8,128)(2,1)S(1)}, bf16[320,1280]{1,0:T(8,128)(2,1)S(1)}, u32[]{:S(2)}, u32[]{:S(2)}) collective-permute-start(bf16[320,1280]{1,0:T(8,128)(2,1)S(1)} %half.3), channel_id=1, source_target_pairs={{0,4},{4,0},{8,12},{12,8},{16,20},{20,16},{24,28},{28,24},{1,5},{5... | collective-permute-start | bytes 2457608 | tf_op jit(solution)/shard_map/ppermute | solution.py:229
  91.3 9.9 %collective-permute-start.23 = (bf16[80,1280]{1,0:T(8,128)(2,1)S(1)}, bf16[80,1280]{1,0:T(8,128)(2,1)S(1)}, u32[]{:S(2)}, u32[]{:S(2)}) collective-permute-start(bf16[80,1280]{1,0:T(8,128)(2,1)S(1)} %get-tuple-element.150), channel_id=1, source_target_pairs={{0,8},{4,12},{8,16},{12,20},{16,24},{20,28},{24,0},{28,4},{1,9},{5... | collective-permute-start | bytes 614408 | tf_op jit(solution)/shard_map/ppermute | solution.py:247
  93.0 10.2 %collective-permute-start.22 = (bf16[80,1280]{1,0:T(8,128)(2,1)S(1)}, bf16[80,1280]{1,0:T(8,128)(2,1)S(1)}, u32[]{:S(2)}, u32[]{:S(2)}) collective-permute-start(bf16[80,1280]{1,0:T(8,128)(2,1)S(1)} %get-tuple-element.151), channel_id=1, source_target_pairs={{0,24},{4,28},{8,0},{12,4},{16,8},{20,12},{24,16},{28,20},{1,25},{... | collective-permute-start | bytes 614408 | tf_op jit(solution)/shard_map/ppermute | solution.py:247
  95.2 17.3 %collective-permute-start.25 = (bf16[80,1280]{1,0:T(8,128)(2,1)S(1)}, bf16[80,1280]{1,0:T(8,128)(2,1)S(1)}, u32[]{:S(2)}, u32[]{:S(2)}) collective-permute-start(bf16[80,1280]{1,0:T(8,128)(2,1)S(1)} %bitcast.75), channel_id=1, source_target_pairs={{0,16},{4,20},{8,24},{12,28},{16,0},{20,4},{24,8},{28,12},{1,17},{... | collective-permute-start | bytes 614408 | tf_op jit(solution)/shard_map/ppermute | solution.py:247
  101.2 11.3 %collective-permute-start.28 = (f32[8,1280]{1,0:T(8,128)S(1)}, f32[8,1280]{1,0:T(8,128)S(1)}, u32[]{:S(2)}, u32[]{:S(2)}) collective-permute-start(f32[8,1280]{1,0:T(8,128)S(1)} %add.38.total_ref), channel_id=1, source_target_pairs={{0,2},{1,3},{2,0},{3,1},{4,6},{5,7},{6,4},{7,5},{8,10},{9,11},{10,... | collective-permute-start | bytes 122888 | tf_op jit(solution)/shard_map/ppermute | solution.py:472
  (11 other events, 89.8 us)

commit v12 on v11

--- a/solution.py
+++ b/solution.py
@@ -10,7 +10,7 @@
 from jax.sharding import PartitionSpec as P
 
 F32 = jnp.float32
-ORDER = 24
+ORDER = 27
 BF16 = jnp.bfloat16
 VMEM = pl.BlockSpec(memory_space=pltpu.VMEM)
 ANY = pl.BlockSpec(memory_space=pl.ANY)
@@ -452,6 +452,9 @@
     early_back, late_back = tied((early_back, late_back), total)
     early_rows = add_rows(early_own, early_back)
     late_rows = add_rows(late_own, late_back)
+    moved = range(quarter, 2 * quarter)
+    send_back([steps[at] for at in moved], [early_rows[at] for at in moved])
+    moved_rows = [returned[steps[at]] for at in moved]
     total = tied(total, (early_rows, late_rows))
     total = pairwise(total, "expert", halves, 1)
     hidden, grad_pre = tied((hidden, grad_pre), in_stay)
@@ -460,10 +463,13 @@
     in_rest = over_pair(weight_gradient(1, 1, grad_pre, rows_m, BF16))
     in_mine = weight_gradient(3, 1, grad_pre, rows_m, F32)
 
-    stage = (out_other, early_rows, late_rows, in_pair, in_stay, total)
-    out_other, early_rows, late_rows, in_pair, in_stay, total = tied(stage, stage)
+    stage = (out_other, early_rows, late_rows, moved_rows, in_pair, in_stay, total)
+    out_other, early_rows, late_rows, moved_rows, in_pair, in_stay, total = tied(stage, stage)
+    for at, value in zip(moved, moved_rows):
+        returned[steps[at]] = value
     in_other = over_half(half_sum(in_stay, in_pair))
-    send_back(early, early_rows)
+    rest = [at for at in range(len(early)) if at not in moved]
+    send_back([steps[at] for at in rest], [early_rows[at] for at in rest])
     send_back(late, late_rows)
     bit = 2
     while bit < groups // 2:

time: 115 us -> 114 us (level)
  waiting for transfers between devices: 55.2 us -> 52.4 us
  starting transfers between devices: 27.7 us -> 29.6 us
    ppermute x6, waiting for transfers between devices: 44.9 us -> 41.5 us  [over_experts(): lax.ppermute(value, 'expert', [(i, (i + 2 * step) % halves) for i in rang...]
    ppermute x6, starting transfers between devices: 8.68 us -> 11.5 us  [over_experts(): lax.ppermute(value, 'expert', [(i, (i + 2 * step) % halves) for i in rang...]
    ppermute x4, waiting for transfers between devices: 1.42 us -> 3.94 us  [over_half(): return lax.ppermute(value, 'expert', [(i, i ^ 1) for i in range(halves)])]
    ppermute x4, waiting for transfers between devices: 8.82 us -> 6.92 us  [pairwise(): lax.ppermute(value, name, [(i, i ^ bit) for i in range(size)])]
  transfers between devices with their start and end apart: 29 -> 29, of which waited for: 10 -> 9; matrix products, arithmetic and copies ran while one was open for 4% -> 5% of each run, Pallas kernels for 17% -> 17%
where the time goes in v12:
time: 114 us
  waiting for transfers between devices  52.4 us (46%)
  starting transfers between devices  29.6 us (26%)
  Pallas kernels  23.9 us (21%)
  local copies, waits for them, and re-layouts  4.46 us (4%)
  other arithmetic  2.43 us (2%)
    ppermute x6, waiting for transfers between devices, over_experts(): lax.ppermute(value, 'expert', [(i, (i + 2 * step) % halves) for i in rang...  41.5 us
    pallas_call x21, Pallas kernels, call(): pl.pallas_call(kernel, out_shape=outs, in_specs=specs or [VMEM] * len(arg...  23.9 us
    ppermute x6, starting transfers between devices, over_experts(): lax.ppermute(value, 'expert', [(i, (i + 2 * step) % halves) for i in rang...  11.5 us
    ppermute x4, waiting for transfers between devices, pairwise(): lax.ppermute(value, name, [(i, i ^ bit) for i in range(size)])  6.92 us
    ppermute x4, starting transfers between devices, over_columns(): lax.ppermute(value, 'dp', [(i, (i + 2 * step) % groups) for i in range(gr...  5.06 us
    ppermute x4, starting transfers between devices, pairwise(): lax.ppermute(value, name, [(i, i ^ bit) for i in range(size)])  4.8 us
    ppermute x4, starting transfers between devices, over_half(): return lax.ppermute(value, 'expert', [(i, i ^ 1) for i in range(halves)])  4.67 us
    unnamed x20, local copies, waits for them, and re-layouts  4.25 us
  transfers between devices with their start and end apart: 29, of which 9 were waited for; matrix products, arithmetic and copies ran while one was open for 5% of the time, Pallas kernels for 17%

profile of v12, /device:TPU:0, one launch (start us, length us, event | category | flops | bytes accessed | tf_op | source)
XLA Modules:
  0.0 113.8 jit_solution(6449841725889547632)
XLA Ops:
  0.6 2.8 %dispatch.1 = (bf16[2,80,1280]{2,1,0:T(8,128)(2,1)}, bf16[2,80,1280]{2,1,0:T(8,128)(2,1)}, bf16[2,80,1280]{2,1,0:T(8,128)(2,1)}, bf16[2,80,1280]{2,1,0:T(8,128)(2,1)}) custom-call(bf16[128,1280]{1,0:T(8,128)(2,1)} %x_ref.1, f32[1280]{0:T(1024)} %gain_ref.1, s32[2,128]{1,0:T(2,128)} %bitcast.70, bf16[128,1280]{1,0:T(8,128)(2,1)} %d_ref.1), custom_call_target="tpu_custom_call" | custom-call | flops 209715200 | bytes 409600 | tf_op jit(solution)/shard_map/dispatch/pallas_call | solution.py:205
  3.4 3.0 %collective-permute-start.4 = (bf16[320,1280]{1,0:T(8,128)(2,1)}, bf16[320,1280]{1,0:T(8,128)(2,1)S(1)}, u32[]{:S(2)}, u32[]{:S(2)}) collective-permute-start(bf16[320,1280]{1,0:T(8,128)(2,1)} %bitcast.64), channel_id=1, source_target_pairs={{0,4},{4,0},{8,12},{12,8},{16,20},{20,16},{24,28},{28,24},{1,5},{5... | collective-permute-start | bytes 2457608 | tf_op jit(solution)/shard_map/ppermute | solution.py:229
  6.5 3.6 %collective-permute-start = (bf16[2,80,1280]{2,1,0:T(8,128)(2,1)}, bf16[2,80,1280]{2,1,0:T(8,128)(2,1)S(1)}, u32[]{:S(2)}, u32[]{:S(2)}) collective-permute-start(bf16[2,80,1280]{2,1,0:T(8,128)(2,1)} %get-tuple-element.77), channel_id=1, source_target_pairs={{0,24},{4,28},{8,0},{12,4},{16,8},{20,12},{24,16},{28,20},{1,25},{... | collective-permute-start | bytes 1228808 | tf_op jit(solution)/shard_map/ppermute | solution.py:247
  10.1 1.5 %collective-permute-start.3 = (bf16[2,80,1280]{2,1,0:T(8,128)(2,1)}, bf16[2,80,1280]{2,1,0:T(8,128)(2,1)}, u32[]{:S(2)}, u32[]{:S(2)}) collective-permute-start(bf16[2,80,1280]{2,1,0:T(8,128)(2,1)} %get-tuple-element.93), channel_id=1, source_target_pairs={{0,2},{1,3},{2,0},{3,1},{4,6},{5,7},{6,4},{7,5},{8,10},{9,11},{10,... | collective-permute-start | bytes 1228808 | tf_op jit(solution)/shard_map/ppermute | solution.py:236
  14.3 6.0 %collective-permute-done = bf16[2,80,1280]{2,1,0:T(8,128)(2,1)S(1)} collective-permute-done((bf16[2,80,1280]{2,1,0:T(8,128)(2,1)}, bf16[2,80,1280]{2,1,0:T(8,128)(2,1)S(1)}, u32[]{:S(2)}, u32[]{:S(2)}) %collective-permute-start) | collective-permute-done | bytes 409632 | tf_op jit(solution)/shard_map/ppermute | solution.py:247
  20.2 9.1 %collective-permute-done.1 = bf16[2,80,1280]{2,1,0:T(8,128)(2,1)S(1)} collective-permute-done((bf16[2,80,1280]{2,1,0:T(8,128)(2,1)}, bf16[2,80,1280]{2,1,0:T(8,128)(2,1)S(1)}, u32[]{:S(2)}, u32[]{:S(2)}) %collective-permute-start.1) | collective-permute-done | bytes 409632 | tf_op jit(solution)/shard_map/ppermute | solution.py:247
  30.2 1.5 %collective-permute-start.7 = (bf16[2,80,1280]{2,1,0:T(8,128)(2,1)S(1)}, bf16[2,80,1280]{2,1,0:T(8,128)(2,1)S(1)}, u32[]{:S(2)}, u32[]{:S(2)}) collective-permute-start(bf16[2,80,1280]{2,1,0:T(8,128)(2,1)S(1)} %collective-permute-done), channel_id=1, source_target_pairs={{0,2},{1,3},{2,0},{3,1},{4,6},{5,7},{6,4},{7,5},{8,10},{9,11},{10,... | collective-permute-start | bytes 1228808 | tf_op jit(solution)/shard_map/ppermute | solution.py:236
  35.1 15.3 %collective-permute-done.5 = bf16[2,80,1280]{2,1,0:T(8,128)(2,1)S(1)} collective-permute-done((bf16[2,80,1280]{2,1,0:T(8,128)(2,1)}, bf16[2,80,1280]{2,1,0:T(8,128)(2,1)S(1)}, u32[]{:S(2)}, u32[]{:S(2)}) %collective-permute-start.5) | collective-permute-done | bytes 409632 | tf_op jit(solution)/shard_map/ppermute | solution.py:247
  50.4 1.6 %collective-permute-start.13 = (bf16[2,80,1280]{2,1,0:T(8,128)(2,1)S(1)}, bf16[2,80,1280]{2,1,0:T(8,128)(2,1)S(1)}, u32[]{:S(2)}, u32[]{:S(2)}) collective-permute-start(bf16[2,80,1280]{2,1,0:T(8,128)(2,1)S(1)} %collective-permute-done.5), channel_id=1, source_target_pairs={{0,2},{1,3},{2,0},{3,1},{4,6},{5,7},{6,4},{7,5},{8,10},{9,11},{10,... | collective-permute-start | bytes 1228808 | tf_op jit(solution)/shard_map/ppermute | solution.py:236
  53.3 3.3 %first.2 = (bf16[480,1280]{1,0:T(8,128)(2,1)S(1)}, f32[480,1280]{1,0:T(8,128)S(1)}, bf16[480,1280]{1,0:T(8,128)(2,1)S(1)}, f32[480,128]{1,0:T(8,128)S(1)}) custom-call(bf16[480,1280]{1,0:T(8,128)(2,1)S(1)} %get-tuple-element.155.m_ref, bf16[480,1280]{1,0:T(8,128)(2,1)S(1)} %get-tuple-element.154.d_ref, bf16[1280,1280]{1,0:T(8,128)(2,1)S(1)} %join.3.first_ref, ...), custom_call_target="tpu_custom_call" | custom-call | flops 1572864000 | bytes 3072000 | tf_op jit(solution)/shard_map/first/pallas_call | solution.py:205
  57.0 2.0 %second.2 = (bf16[480,1280]{1,0:T(8,128)(2,1)S(1)}, f32[480,128]{1,0:T(8,128)S(1)}) custom-call(bf16[480,1280]{1,0:T(8,128)(2,1)S(1)} %get-tuple-element.154.d_ref, bf16[1280,1280]{1,0:T(8,128)(2,1)S(1)} %join.2.second_ref, bf16[480,1280]{1,0:T(8,128)(2,1)S(1)} %get-tuple-element.99.hidden_ref, f32[480,1280]{1,0:T(8,128)S(1)} %get-tuple-element.100.slope_ref, ...), custom_call_target="tpu_custom_call" | custom-call | flops 1572864000 | bytes 3072000 | tf_op jit(solution)/shard_map/second/pallas_call | solution.py:205
  59.0 1.9 %rows.2 = (f32[240,1280]{1,0:T(8,128)S(1)}, bf16[240,1280]{1,0:T(8,128)(2,1)S(1)}, f32[8,1280]{1,0:T(8,128)S(1)}) custom-call(bf16[480,1280]{1,0:T(8,128)(2,1)S(1)} %get-tuple-element.155.m_ref, bf16[480,1280]{1,0:T(8,128)(2,1)S(1)} %get-tuple-element.102.pre_ref, f32[480,128]{1,0:T(8,128)S(1)} %get-tuple-element.103.logit_ref, ...), custom_call_target="tpu_custom_call" | custom-call | flops 1572864000 | bytes 3072000 | tf_op jit(solution)/shard_map/rows/pallas_call | solution.py:205
  61.0 1.6 %collective-permute-start.12 = (bf16[240,1280]{1,0:T(8,128)(2,1)S(1)}, bf16[240,1280]{1,0:T(8,128)(2,1)S(1)}, u32[]{:S(2)}, u32[]{:S(2)}) collective-permute-start(bf16[240,1280]{1,0:T(8,128)(2,1)S(1)} %get-tuple-element.105), channel_id=1, source_target_pairs={{0,2},{1,3},{2,0},{3,1},{4,6},{5,7},{6,4},{7,5},{8,10},{9,11},{10,... | collective-permute-start | bytes 1843208 | tf_op jit(solution)/shard_map/ppermute | solution.py:242
  62.7 1.5 %first.3 = (bf16[160,1280]{1,0:T(8,128)(2,1)S(1)}, f32[160,1280]{1,0:T(8,128)S(1)}, bf16[160,1280]{1,0:T(8,128)(2,1)S(1)}, f32[160,128]{1,0:T(8,128)S(1)}) custom-call(bf16[160,1280]{1,0:T(8,128)(2,1)S(1)} %pad_maximum_fusion.2.m_ref, bf16[160,1280]{1,0:T(8,128)(2,1)S(1)} %pad_maximum_fusion.3.d_ref, bf16[1280,1280]{1,0:T(8,128)(2,1)S(1)} %join.3.first_ref, ...), custom_call_target="tpu_custom_call" | custom-call | flops 524288000 | bytes 1024000 | tf_op jit(solution)/shard_map/first/pallas_call | solution.py:205
  70.3 1.6 %collective-permute-start.17 = (f32[8,1280]{1,0:T(8,128)S(1)}, f32[8,1280]{1,0:T(8,128)S(1)}, u32[]{:S(2)}, u32[]{:S(2)}) collective-permute-start(f32[8,1280]{1,0:T(8,128)S(1)} %add.33), channel_id=1, source_target_pairs={{0,8},{4,12},{8,0},{12,4},{16,24},{20,28},{24,16},{28,20},{1,9},{5... | collective-permute-start | bytes 122888 | tf_op jit(solution)/shard_map/ppermute | solution.py:250
  76.1 2.3 %collective-permute-start.18 = (f32[8,1280]{1,0:T(8,128)S(1)}, f32[8,1280]{1,0:T(8,128)S(1)}, u32[]{:S(2)}, u32[]{:S(2)}) collective-permute-start(f32[8,1280]{1,0:T(8,128)S(1)} %add.34), channel_id=1, source_target_pairs={{0,16},{4,20},{8,24},{12,28},{16,0},{20,4},{24,8},{28,12},{1,17},{... | collective-permute-start | bytes 122888 | tf_op jit(solution)/shard_map/ppermute | solution.py:250
  79.2 2.5 %collective-permute-done.18 = f32[8,1280]{1,0:T(8,128)S(1)} collective-permute-done((f32[8,1280]{1,0:T(8,128)S(1)}, f32[8,1280]{1,0:T(8,128)S(1)}, u32[]{:S(2)}, u32[]{:S(2)}) %collective-permute-start.18) | collective-permute-done | bytes 40992 | tf_op jit(solution)/shard_map/ppermute | solution.py:250
  82.0 3.2 %collective-permute-start.19 = (bf16[80,1280]{1,0:T(8,128)(2,1)S(1)}, bf16[80,1280]{1,0:T(8,128)(2,1)S(1)}, u32[]{:S(2)}, u32[]{:S(2)}) collective-permute-start(bf16[80,1280]{1,0:T(8,128)(2,1)S(1)} %slice.87), channel_id=1, source_target_pairs={{0,24},{4,28},{8,0},{12,4},{16,8},{20,12},{24,16},{28,20},{1,25},{... | collective-permute-start | bytes 614408 | tf_op jit(solution)/shard_map/ppermute | solution.py:247
  86.7 4.1 %collective-permute-done.21 = f32[8,1280]{1,0:T(8,128)S(1)} collective-permute-done((f32[8,1280]{1,0:T(8,128)S(1)}, f32[8,1280]{1,0:T(8,128)S(1)}, u32[]{:S(2)}, u32[]{:S(2)}) %collective-permute-start.21) | collective-permute-done | bytes 40992 | tf_op jit(solution)/shard_map/ppermute | solution.py:250
  92.6 1.8 %collective-permute-start.23 = (bf16[80,1280]{1,0:T(8,128)(2,1)S(1)}, bf16[80,1280]{1,0:T(8,128)(2,1)S(1)}, u32[]{:S(2)}, u32[]{:S(2)}) collective-permute-start(bf16[80,1280]{1,0:T(8,128)(2,1)S(1)} %bitcast.73), channel_id=1, source_target_pairs={{0,16},{4,20},{8,24},{12,28},{16,0},{20,4},{24,8},{28,12},{1,17},{... | collective-permute-start | bytes 614408 | tf_op jit(solution)/shard_map/ppermute | solution.py:247
  94.4 2.2 %collective-permute-start.24 = (bf16[80,1280]{1,0:T(8,128)(2,1)S(1)}, bf16[80,1280]{1,0:T(8,128)(2,1)S(1)}, u32[]{:S(2)}, u32[]{:S(2)}) collective-permute-start(bf16[80,1280]{1,0:T(8,128)(2,1)S(1)} %get-tuple-element.151), channel_id=1, source_target_pairs={{0,8},{4,12},{8,16},{12,20},{16,24},{20,28},{24,0},{28,4},{1,9},{5... | collective-permute-start | bytes 614408 | tf_op jit(solution)/shard_map/ppermute | solution.py:247
  97.8 11.0 %collective-permute-done.23 = bf16[80,1280]{1,0:T(8,128)(2,1)S(1)} collective-permute-done((bf16[80,1280]{1,0:T(8,128)(2,1)S(1)}, bf16[80,1280]{1,0:T(8,128)(2,1)S(1)}, u32[]{:S(2)}, u32[]{:S(2)}) %collective-permute-start.23) | collective-permute-done | bytes 204832 | tf_op jit(solution)/shard_map/ppermute | solution.py:247
  108.8 2.9 %collective-permute-done.26.other_ref = bf16[320,1280]{1,0:T(8,128)(2,1)S(1)} collective-permute-done((bf16[320,1280]{1,0:T(8,128)(2,1)S(1)}, bf16[320,1280]{1,0:T(8,128)(2,1)S(1)}, u32[]{:S(2)}, u32[]{:S(2)}) %collective-permute-start.26) | collective-permute-done | bytes 819232 | tf_op jit(solution)/shard_map/ppermute | solution.py:229
  111.8 2.0 %finish.1 = (bf16[128,1280]{1,0:T(8,128)(2,1)}, bf16[320,1280]{1,0:T(8,128)(2,1)}, f32[4,1280]{1,0:T(4,128)}, f32[1280]{0:T(1024)}) custom-call(f32[128,1280]{1,0:T(8,128)S(1)} %get-tuple-element.90.norm_ref, f32[128,128]{1,0:T(8,128)S(1)} %get-tuple-element.91.deviation_ref, bf16[320,128]{1,0:T(8,128)(2,1)S(1)} %get-tuple-element.92.places_ref, ...), custom_call_target="tpu_custom_call" | custom-call | tf_op jit(solution)/shard_map/finish/pallas_call | solution.py:205
  (97 shorter events, 24.5 us)
Async XLA Ops:
  3.4 25.9 %collective-permute-start.4 = (bf16[320,1280]{1,0:T(8,128)(2,1)}, bf16[320,1280]{1,0:T(8,128)(2,1)S(1)}, u32[]{:S(2)}, u32[]{:S(2)}) collective-permute-start(bf16[320,1280]{1,0:T(8,128)(2,1)} %bitcast.64), channel_id=1, source_target_pairs={{0,4},{4,0},{8,12},{12,8},{16,20},{20,16},{24,28},{28,24},{1,5},{5... | collective-permute-start | bytes 2457608 | tf_op jit(solution)/shard_map/ppermute | solution.py:229
  6.5 22.9 %collective-permute-start.2 = (bf16[320,1280]{1,0:T(8,128)(2,1)}, bf16[320,1280]{1,0:T(8,128)(2,1)S(1)}, u32[]{:S(2)}, u32[]{:S(2)}) collective-permute-start(bf16[320,1280]{1,0:T(8,128)(2,1)} %bitcast.65), channel_id=1, source_target_pairs={{0,1},{1,0},{2,3},{3,2},{4,5},{5,4},{6,7},{7,6},{8,9},{9,8},{10,11... | collective-permute-start | bytes 2457608 | tf_op jit(solution)/shard_map/ppermute | solution.py:232
  6.5 13.8 %collective-permute-start = (bf16[2,80,1280]{2,1,0:T(8,128)(2,1)}, bf16[2,80,1280]{2,1,0:T(8,128)(2,1)S(1)}, u32[]{:S(2)}, u32[]{:S(2)}) collective-permute-start(bf16[2,80,1280]{2,1,0:T(8,128)(2,1)} %get-tuple-element.77), channel_id=1, source_target_pairs={{0,24},{4,28},{8,0},{12,4},{16,8},{20,12},{24,16},{28,20},{1,25},{... | collective-permute-start | bytes 1228808 | tf_op jit(solution)/shard_map/ppermute | solution.py:247
  10.1 19.3 %collective-permute-start.1 = (bf16[2,80,1280]{2,1,0:T(8,128)(2,1)}, bf16[2,80,1280]{2,1,0:T(8,128)(2,1)S(1)}, u32[]{:S(2)}, u32[]{:S(2)}) collective-permute-start(bf16[2,80,1280]{2,1,0:T(8,128)(2,1)} %get-tuple-element.78), channel_id=1, source_target_pairs={{0,8},{4,12},{8,16},{12,20},{16,24},{20,28},{24,0},{28,4},{1,9},{5... | collective-permute-start | bytes 1228808 | tf_op jit(solution)/shard_map/ppermute | solution.py:247
  10.1 19.3 %collective-permute-start.3 = (bf16[2,80,1280]{2,1,0:T(8,128)(2,1)}, bf16[2,80,1280]{2,1,0:T(8,128)(2,1)}, u32[]{:S(2)}, u32[]{:S(2)}) collective-permute-start(bf16[2,80,1280]{2,1,0:T(8,128)(2,1)} %get-tuple-element.93), channel_id=1, source_target_pairs={{0,2},{1,3},{2,0},{3,1},{4,6},{5,7},{6,4},{7,5},{8,10},{9,11},{10,... | collective-permute-start | bytes 1228808 | tf_op jit(solution)/shard_map/ppermute | solution.py:236
  29.4 21.0 %collective-permute-start.5 = (bf16[2,80,1280]{2,1,0:T(8,128)(2,1)}, bf16[2,80,1280]{2,1,0:T(8,128)(2,1)S(1)}, u32[]{:S(2)}, u32[]{:S(2)}) collective-permute-start(bf16[2,80,1280]{2,1,0:T(8,128)(2,1)} %get-tuple-element.82), channel_id=1, source_target_pairs={{0,16},{4,20},{8,24},{12,28},{16,0},{20,4},{24,8},{28,12},{1,17},{... | collective-permute-start | bytes 1228808 | tf_op jit(solution)/shard_map/ppermute | solution.py:247
  30.2 20.3 %collective-permute-start.7 = (bf16[2,80,1280]{2,1,0:T(8,128)(2,1)S(1)}, bf16[2,80,1280]{2,1,0:T(8,128)(2,1)S(1)}, u32[]{:S(2)}, u32[]{:S(2)}) collective-permute-start(bf16[2,80,1280]{2,1,0:T(8,128)(2,1)S(1)} %collective-permute-done), channel_id=1, source_target_pairs={{0,2},{1,3},{2,0},{3,1},{4,6},{5,7},{6,4},{7,5},{8,10},{9,11},{10,... | collective-permute-start | bytes 1228808 | tf_op jit(solution)/shard_map/ppermute | solution.py:236
  31.7 18.8 %collective-permute-start.8 = (bf16[2,80,1280]{2,1,0:T(8,128)(2,1)S(1)}, bf16[2,80,1280]{2,1,0:T(8,128)(2,1)S(1)}, u32[]{:S(2)}, u32[]{:S(2)}) collective-permute-start(bf16[2,80,1280]{2,1,0:T(8,128)(2,1)S(1)} %collective-permute-done.1), channel_id=1, source_target_pairs={{0,2},{1,3},{2,0},{3,1},{4,6},{5,7},{6,4},{7,5},{8,10},{9,11},{10,... | collective-permute-start | bytes 1228808 | tf_op jit(solution)/shard_map/ppermute | solution.py:236
  32.2 18.2 %collective-permute-start.6 = (bf16[320,1280]{1,0:T(8,128)(2,1)S(1)}, bf16[320,1280]{1,0:T(8,128)(2,1)S(1)}, u32[]{:S(2)}, u32[]{:S(2)}) collective-permute-start(bf16[320,1280]{1,0:T(8,128)(2,1)S(1)} %collective-permute-done.4.refs_2_), channel_id=1, source_target_pairs={{0,1},{1,0},{2,3},{3,2},{4,5},{5,4},{6,7},{7,6},{8,9},{9,8},{10,11... | collective-permute-start | bytes 2457608 | tf_op jit(solution)/shard_map/ppermute | solution.py:232
  32.2 20.9 %collective-permute-start.9 = (bf16[320,1280]{1,0:T(8,128)(2,1)}, bf16[320,1280]{1,0:T(8,128)(2,1)S(1)}, u32[]{:S(2)}, u32[]{:S(2)}) collective-permute-start(bf16[320,1280]{1,0:T(8,128)(2,1)} %bitcast.67), channel_id=1, source_target_pairs={{0,4},{4,0},{8,12},{12,8},{16,20},{20,16},{24,28},{28,24},{1,5},{5... | collective-permute-start | bytes 2457608 | tf_op jit(solution)/shard_map/ppermute | solution.py:229
  50.4 12.1 %collective-permute-start.13 = (bf16[2,80,1280]{2,1,0:T(8,128)(2,1)S(1)}, bf16[2,80,1280]{2,1,0:T(8,128)(2,1)S(1)}, u32[]{:S(2)}, u32[]{:S(2)}) collective-permute-start(bf16[2,80,1280]{2,1,0:T(8,128)(2,1)S(1)} %collective-permute-done.5), channel_id=1, source_target_pairs={{0,2},{1,3},{2,0},{3,1},{4,6},{5,7},{6,4},{7,5},{8,10},{9,11},{10,... | collective-permute-start | bytes 1228808 | tf_op jit(solution)/shard_map/ppermute | solution.py:236
  61.0 20.8 %collective-permute-start.12 = (bf16[240,1280]{1,0:T(8,128)(2,1)S(1)}, bf16[240,1280]{1,0:T(8,128)(2,1)S(1)}, u32[]{:S(2)}, u32[]{:S(2)}) collective-permute-start(bf16[240,1280]{1,0:T(8,128)(2,1)S(1)} %get-tuple-element.105), channel_id=1, source_target_pairs={{0,2},{1,3},{2,0},{3,1},{4,6},{5,7},{6,4},{7,5},{8,10},{9,11},{10,... | collective-permute-start | bytes 1843208 | tf_op jit(solution)/shard_map/ppermute | solution.py:242
  69.5 21.3 %collective-permute-start.20 = (bf16[320,1280]{1,0:T(8,128)(2,1)S(1)}, bf16[320,1280]{1,0:T(8,128)(2,1)S(1)}, u32[]{:S(2)}, u32[]{:S(2)}) collective-permute-start(bf16[320,1280]{1,0:T(8,128)(2,1)S(1)} %half.2), channel_id=1, source_target_pairs={{0,4},{4,0},{8,12},{12,8},{16,20},{20,16},{24,28},{28,24},{1,5},{5... | collective-permute-start | bytes 2457608 | tf_op jit(solution)/shard_map/ppermute | solution.py:229
  70.3 5.7 %collective-permute-start.17 = (f32[8,1280]{1,0:T(8,128)S(1)}, f32[8,1280]{1,0:T(8,128)S(1)}, u32[]{:S(2)}, u32[]{:S(2)}) collective-permute-start(f32[8,1280]{1,0:T(8,128)S(1)} %add.33), channel_id=1, source_target_pairs={{0,8},{4,12},{8,0},{12,4},{16,24},{20,28},{24,16},{28,20},{1,9},{5... | collective-permute-start | bytes 122888 | tf_op jit(solution)/shard_map/ppermute | solution.py:250
  71.9 9.9 %collective-permute-start.16 = (bf16[80,1280]{1,0:T(8,128)(2,1)S(1)}, bf16[80,1280]{1,0:T(8,128)(2,1)S(1)}, u32[]{:S(2)}, u32[]{:S(2)}) collective-permute-start(bf16[80,1280]{1,0:T(8,128)(2,1)S(1)} %get-tuple-element.124), channel_id=1, source_target_pairs={{0,2},{1,3},{2,0},{3,1},{4,6},{5,7},{6,4},{7,5},{8,10},{9,11},{10,... | collective-permute-start | bytes 614408 | tf_op jit(solution)/shard_map/ppermute | solution.py:242
  73.3 17.5 %collective-permute-start.22 = (bf16[320,1280]{1,0:T(8,128)(2,1)S(1)}, bf16[320,1280]{1,0:T(8,128)(2,1)S(1)}, u32[]{:S(2)}, u32[]{:S(2)}) collective-permute-start(bf16[320,1280]{1,0:T(8,128)(2,1)S(1)} %weights.10), channel_id=1, source_target_pairs={{0,1},{1,0},{2,3},{3,2},{4,5},{5,4},{6,7},{7,6},{8,9},{9,8},{10,11... | collective-permute-start | bytes 2457608 | tf_op jit(solution)/shard_map/ppermute | solution.py:232
  76.1 5.7 %collective-permute-start.18 = (f32[8,1280]{1,0:T(8,128)S(1)}, f32[8,1280]{1,0:T(8,128)S(1)}, u32[]{:S(2)}, u32[]{:S(2)}) collective-permute-start(f32[8,1280]{1,0:T(8,128)S(1)} %add.34), channel_id=1, source_target_pairs={{0,16},{4,20},{8,24},{12,28},{16,0},{20,4},{24,8},{28,12},{1,17},{... | collective-permute-start | bytes 122888 | tf_op jit(solution)/shard_map/ppermute | solution.py:250
  81.7 12.7 %collective-permute-start.25 = (bf16[320,1280]{1,0:T(8,128)(2,1)S(1)}, bf16[320,1280]{1,0:T(8,128)(2,1)S(1)}, u32[]{:S(2)}, u32[]{:S(2)}) collective-permute-start(bf16[320,1280]{1,0:T(8,128)(2,1)S(1)} %weights.13), channel_id=1, source_target_pairs={{0,1},{1,0},{2,3},{3,2},{4,5},{5,4},{6,7},{7,6},{8,9},{9,8},{10,11... | collective-permute-start | bytes 2457608 | tf_op jit(solution)/shard_map/ppermute | solution.py:232
  82.0 8.8 %collective-permute-start.19 = (bf16[80,1280]{1,0:T(8,128)(2,1)S(1)}, bf16[80,1280]{1,0:T(8,128)(2,1)S(1)}, u32[]{:S(2)}, u32[]{:S(2)}) collective-permute-start(bf16[80,1280]{1,0:T(8,128)(2,1)S(1)} %slice.87), channel_id=1, source_target_pairs={{0,24},{4,28},{8,0},{12,4},{16,8},{20,12},{24,16},{28,20},{1,25},{... | collective-permute-start | bytes 614408 | tf_op jit(solution)/shard_map/ppermute | solution.py:247
  90.8 21.0 %collective-permute-start.27 = (bf16[320,1280]{1,0:T(8,128)(2,1)S(1)}, bf16[320,1280]{1,0:T(8,128)(2,1)S(1)}, u32[]{:S(2)}, u32[]{:S(2)}) collective-permute-start(bf16[320,1280]{1,0:T(8,128)(2,1)S(1)} %weights.15), channel_id=1, source_target_pairs={{0,1},{1,0},{2,3},{3,2},{4,5},{5,4},{6,7},{7,6},{8,9},{9,8},{10,11... | collective-permute-start | bytes 2457608 | tf_op jit(solution)/shard_map/ppermute | solution.py:232
  91.0 20.7 %collective-permute-start.26 = (bf16[320,1280]{1,0:T(8,128)(2,1)S(1)}, bf16[320,1280]{1,0:T(8,128)(2,1)S(1)}, u32[]{:S(2)}, u32[]{:S(2)}) collective-permute-start(bf16[320,1280]{1,0:T(8,128)(2,1)S(1)} %half.3), channel_id=1, source_target_pairs={{0,4},{4,0},{8,12},{12,8},{16,20},{20,16},{24,28},{28,24},{1,5},{5... | collective-permute-start | bytes 2457608 | tf_op jit(solution)/shard_map/ppermute | solution.py:229
  91.6 20.2 %collective-permute-start.28 = (f32[8,1280]{1,0:T(8,128)S(1)}, f32[8,1280]{1,0:T(8,128)S(1)}, u32[]{:S(2)}, u32[]{:S(2)}) collective-permute-start(f32[8,1280]{1,0:T(8,128)S(1)} %add.38.total_ref), channel_id=1, source_target_pairs={{0,2},{1,3},{2,0},{3,1},{4,6},{5,7},{6,4},{7,5},{8,10},{9,11},{10,... | collective-permute-start | bytes 122888 | tf_op jit(solution)/shard_map/ppermute | solution.py:478
  92.6 16.2 %collective-permute-start.23 = (bf16[80,1280]{1,0:T(8,128)(2,1)S(1)}, bf16[80,1280]{1,0:T(8,128)(2,1)S(1)}, u32[]{:S(2)}, u32[]{:S(2)}) collective-permute-start(bf16[80,1280]{1,0:T(8,128)(2,1)S(1)} %bitcast.73), channel_id=1, source_target_pairs={{0,16},{4,20},{8,24},{12,28},{16,0},{20,4},{24,8},{28,12},{1,17},{... | collective-permute-start | bytes 614408 | tf_op jit(solution)/shard_map/ppermute | solution.py:247
  94.4 14.4 %collective-permute-start.24 = (bf16[80,1280]{1,0:T(8,128)(2,1)S(1)}, bf16[80,1280]{1,0:T(8,128)(2,1)S(1)}, u32[]{:S(2)}, u32[]{:S(2)}) collective-permute-start(bf16[80,1280]{1,0:T(8,128)(2,1)S(1)} %get-tuple-element.151), channel_id=1, source_target_pairs={{0,8},{4,12},{8,16},{12,20},{16,24},{20,28},{24,0},{28,4},{1,9},{5... | collective-permute-start | bytes 614408 | tf_op jit(solution)/shard_map/ppermute | solution.py:247
  (11 other events, 86.1 us)

commit v13 on v12

--- a/solution.py
+++ b/solution.py
@@ -106,10 +106,11 @@
 
 def finish_kernel(
     norm_ref, deviation_ref, places_ref, gain_ref, d_ref, rows_ref, stay_ref, pair_ref, other_ref,
-    total_ref, last_ref, out_ref, sum_ref, router_ref, gain_grad_ref
+    sent_ref, out_ref, sum_ref, router_ref, gain_grad_ref
 ):
+    units = sum_ref.shape[0]
     sum_ref[...] = (
-        stay_ref[...] + pair_ref[...].astype(F32) + other_ref[...].astype(F32)
+        stay_ref[...] + pair_ref[...].astype(F32) + other_ref[:units, :].astype(F32)
     ).astype(BF16)
     normalized_rows = norm_ref[...]
     scaled_rows = dot(places_ref[...], rows_ref[...], 0, 0) * gain_ref[...][None, :]
@@ -120,7 +121,9 @@
     )
     out_ref[...] = (d_ref[...].astype(F32) + norm_backward).astype(BF16)
     experts = router_ref.shape[0]
-    total = total_ref[...] + last_ref[...]
+    mine, others = sent_ref[units:, :].astype(F32), other_ref[units:, :].astype(F32)
+    lines = mine.shape[0] // 2
+    total = (mine[:lines] + mine[lines:]) + (others[:lines] + others[lines:])
     router_ref[...] = total[:experts]
     gain_grad_ref[...] = jnp.sum(total[experts:], axis=0) / gain_ref[...]
 
@@ -186,6 +189,14 @@
 
 def half_kernel(stay_ref, pair_ref, out_ref):
     out_ref[...] = (stay_ref[...] + pair_ref[...].astype(F32)).astype(BF16)
+
+
+def half_total_kernel(stay_ref, pair_ref, total_ref, out_ref):
+    units = stay_ref.shape[0]
+    out_ref[:units, :] = (stay_ref[...] + pair_ref[...].astype(F32)).astype(BF16)
+    total = total_ref[...]
+    rounded = total.astype(BF16).astype(F32)
+    out_ref[units:, :] = jnp.concatenate([rounded, total - rounded], axis=0).astype(BF16)
 
 
 def tied(values, after):
@@ -456,27 +467,32 @@
     send_back([steps[at] for at in moved], [early_rows[at] for at in moved])
     moved_rows = [returned[steps[at]] for at in moved]
     total = tied(total, (early_rows, late_rows))
-    total = pairwise(total, "expert", halves, 1)
+    bit = 2
+    while bit < groups:
+        total = pairwise(total, "dp", groups, bit)
+        bit *= 2
     hidden, grad_pre = tied((hidden, grad_pre), in_stay)
     out_rest = over_pair(weight_gradient(1, 1, hidden, grad_y, BF16))
     out_mine = weight_gradient(3, 1, hidden, grad_y, F32)
     in_rest = over_pair(weight_gradient(1, 1, grad_pre, rows_m, BF16))
     in_mine = weight_gradient(3, 1, grad_pre, rows_m, F32)
 
-    stage = (out_other, early_rows, late_rows, moved_rows, in_pair, in_stay, total)
-    out_other, early_rows, late_rows, moved_rows, in_pair, in_stay, total = tied(stage, stage)
+    in_half = call(
+        half_total_kernel,
+        "half",
+        shape(BF16, units + 2 * total.shape[0], width),
+        (in_stay, in_pair, total),
+    )
+    stage = (out_other, early_rows, late_rows, moved_rows, in_half, out_mine, in_mine)
+    out_other, early_rows, late_rows, moved_rows, in_half, out_mine, in_mine = tied(stage, stage)
     for at, value in zip(moved, moved_rows):
         returned[steps[at]] = value
-    in_other = over_half(half_sum(in_stay, in_pair))
+    in_other = over_half(in_half)
+    grad_out = (out_mine + out_rest.astype(F32) + out_other.astype(F32)).astype(BF16)[None]
+    early_rows, late_rows = tied((early_rows, late_rows), grad_out)
     rest = [at for at in range(len(early)) if at not in moved]
     send_back([steps[at] for at in rest], [early_rows[at] for at in rest])
     send_back(late, late_rows)
-    bit = 2
-    while bit < groups // 2:
-        total = pairwise(total, "dp", groups, bit)
-        bit *= 2
-    last = lax.ppermute(total, "dp", [(i, i ^ bit) for i in range(groups)])
-    grad_out = (out_mine + out_rest.astype(F32) + out_other.astype(F32)).astype(BF16)[None]
 
     returned = tied(returned, (in_other, grad_out))
     norm, deviation, places = prepared
@@ -499,8 +515,7 @@
             in_mine,
             in_rest,
             in_other,
-            total,
-            last,
+            in_half,
         ),
     )
     return (input_grad, grad_in.T[None], grad_out, grad_router.T, grad_gain)

time: 114 us -> 113 us (level)
    ppermute x4, waiting for transfers between devices: 6.92 us -> 4.39 us  [pairwise(): lax.ppermute(value, name, [(i, i ^ bit) for i in range(size)])]
  transfers between devices with their start and end apart: 29 -> 28, of which waited for: 9 -> 10; matrix products, arithmetic and copies ran while one was open for 5% -> 5% of each run, Pallas kernels for 17% -> 17%
where the time goes in v13:
time: 113 us
  waiting for transfers between devices  51.5 us (46%)
  starting transfers between devices  30 us (27%)
  Pallas kernels  23.9 us (21%)
  local copies, waits for them, and re-layouts  4.46 us (4%)
  other arithmetic  2.37 us (2%)
    ppermute x6, waiting for transfers between devices, over_experts(): lax.ppermute(value, 'expert', [(i, (i + 2 * step) % halves) for i in rang...  42.6 us
    pallas_call x21, Pallas kernels, call(): pl.pallas_call(kernel, out_shape=outs, in_specs=specs or [VMEM] * len(arg...  23.9 us
    ppermute x6, starting transfers between devices, over_experts(): lax.ppermute(value, 'expert', [(i, (i + 2 * step) % halves) for i in rang...  11.6 us
    ppermute x4, starting transfers between devices, pairwise(): lax.ppermute(value, name, [(i, i ^ bit) for i in range(size)])  5.78 us
    ppermute x4, starting transfers between devices, over_columns(): lax.ppermute(value, 'dp', [(i, (i + 2 * step) % groups) for i in range(gr...  5.06 us
    ppermute x4, starting transfers between devices, over_half(): return lax.ppermute(value, 'expert', [(i, i ^ 1) for i in range(halves)])  5.02 us
    ppermute x4, waiting for transfers between devices, over_half(): return lax.ppermute(value, 'expert', [(i, i ^ 1) for i in range(halves)])  4.47 us
    ppermute x4, waiting for transfers between devices, pairwise(): lax.ppermute(value, name, [(i, i ^ bit) for i in range(size)])  4.39 us
  transfers between devices with their start and end apart: 28, of which 10 were waited for; matrix products, arithmetic and copies ran while one was open for 5% of the time, Pallas kernels for 17%

profile of v13, /device:TPU:0, one launch (start us, length us, event | category | flops | bytes accessed | tf_op | source)
XLA Modules:
  0.0 113.2 jit_solution(15112958339500199720)
XLA Ops:
  0.6 2.8 %dispatch.1 = (bf16[2,80,1280]{2,1,0:T(8,128)(2,1)}, bf16[2,80,1280]{2,1,0:T(8,128)(2,1)}, bf16[2,80,1280]{2,1,0:T(8,128)(2,1)}, bf16[2,80,1280]{2,1,0:T(8,128)(2,1)}) custom-call(bf16[128,1280]{1,0:T(8,128)(2,1)} %x_ref.1, f32[1280]{0:T(1024)} %gain_ref.1, s32[2,128]{1,0:T(2,128)} %bitcast.70, bf16[128,1280]{1,0:T(8,128)(2,1)} %d_ref.1), custom_call_target="tpu_custom_call" | custom-call | flops 209715200 | bytes 409600 | tf_op jit(solution)/shard_map/dispatch/pallas_call | solution.py:216
  3.4 3.0 %collective-permute-start.4 = (bf16[320,1280]{1,0:T(8,128)(2,1)}, bf16[320,1280]{1,0:T(8,128)(2,1)S(1)}, u32[]{:S(2)}, u32[]{:S(2)}) collective-permute-start(bf16[320,1280]{1,0:T(8,128)(2,1)} %bitcast.64), channel_id=1, source_target_pairs={{0,4},{4,0},{8,12},{12,8},{16,20},{20,16},{24,28},{28,24},{1,5},{5... | collective-permute-start | bytes 2457608 | tf_op jit(solution)/shard_map/ppermute | solution.py:240
  6.5 3.6 %collective-permute-start = (bf16[2,80,1280]{2,1,0:T(8,128)(2,1)}, bf16[2,80,1280]{2,1,0:T(8,128)(2,1)S(1)}, u32[]{:S(2)}, u32[]{:S(2)}) collective-permute-start(bf16[2,80,1280]{2,1,0:T(8,128)(2,1)} %get-tuple-element.79), channel_id=1, source_target_pairs={{0,24},{4,28},{8,0},{12,4},{16,8},{20,12},{24,16},{28,20},{1,25},{... | collective-permute-start | bytes 1228808 | tf_op jit(solution)/shard_map/ppermute | solution.py:258
  14.3 6.0 %collective-permute-done = bf16[2,80,1280]{2,1,0:T(8,128)(2,1)S(1)} collective-permute-done((bf16[2,80,1280]{2,1,0:T(8,128)(2,1)}, bf16[2,80,1280]{2,1,0:T(8,128)(2,1)S(1)}, u32[]{:S(2)}, u32[]{:S(2)}) %collective-permute-start) | collective-permute-done | bytes 409632 | tf_op jit(solution)/shard_map/ppermute | solution.py:258
  20.2 9.1 %collective-permute-done.1 = bf16[2,80,1280]{2,1,0:T(8,128)(2,1)S(1)} collective-permute-done((bf16[2,80,1280]{2,1,0:T(8,128)(2,1)}, bf16[2,80,1280]{2,1,0:T(8,128)(2,1)S(1)}, u32[]{:S(2)}, u32[]{:S(2)}) %collective-permute-start.1) | collective-permute-done | bytes 409632 | tf_op jit(solution)/shard_map/ppermute | solution.py:258
  30.2 1.5 %collective-permute-start.7 = (bf16[2,80,1280]{2,1,0:T(8,128)(2,1)S(1)}, bf16[2,80,1280]{2,1,0:T(8,128)(2,1)S(1)}, u32[]{:S(2)}, u32[]{:S(2)}) collective-permute-start(bf16[2,80,1280]{2,1,0:T(8,128)(2,1)S(1)} %collective-permute-done), channel_id=1, source_target_pairs={{0,2},{1,3},{2,0},{3,1},{4,6},{5,7},{6,4},{7,5},{8,10},{9,11},{10,... | collective-permute-start | bytes 1228808 | tf_op jit(solution)/shard_map/ppermute | solution.py:247
  35.1 15.3 %collective-permute-done.5 = bf16[2,80,1280]{2,1,0:T(8,128)(2,1)S(1)} collective-permute-done((bf16[2,80,1280]{2,1,0:T(8,128)(2,1)}, bf16[2,80,1280]{2,1,0:T(8,128)(2,1)S(1)}, u32[]{:S(2)}, u32[]{:S(2)}) %collective-permute-start.5) | collective-permute-done | bytes 409632 | tf_op jit(solution)/shard_map/ppermute | solution.py:258
  50.4 1.6 %collective-permute-start.13 = (bf16[2,80,1280]{2,1,0:T(8,128)(2,1)S(1)}, bf16[2,80,1280]{2,1,0:T(8,128)(2,1)S(1)}, u32[]{:S(2)}, u32[]{:S(2)}) collective-permute-start(bf16[2,80,1280]{2,1,0:T(8,128)(2,1)S(1)} %collective-permute-done.5), channel_id=1, source_target_pairs={{0,2},{1,3},{2,0},{3,1},{4,6},{5,7},{6,4},{7,5},{8,10},{9,11},{10,... | collective-permute-start | bytes 1228808 | tf_op jit(solution)/shard_map/ppermute | solution.py:247
  53.3 3.3 %first.2 = (bf16[480,1280]{1,0:T(8,128)(2,1)S(1)}, f32[480,1280]{1,0:T(8,128)S(1)}, bf16[480,1280]{1,0:T(8,128)(2,1)S(1)}, f32[480,128]{1,0:T(8,128)S(1)}) custom-call(bf16[480,1280]{1,0:T(8,128)(2,1)S(1)} %get-tuple-element.159.m_ref, bf16[480,1280]{1,0:T(8,128)(2,1)S(1)} %get-tuple-element.158.d_ref, bf16[1280,1280]{1,0:T(8,128)(2,1)S(1)} %join.3.first_ref, ...), custom_call_target="tpu_custom_call" | custom-call | flops 1572864000 | bytes 3072000 | tf_op jit(solution)/shard_map/first/pallas_call | solution.py:216
  57.0 2.1 %second.2 = (bf16[480,1280]{1,0:T(8,128)(2,1)S(1)}, f32[480,128]{1,0:T(8,128)S(1)}) custom-call(bf16[480,1280]{1,0:T(8,128)(2,1)S(1)} %get-tuple-element.158.d_ref, bf16[1280,1280]{1,0:T(8,128)(2,1)S(1)} %join.2.second_ref, bf16[480,1280]{1,0:T(8,128)(2,1)S(1)} %get-tuple-element.101.hidden_ref, f32[480,1280]{1,0:T(8,128)S(1)} %get-tuple-element.102.slope_ref, ...), custom_call_target="tpu_custom_call" | custom-call | flops 1572864000 | bytes 3072000 | tf_op jit(solution)/shard_map/second/pallas_call | solution.py:216
  59.1 1.9 %rows.2 = (f32[240,1280]{1,0:T(8,128)S(1)}, bf16[240,1280]{1,0:T(8,128)(2,1)S(1)}, f32[8,1280]{1,0:T(8,128)S(1)}) custom-call(bf16[480,1280]{1,0:T(8,128)(2,1)S(1)} %get-tuple-element.159.m_ref, bf16[480,1280]{1,0:T(8,128)(2,1)S(1)} %get-tuple-element.104.pre_ref, f32[480,128]{1,0:T(8,128)S(1)} %get-tuple-element.105.logit_ref, ...), custom_call_target="tpu_custom_call" | custom-call | flops 1572864000 | bytes 3072000 | tf_op jit(solution)/shard_map/rows/pallas_call | solution.py:216
  61.0 1.6 %collective-permute-start.12 = (bf16[240,1280]{1,0:T(8,128)(2,1)S(1)}, bf16[240,1280]{1,0:T(8,128)(2,1)S(1)}, u32[]{:S(2)}, u32[]{:S(2)}) collective-permute-start(bf16[240,1280]{1,0:T(8,128)(2,1)S(1)} %get-tuple-element.107), channel_id=1, source_target_pairs={{0,2},{1,3},{2,0},{3,1},{4,6},{5,7},{6,4},{7,5},{8,10},{9,11},{10,... | collective-permute-start | bytes 1843208 | tf_op jit(solution)/shard_map/ppermute | solution.py:253
  62.7 1.5 %first.3 = (bf16[160,1280]{1,0:T(8,128)(2,1)S(1)}, f32[160,1280]{1,0:T(8,128)S(1)}, bf16[160,1280]{1,0:T(8,128)(2,1)S(1)}, f32[160,128]{1,0:T(8,128)S(1)}) custom-call(bf16[160,1280]{1,0:T(8,128)(2,1)S(1)} %pad_maximum_fusion.2.m_ref, bf16[160,1280]{1,0:T(8,128)(2,1)S(1)} %pad_maximum_fusion.3.d_ref, bf16[1280,1280]{1,0:T(8,128)(2,1)S(1)} %join.3.first_ref, ...), custom_call_target="tpu_custom_call" | custom-call | flops 524288000 | bytes 1024000 | tf_op jit(solution)/shard_map/first/pallas_call | solution.py:216
  70.3 1.6 %collective-permute-start.17 = (f32[8,1280]{1,0:T(8,128)S(1)}, f32[8,1280]{1,0:T(8,128)S(1)}, u32[]{:S(2)}, u32[]{:S(2)}) collective-permute-start(f32[8,1280]{1,0:T(8,128)S(1)} %add.33), channel_id=1, source_target_pairs={{0,8},{4,12},{8,0},{12,4},{16,24},{20,28},{24,16},{28,20},{1,9},{5... | collective-permute-start | bytes 122888 | tf_op jit(solution)/shard_map/ppermute | solution.py:261
  76.1 2.3 %collective-permute-start.18 = (f32[8,1280]{1,0:T(8,128)S(1)}, f32[8,1280]{1,0:T(8,128)S(1)}, u32[]{:S(2)}, u32[]{:S(2)}) collective-permute-start(f32[8,1280]{1,0:T(8,128)S(1)} %add.34), channel_id=1, source_target_pairs={{0,16},{4,20},{8,24},{12,28},{16,0},{20,4},{24,8},{28,12},{1,17},{... | collective-permute-start | bytes 122888 | tf_op jit(solution)/shard_map/ppermute | solution.py:261
  79.3 2.5 %collective-permute-done.18 = f32[8,1280]{1,0:T(8,128)S(1)} collective-permute-done((f32[8,1280]{1,0:T(8,128)S(1)}, f32[8,1280]{1,0:T(8,128)S(1)}, u32[]{:S(2)}, u32[]{:S(2)}) %collective-permute-start.18) | collective-permute-done | bytes 40992 | tf_op jit(solution)/shard_map/ppermute | solution.py:261
  82.0 3.2 %collective-permute-start.19 = (bf16[80,1280]{1,0:T(8,128)(2,1)S(1)}, bf16[80,1280]{1,0:T(8,128)(2,1)S(1)}, u32[]{:S(2)}, u32[]{:S(2)}) collective-permute-start(bf16[80,1280]{1,0:T(8,128)(2,1)S(1)} %slice.87), channel_id=1, source_target_pairs={{0,24},{4,28},{8,0},{12,4},{16,8},{20,12},{24,16},{28,20},{1,25},{... | collective-permute-start | bytes 614408 | tf_op jit(solution)/shard_map/ppermute | solution.py:258
  85.3 1.5 %collective-permute-start.22 = (f32[8,1280]{1,0:T(8,128)S(1)}, f32[8,1280]{1,0:T(8,128)S(1)}, u32[]{:S(2)}, u32[]{:S(2)}) collective-permute-start(f32[8,1280]{1,0:T(8,128)S(1)} %add.35), channel_id=1, source_target_pairs={{0,2},{1,3},{2,0},{3,1},{4,6},{5,7},{6,4},{7,5},{8,10},{9,11},{10,... | collective-permute-start | bytes 122888 | tf_op jit(solution)/shard_map/ppermute | solution.py:261
  87.7 1.7 %collective-permute-done.22 = f32[8,1280]{1,0:T(8,128)S(1)} collective-permute-done((f32[8,1280]{1,0:T(8,128)S(1)}, f32[8,1280]{1,0:T(8,128)S(1)}, u32[]{:S(2)}, u32[]{:S(2)}) %collective-permute-start.22) | collective-permute-done | bytes 40992 | tf_op jit(solution)/shard_map/ppermute | solution.py:261
  92.0 1.8 %collective-permute-start.24 = (bf16[80,1280]{1,0:T(8,128)(2,1)S(1)}, bf16[80,1280]{1,0:T(8,128)(2,1)S(1)}, u32[]{:S(2)}, u32[]{:S(2)}) collective-permute-start(bf16[80,1280]{1,0:T(8,128)(2,1)S(1)} %bitcast.73), channel_id=1, source_target_pairs={{0,16},{4,20},{8,24},{12,28},{16,0},{20,4},{24,8},{28,12},{1,17},{... | collective-permute-start | bytes 614408 | tf_op jit(solution)/shard_map/ppermute | solution.py:258
  93.8 2.1 %collective-permute-start.25 = (bf16[80,1280]{1,0:T(8,128)(2,1)S(1)}, bf16[80,1280]{1,0:T(8,128)(2,1)S(1)}, u32[]{:S(2)}, u32[]{:S(2)}) collective-permute-start(bf16[80,1280]{1,0:T(8,128)(2,1)S(1)} %get-tuple-element.155), channel_id=1, source_target_pairs={{0,8},{4,12},{8,16},{12,20},{16,24},{20,28},{24,0},{28,4},{1,9},{5... | collective-permute-start | bytes 614408 | tf_op jit(solution)/shard_map/ppermute | solution.py:258
  96.0 12.1 %collective-permute-done.24 = bf16[80,1280]{1,0:T(8,128)(2,1)S(1)} collective-permute-done((bf16[80,1280]{1,0:T(8,128)(2,1)S(1)}, bf16[80,1280]{1,0:T(8,128)(2,1)S(1)}, u32[]{:S(2)}, u32[]{:S(2)}) %collective-permute-start.24) | collective-permute-done | bytes 204832 | tf_op jit(solution)/shard_map/ppermute | solution.py:258
  108.1 3.0 %collective-permute-done.26.other_ref = bf16[336,1280]{1,0:T(8,128)(2,1)S(1)} collective-permute-done((bf16[336,1280]{1,0:T(8,128)(2,1)S(1)}, bf16[336,1280]{1,0:T(8,128)(2,1)S(1)}, u32[]{:S(2)}, u32[]{:S(2)}) %collective-permute-start.26) | collective-permute-done | bytes 860192 | tf_op jit(solution)/shard_map/ppermute | solution.py:240
  111.2 2.0 %finish.1 = (bf16[128,1280]{1,0:T(8,128)(2,1)}, bf16[320,1280]{1,0:T(8,128)(2,1)}, f32[4,1280]{1,0:T(4,128)}, f32[1280]{0:T(1024)}) custom-call(f32[128,1280]{1,0:T(8,128)S(1)} %get-tuple-element.92.norm_ref, f32[128,128]{1,0:T(8,128)S(1)} %get-tuple-element.93.deviation_ref, bf16[320,128]{1,0:T(8,128)(2,1)S(1)} %get-tuple-element.94.places_ref, ...), custom_call_target="tpu_custom_call" | custom-call | tf_op jit(solution)/shard_map/finish/pallas_call | solution.py:216
  (95 shorter events, 25.0 us)
Async XLA Ops:
  3.4 25.9 %collective-permute-start.4 = (bf16[320,1280]{1,0:T(8,128)(2,1)}, bf16[320,1280]{1,0:T(8,128)(2,1)S(1)}, u32[]{:S(2)}, u32[]{:S(2)}) collective-permute-start(bf16[320,1280]{1,0:T(8,128)(2,1)} %bitcast.64), channel_id=1, source_target_pairs={{0,4},{4,0},{8,12},{12,8},{16,20},{20,16},{24,28},{28,24},{1,5},{5... | collective-permute-start | bytes 2457608 | tf_op jit(solution)/shard_map/ppermute | solution.py:240
  6.5 22.9 %collective-permute-start.2 = (bf16[320,1280]{1,0:T(8,128)(2,1)}, bf16[320,1280]{1,0:T(8,128)(2,1)S(1)}, u32[]{:S(2)}, u32[]{:S(2)}) collective-permute-start(bf16[320,1280]{1,0:T(8,128)(2,1)} %bitcast.65), channel_id=1, source_target_pairs={{0,1},{1,0},{2,3},{3,2},{4,5},{5,4},{6,7},{7,6},{8,9},{9,8},{10,11... | collective-permute-start | bytes 2457608 | tf_op jit(solution)/shard_map/ppermute | solution.py:243
  6.5 13.8 %collective-permute-start = (bf16[2,80,1280]{2,1,0:T(8,128)(2,1)}, bf16[2,80,1280]{2,1,0:T(8,128)(2,1)S(1)}, u32[]{:S(2)}, u32[]{:S(2)}) collective-permute-start(bf16[2,80,1280]{2,1,0:T(8,128)(2,1)} %get-tuple-element.79), channel_id=1, source_target_pairs={{0,24},{4,28},{8,0},{12,4},{16,8},{20,12},{24,16},{28,20},{1,25},{... | collective-permute-start | bytes 1228808 | tf_op jit(solution)/shard_map/ppermute | solution.py:258
  10.1 19.3 %collective-permute-start.1 = (bf16[2,80,1280]{2,1,0:T(8,128)(2,1)}, bf16[2,80,1280]{2,1,0:T(8,128)(2,1)S(1)}, u32[]{:S(2)}, u32[]{:S(2)}) collective-permute-start(bf16[2,80,1280]{2,1,0:T(8,128)(2,1)} %get-tuple-element.80), channel_id=1, source_target_pairs={{0,8},{4,12},{8,16},{12,20},{16,24},{20,28},{24,0},{28,4},{1,9},{5... | collective-permute-start | bytes 1228808 | tf_op jit(solution)/shard_map/ppermute | solution.py:258
  10.1 19.3 %collective-permute-start.3 = (bf16[2,80,1280]{2,1,0:T(8,128)(2,1)}, bf16[2,80,1280]{2,1,0:T(8,128)(2,1)}, u32[]{:S(2)}, u32[]{:S(2)}) collective-permute-start(bf16[2,80,1280]{2,1,0:T(8,128)(2,1)} %get-tuple-element.95), channel_id=1, source_target_pairs={{0,2},{1,3},{2,0},{3,1},{4,6},{5,7},{6,4},{7,5},{8,10},{9,11},{10,... | collective-permute-start | bytes 1228808 | tf_op jit(solution)/shard_map/ppermute | solution.py:247
  29.4 21.0 %collective-permute-start.5 = (bf16[2,80,1280]{2,1,0:T(8,128)(2,1)}, bf16[2,80,1280]{2,1,0:T(8,128)(2,1)S(1)}, u32[]{:S(2)}, u32[]{:S(2)}) collective-permute-start(bf16[2,80,1280]{2,1,0:T(8,128)(2,1)} %get-tuple-element.84), channel_id=1, source_target_pairs={{0,16},{4,20},{8,24},{12,28},{16,0},{20,4},{24,8},{28,12},{1,17},{... | collective-permute-start | bytes 1228808 | tf_op jit(solution)/shard_map/ppermute | solution.py:258
  30.2 20.3 %collective-permute-start.7 = (bf16[2,80,1280]{2,1,0:T(8,128)(2,1)S(1)}, bf16[2,80,1280]{2,1,0:T(8,128)(2,1)S(1)}, u32[]{:S(2)}, u32[]{:S(2)}) collective-permute-start(bf16[2,80,1280]{2,1,0:T(8,128)(2,1)S(1)} %collective-permute-done), channel_id=1, source_target_pairs={{0,2},{1,3},{2,0},{3,1},{4,6},{5,7},{6,4},{7,5},{8,10},{9,11},{10,... | collective-permute-start | bytes 1228808 | tf_op jit(solution)/shard_map/ppermute | solution.py:247
  31.7 18.8 %collective-permute-start.8 = (bf16[2,80,1280]{2,1,0:T(8,128)(2,1)S(1)}, bf16[2,80,1280]{2,1,0:T(8,128)(2,1)S(1)}, u32[]{:S(2)}, u32[]{:S(2)}) collective-permute-start(bf16[2,80,1280]{2,1,0:T(8,128)(2,1)S(1)} %collective-permute-done.1), channel_id=1, source_target_pairs={{0,2},{1,3},{2,0},{3,1},{4,6},{5,7},{6,4},{7,5},{8,10},{9,11},{10,... | collective-permute-start | bytes 1228808 | tf_op jit(solution)/shard_map/ppermute | solution.py:247
  32.2 18.2 %collective-permute-start.6 = (bf16[320,1280]{1,0:T(8,128)(2,1)S(1)}, bf16[320,1280]{1,0:T(8,128)(2,1)S(1)}, u32[]{:S(2)}, u32[]{:S(2)}) collective-permute-start(bf16[320,1280]{1,0:T(8,128)(2,1)S(1)} %collective-permute-done.4.refs_2_), channel_id=1, source_target_pairs={{0,1},{1,0},{2,3},{3,2},{4,5},{5,4},{6,7},{7,6},{8,9},{9,8},{10,11... | collective-permute-start | bytes 2457608 | tf_op jit(solution)/shard_map/ppermute | solution.py:243
  32.2 20.9 %collective-permute-start.9 = (bf16[320,1280]{1,0:T(8,128)(2,1)}, bf16[320,1280]{1,0:T(8,128)(2,1)S(1)}, u32[]{:S(2)}, u32[]{:S(2)}) collective-permute-start(bf16[320,1280]{1,0:T(8,128)(2,1)} %bitcast.67), channel_id=1, source_target_pairs={{0,4},{4,0},{8,12},{12,8},{16,20},{20,16},{24,28},{28,24},{1,5},{5... | collective-permute-start | bytes 2457608 | tf_op jit(solution)/shard_map/ppermute | solution.py:240
  50.4 12.1 %collective-permute-start.13 = (bf16[2,80,1280]{2,1,0:T(8,128)(2,1)S(1)}, bf16[2,80,1280]{2,1,0:T(8,128)(2,1)S(1)}, u32[]{:S(2)}, u32[]{:S(2)}) collective-permute-start(bf16[2,80,1280]{2,1,0:T(8,128)(2,1)S(1)} %collective-permute-done.5), channel_id=1, source_target_pairs={{0,2},{1,3},{2,0},{3,1},{4,6},{5,7},{6,4},{7,5},{8,10},{9,11},{10,... | collective-permute-start | bytes 1228808 | tf_op jit(solution)/shard_map/ppermute | solution.py:247
  52.0 4.8 %collective-permute-start.11 = (bf16[320,1280]{1,0:T(8,128)(2,1)S(1)}, bf16[320,1280]{1,0:T(8,128)(2,1)S(1)}, u32[]{:S(2)}, u32[]{:S(2)}) collective-permute-start(bf16[320,1280]{1,0:T(8,128)(2,1)S(1)} %bitcast.68), channel_id=1, source_target_pairs={{0,1},{1,0},{2,3},{3,2},{4,5},{5,4},{6,7},{7,6},{8,9},{9,8},{10,11... | collective-permute-start | bytes 2457608 | tf_op jit(solution)/shard_map/ppermute | solution.py:243
  61.0 20.8 %collective-permute-start.12 = (bf16[240,1280]{1,0:T(8,128)(2,1)S(1)}, bf16[240,1280]{1,0:T(8,128)(2,1)S(1)}, u32[]{:S(2)}, u32[]{:S(2)}) collective-permute-start(bf16[240,1280]{1,0:T(8,128)(2,1)S(1)} %get-tuple-element.107), channel_id=1, source_target_pairs={{0,2},{1,3},{2,0},{3,1},{4,6},{5,7},{6,4},{7,5},{8,10},{9,11},{10,... | collective-permute-start | bytes 1843208 | tf_op jit(solution)/shard_map/ppermute | solution.py:253
  69.5 20.4 %collective-permute-start.20 = (bf16[320,1280]{1,0:T(8,128)(2,1)S(1)}, bf16[320,1280]{1,0:T(8,128)(2,1)S(1)}, u32[]{:S(2)}, u32[]{:S(2)}) collective-permute-start(bf16[320,1280]{1,0:T(8,128)(2,1)S(1)} %half.2), channel_id=1, source_target_pairs={{0,4},{4,0},{8,12},{12,8},{16,20},{20,16},{24,28},{28,24},{1,5},{5... | collective-permute-start | bytes 2457608 | tf_op jit(solution)/shard_map/ppermute | solution.py:240
  70.3 5.7 %collective-permute-start.17 = (f32[8,1280]{1,0:T(8,128)S(1)}, f32[8,1280]{1,0:T(8,128)S(1)}, u32[]{:S(2)}, u32[]{:S(2)}) collective-permute-start(f32[8,1280]{1,0:T(8,128)S(1)} %add.33), channel_id=1, source_target_pairs={{0,8},{4,12},{8,0},{12,4},{16,24},{20,28},{24,16},{28,20},{1,9},{5... | collective-permute-start | bytes 122888 | tf_op jit(solution)/shard_map/ppermute | solution.py:261
  71.9 9.9 %collective-permute-start.16 = (bf16[80,1280]{1,0:T(8,128)(2,1)S(1)}, bf16[80,1280]{1,0:T(8,128)(2,1)S(1)}, u32[]{:S(2)}, u32[]{:S(2)}) collective-permute-start(bf16[80,1280]{1,0:T(8,128)(2,1)S(1)} %get-tuple-element.126), channel_id=1, source_target_pairs={{0,2},{1,3},{2,0},{3,1},{4,6},{5,7},{6,4},{7,5},{8,10},{9,11},{10,... | collective-permute-start | bytes 614408 | tf_op jit(solution)/shard_map/ppermute | solution.py:253
  73.4 16.0 %collective-permute-start.21 = (bf16[320,1280]{1,0:T(8,128)(2,1)S(1)}, bf16[320,1280]{1,0:T(8,128)(2,1)S(1)}, u32[]{:S(2)}, u32[]{:S(2)}) collective-permute-start(bf16[320,1280]{1,0:T(8,128)(2,1)S(1)} %weights.10), channel_id=1, source_target_pairs={{0,1},{1,0},{2,3},{3,2},{4,5},{5,4},{6,7},{7,6},{8,9},{9,8},{10,11... | collective-permute-start | bytes 2457608 | tf_op jit(solution)/shard_map/ppermute | solution.py:243
  76.1 5.7 %collective-permute-start.18 = (f32[8,1280]{1,0:T(8,128)S(1)}, f32[8,1280]{1,0:T(8,128)S(1)}, u32[]{:S(2)}, u32[]{:S(2)}) collective-permute-start(f32[8,1280]{1,0:T(8,128)S(1)} %add.34), channel_id=1, source_target_pairs={{0,16},{4,20},{8,24},{12,28},{16,0},{20,4},{24,8},{28,12},{1,17},{... | collective-permute-start | bytes 122888 | tf_op jit(solution)/shard_map/ppermute | solution.py:261
  81.7 9.1 %collective-permute-start.23 = (bf16[320,1280]{1,0:T(8,128)(2,1)S(1)}, bf16[320,1280]{1,0:T(8,128)(2,1)S(1)}, u32[]{:S(2)}, u32[]{:S(2)}) collective-permute-start(bf16[320,1280]{1,0:T(8,128)(2,1)S(1)} %weights.14), channel_id=1, source_target_pairs={{0,1},{1,0},{2,3},{3,2},{4,5},{5,4},{6,7},{7,6},{8,9},{9,8},{10,11... | collective-permute-start | bytes 2457608 | tf_op jit(solution)/shard_map/ppermute | solution.py:243
  82.0 7.5 %collective-permute-start.19 = (bf16[80,1280]{1,0:T(8,128)(2,1)S(1)}, bf16[80,1280]{1,0:T(8,128)(2,1)S(1)}, u32[]{:S(2)}, u32[]{:S(2)}) collective-permute-start(bf16[80,1280]{1,0:T(8,128)(2,1)S(1)} %slice.87), channel_id=1, source_target_pairs={{0,24},{4,28},{8,0},{12,4},{16,8},{20,12},{24,16},{28,20},{1,25},{... | collective-permute-start | bytes 614408 | tf_op jit(solution)/shard_map/ppermute | solution.py:258
  89.3 21.8 %collective-permute-start.27 = (bf16[320,1280]{1,0:T(8,128)(2,1)S(1)}, bf16[320,1280]{1,0:T(8,128)(2,1)S(1)}, u32[]{:S(2)}, u32[]{:S(2)}) collective-permute-start(bf16[320,1280]{1,0:T(8,128)(2,1)S(1)} %weights.15), channel_id=1, source_target_pairs={{0,1},{1,0},{2,3},{3,2},{4,5},{5,4},{6,7},{7,6},{8,9},{9,8},{10,11... | collective-permute-start | bytes 2457608 | tf_op jit(solution)/shard_map/ppermute | solution.py:243
  89.9 21.2 %collective-permute-start.26 = (bf16[336,1280]{1,0:T(8,128)(2,1)S(1)}, bf16[336,1280]{1,0:T(8,128)(2,1)S(1)}, u32[]{:S(2)}, u32[]{:S(2)}) collective-permute-start(bf16[336,1280]{1,0:T(8,128)(2,1)S(1)} %half.3.sent_ref), channel_id=1, source_target_pairs={{0,4},{4,0},{8,12},{12,8},{16,20},{20,16},{24,28},{28,24},{1,5},{5... | collective-permute-start | bytes 2580488 | tf_op jit(solution)/shard_map/ppermute | solution.py:240
  92.0 16.1 %collective-permute-start.24 = (bf16[80,1280]{1,0:T(8,128)(2,1)S(1)}, bf16[80,1280]{1,0:T(8,128)(2,1)S(1)}, u32[]{:S(2)}, u32[]{:S(2)}) collective-permute-start(bf16[80,1280]{1,0:T(8,128)(2,1)S(1)} %bitcast.73), channel_id=1, source_target_pairs={{0,16},{4,20},{8,24},{12,28},{16,0},{20,4},{24,8},{28,12},{1,17},{... | collective-permute-start | bytes 614408 | tf_op jit(solution)/shard_map/ppermute | solution.py:258
  93.8 14.3 %collective-permute-start.25 = (bf16[80,1280]{1,0:T(8,128)(2,1)S(1)}, bf16[80,1280]{1,0:T(8,128)(2,1)S(1)}, u32[]{:S(2)}, u32[]{:S(2)}) collective-permute-start(bf16[80,1280]{1,0:T(8,128)(2,1)S(1)} %get-tuple-element.155), channel_id=1, source_target_pairs={{0,8},{4,12},{8,16},{12,20},{16,24},{20,28},{24,0},{28,4},{1,9},{5... | collective-permute-start | bytes 614408 | tf_op jit(solution)/shard_map/ppermute | solution.py:258
  (10 other events, 90.1 us)
